TPU v7x, 32 devices: a whole 2x2x4 slice. The times are simulated.
32 devices in a mesh: seg: 8 (over z, core), fsdp: 4 (over y, x).
Axes of the slice: x: 2, y: 2, z: 4, core: 2. Of those that a mesh axis runs over, the one named last changes fastest.
Arguments:
- frames: bfloat16 [4, 64, 16, 1024], P('fsdp', 'seg'), may hold values from -6 to 6
- memory_in: bfloat16 [4, 64, 1024], P('fsdp', 'seg'), may hold values from -6 to 6
- lengths: int32 [4], P('fsdp'), may hold values from 1 to 64, as said below
- ln_gain: float32 [1024], replicated, may hold values from 0.25 to 1.75
- w_query: bfloat16 [1024, 1024], P('fsdp'), may hold values from -1 to 1
- w_key: bfloat16 [1024, 1024], P('fsdp'), may hold values from -12 to 12
- w_value: bfloat16 [1024, 1024], P('fsdp'), may hold values from -0.1875 to 0.1875
- w_out: bfloat16 [1024, 1024], P('fsdp'), may hold values from -0.1875 to 0.1875
- grad_frames: bfloat16 [4, 64, 16, 1024], P('fsdp', 'seg'), may hold values from -6 to 6
- grad_memory: bfloat16 [4, 64, 1024], P('fsdp', 'seg'), may hold values from -6 to 6
Outputs:
- frames_out: bfloat16 [4, 64, 16, 1024], P('fsdp', 'seg')
- memory_out: bfloat16 [4, 64, 1024], P('fsdp', 'seg')
- value_grad: float32 [1024, 1024], P('fsdp')
Inputs may be any that keep to these rules, and one draw needn't show every extreme that they name: `lengths`: in every aligned block of 1 utterances (those of one fsdp index) at least one has length 64.
All inputs are finite; a program needn't handle non-finite values.
Results may differ from a plain program's by a relative error of at most 0.04.
Values may be sent and summed in bfloat16 or wider, within the bound.
No kernel may reach another device: no remote copies, remote signals or barrier semaphores. Data moves between devices by JAX's collectives and lax.ppermute only.
A program may use at most 64 MiB of HBM per device.

v0:
```python
import math

import jax
import jax.numpy as jnp
from jax import lax
from jax.sharding import PartitionSpec as P

HEADS = 16
LEFT = 16
MEMORY = 8


epsilon = 1e-05
masked_score = -1e30


def passed_along(array, axis, by):
    size = lax.axis_size(axis)
    pairs = [(i, i + by) for i in range(size) if 0 <= i + by < size]
    return lax.ppermute(array, axis, pairs)


def on_device(
    frames, memory_in, lengths, ln_gain, w_query, w_key, w_value, w_out, grad_frames, grad_memory
):
    utterances = frames.shape[0]
    local_segs = frames.shape[1]
    frame_count = frames.shape[2]
    model_width = frames.shape[3]
    head_dim = model_width // HEADS
    query_count = frame_count + 1
    segment = lax.axis_index("seg")
    first_global = segment * local_segs
    wide_frames = frames.astype(jnp.float32)
    row_mean = jnp.mean(wide_frames, axis=-1, keepdims=True)
    centred = wide_frames - row_mean
    row_var = jnp.mean(centred * centred, axis=-1, keepdims=True)
    normed = (centred * lax.rsqrt(row_var + epsilon) * ln_gain).astype(jnp.bfloat16)
    summary = jnp.mean(normed.astype(jnp.float32), axis=2).astype(jnp.bfloat16)
    query_rows = jnp.concatenate([normed, summary[:, :, None, :]], axis=2)
    tail_rows = normed[:, local_segs - 1, frame_count - LEFT :]
    incoming = passed_along(tail_rows, "seg", 1)
    left_rows = jnp.concatenate(
        [incoming[:, None], normed[:, : local_segs - 1, frame_count - LEFT :]], axis=1
    )
    earlier = passed_along(memory_in, "seg", 1)
    extended = jnp.concatenate([earlier, memory_in], axis=1)
    local_pos = jnp.arange(local_segs)[:, None]
    slot_pos = jnp.arange(MEMORY)[None, :]
    bank_index = MEMORY + local_pos - 1 - slot_pos
    bank_valid = first_global + local_pos - 1 - slot_pos >= 0
    taken = jnp.take(extended, bank_index.reshape(-1), axis=1).reshape(
        utterances, local_segs, MEMORY, model_width
    )
    memory_rows = jnp.where(bank_valid[None, :, :, None], taken, jnp.zeros((), taken.dtype))
    key_rows = jnp.concatenate([memory_rows, left_rows, normed], axis=2)
    key_count = key_rows.shape[2]
    query_flat = query_rows.reshape(-1, model_width)
    key_flat = key_rows.reshape(-1, model_width)
    columns = query_flat
    queries = jnp.dot(
        columns,
        lax.all_gather(w_query, "fsdp", axis=0, tiled=True),
        preferred_element_type=jnp.float32,
    ).astype(jnp.bfloat16)
    columns = key_flat
    key_proj = jnp.dot(
        columns,
        lax.all_gather(w_key, "fsdp", axis=0, tiled=True),
        preferred_element_type=jnp.float32,
    )
    value_proj = jnp.dot(
        columns,
        lax.all_gather(w_value, "fsdp", axis=0, tiled=True),
        preferred_element_type=jnp.float32,
    )
    key_proj = key_proj.astype(jnp.bfloat16).reshape(
        utterances, local_segs, key_count, HEADS, head_dim
    )
    value_proj = value_proj.astype(jnp.bfloat16).reshape(
        utterances, local_segs, key_count, HEADS, head_dim
    )
    queries = queries.reshape(utterances, local_segs, query_count, HEADS, head_dim)
    scores = jnp.einsum(
        "utqhd,utkhd->uthqk", queries, key_proj, preferred_element_type=jnp.float32
    ) / math.sqrt(head_dim)
    key_slot = jnp.arange(key_count)[None, :]
    global_seg = first_global + local_pos
    valid_key = jnp.where(
        key_slot < MEMORY,
        global_seg - 1 - key_slot >= 0,
        jnp.where(key_slot < MEMORY + LEFT, global_seg >= 1, True),
    )
    scores = jnp.where(valid_key[None, :, None, None, :], scores, masked_score)
    highest = jnp.max(scores, axis=-1, keepdims=True)
    exponent = jnp.exp(scores - highest)
    soft_weights = (exponent / jnp.sum(exponent, axis=-1, keepdims=True)).astype(jnp.bfloat16)
    attended = jnp.einsum(
        "uthqk,utkhd->utqhd", soft_weights, value_proj, preferred_element_type=jnp.float32
    )
    attended = attended.astype(jnp.bfloat16).reshape(-1, model_width)
    upstream = jnp.concatenate([grad_frames, grad_memory[:, :, None, :]], axis=2).reshape(
        -1, model_width
    )
    columns = attended
    projected = jnp.dot(
        columns,
        lax.all_gather(w_out, "fsdp", axis=0, tiled=True),
        preferred_element_type=jnp.float32,
    )
    back_proj = lax.dot_general(
        upstream,
        lax.all_gather(w_out, "fsdp", axis=0, tiled=True),
        (((1,), (1,)), ((), ())),
        preferred_element_type=jnp.float32,
    )
    projected = projected.reshape(utterances, local_segs, query_count, model_width)
    live_mask = (first_global + jnp.arange(local_segs)[None, :] < lengths[:, None]).astype(
        jnp.float32
    )
    frames_out = (wide_frames + live_mask[:, :, None, None] * projected[:, :, :frame_count]).astype(
        jnp.bfloat16
    )
    memory_out = (live_mask[:, :, None] * projected[:, :, frame_count]).astype(jnp.bfloat16)
    back_proj = back_proj.reshape(utterances, local_segs, query_count, model_width)
    grad_attended = (live_mask[:, :, None, None] * back_proj).astype(jnp.bfloat16)
    grad_attended = grad_attended.reshape(utterances, local_segs, query_count, HEADS, head_dim)
    grad_values = jnp.einsum(
        "uthqk,utqhd->utkhd", soft_weights, grad_attended, preferred_element_type=jnp.float32
    )
    grad_values = grad_values.astype(jnp.bfloat16).reshape(-1, model_width)
    columns = key_flat
    grad_part = lax.psum_scatter(
        lax.dot_general(
            columns, grad_values, (((0,), (0,)), ((), ())), preferred_element_type=jnp.float32
        ).astype(jnp.bfloat16),
        "fsdp",
        scatter_dimension=0,
        tiled=True,
    )
    value_grad = lax.psum(grad_part, "seg").astype(jnp.float32)
    return (frames_out, memory_out, value_grad)


def solution(mesh):
    return jax.shard_map(
        on_device,
        mesh=mesh,
        in_specs=(
            P("fsdp", "seg", None, None),
            P("fsdp", "seg", None),
            P("fsdp"),
            P(),
            P("fsdp", None),
            P("fsdp", None),
            P("fsdp", None),
            P("fsdp", None),
            P("fsdp", "seg", None, None),
            P("fsdp", "seg", None),
        ),
        out_specs=(P("fsdp", "seg", None, None), P("fsdp", "seg", None), P("fsdp", None)),
        check_vma=False,
    )
```

profile of v0, /device:TPU:0, one launch (start us, length us, event | category | flops | bytes accessed | tf_op | source)
XLA Modules:
  0.0 264.9 jit_solution(16414111355024861088)
XLA Ops:
  7.2 0.7 all-gather.9.cloned.1.call-update
  8.0 0.7 all-gather.7.cloned.1.call-update
  8.7 0.7 all-gather.11.cloned.1.call-update
  10.1 2.4 collective-permute-start.1
  12.5 4.6 %collective-permute-start = (bf16[1,8,1024]{2,1,0:T(8,128)(2,1)S(1)}, bf16[1,8,1024]{2,1,0:T(8,128)(2,1)S(1)}, u32[]{:S(2)}, u32[]{:S(2)}) collective-permute-start(bf16[1,8,1024]{2,1,0:T(8,128)(2,1)S(1)} %copy-done.6), channel_id=1, source_target_pairs={{0,4},{4,8},{8,12},{12,16},{16,20},{20,24},{24,28},{1,5},{5,9},{9,... | collective-permute-start | bytes 49160 | tf_op jit(solution)/shard_map/ppermute | solution.py:20
  18.5 0.7 gather_fusion
  19.4 28.5 %all-gather.9.cloned.1.call-done = bf16[1024,1024]{1,0:T(8,128)(2,1)} async-done(((bf16[256,1024]{1,0:T(8,128)(2,1)}), bf16[1024,1024]{1,0:T(8,128)(2,1)}) %all-gather.9.cloned.1.call-update) | async-done | bytes 2097168 | tf_op jit(solution)/shard_map/all_gather | solution.py:69
  47.9 2.4 convolution_convert_fusion.3
  50.4 0.8 reshape.362
  51.2 33.9 %all-gather.7.cloned.1.call-done = bf16[1024,1024]{1,0:T(8,128)(2,1)} async-done(((bf16[256,1024]{1,0:T(8,128)(2,1)}), bf16[1024,1024]{1,0:T(8,128)(2,1)}) %all-gather.7.cloned.1.call-update) | async-done | bytes 2097168 | tf_op jit(solution)/shard_map/all_gather | solution.py:63
  85.1 2.1 convolution_convert_fusion.5
  87.2 1.2 reshape.361
  88.3 34.0 %all-gather.11.cloned.1.call-done = bf16[1024,1024]{1,0:T(8,128)(2,1)} async-done(((bf16[256,1024]{1,0:T(8,128)(2,1)}), bf16[1024,1024]{1,0:T(8,128)(2,1)}) %all-gather.11.cloned.1.call-update) | async-done | bytes 2097168 | tf_op jit(solution)/shard_map/all_gather | solution.py:108
  122.3 2.4 fusion.19
  124.7 1.2 reshape.379
  125.9 1.9 multiply_select_fusion
  127.8 1.0 fusion.42
  128.8 6.9 %fusion.7 = bf16[1,8,40,16,64]{4,2,3,1,0:T(8,128)(2,1)} fusion(bf16[8,17,16,64]{3,2,1,0:T(8,128)(2,1)S(1)} %copy-done.4, f32[8,16,17]{2,1,0:T(8,128)S(1)} %fusion.42, f32[8,16,17,40]{3,2,1,0:T(8,128)S(1)} %multiply_select_fusion), kind=kOutput, calls=%fused_computation.12 | convolution fusion | flops 11732135 | bytes 1290752 | tf_op jit(solution)/shard_map/uthqk,utqhd->utkhd/dot_general | solution.py:128
  135.8 1.5 copy.27
  137.3 1.7 reshape.365
  139.0 3.9 %convolution_convert_fusion = bf16[1024,1024]{1,0:T(8,128)(2,1)} fusion(bf16[320,1024]{1,0:T(8,128)(2,1)} %bitcast.64, bf16[320,1024]{1,0:T(8,128)(2,1)} %reshape.365), kind=kOutput, calls=%fused_computation.6 | convolution fusion | flops 672137216 | bytes 3407872 | tf_op jit(solution)/shard_map/dot_general | solution.py:134
  143.1 16.2 %all-gather.5.cloned.1.call-done = bf16[1024,1024]{1,0:T(8,128)(2,1)} async-done(((bf16[256,1024]{1,0:T(8,128)(2,1)}), bf16[1024,1024]{1,0:T(8,128)(2,1)}) %all-gather.5.cloned.1.call-update) | async-done | bytes 2097168 | tf_op jit(solution)/shard_map/all_gather | solution.py:74
  159.3 3.3 %convolution_convert_fusion.4 = bf16[320,1024]{1,0:T(8,128)(2,1)} fusion(bf16[320,1024]{1,0:T(8,128)(2,1)S(1)} %bitcast.65, bf16[1024,1024]{1,0:T(8,128)(2,1)} %all-gather.5.cloned.1.call-done), kind=kOutput, calls=%fused_computation.15 | convolution fusion | flops 671416320 | bytes 3407872 | tf_op jit(solution)/shard_map/dot_general | solution.py:72
  162.6 1.9 reshape.359
  164.6 6.4 %fusion.10 = bf16[1,8,17,16,64]{4,2,3,1,0:T(8,128)(2,1)} fusion(bf16[8,40,16,64]{3,2,1,0:T(8,128)(2,1)S(1)} %reshape.359, f32[8,16,17]{2,1,0:T(8,128)S(1)} %fusion.42, f32[8,16,17,40]{3,2,1,0:T(8,128)S(1)} %multiply_select_fusion), kind=kOutput, calls=%fused_computation.18 | convolution fusion | flops 11543719 | bytes 1290752 | tf_op jit(solution)/shard_map/uthqk,utkhd->utqhd/dot_general | solution.py:98
  170.9 1.4 copy.29
  172.8 0.6 fusion.13
  173.4 24.0 %reduce-scatter.2.cloned.1.call-done = bf16[256,1024]{1,0:T(8,128)(2,1)} async-done(((bf16[1024,1024]{1,0:T(8,128)(2,1)}), bf16[256,1024]{1,0:T(8,128)(2,1)}) %reduce-scatter.2.cloned.1.call-update) | async-done | bytes 524304 | tf_op jit(solution)/shard_map/reduce_scatter | solution.py:133
  197.5 0.6 copy.28
  198.1 0.8 fusion.29
  199.0 56.9 %all-reduce.2.cloned.1.call-done = bf16[256,1024]{1,0:T(8,128)(2,1)} async-done(((bf16[256,1024]{1,0:T(8,128)(2,1)}), bf16[256,1024]{1,0:T(8,128)(2,1)}) %all-reduce.2.cloned.1.call-update) | async-done | bytes 524304 | tf_op jit(solution)/shard_map/psum | solution.py:141
  255.9 2.1 convert_element_type.112
  (57 shorter events, 2.5 us)
Async XLA Ops:
  7.2 2.3 copy-start
  7.2 2.6 %copy-start.7 = (f32[1024]{0:T(1024)S(1)}, f32[1024]{0:T(1024)}, u32[]{:S(2)}) copy-start(f32[1024]{0:T(1024)} %param.13) | copy-start | bytes 12292
  7.2 5.3 %copy-start.6 = (bf16[1,8,1024]{2,1,0:T(8,128)(2,1)S(1)}, bf16[1,8,1024]{2,1,0:T(8,128)(2,1)}, u32[]{:S(2)}) copy-start(bf16[1,8,1024]{2,1,0:T(8,128)(2,1)} %param.11) | copy-start | bytes 49156
  7.2 40.7 %all-gather.9.cloned.1.call-start = ((), (), s32[]{:S(2)}) async-start(), calls=%async_computation.3 | async-start | bytes 2621440 | tf_op jit(solution)/shard_map/all_gather | solution.py:69
  7.9 77.2 %all-gather.7.cloned.1.call-start = ((), (), s32[]{:S(2)}) async-start(), calls=%async_computation.2 | async-start | bytes 2621440 | tf_op jit(solution)/shard_map/all_gather | solution.py:63
  8.7 113.6 %all-gather.11.cloned.1.call-start = ((), (), s32[]{:S(2)}) async-start(), calls=%async_computation.4 | async-start | bytes 2621440 | tf_op jit(solution)/shard_map/all_gather | solution.py:108
  9.4 149.9 %all-gather.5.cloned.1.call-start = ((), (), s32[]{:S(2)}) async-start(), calls=%async_computation.1 | async-start | bytes 2621440 | tf_op jit(solution)/shard_map/all_gather | solution.py:74
  9.8 8.7 %copy-start.5 = (bf16[1,8,1024]{2,1,0:T(8,128)(2,1)S(1)}, bf16[1,8,1024]{2,1,0:T(8,128)(2,1)}, u32[]{:S(2)}) copy-start(bf16[1,8,1024]{2,1,0:T(8,128)(2,1)} %param.19) | copy-start | bytes 49156
  10.1 9.2 %collective-permute-start.1 = (bf16[1,16,1024]{2,1,0:T(8,128)(2,1)S(1)}, bf16[1,16,1024]{2,1,0:T(8,128)(2,1)S(1)}, u32[]{:S(2)}, u32[]{:S(2)}) collective-permute-start(bf16[1,16,1024]{2,1,0:T(8,128)(2,1)S(1)} %slice_bitcast_fusion.1), channel_id=1, source_target_pairs={{0,4},{4,8},{8,12},{12,16},{16,20},{20,24},{24,28},{1,5},{5,9},{9,... | collective-permute-start | bytes 98312 | tf_op jit(solution)/shard_map/ppermute | solution.py:20
  12.5 6.0 %collective-permute-start = (bf16[1,8,1024]{2,1,0:T(8,128)(2,1)S(1)}, bf16[1,8,1024]{2,1,0:T(8,128)(2,1)S(1)}, u32[]{:S(2)}, u32[]{:S(2)}) collective-permute-start(bf16[1,8,1024]{2,1,0:T(8,128)(2,1)S(1)} %copy-done.6), channel_id=1, source_target_pairs={{0,4},{4,8},{8,12},{12,16},{16,20},{20,24},{24,28},{1,5},{5,9},{9,... | collective-permute-start | bytes 49160 | tf_op jit(solution)/shard_map/ppermute | solution.py:20
  17.1 180.3 %reduce-scatter.2.cloned.1.call-start = ((), (), s32[]{:S(2)}) async-start(), calls=%async_computation.5 | async-start | bytes 2621440 | tf_op jit(solution)/shard_map/reduce_scatter | solution.py:133
  19.4 28.5 %copy-start.2 = (bf16[1,8,40,1024]{3,2,1,0:T(8,128)(2,1)}, bf16[1,8,40,1024]{3,2,1,0:T(8,128)(2,1)S(1)}, u32[]{:S(2)}) copy-start(bf16[1,8,40,1024]{3,2,1,0:T(8,128)(2,1)S(1)} %pad_maximum_fusion) | copy-start | bytes 1966084
  51.2 71.1 %copy-start.8 = (bf16[1,8,16,1024]{3,2,1,0:T(8,128)(2,1)S(1)}, bf16[1,8,16,1024]{3,2,1,0:T(8,128)(2,1)}, u32[]{:S(2)}) copy-start(bf16[1,8,16,1024]{3,2,1,0:T(8,128)(2,1)} %param.18) | copy-start | bytes 786436
  127.8 1.1 copy-start.4
  142.9 16.5 %copy-start.3 = (bf16[1,8,40,1024]{3,2,1,0:T(8,128)(2,1)S(1)}, bf16[1,8,40,1024]{3,2,1,0:T(8,128)(2,1)}, u32[]{:S(2)}) copy-start(bf16[1,8,40,1024]{3,2,1,0:T(8,128)(2,1)} %copy-done.2) | copy-start | bytes 1966084
  142.9 113.0 %all-reduce.2.cloned.1.call-start = ((), (), s32[]{:S(2)}) async-start(), calls=%async_computation.6 | async-start | bytes 1048576 | tf_op jit(solution)/shard_map/psum | solution.py:141
  170.9 1.8 copy-start.1
Sparse Core Ops, SparseCore 0:
  9.9 38.0 all-gather.8
  49.8 35.2 all-gather.6
  87.0 35.2 all-gather.10
  124.0 35.2 all-gather.4
  162.2 35.1 reduce-scatter.1
  199.7 56.1 all-reduce.1
where the time goes:
time: 265 us
  waiting for transfers between devices  196 us (74%)
  matrix products  29.8 us (11%)
  between operations  15.1 us (6%)
  local copies, waits for them, and re-layouts  11.9 us (4%)
  starting transfers between devices  7.37 us (3%)
  other arithmetic  5.06 us (2%)
    psum x1, waiting for transfers between devices, on_device(): value_grad = lax.psum(grad_part, 'seg').astype(jnp.float32)  56.9 us
    all_gather x1, waiting for transfers between devices, on_device(): lax.all_gather(w_out, 'fsdp', axis=0, tiled=True)  34 us
    all_gather x1, waiting for transfers between devices, on_device(): lax.all_gather(w_query, 'fsdp', axis=0, tiled=True)  33.9 us
    all_gather x1, waiting for transfers between devices, on_device(): lax.all_gather(w_key, 'fsdp', axis=0, tiled=True)  28.5 us
    reduce_scatter x1, waiting for transfers between devices, on_device(): lax.psum_scatter(lax.dot_general(columns, grad_values, (((0,), (0,)), (()...  24 us
    all_gather x1, waiting for transfers between devices, on_device(): lax.all_gather(w_value, 'fsdp', axis=0, tiled=True)  16.2 us
    ppermute x2, starting transfers between devices, passed_along(): return lax.ppermute(array, axis, pairs)  6.95 us
    dot_general x1, matrix products, on_device(): jnp.einsum('uthqk,utqhd->utkhd', soft_weights, grad_attended, preferred_e...  6.93 us
  transfers between devices with their start and end apart: 8, of which 6 were waited for; matrix products, arithmetic and copies ran while one was open for 17% of the time, Pallas kernels for 0%

commit v1 on v0

v1 whole, which is shorter than its diff:
```python
import functools
import math

import jax
import jax.numpy as jnp
from jax import lax
from jax.experimental import pallas as pl
from jax.experimental.pallas import tpu as pltpu
from jax.sharding import PartitionSpec as P

HEADS = 16
LEFT = 16
MEMORY = 8


epsilon = 1e-05
masked_score = -1e30
bf16 = jnp.bfloat16
f32 = jnp.float32
vmem = pl.BlockSpec(memory_space=pltpu.VMEM)
smem = pl.BlockSpec(memory_space=pltpu.SMEM)
NT = (((1,), (1,)), ((), ()))
TN = (((0,), (0,)), ((), ()))


def cost(flops, moved):
    return pl.CostEstimate(flops=flops, bytes_accessed=moved, transcendentals=0)


def params():
    return pltpu.CompilerParams(vmem_limit_bytes=40 * 1024 * 1024)


def swapped(array, axis, bit):
    size = lax.axis_size(axis)
    return lax.ppermute(array, axis, [(i, i ^ bit) for i in range(size)])


def passed_along(array, axis, by):
    size = lax.axis_size(axis)
    return lax.ppermute(array, axis, [(i, i + by) for i in range(size - by)])


def halving_bits(size):
    return [1 << b for b in range(size.bit_length() - 1)]


def pack_kernel(scal, wq, wk, wv, wo, gf, gm, oq, ok, ov, oo, u):
    oq[...] = wq[...]
    ok[...] = wk[...]
    oo[...] = wo[...]
    ov[...] = wv[...]
    rows = gf.shape[0]
    u[:rows, :] = gf[...]
    u[rows:, :] = jnp.concatenate([jnp.zeros(gm.shape, gm.dtype), gm[...]], axis=0)


def normed_rows(rows, gain):
    wide = rows.astype(f32)
    centred = wide - jnp.mean(wide, axis=-1, keepdims=True)
    var = jnp.mean(centred * centred, axis=-1, keepdims=True)
    return (centred * lax.rsqrt(var + epsilon) * gain).astype(bf16)


def norm_kernel(frame_count, frames, halo, mem, halo_mem, gain, x):
    rows, width = frames.shape
    segs = rows // frame_count
    gain_row = gain[...]
    x[:LEFT, :] = normed_rows(halo[...], gain_row)
    x[LEFT : LEFT + 2 * MEMORY, :] = jnp.concatenate(
        [halo_mem[...], jnp.zeros_like(halo_mem)], axis=0
    )
    start = LEFT + 2 * MEMORY
    normed = normed_rows(frames[...], gain_row)
    x[start : start + rows, :] = normed
    summary = jnp.sum(normed.astype(f32).reshape(segs, frame_count, width), axis=1) / frame_count
    x[start + rows :, :] = jnp.concatenate([mem[...], summary.astype(bf16)], axis=0)


def merge_kernel(count, *refs):
    parts, x_all, x_turned = refs[:count], refs[count], refs[count + 1]
    rows = parts[0].shape[0]
    for i in range(count):
        x_all[i * rows : (i + 1) * rows, :] = parts[i][...]
    x_turned[...] = x_all[...].T


def assemble(scal, pieces, whole, rows):
    own = scal[1]
    for j, piece in enumerate(pieces):
        at = pl.multiple_of((own ^ j) * rows, rows)
        whole[pl.ds(at, rows), :] = piece[...]


def chunk_kernel(count, group, scal, *refs):
    pieces, outs, whole = refs[:count], refs[count : count + group], refs[count + group]
    assemble(scal, pieces, whole, pieces[0].shape[0])
    rows = outs[0].shape[0]
    for i in range(group):
        at = pl.multiple_of((scal[0] ^ i) * rows, rows)
        outs[i][...] = whole[pl.ds(at, rows), :]


def head_stack(array, heads):
    width = array.shape[1]
    head = lax.broadcasted_iota(jnp.int32, array.shape, 1) // (width // heads)
    zero = jnp.zeros_like(array)
    return jnp.concatenate([jnp.where(head == h, array, zero) for h in range(heads)], axis=0)


def weights_kernel(count, heads, frame_count, segs, scal, x_all, *refs):
    wq_parts, wk_parts = refs[:count], refs[count : 2 * count]
    soft, wq, wk = refs[2 * count :]
    part_rows = wq_parts[0].shape[0]
    assemble(scal, wq_parts, wq, part_rows)
    assemble(scal, wk_parts, wk, part_rows)
    blocks, keys, lanes = soft.shape
    queries = lanes // heads
    first = keys - queries
    frames = segs * frame_count
    q_all = jnp.dot(x_all[...], wq[...], preferred_element_type=f32).astype(bf16)
    k_all = jnp.dot(x_all[...], wk[...], preferred_element_type=f32).astype(bf16)
    key = lax.broadcasted_iota(jnp.int32, (keys, lanes), 0)
    row = lax.broadcasted_iota(jnp.int32, (keys, lanes), 1)
    for h in range(1, heads):
        row = jnp.where(row >= queries, row - queries, row)
    at = jnp.where(row < frames, row // frame_count, jnp.maximum(row - frames - segs, 0))
    own = key - first
    own_seg = own // frame_count
    own_mem = own - frames
    valid_own = ((own >= 0) & (own < frames) & ((own_seg == at) | (own_seg == at - 1))) | (
        (own_mem >= 0) & (own_mem < segs) & (own_mem < at) & (own_mem >= at - MEMORY)
    )
    halo_mem = key - LEFT
    valid_halo = ((key < LEFT) & (at == 0)) | (
        (halo_mem >= 0) & (halo_mem < MEMORY) & (halo_mem >= at)
    )
    head_dim = wq.shape[1] // heads
    scale = 1.0 / math.sqrt(head_dim)
    for i in range(blocks):
        base = (scal[2] // segs ^ i) * segs
        valid = valid_own | (valid_halo & (base > 0))
        q_i = head_stack(q_all[i * keys + first : (i + 1) * keys], heads)
        scores = (
            lax.dot_general(k_all[i * keys : (i + 1) * keys], q_i, NT, preferred_element_type=f32)
            * scale
        )
        scores = jnp.where(valid, scores, masked_score)
        exponent = jnp.exp(scores - jnp.max(scores, axis=0, keepdims=True))
        soft[i] = (exponent / jnp.sum(exponent, axis=0, keepdims=True)).astype(bf16)


def grad_kernel(count, group, heads, frame_count, segs, scal, x_turned, soft, *refs):
    up, wo_parts = refs[:group], refs[group : 2 * group]
    outs, wo, whole = refs[2 * group : 2 * group + count], refs[-2], refs[-1]
    width = wo_parts[0].shape[1]
    blocks, keys, lanes = soft.shape
    queries = lanes // heads
    frames = segs * frame_count
    for i in range(group):
        at = pl.multiple_of((scal[0] ^ i) * width, width)
        wo[:, pl.ds(at, width)] = wo_parts[i][...]
    row = lax.broadcasted_iota(jnp.int32, (queries, width), 0)
    seg_of = jnp.where(row < frames, row // frame_count, row - frames - segs)
    values = []
    for i in range(group):
        base = (scal[2] // segs ^ i) * segs
        back = lax.dot_general(up[i][...], wo[...], NT, preferred_element_type=f32)
        live = (base + seg_of < scal[3]).astype(f32)
        grad_attended = head_stack((live * back).astype(bf16), heads)
        values.append(
            jnp.dot(soft[i], grad_attended, preferred_element_type=f32).astype(bf16)
        )
    whole[...] = jnp.dot(
        x_turned[...], jnp.concatenate(values, axis=0), preferred_element_type=f32
    ).astype(bf16)
    rows = outs[0].shape[0]
    for j in range(count):
        at = pl.multiple_of((scal[1] ^ j) * rows, rows)
        outs[j][...] = whole[pl.ds(at, rows), :]


def out_kernel(count, heads, scal, x_all, soft, wo, *refs):
    wv_parts, keep, send, wv = refs[:count], refs[count], refs[count + 1], refs[count + 2]
    assemble(scal, wv_parts, wv, wv_parts[0].shape[0])
    blocks, keys, lanes = soft.shape
    queries = lanes // heads
    v_all = jnp.dot(x_all[...], wv[...], preferred_element_type=f32).astype(bf16)
    width = wv.shape[1]
    head = lax.broadcasted_iota(jnp.int32, (queries, width), 1) // (width // heads)
    for i in range(blocks):
        stacked = lax.dot_general(
            soft[i], v_all[i * keys : (i + 1) * keys], TN, preferred_element_type=f32
        )
        attended = stacked[:queries]
        for h in range(1, heads):
            attended = jnp.where(head == h, stacked[h * queries : (h + 1) * queries], attended)
        projected = jnp.dot(attended.astype(bf16), wo[...], preferred_element_type=f32)
        into = send if i & 1 else keep
        into[i // 2] = projected.astype(into.dtype)


def on_device(
    frames, memory_in, lengths, ln_gain, w_query, w_key, w_value, w_out, grad_frames, grad_memory
):
    utterances, segs, frame_count, width = frames.shape
    seg_size = lax.axis_size("seg")
    fsdp_size = lax.axis_size("fsdp")
    group = 4
    assert utterances == 1 and segs == MEMORY and frame_count == LEFT and seg_size % group == 0
    heads = HEADS // group
    block = width // group
    rows = w_query.shape[0]
    frame_rows = segs * frame_count
    queries = frame_rows + 2 * segs
    keys = LEFT + 2 * MEMORY + queries
    seg = lax.axis_index("seg")
    member = seg % group
    scal = jnp.stack(
        [member, lax.axis_index("fsdp"), seg * segs, lengths[0]]
    ).astype(jnp.int32)
    flat_frames = frames.reshape(frame_rows, width)
    flat_mem = memory_in.reshape(segs, width)

    halo = passed_along(frames[0, segs - 1, frame_count - LEFT :], "seg", 1)
    halo_mem = passed_along(flat_mem[segs - MEMORY :], "seg", 1)

    column = pl.BlockSpec((rows, block), lambda i, s: (0, s[0]))
    whole = lambda a, b: pl.BlockSpec((a, b), lambda i, s: (0, 0))
    wq, wk, wv, wo, up = pl.pallas_call(
        pack_kernel,
        grid_spec=pltpu.PrefetchScalarGridSpec(
            num_scalar_prefetch=1,
            grid=(1,),
            in_specs=[column] * 4 + [whole(frame_rows, width), whole(segs, width)],
            out_specs=[whole(rows, block)] * 4 + [whole(queries, width)],
        ),
        out_shape=[jax.ShapeDtypeStruct((rows, block), bf16)] * 4
        + [jax.ShapeDtypeStruct((queries, width), bf16)],
        compiler_params=params(),
        cost_estimate=cost(0, 4 * 1024 * 1024),
        name="pack",
    )(
        scal, w_query, w_key, w_value, w_out,
        grad_frames.reshape(frame_rows, width), grad_memory.reshape(segs, width),
    )

    x_own = pl.pallas_call(
        functools.partial(norm_kernel, frame_count),
        in_specs=[vmem] * 5,
        out_specs=vmem,
        out_shape=jax.ShapeDtypeStruct((keys, width), bf16),
        compiler_params=params(),
        cost_estimate=cost(0, 2 * 1024 * 1024),
        name="norm",
    )(flat_frames, halo, flat_mem, halo_mem, ln_gain.reshape(1, width))

    bits = halving_bits(fsdp_size)

    def gathered(piece, order):
        pieces = {0: piece}
        for bit in order:
            for have in sorted(pieces):
                pieces[have ^ bit] = swapped(pieces[have], "fsdp", bit)
        return [pieces[j] for j in range(fsdp_size)]

    def grouped(piece):
        far = swapped(piece, "seg", 2)
        return [piece, swapped(piece, "seg", 1), far, swapped(far, "seg", 1)]

    wo_parts = gathered(wo, bits)
    wq_parts = gathered(wq, bits[::-1])
    wk_parts = gathered(wk, bits)
    wv_parts = gathered(wv, bits[::-1])
    up_parts = grouped(up)
    x_parts = grouped(x_own)

    chunks = pl.pallas_call(
        functools.partial(chunk_kernel, fsdp_size, group),
        in_specs=[smem] + [vmem] * fsdp_size,
        out_specs=[vmem] * group,
        out_shape=[jax.ShapeDtypeStruct((block, block), bf16)] * group,
        scratch_shapes=[pltpu.VMEM((width, block), bf16)],
        compiler_params=params(),
        cost_estimate=cost(0, 1024 * 1024),
        name="wo_chunks",
    )(scal, *wo_parts)
    wo_rows = [chunks[0]] + [swapped(chunks[i], "seg", i) for i in range(1, group)]

    x_all, x_turned = pl.pallas_call(
        functools.partial(merge_kernel, group),
        in_specs=[vmem] * group,
        out_specs=[vmem] * 2,
        out_shape=[
            jax.ShapeDtypeStruct((group * keys, width), bf16),
            jax.ShapeDtypeStruct((width, group * keys), bf16),
        ],
        compiler_params=params(),
        cost_estimate=cost(0, 5 * 1024 * 1024),
        name="merge",
    )(*x_parts)

    soft = pl.pallas_call(
        functools.partial(weights_kernel, fsdp_size, heads, frame_count, segs),
        in_specs=[smem] + [vmem] * (1 + 2 * fsdp_size),
        out_specs=vmem,
        out_shape=jax.ShapeDtypeStruct((group, keys, heads * queries), bf16),
        scratch_shapes=[pltpu.VMEM((width, block), bf16)] * 2,
        compiler_params=params(),
        cost_estimate=cost(2 * 2 * group * keys * width * block, 4 * 1024 * 1024),
        name="soft_weights",
    )(scal, x_all, *wq_parts, *wk_parts)

    *grad_chunks, wo_mine = pl.pallas_call(
        functools.partial(grad_kernel, fsdp_size, group, heads, frame_count, segs),
        in_specs=[smem] + [vmem] * (2 + 2 * group),
        out_specs=[vmem] * (fsdp_size + 1),
        out_shape=[jax.ShapeDtypeStruct((rows, block), bf16)] * fsdp_size
        + [jax.ShapeDtypeStruct((block, width), bf16)],
        scratch_shapes=[pltpu.VMEM((width, block), bf16)],
        compiler_params=params(),
        cost_estimate=cost(2 * 2 * group * keys * width * block, 5 * 1024 * 1024),
        name="value_grad",
    )(scal, x_turned, soft, *up_parts, *wo_rows)

    grad_sum = grad_chunks[0].astype(f32)
    for j in range(1, fsdp_size):
        grad_sum = grad_sum + swapped(grad_chunks[j], "fsdp", j).astype(f32)
    bit = group
    while bit < seg_size:
        mine = grad_sum.astype(bf16)
        grad_sum = mine.astype(f32) + swapped(mine, "seg", bit).astype(f32)
        bit *= 2
    mine = grad_sum.astype(bf16)

    keep, send = pl.pallas_call(
        functools.partial(out_kernel, fsdp_size, heads),
        in_specs=[smem] + [vmem] * (3 + fsdp_size),
        out_specs=[vmem] * 2,
        out_shape=[
            jax.ShapeDtypeStruct((group // 2, queries, width), f32),
            jax.ShapeDtypeStruct((group // 2, queries, width), bf16),
        ],
        scratch_shapes=[pltpu.VMEM((width, block), bf16)],
        compiler_params=params(),
        cost_estimate=cost(2 * 2 * group * keys * width * block, 5 * 1024 * 1024),
        name="attend_project",
    )(scal, x_all, soft, wo_mine, *wv_parts)
    keep = keep + swapped(send, "seg", 1).astype(f32)
    projected = keep[0] + swapped(keep[1].astype(bf16), "seg", 2).astype(f32)

    live = (seg * segs + jnp.arange(segs) < lengths[0]).astype(f32)
    frames_out = (
        frames.astype(f32)
        + live[None, :, None, None]
        * projected[:frame_rows].reshape(1, segs, frame_count, width)
    ).astype(bf16)
    memory_out = (live[None, :, None] * projected[None, frame_rows + segs :]).astype(bf16)

    far = swapped(mine, "seg", 2)
    high = (member & 2) > 0
    pair = jnp.stack([jnp.where(high, far, mine), jnp.where(high, mine, far)])
    near = swapped(pair, "seg", 1)
    odd = (member & 1) > 0
    value_grad = jnp.concatenate(
        [
            part[j]
            for j in range(2)
            for part in (jnp.where(odd, near, pair), jnp.where(odd, pair, near))
        ],
        axis=1,
    ).astype(f32)
    return (frames_out, memory_out, value_grad)


def solution(mesh):
    return jax.shard_map(
        on_device,
        mesh=mesh,
        in_specs=(
            P("fsdp", "seg", None, None),
            P("fsdp", "seg", None),
            P("fsdp"),
            P(),
            P("fsdp", None),
            P("fsdp", None),
            P("fsdp", None),
            P("fsdp", None),
            P("fsdp", "seg", None, None),
            P("fsdp", "seg", None),
        ),
        out_specs=(P("fsdp", "seg", None, None), P("fsdp", "seg", None), P("fsdp", None)),
        check_vma=False,
    )
```

time: 265 us -> 93.3 us (0.35)
  waiting for transfers between devices: 196 us -> 37.5 us
  matrix products: 29.8 us -> 0 us
  starting transfers between devices: 7.37 us -> 31 us
  between operations: 15.1 us -> 1.49 us
  Pallas kernels: 0 us -> 10.5 us
  local copies, waits for them, and re-layouts: 11.9 us -> 9.07 us
    all_gather x4 -> x0, waiting for transfers between devices: 113 us -> none  [the longest x1 34 us: on_device(): lax.all_gather(w_out, 'fsdp', axis=0, tiled=True)]
    psum x1 -> x0, waiting for transfers between devices: 56.9 us -> none  [on_device(): value_grad = lax.psum(grad_part, 'seg').astype(jnp.float32)]
    ppermute x2 -> x31, waiting for transfers between devices: 0.01 us -> 37.5 us  [the longest x29 36.5 us: swapped(): return lax.ppermute(array, axis, [(i, i ^ bit) for i in range(size)])]
    dot_general x9 -> x0, matrix products: 29.8 us -> none  [the longest x1 6.93 us: on_device(): jnp.einsum('uthqk,utqhd->utkhd', soft_weights, grad_attended, preferred_e...]
    ppermute x2 -> x31, starting transfers between devices: 6.95 us -> 31 us  [the longest x29 24 us: swapped(): return lax.ppermute(array, axis, [(i, i ^ bit) for i in range(size)])]
    reduce_scatter x1 -> x0, waiting for transfers between devices: 24 us -> none  [on_device(): lax.psum_scatter(lax.dot_general(columns, grad_values, (((0,), (0,)), (()...]
    pallas_call x0 -> x7, Pallas kernels: none -> 10.5 us  [the longest x1 3.13 us: on_device(): pl.pallas_call(functools.partial(grad_kernel, fsdp_size, group, heads, fr...]
    unnamed x19 -> x20, local copies, waits for them, and re-layouts: 0.74 us -> 8.19 us
  transfers between devices with their start and end apart: 8 -> 31, of which waited for: 6 -> 19; matrix products, arithmetic and copies ran while one was open for 17% -> 2% of each run, Pallas kernels for 0% -> 11%
where the time goes in v1:
time: 93.3 us; the launch traced here: 92.7 us
  waiting for transfers between devices  37.5 us (40%)
  starting transfers between devices  31 us (33%)
  Pallas kernels  10.5 us (11%)
  local copies, waits for them, and re-layouts  9.07 us (10%)
  other arithmetic  3.14 us (3%)
  between operations  1.49 us (2%)
    ppermute x29, waiting for transfers between devices, swapped(): return lax.ppermute(array, axis, [(i, i ^ bit) for i in range(size)])  36.5 us
    ppermute x29, starting transfers between devices, swapped(): return lax.ppermute(array, axis, [(i, i ^ bit) for i in range(size)])  24 us
    unnamed x20, local copies, waits for them, and re-layouts  8.19 us
    ppermute x2, starting transfers between devices, passed_along(): return lax.ppermute(array, axis, [(i, i + by) for i in range(size - by)])  6.94 us
    pallas_call x1, Pallas kernels, on_device(): pl.pallas_call(functools.partial(grad_kernel, fsdp_size, group, heads, fr...  3.13 us
    pallas_call x1, Pallas kernels, on_device(): pl.pallas_call(functools.partial(out_kernel, fsdp_size, heads), in_specs=...  2.96 us
    pallas_call x1, Pallas kernels, on_device(): pl.pallas_call(functools.partial(weights_kernel, fsdp_size, heads, frame_...  2.31 us
  transfers between devices with their start and end apart: 31, of which 19 were waited for; matrix products, arithmetic and copies ran while one was open for 2% of the time, Pallas kernels for 11%

profile of v1, /device:TPU:0, one launch (start us, length us, event | category | flops | bytes accessed | tf_op | source)
XLA Modules:
  0.0 92.7 jit_solution(18090862191318161882)
XLA Ops:
  1.4 2.3 %collective-permute-start = (bf16[16,1024]{1,0:T(8,128)(2,1)S(1)}, bf16[16,1024]{1,0:T(8,128)(2,1)S(1)}, u32[]{:S(2)}, u32[]{:S(2)}) collective-permute-start(bf16[16,1024]{1,0:T(8,128)(2,1)S(1)} %slice_bitcast_fusion.5), channel_id=1, source_target_pairs={{0,4},{4,8},{8,12},{12,16},{16,20},{20,24},{24,28},{1,5},{5,9},{9,... | collective-permute-start | bytes 98312 | tf_op jit(solution)/shard_map/ppermute | solution.py:41
  3.7 4.6 %collective-permute-start.1 = (bf16[8,1024]{1,0:T(8,128)(2,1)}, bf16[8,1024]{1,0:T(8,128)(2,1)S(1)}, u32[]{:S(2)}, u32[]{:S(2)}) collective-permute-start(bf16[8,1024]{1,0:T(8,128)(2,1)} %bitcast.35), channel_id=1, source_target_pairs={{0,4},{4,8},{8,12},{12,16},{16,20},{20,24},{24,28},{1,5},{5,9},{9,... | collective-permute-start | bytes 49160 | tf_op jit(solution)/shard_map/ppermute | solution.py:41
  12.1 2.3 %collective-permute-start.3 = (bf16[176,1024]{1,0:T(8,128)(2,1)S(1)}, bf16[176,1024]{1,0:T(8,128)(2,1)S(1)}, u32[]{:S(2)}, u32[]{:S(2)}) collective-permute-start(bf16[176,1024]{1,0:T(8,128)(2,1)S(1)} %norm.1.refs_0_), channel_id=1, source_target_pairs={{0,8},{4,12},{8,0},{12,4},{16,24},{20,28},{24,16},{28,20},{1,9},{5... | collective-permute-start | bytes 1081352 | tf_op jit(solution)/shard_map/ppermute | solution.py:36
  15.1 1.0 %copy-done.2 = bf16[256,1024]{1,0:T(8,128)(2,1)S(1)} copy-done((bf16[256,1024]{1,0:T(8,128)(2,1)S(1)}, bf16[256,1024]{1,0:T(8,128)(2,1)}, u32[]{:S(2)}) %copy-start.2) | copy-done | bytes 524312
  16.2 1.0 %copy-done.3 = bf16[256,1024]{1,0:T(8,128)(2,1)S(1)} copy-done((bf16[256,1024]{1,0:T(8,128)(2,1)S(1)}, bf16[256,1024]{1,0:T(8,128)(2,1)}, u32[]{:S(2)}) %copy-start.3) | copy-done | bytes 524312
  17.2 1.0 %copy-done.4 = bf16[256,1024]{1,0:T(8,128)(2,1)S(1)} copy-done((bf16[256,1024]{1,0:T(8,128)(2,1)S(1)}, bf16[256,1024]{1,0:T(8,128)(2,1)}, u32[]{:S(2)}) %copy-start.4) | copy-done | bytes 524312
  18.3 1.0 %copy-done.5 = bf16[256,1024]{1,0:T(8,128)(2,1)S(1)} copy-done((bf16[256,1024]{1,0:T(8,128)(2,1)S(1)}, bf16[256,1024]{1,0:T(8,128)(2,1)}, u32[]{:S(2)}) %copy-start.5) | copy-done | bytes 524312
  21.6 1.6 %collective-permute-start.8 = (bf16[256,256]{1,0:T(8,128)(2,1)S(1)}, bf16[256,256]{1,0:T(8,128)(2,1)S(1)}, u32[]{:S(2)}, u32[]{:S(2)}) collective-permute-start(bf16[256,256]{1,0:T(8,128)(2,1)S(1)} %get-tuple-element.23.refs_4_), channel_id=1, source_target_pairs={{0,1},{1,0},{2,3},{3,2},{4,5},{5,4},{6,7},{7,6},{8,9},{9,8},{10,11... | collective-permute-start | bytes 393224 | tf_op jit(solution)/shard_map/ppermute | solution.py:36
  23.2 1.5 %collective-permute-start.6 = (bf16[256,256]{1,0:T(8,128)(2,1)S(1)}, bf16[256,256]{1,0:T(8,128)(2,1)S(1)}, u32[]{:S(2)}, u32[]{:S(2)}) collective-permute-start(bf16[256,256]{1,0:T(8,128)(2,1)S(1)} %get-tuple-element.22.refs_0_), channel_id=1, source_target_pairs={{0,2},{1,3},{2,0},{3,1},{4,6},{5,7},{6,4},{7,5},{8,10},{9,11},{10,... | collective-permute-start | bytes 393224 | tf_op jit(solution)/shard_map/ppermute | solution.py:36
  25.7 1.4 %collective-permute-done.8.refs_5_ = bf16[256,256]{1,0:T(8,128)(2,1)S(1)} collective-permute-done((bf16[256,256]{1,0:T(8,128)(2,1)S(1)}, bf16[256,256]{1,0:T(8,128)(2,1)S(1)}, u32[]{:S(2)}, u32[]{:S(2)}) %collective-permute-start.8) | collective-permute-done | bytes 131104 | tf_op jit(solution)/shard_map/ppermute | solution.py:36
  27.3 1.9 %collective-permute-done.6.refs_2_ = bf16[256,256]{1,0:T(8,128)(2,1)S(1)} collective-permute-done((bf16[256,256]{1,0:T(8,128)(2,1)S(1)}, bf16[256,256]{1,0:T(8,128)(2,1)S(1)}, u32[]{:S(2)}, u32[]{:S(2)}) %collective-permute-start.6) | collective-permute-done | bytes 131104 | tf_op jit(solution)/shard_map/ppermute | solution.py:36
  31.7 2.4 %collective-permute-done.14.refs_1_ = bf16[256,256]{1,0:T(8,128)(2,1)S(1)} collective-permute-done((bf16[256,256]{1,0:T(8,128)(2,1)S(1)}, bf16[256,256]{1,0:T(8,128)(2,1)S(1)}, u32[]{:S(2)}, u32[]{:S(2)}) %collective-permute-start.14) | collective-permute-done | bytes 131104 | tf_op jit(solution)/shard_map/ppermute | solution.py:36
  34.2 1.4 %collective-permute-start.10 = (bf16[256,256]{1,0:T(8,128)(2,1)S(1)}, bf16[256,256]{1,0:T(8,128)(2,1)S(1)}, u32[]{:S(2)}, u32[]{:S(2)}) collective-permute-start(bf16[256,256]{1,0:T(8,128)(2,1)S(1)} %collective-permute-done.8.refs_5_), channel_id=1, source_target_pairs={{0,2},{1,3},{2,0},{3,1},{4,6},{5,7},{6,4},{7,5},{8,10},{9,11},{10,... | collective-permute-start | bytes 393224 | tf_op jit(solution)/shard_map/ppermute | solution.py:36
  36.8 2.7 %collective-permute-done.10.refs_7_ = bf16[256,256]{1,0:T(8,128)(2,1)S(1)} collective-permute-done((bf16[256,256]{1,0:T(8,128)(2,1)S(1)}, bf16[256,256]{1,0:T(8,128)(2,1)S(1)}, u32[]{:S(2)}, u32[]{:S(2)}) %collective-permute-start.10) | collective-permute-done | bytes 131104 | tf_op jit(solution)/shard_map/ppermute | solution.py:36
  40.0 1.2 %collective-permute-done.16.refs_3_ = bf16[256,256]{1,0:T(8,128)(2,1)S(1)} collective-permute-done((bf16[256,256]{1,0:T(8,128)(2,1)S(1)}, bf16[256,256]{1,0:T(8,128)(2,1)S(1)}, u32[]{:S(2)}, u32[]{:S(2)}) %collective-permute-start.16) | collective-permute-done | bytes 131104 | tf_op jit(solution)/shard_map/ppermute | solution.py:36
  41.2 1.3 %collective-permute-start.7 = (bf16[256,256]{1,0:T(8,128)(2,1)S(1)}, bf16[256,256]{1,0:T(8,128)(2,1)S(1)}, u32[]{:S(2)}, u32[]{:S(2)}) collective-permute-start(bf16[256,256]{1,0:T(8,128)(2,1)S(1)} %collective-permute-done.6.refs_2_), channel_id=1, source_target_pairs={{0,1},{1,0},{2,3},{3,2},{4,5},{5,4},{6,7},{7,6},{8,9},{9,8},{10,11... | collective-permute-start | bytes 393224 | tf_op jit(solution)/shard_map/ppermute | solution.py:36
  43.2 3.0 %collective-permute-done.7.refs_3_ = bf16[256,256]{1,0:T(8,128)(2,1)S(1)} collective-permute-done((bf16[256,256]{1,0:T(8,128)(2,1)S(1)}, bf16[256,256]{1,0:T(8,128)(2,1)S(1)}, u32[]{:S(2)}, u32[]{:S(2)}) %collective-permute-start.7) | collective-permute-done | bytes 131104 | tf_op jit(solution)/shard_map/ppermute | solution.py:36
  48.5 2.3 %soft_weights.1.soft = bf16[4,176,576]{2,1,0:T(8,128)(2,1)S(1)} custom-call(s32[4]{0:T(128)S(1)} %pad_add_fusion.scal, bf16[704,1024]{1,0:T(8,128)(2,1)S(1)} %get-tuple-element.21.x_all, bf16[256,256]{1,0:T(8,128)(2,1)S(1)} %get-tuple-element.22.refs_0_, bf16[256,256]{1,0:T(8,128)(2,1)S(1)} %collective-permute-done.5.refs_1_, ...), custom_call_target="tpu_custom_call" | custom-call | flops 738197504 | bytes 4194304 | tf_op jit(solution)/shard_map/soft_weights/pallas_call | solution.py:303
  50.9 1.2 %collective-permute-start.21 = (bf16[256,256]{1,0:T(8,128)(2,1)S(1)}, bf16[256,256]{1,0:T(8,128)(2,1)S(1)}, u32[]{:S(2)}, u32[]{:S(2)}) collective-permute-start(bf16[256,256]{1,0:T(8,128)(2,1)S(1)} %get-tuple-element.32.refs_0_), channel_id=1, source_target_pairs={{0,2},{1,3},{2,0},{3,1},{4,6},{5,7},{6,4},{7,5},{8,10},{9,11},{10,... | collective-permute-start | bytes 393224 | tf_op jit(solution)/shard_map/ppermute | solution.py:36
  52.5 2.0 %collective-permute-done.19.refs_7_ = bf16[256,256]{1,0:T(8,128)(2,1)S(1)} collective-permute-done((bf16[256,256]{1,0:T(8,128)(2,1)S(1)}, bf16[256,256]{1,0:T(8,128)(2,1)S(1)}, u32[]{:S(2)}, u32[]{:S(2)}) %collective-permute-start.19) | collective-permute-done | bytes 131104 | tf_op jit(solution)/shard_map/ppermute | solution.py:36
  54.5 3.1 %value_grad.1 = (bf16[256,256]{1,0:T(8,128)(2,1)S(1)}, bf16[256,256]{1,0:T(8,128)(2,1)S(1)}, bf16[256,256]{1,0:T(8,128)(2,1)S(1)}, bf16[256,256]{1,0:T(8,128)(2,1)S(1)}, bf16[256,1024]{1,0:T(8,128)(2,1)S(1)}) custom-call(s32[4]{0:T(128)S(1)} %pad_add_fusion.scal, bf16[1024,704]{1,0:T(8,128)(2,1)S(1)} %get-tuple-element.24.x_turned, ...), custom_call_target="tpu_custom_call" | custom-call | flops 738197504 | bytes 5242880 | tf_op jit(solution)/shard_map/value_grad/pallas_call | solution.py:314
  57.7 1.4 %collective-permute-start.25 = (bf16[256,256]{1,0:T(8,128)(2,1)S(1)}, bf16[256,256]{1,0:T(8,128)(2,1)S(1)}, u32[]{:S(2)}, u32[]{:S(2)}) collective-permute-start(bf16[256,256]{1,0:T(8,128)(2,1)S(1)} %get-tuple-element.36), channel_id=1, source_target_pairs={{0,1},{1,0},{2,3},{3,2},{4,5},{5,4},{6,7},{7,6},{8,9},{9,8},{10,11... | collective-permute-start | bytes 393224 | tf_op jit(solution)/shard_map/ppermute | solution.py:36
  59.1 1.8 %collective-permute-start.26 = (bf16[256,256]{1,0:T(8,128)(2,1)S(1)}, bf16[256,256]{1,0:T(8,128)(2,1)S(1)}, u32[]{:S(2)}, u32[]{:S(2)}) collective-permute-start(bf16[256,256]{1,0:T(8,128)(2,1)S(1)} %get-tuple-element.37), channel_id=1, source_target_pairs={{0,2},{1,3},{2,0},{3,1},{4,6},{5,7},{6,4},{7,5},{8,10},{9,11},{10,... | collective-permute-start | bytes 393224 | tf_op jit(solution)/shard_map/ppermute | solution.py:36
  61.2 1.3 %collective-permute-start.20 = (bf16[256,256]{1,0:T(8,128)(2,1)S(1)}, bf16[256,256]{1,0:T(8,128)(2,1)S(1)}, u32[]{:S(2)}, u32[]{:S(2)}) collective-permute-start(bf16[256,256]{1,0:T(8,128)(2,1)S(1)} %get-tuple-element.32.refs_0_), channel_id=1, source_target_pairs={{0,1},{1,0},{2,3},{3,2},{4,5},{5,4},{6,7},{7,6},{8,9},{9,8},{10,11... | collective-permute-start | bytes 393224 | tf_op jit(solution)/shard_map/ppermute | solution.py:36
  64.0 2.9 %collective-permute-done.26 = bf16[256,256]{1,0:T(8,128)(2,1)S(1)} collective-permute-done((bf16[256,256]{1,0:T(8,128)(2,1)S(1)}, bf16[256,256]{1,0:T(8,128)(2,1)S(1)}, u32[]{:S(2)}, u32[]{:S(2)}) %collective-permute-start.26) | collective-permute-done | bytes 131104 | tf_op jit(solution)/shard_map/ppermute | solution.py:36
  66.9 1.2 %collective-permute-done.27 = bf16[256,256]{1,0:T(8,128)(2,1)S(1)} collective-permute-done((bf16[256,256]{1,0:T(8,128)(2,1)S(1)}, bf16[256,256]{1,0:T(8,128)(2,1)S(1)}, u32[]{:S(2)}, u32[]{:S(2)}) %collective-permute-start.27) | collective-permute-done | bytes 131104 | tf_op jit(solution)/shard_map/ppermute | solution.py:36
  68.2 1.8 %collective-permute-start.28 = (bf16[256,256]{1,0:T(8,128)(2,1)S(1)}, bf16[256,256]{1,0:T(8,128)(2,1)S(1)}, u32[]{:S(2)}, u32[]{:S(2)}) collective-permute-start(bf16[256,256]{1,0:T(8,128)(2,1)S(1)} %add_convert_fusion.2), channel_id=1, source_target_pairs={{0,16},{4,20},{8,24},{12,28},{16,0},{20,4},{24,8},{28,12},{1,17},{... | collective-permute-start | bytes 393224 | tf_op jit(solution)/shard_map/ppermute | solution.py:36
  70.1 2.1 %collective-permute-done.22.refs_3_ = bf16[256,256]{1,0:T(8,128)(2,1)S(1)} collective-permute-done((bf16[256,256]{1,0:T(8,128)(2,1)S(1)}, bf16[256,256]{1,0:T(8,128)(2,1)S(1)}, u32[]{:S(2)}, u32[]{:S(2)}) %collective-permute-start.22) | collective-permute-done | bytes 131104 | tf_op jit(solution)/shard_map/ppermute | solution.py:36
  72.1 3.0 %attend_project.1 = (f32[2,144,1024]{2,1,0:T(8,128)S(1)}, bf16[2,144,1024]{2,1,0:T(8,128)(2,1)S(1)}) custom-call(s32[4]{0:T(128)S(1)} %pad_add_fusion.scal, bf16[704,1024]{1,0:T(8,128)(2,1)S(1)} %get-tuple-element.21.x_all, bf16[4,176,576]{2,1,0:T(8,128)(2,1)S(1)} %soft_weights.1.soft, bf16[256,1024]{1,0:T(8,128)(2,1)S(1)} %get-tuple-element.31.wo, ...), custom_call_target="tpu_custom_call" | custom-call | flops 738197504 | bytes 5242880 | tf_op jit(solution)/shard_map/attend_project/pallas_call | solution.py:336
  76.2 5.0 %collective-permute-done.29 = bf16[256,256]{1,0:T(8,128)(2,1)S(1)} collective-permute-done((bf16[256,256]{1,0:T(8,128)(2,1)S(1)}, bf16[256,256]{1,0:T(8,128)(2,1)S(1)}, u32[]{:S(2)}, u32[]{:S(2)}) %collective-permute-start.29) | collective-permute-done | bytes 131104 | tf_op jit(solution)/shard_map/ppermute | solution.py:36
  82.9 1.1 %maximum_convert_fusion = f32[256,1024]{1,0:T(8,128)} fusion(bf16[256,256]{1,0:T(8,128)(2,1)S(1)} %get-tuple-element.44, bf16[256,256]{1,0:T(8,128)(2,1)S(1)} %get-tuple-element.47, bf16[256,256]{1,0:T(8,128)(2,1)S(1)} %get-tuple-element.43, bf16[256,256]{1,0:T(8,128)(2,1)S(1)} %get-tuple-element.48), kind=kLoop, calls=%fused_computation.4 | loop fusion | flops 2097152 | bytes 1572864 | tf_op jit(solution)/shard_map/convert_element_type | solution.py:372
  84.0 7.0 %collective-permute-done.24 = bf16[144,1024]{1,0:T(8,128)(2,1)S(1)} collective-permute-done((bf16[144,1024]{1,0:T(8,128)(2,1)S(1)}, bf16[144,1024]{1,0:T(8,128)(2,1)S(1)}, u32[]{:S(2)}, u32[]{:S(2)}) %collective-permute-start.24) | collective-permute-done | bytes 294944 | tf_op jit(solution)/shard_map/ppermute | solution.py:36
  (73 shorter events, 22.0 us)
Async XLA Ops:
  1.4 8.0 %collective-permute-start = (bf16[16,1024]{1,0:T(8,128)(2,1)S(1)}, bf16[16,1024]{1,0:T(8,128)(2,1)S(1)}, u32[]{:S(2)}, u32[]{:S(2)}) collective-permute-start(bf16[16,1024]{1,0:T(8,128)(2,1)S(1)} %slice_bitcast_fusion.5), channel_id=1, source_target_pairs={{0,4},{4,8},{8,12},{12,16},{16,20},{20,24},{24,28},{1,5},{5,9},{9,... | collective-permute-start | bytes 98312 | tf_op jit(solution)/shard_map/ppermute | solution.py:41
  3.7 5.6 %collective-permute-start.1 = (bf16[8,1024]{1,0:T(8,128)(2,1)}, bf16[8,1024]{1,0:T(8,128)(2,1)S(1)}, u32[]{:S(2)}, u32[]{:S(2)}) collective-permute-start(bf16[8,1024]{1,0:T(8,128)(2,1)} %bitcast.35), channel_id=1, source_target_pairs={{0,4},{4,8},{8,12},{12,16},{16,20},{20,24},{24,28},{1,5},{5,9},{9,... | collective-permute-start | bytes 49160 | tf_op jit(solution)/shard_map/ppermute | solution.py:41
  12.1 19.1 %collective-permute-start.3 = (bf16[176,1024]{1,0:T(8,128)(2,1)S(1)}, bf16[176,1024]{1,0:T(8,128)(2,1)S(1)}, u32[]{:S(2)}, u32[]{:S(2)}) collective-permute-start(bf16[176,1024]{1,0:T(8,128)(2,1)S(1)} %norm.1.refs_0_), channel_id=1, source_target_pairs={{0,8},{4,12},{8,0},{12,4},{16,24},{20,28},{24,16},{28,20},{1,9},{5... | collective-permute-start | bytes 1081352 | tf_op jit(solution)/shard_map/ppermute | solution.py:36
  21.6 5.5 %collective-permute-start.8 = (bf16[256,256]{1,0:T(8,128)(2,1)S(1)}, bf16[256,256]{1,0:T(8,128)(2,1)S(1)}, u32[]{:S(2)}, u32[]{:S(2)}) collective-permute-start(bf16[256,256]{1,0:T(8,128)(2,1)S(1)} %get-tuple-element.23.refs_4_), channel_id=1, source_target_pairs={{0,1},{1,0},{2,3},{3,2},{4,5},{5,4},{6,7},{7,6},{8,9},{9,8},{10,11... | collective-permute-start | bytes 393224 | tf_op jit(solution)/shard_map/ppermute | solution.py:36
  23.2 6.0 %collective-permute-start.6 = (bf16[256,256]{1,0:T(8,128)(2,1)S(1)}, bf16[256,256]{1,0:T(8,128)(2,1)S(1)}, u32[]{:S(2)}, u32[]{:S(2)}) collective-permute-start(bf16[256,256]{1,0:T(8,128)(2,1)S(1)} %get-tuple-element.22.refs_0_), channel_id=1, source_target_pairs={{0,2},{1,3},{2,0},{3,1},{4,6},{5,7},{6,4},{7,5},{8,10},{9,11},{10,... | collective-permute-start | bytes 393224 | tf_op jit(solution)/shard_map/ppermute | solution.py:36
  24.7 5.6 %collective-permute-start.5 = (bf16[256,256]{1,0:T(8,128)(2,1)S(1)}, bf16[256,256]{1,0:T(8,128)(2,1)S(1)}, u32[]{:S(2)}, u32[]{:S(2)}) collective-permute-start(bf16[256,256]{1,0:T(8,128)(2,1)S(1)} %get-tuple-element.22.refs_0_), channel_id=1, source_target_pairs={{0,1},{1,0},{2,3},{3,2},{4,5},{5,4},{6,7},{7,6},{8,9},{9,8},{10,11... | collective-permute-start | bytes 393224 | tf_op jit(solution)/shard_map/ppermute | solution.py:36
  25.2 6.0 %collective-permute-start.9 = (bf16[256,256]{1,0:T(8,128)(2,1)S(1)}, bf16[256,256]{1,0:T(8,128)(2,1)S(1)}, u32[]{:S(2)}, u32[]{:S(2)}) collective-permute-start(bf16[256,256]{1,0:T(8,128)(2,1)S(1)} %get-tuple-element.23.refs_4_), channel_id=1, source_target_pairs={{0,2},{1,3},{2,0},{3,1},{4,6},{5,7},{6,4},{7,5},{8,10},{9,11},{10,... | collective-permute-start | bytes 393224 | tf_op jit(solution)/shard_map/ppermute | solution.py:36
  27.2 12.4 %collective-permute-start.12 = (bf16[144,1024]{1,0:T(8,128)(2,1)S(1)}, bf16[144,1024]{1,0:T(8,128)(2,1)S(1)}, u32[]{:S(2)}, u32[]{:S(2)}) collective-permute-start(bf16[144,1024]{1,0:T(8,128)(2,1)S(1)} %get-tuple-element.25.refs_0_), channel_id=1, source_target_pairs={{0,8},{4,12},{8,0},{12,4},{16,24},{20,28},{24,16},{28,20},{1,9},{5... | collective-permute-start | bytes 884744 | tf_op jit(solution)/shard_map/ppermute | solution.py:36
  29.2 5.0 %collective-permute-start.14 = (bf16[256,256]{1,0:T(8,128)(2,1)S(1)}, bf16[256,256]{1,0:T(8,128)(2,1)S(1)}, u32[]{:S(2)}, u32[]{:S(2)}) collective-permute-start(bf16[256,256]{1,0:T(8,128)(2,1)S(1)} %get-tuple-element.26.refs_0_), channel_id=1, source_target_pairs={{0,1},{1,0},{2,3},{3,2},{4,5},{5,4},{6,7},{7,6},{8,9},{9,8},{10,11... | collective-permute-start | bytes 393224 | tf_op jit(solution)/shard_map/ppermute | solution.py:36
  30.3 5.9 %collective-permute-start.15 = (bf16[256,256]{1,0:T(8,128)(2,1)S(1)}, bf16[256,256]{1,0:T(8,128)(2,1)S(1)}, u32[]{:S(2)}, u32[]{:S(2)}) collective-permute-start(bf16[256,256]{1,0:T(8,128)(2,1)S(1)} %get-tuple-element.26.refs_0_), channel_id=1, source_target_pairs={{0,2},{1,3},{2,0},{3,1},{4,6},{5,7},{6,4},{7,5},{8,10},{9,11},{10,... | collective-permute-start | bytes 393224 | tf_op jit(solution)/shard_map/ppermute | solution.py:36
  31.2 15.0 %collective-permute-start.2 = (bf16[176,1024]{1,0:T(8,128)(2,1)S(1)}, bf16[176,1024]{1,0:T(8,128)(2,1)S(1)}, u32[]{:S(2)}, u32[]{:S(2)}) collective-permute-start(bf16[176,1024]{1,0:T(8,128)(2,1)S(1)} %norm.1.refs_0_), channel_id=1, source_target_pairs={{0,4},{4,0},{8,12},{12,8},{16,20},{20,16},{24,28},{28,24},{1,5},{5... | collective-permute-start | bytes 1081352 | tf_op jit(solution)/shard_map/ppermute | solution.py:36
  31.2 15.9 %collective-permute-start.4 = (bf16[176,1024]{1,0:T(8,128)(2,1)S(1)}, bf16[176,1024]{1,0:T(8,128)(2,1)S(1)}, u32[]{:S(2)}, u32[]{:S(2)}) collective-permute-start(bf16[176,1024]{1,0:T(8,128)(2,1)S(1)} %collective-permute-done.3.refs_2_), channel_id=1, source_target_pairs={{0,4},{4,0},{8,12},{12,8},{16,20},{20,16},{24,28},{28,24},{1,5},{5... | collective-permute-start | bytes 1081352 | tf_op jit(solution)/shard_map/ppermute | solution.py:36
  34.2 5.3 %collective-permute-start.10 = (bf16[256,256]{1,0:T(8,128)(2,1)S(1)}, bf16[256,256]{1,0:T(8,128)(2,1)S(1)}, u32[]{:S(2)}, u32[]{:S(2)}) collective-permute-start(bf16[256,256]{1,0:T(8,128)(2,1)S(1)} %collective-permute-done.8.refs_5_), channel_id=1, source_target_pairs={{0,2},{1,3},{2,0},{3,1},{4,6},{5,7},{6,4},{7,5},{8,10},{9,11},{10,... | collective-permute-start | bytes 393224 | tf_op jit(solution)/shard_map/ppermute | solution.py:36
  36.3 5.0 %collective-permute-start.16 = (bf16[256,256]{1,0:T(8,128)(2,1)S(1)}, bf16[256,256]{1,0:T(8,128)(2,1)S(1)}, u32[]{:S(2)}, u32[]{:S(2)}) collective-permute-start(bf16[256,256]{1,0:T(8,128)(2,1)S(1)} %collective-permute-done.14.refs_1_), channel_id=1, source_target_pairs={{0,2},{1,3},{2,0},{3,1},{4,6},{5,7},{6,4},{7,5},{8,10},{9,11},{10,... | collective-permute-start | bytes 393224 | tf_op jit(solution)/shard_map/ppermute | solution.py:36
  39.5 11.4 %collective-permute-start.11 = (bf16[144,1024]{1,0:T(8,128)(2,1)S(1)}, bf16[144,1024]{1,0:T(8,128)(2,1)S(1)}, u32[]{:S(2)}, u32[]{:S(2)}) collective-permute-start(bf16[144,1024]{1,0:T(8,128)(2,1)S(1)} %get-tuple-element.25.refs_0_), channel_id=1, source_target_pairs={{0,4},{4,0},{8,12},{12,8},{16,20},{20,16},{24,28},{28,24},{1,5},{5... | collective-permute-start | bytes 884744 | tf_op jit(solution)/shard_map/ppermute | solution.py:36
  39.5 15.0 %collective-permute-start.13 = (bf16[144,1024]{1,0:T(8,128)(2,1)S(1)}, bf16[144,1024]{1,0:T(8,128)(2,1)S(1)}, u32[]{:S(2)}, u32[]{:S(2)}) collective-permute-start(bf16[144,1024]{1,0:T(8,128)(2,1)S(1)} %collective-permute-done.12.refs_2_), channel_id=1, source_target_pairs={{0,4},{4,0},{8,12},{12,8},{16,20},{20,16},{24,28},{28,24},{1,5},{5... | collective-permute-start | bytes 884744 | tf_op jit(solution)/shard_map/ppermute | solution.py:36
  41.2 5.0 %collective-permute-start.7 = (bf16[256,256]{1,0:T(8,128)(2,1)S(1)}, bf16[256,256]{1,0:T(8,128)(2,1)S(1)}, u32[]{:S(2)}, u32[]{:S(2)}) collective-permute-start(bf16[256,256]{1,0:T(8,128)(2,1)S(1)} %collective-permute-done.6.refs_2_), channel_id=1, source_target_pairs={{0,1},{1,0},{2,3},{3,2},{4,5},{5,4},{6,7},{7,6},{8,9},{9,8},{10,11... | collective-permute-start | bytes 393224 | tf_op jit(solution)/shard_map/ppermute | solution.py:36
  46.2 5.9 %collective-permute-start.17 = (bf16[256,256]{1,0:T(8,128)(2,1)S(1)}, bf16[256,256]{1,0:T(8,128)(2,1)S(1)}, u32[]{:S(2)}, u32[]{:S(2)}) collective-permute-start(bf16[256,256]{1,0:T(8,128)(2,1)S(1)} %get-tuple-element.28), channel_id=1, source_target_pairs={{0,4},{4,0},{8,12},{12,8},{16,20},{20,16},{24,28},{28,24},{1,5},{5... | collective-permute-start | bytes 393224 | tf_op jit(solution)/shard_map/ppermute | solution.py:36
  46.2 6.3 %collective-permute-start.18 = (bf16[256,256]{1,0:T(8,128)(2,1)S(1)}, bf16[256,256]{1,0:T(8,128)(2,1)S(1)}, u32[]{:S(2)}, u32[]{:S(2)}) collective-permute-start(bf16[256,256]{1,0:T(8,128)(2,1)S(1)} %get-tuple-element.29), channel_id=1, source_target_pairs={{0,8},{4,12},{8,0},{12,4},{16,24},{20,28},{24,16},{28,20},{1,9},{5... | collective-permute-start | bytes 393224 | tf_op jit(solution)/shard_map/ppermute | solution.py:36
  47.1 7.4 %collective-permute-start.19 = (bf16[256,256]{1,0:T(8,128)(2,1)S(1)}, bf16[256,256]{1,0:T(8,128)(2,1)S(1)}, u32[]{:S(2)}, u32[]{:S(2)}) collective-permute-start(bf16[256,256]{1,0:T(8,128)(2,1)S(1)} %get-tuple-element.30), channel_id=1, source_target_pairs={{0,12},{4,8},{8,4},{12,0},{16,28},{20,24},{24,20},{28,16},{1,13},{... | collective-permute-start | bytes 393224 | tf_op jit(solution)/shard_map/ppermute | solution.py:36
  50.9 11.7 %collective-permute-start.21 = (bf16[256,256]{1,0:T(8,128)(2,1)S(1)}, bf16[256,256]{1,0:T(8,128)(2,1)S(1)}, u32[]{:S(2)}, u32[]{:S(2)}) collective-permute-start(bf16[256,256]{1,0:T(8,128)(2,1)S(1)} %get-tuple-element.32.refs_0_), channel_id=1, source_target_pairs={{0,2},{1,3},{2,0},{3,1},{4,6},{5,7},{6,4},{7,5},{8,10},{9,11},{10,... | collective-permute-start | bytes 393224 | tf_op jit(solution)/shard_map/ppermute | solution.py:36
  57.7 6.4 %collective-permute-start.25 = (bf16[256,256]{1,0:T(8,128)(2,1)S(1)}, bf16[256,256]{1,0:T(8,128)(2,1)S(1)}, u32[]{:S(2)}, u32[]{:S(2)}) collective-permute-start(bf16[256,256]{1,0:T(8,128)(2,1)S(1)} %get-tuple-element.36), channel_id=1, source_target_pairs={{0,1},{1,0},{2,3},{3,2},{4,5},{5,4},{6,7},{7,6},{8,9},{9,8},{10,11... | collective-permute-start | bytes 393224 | tf_op jit(solution)/shard_map/ppermute | solution.py:36
  59.1 7.9 %collective-permute-start.26 = (bf16[256,256]{1,0:T(8,128)(2,1)S(1)}, bf16[256,256]{1,0:T(8,128)(2,1)S(1)}, u32[]{:S(2)}, u32[]{:S(2)}) collective-permute-start(bf16[256,256]{1,0:T(8,128)(2,1)S(1)} %get-tuple-element.37), channel_id=1, source_target_pairs={{0,2},{1,3},{2,0},{3,1},{4,6},{5,7},{6,4},{7,5},{8,10},{9,11},{10,... | collective-permute-start | bytes 393224 | tf_op jit(solution)/shard_map/ppermute | solution.py:36
  60.9 7.3 %collective-permute-start.27 = (bf16[256,256]{1,0:T(8,128)(2,1)S(1)}, bf16[256,256]{1,0:T(8,128)(2,1)S(1)}, u32[]{:S(2)}, u32[]{:S(2)}) collective-permute-start(bf16[256,256]{1,0:T(8,128)(2,1)S(1)} %get-tuple-element.38), channel_id=1, source_target_pairs={{0,3},{1,2},{2,1},{3,0},{4,7},{5,6},{6,5},{7,4},{8,11},{9,10},{10,... | collective-permute-start | bytes 393224 | tf_op jit(solution)/shard_map/ppermute | solution.py:36
  61.2 8.8 %collective-permute-start.20 = (bf16[256,256]{1,0:T(8,128)(2,1)S(1)}, bf16[256,256]{1,0:T(8,128)(2,1)S(1)}, u32[]{:S(2)}, u32[]{:S(2)}) collective-permute-start(bf16[256,256]{1,0:T(8,128)(2,1)S(1)} %get-tuple-element.32.refs_0_), channel_id=1, source_target_pairs={{0,1},{1,0},{2,3},{3,2},{4,5},{5,4},{6,7},{7,6},{8,9},{9,8},{10,11... | collective-permute-start | bytes 393224 | tf_op jit(solution)/shard_map/ppermute | solution.py:36
  62.6 9.5 %collective-permute-start.22 = (bf16[256,256]{1,0:T(8,128)(2,1)S(1)}, bf16[256,256]{1,0:T(8,128)(2,1)S(1)}, u32[]{:S(2)}, u32[]{:S(2)}) collective-permute-start(bf16[256,256]{1,0:T(8,128)(2,1)S(1)} %collective-permute-done.21.refs_2_), channel_id=1, source_target_pairs={{0,1},{1,0},{2,3},{3,2},{4,5},{5,4},{6,7},{7,6},{8,9},{9,8},{10,11... | collective-permute-start | bytes 393224 | tf_op jit(solution)/shard_map/ppermute | solution.py:36
  68.2 7.6 %collective-permute-start.28 = (bf16[256,256]{1,0:T(8,128)(2,1)S(1)}, bf16[256,256]{1,0:T(8,128)(2,1)S(1)}, u32[]{:S(2)}, u32[]{:S(2)}) collective-permute-start(bf16[256,256]{1,0:T(8,128)(2,1)S(1)} %add_convert_fusion.2), channel_id=1, source_target_pairs={{0,16},{4,20},{8,24},{12,28},{16,0},{20,4},{24,8},{28,12},{1,17},{... | collective-permute-start | bytes 393224 | tf_op jit(solution)/shard_map/ppermute | solution.py:36
  75.1 6.2 %collective-permute-start.23 = (bf16[2,144,1024]{2,1,0:T(8,128)(2,1)S(1)}, bf16[2,144,1024]{2,1,0:T(8,128)(2,1)S(1)}, u32[]{:S(2)}, u32[]{:S(2)}) collective-permute-start(bf16[2,144,1024]{2,1,0:T(8,128)(2,1)S(1)} %get-tuple-element.34), channel_id=1, source_target_pairs={{0,4},{4,0},{8,12},{12,8},{16,20},{20,16},{24,28},{28,24},{1,5},{5... | collective-permute-start | bytes 1769480 | tf_op jit(solution)/shard_map/ppermute | solution.py:36
  75.9 5.3 %collective-permute-start.29 = (bf16[256,256]{1,0:T(8,128)(2,1)S(1)}, bf16[256,256]{1,0:T(8,128)(2,1)S(1)}, u32[]{:S(2)}, u32[]{:S(2)}) collective-permute-start(bf16[256,256]{1,0:T(8,128)(2,1)S(1)} %add_convert_fusion.1), channel_id=1, source_target_pairs={{0,8},{4,12},{8,0},{12,4},{16,24},{20,28},{24,16},{28,20},{1,9},{5... | collective-permute-start | bytes 393224 | tf_op jit(solution)/shard_map/ppermute | solution.py:36
  81.2 1.6 %collective-permute-start.30 = (bf16[2,256,256]{2,1,0:T(8,128)(2,1)S(1)}, bf16[2,256,256]{2,1,0:T(8,128)(2,1)S(1)}, u32[]{:S(2)}, u32[]{:S(2)}) collective-permute-start(bf16[2,256,256]{2,1,0:T(8,128)(2,1)S(1)} %pad_maximum_fusion), channel_id=1, source_target_pairs={{0,4},{4,0},{8,12},{12,8},{16,20},{20,16},{24,28},{28,24},{1,5},{5... | collective-permute-start | bytes 786440 | tf_op jit(solution)/shard_map/ppermute | solution.py:36
  81.6 9.5 %collective-permute-start.24 = (bf16[144,1024]{1,0:T(8,128)(2,1)S(1)}, bf16[144,1024]{1,0:T(8,128)(2,1)S(1)}, u32[]{:S(2)}, u32[]{:S(2)}) collective-permute-start(bf16[144,1024]{1,0:T(8,128)(2,1)S(1)} %fusion.1), channel_id=1, source_target_pairs={{0,8},{4,12},{8,0},{12,4},{16,24},{20,28},{24,16},{28,20},{1,9},{5... | collective-permute-start | bytes 884744 | tf_op jit(solution)/shard_map/ppermute | solution.py:36
  84.0 7.8 %copy-start.1 = (bf16[1,8,16,1024]{3,2,1,0:T(8,128)(2,1)S(1)}, bf16[1,8,16,1024]{3,2,1,0:T(8,128)(2,1)}, u32[]{:S(2)}) copy-start(bf16[1,8,16,1024]{3,2,1,0:T(8,128)(2,1)} %param.10) | copy-start | bytes 786436
  (9 other events, 8.2 us)

commit v2 on v1

v2 whole, which is shorter than its diff:
```python
import functools
import math

import jax
import jax.numpy as jnp
from jax import lax
from jax.experimental import pallas as pl
from jax.experimental.pallas import tpu as pltpu
from jax.sharding import PartitionSpec as P

HEADS = 16
LEFT = 16
MEMORY = 8
GROUP = 4


epsilon = 1e-05
masked_score = -1e30
bf16 = jnp.bfloat16
f32 = jnp.float32
vmem = pl.BlockSpec(memory_space=pltpu.VMEM)
smem = pl.BlockSpec(memory_space=pltpu.SMEM)
hbm = pl.BlockSpec(memory_space=pltpu.HBM)
NT = (((1,), (1,)), ((), ()))
TN = (((0,), (0,)), ((), ()))


def params(mib=40):
    return pltpu.CompilerParams(vmem_limit_bytes=mib * 1024 * 1024)


def swapped(array, axis, bit):
    size = lax.axis_size(axis)
    return lax.ppermute(array, axis, [(i, i ^ bit) for i in range(size)])


def halving_bits(size):
    return [1 << b for b in range(size.bit_length() - 1)]


def member_of():
    return lax.axis_index("seg") % GROUP


def aligned(start, step):
    return pl.multiple_of(start * step, step)


def normed_rows(rows, gain):
    wide = rows.astype(f32)
    centred = wide - jnp.mean(wide, axis=-1, keepdims=True)
    var = jnp.mean(centred * centred, axis=-1, keepdims=True)
    return (centred * lax.rsqrt(var + epsilon) * gain).astype(bf16)


def pack_kernel(frame_count, wq, wk, wv, frames, gf, mem, gm, gain, *refs):
    blocks, (tokens, raw, few, one, sems) = refs[:-5], refs[-5:]
    width = blocks[0].shape[1] // 3
    rows, model_width = gf.shape
    segs = mem.shape[0]
    half = tokens.shape[0] // 2
    copies = [
        pltpu.make_async_copy(frames, raw, sems.at[0]),
        pltpu.make_async_copy(gain, one, sems.at[1]),
        pltpu.make_async_copy(mem, few.at[0], sems.at[2]),
        pltpu.make_async_copy(gm, few.at[1], sems.at[3]),
        pltpu.make_async_copy(gf, tokens.at[pl.ds(half, rows)], sems.at[4]),
    ]
    for i, block in enumerate(blocks):
        at = aligned(member_of() ^ i, width)
        for j, w in enumerate((wq, wk, wv)):
            into = block.at[:, pl.ds(j * width, width)]
            sem = sems.at[5 + 3 * i + j]
            copies.append(pltpu.make_async_copy(w.at[:, pl.ds(at, width)], into, sem))
    for copy in copies:
        copy.start()
    for copy in copies[:4]:
        copy.wait()
    normed = normed_rows(raw[...], one[...])
    tokens[:rows, :] = normed
    summary = jnp.sum(normed.astype(f32).reshape(segs, frame_count, model_width), axis=1)
    tokens[rows:half, :] = jnp.concatenate(
        [few[0], (summary / frame_count).astype(bf16)], axis=0
    )
    tokens[half + rows :, :] = jnp.concatenate([jnp.zeros_like(few[1]), few[1]], axis=0)
    for copy in copies[4:]:
        copy.wait()


def merge_kernel(group, *refs):
    parts, halo_a, halo_b, x_all, x_turned, u_all = refs[:group], *refs[group:]
    half = parts[0].shape[0] // 2
    halo = halo_a.shape[0]
    odd = (member_of() & 1) > 0
    x_all[:halo, :] = jnp.where(odd, halo_b[...], halo_a[...])
    for i in range(group):
        at = aligned(member_of() ^ i, half)
        x_all[pl.ds(pl.multiple_of(halo + at, 16), half), :] = parts[i][:half, :]
        u_all[pl.ds(at, half), :] = parts[i][half:, :]
    x_turned[...] = x_all[...].T


def assemble(pieces, whole, crossed):
    own = lax.axis_index("fsdp")
    rows = pieces[0].shape[0]
    flip = lax.axis_index("seg") & 1 if crossed else 0
    for j, piece in enumerate(pieces):
        apart = j ^ (3 * flip) if j in (1, 2) else j
        whole[pl.ds(aligned(own ^ apart, rows), rows), :] = piece[...]


def head_stack(array, heads):
    width = array.shape[1]
    head = lax.broadcasted_iota(jnp.int32, array.shape, 1) // (width // heads)
    zero = jnp.zeros_like(array)
    return jnp.concatenate([jnp.where(head == h, array, zero) for h in range(heads)], axis=0)


def weights_kernel(heads, frame_count, segs, crossed, x_all, *refs):
    soft, values, wqkv = refs[-3:]
    assemble(refs[:-3], wqkv, crossed)
    blocks, keys, lanes = soft.shape
    queries = lanes // heads
    halo = keys - queries
    frames = segs * frame_count
    block = values.shape[1]
    projected = jnp.dot(x_all[...], wqkv[...], preferred_element_type=f32).astype(bf16)
    q_all, k_all = projected[:, :block], projected[:, block : 2 * block]
    values[...] = projected[:, 2 * block :]
    key = lax.broadcasted_iota(jnp.int32, (keys, lanes), 0)
    row = lax.broadcasted_iota(jnp.int32, (keys, lanes), 1)
    for h in range(1, heads):
        row = jnp.where(row >= queries, row - queries, row)
    at = jnp.where(row < frames, row // frame_count, jnp.maximum(row - frames - segs, 0))
    own = key - halo
    own_seg = own // frame_count
    own_mem = own - frames
    valid_own = ((own >= 0) & (own < frames) & ((own_seg == at) | (own_seg == at - 1))) | (
        (own_mem >= 0) & (own_mem < segs) & (own_mem < at) & (own_mem >= at - MEMORY)
    )
    halo_mem = key - LEFT
    valid_halo = ((key < LEFT) & (at == 0)) | (
        (halo_mem >= 0) & (halo_mem < MEMORY) & (halo_mem >= at)
    )
    inside = lax.axis_index("seg") >= blocks
    scale = 1.0 / math.sqrt(block // heads)
    for b in range(blocks):
        valid = valid_own | (valid_halo & inside if b == 0 else valid_halo)
        start = b * queries
        q_b = head_stack(q_all[halo + start : halo + start + queries], heads)
        scores = (
            lax.dot_general(k_all[start : start + keys], q_b, NT, preferred_element_type=f32)
            * scale
        )
        scores = jnp.where(valid, scores, masked_score)
        exponent = jnp.exp(scores - jnp.max(scores, axis=0, keepdims=True))
        soft[b] = (exponent / jnp.sum(exponent, axis=0, keepdims=True)).astype(bf16)


def grad_kernel(count, heads, frame_count, segs, crossed, lengths, x_turned, u_all, soft, *refs):
    outputs = 2 if crossed else count
    wo_from, outs = refs[: -outputs - 3], refs[-outputs - 3 : -3]
    wo, values, whole = refs[-3:]
    blocks, keys, lanes = soft.shape
    queries = lanes // heads
    frames = segs * frame_count
    chosen = wo_from[0][...]
    if len(wo_from) > 1:
        apart = lax.axis_index("fsdp") ^ member_of()
        chosen = jnp.where(
            apart == 0, chosen, jnp.where(apart == 3, wo_from[2][...], wo_from[1][...])
        )
    wo[...] = chosen
    back = lax.dot_general(u_all[...], chosen, NT, preferred_element_type=f32)
    row = lax.broadcasted_iota(jnp.int32, (queries, wo.shape[0]), 0)
    seg_of = jnp.where(row < frames, row // frame_count, row - frames - segs)
    first = lax.axis_index("seg") - member_of()
    values[: keys - queries, :] = jnp.zeros((keys - queries, values.shape[1]), f32)
    for b in range(blocks):
        start = b * queries
        live = ((first + b) * segs + seg_of < lengths[0]).astype(f32)
        grad_attended = head_stack((live * back[start : start + queries]).astype(bf16), heads)
        term = jnp.dot(soft[b], grad_attended, preferred_element_type=f32)
        split = keys - queries
        values[start : start + split, :] += term[:split]
        values[start + split : start + keys, :] = term[split:]
    whole[...] = jnp.dot(
        x_turned[...], values[...].astype(bf16), preferred_element_type=f32
    )
    own = lax.axis_index("fsdp")
    rows = whole.shape[0] // count

    def part(apart, into):
        return whole[pl.ds(aligned(own ^ apart, rows), rows), :].astype(into.dtype)

    if crossed:
        keep, send = outs
        along = 1 + (lax.axis_index("seg") & 1)
        keep[0] = part(0, keep)
        keep[1] = part(along ^ 3, keep)
        send[0] = part(along, send)
        send[1] = part(3, send)
    else:
        for j in range(count):
            outs[j][...] = part(j, outs[j])


def out_kernel(heads, soft, values, wo, keep, send):
    blocks, keys, lanes = soft.shape
    queries = lanes // heads
    width = values.shape[1]
    head = lax.broadcasted_iota(jnp.int32, (queries, width), 1) // (width // heads)
    for i in range(blocks):
        b = member_of() ^ i
        stacked = lax.dot_general(
            soft[b],
            values[pl.ds(aligned(b, queries), keys), :],
            TN,
            preferred_element_type=f32,
        )
        attended = stacked[:queries]
        for h in range(1, heads):
            attended = jnp.where(head == h, stacked[h * queries : (h + 1) * queries], attended)
        projected = jnp.dot(attended.astype(bf16), wo[...], preferred_element_type=f32)
        into = send if i & 1 else keep
        into[i // 2] = projected.astype(into.dtype)


def gathered(piece):
    size = lax.axis_size("fsdp")
    pieces = {0: piece}
    bit = 1
    while bit < size:
        for have in sorted(pieces):
            pieces[have ^ bit] = swapped(pieces[have], "fsdp", bit)
        bit *= 2
    return [pieces[j] for j in range(size)]


def pairs(seg_size):
    straight, turned, beside, across = [], [], [], []
    for s in range(seg_size):
        along = 2 if s & 1 else 1
        for f in range(GROUP):
            straight.append((s * GROUP + f, s * GROUP + (f ^ along)))
            turned.append((s * GROUP + f, s * GROUP + (f ^ along ^ 3)))
        k = s % GROUP
        beside.append((s * GROUP + k, s * GROUP + (k ^ 1)))
        beside.append(((s ^ 1) * GROUP + k, s * GROUP + (k ^ 2)))
        across.append((s * GROUP + (k ^ 2), s * GROUP + (k ^ 3)))
    return straight, turned, beside, across


def on_device(
    frames, memory_in, lengths, ln_gain, w_query, w_key, w_value, w_out, grad_frames, grad_memory
):
    utterances, segs, frame_count, width = frames.shape
    seg_size = lax.axis_size("seg")
    fsdp_size = lax.axis_size("fsdp")
    group = GROUP
    assert utterances == 1 and segs == MEMORY and frame_count == LEFT and seg_size % group == 0
    heads = HEADS // group
    block = width // group
    rows = w_query.shape[0]
    frame_rows = segs * frame_count
    queries = frame_rows + 2 * segs
    halo_rows = LEFT + 2 * MEMORY
    keys = halo_rows + queries
    all_rows = halo_rows + group * queries
    seg = lax.axis_index("seg")
    member = seg % group

    crossed = fsdp_size == group
    *own_blocks, tokens = pl.pallas_call(
        functools.partial(pack_kernel, frame_count),
        in_specs=[hbm] * 8,
        out_specs=[vmem] * (2 + crossed),
        out_shape=[jax.ShapeDtypeStruct((rows, 3 * block), bf16)] * (1 + crossed)
        + [
            jax.ShapeDtypeStruct((2 * queries, width), bf16),
        ],
        scratch_shapes=[
            pltpu.VMEM((frame_rows, width), bf16),
            pltpu.VMEM((2, segs, width), bf16),
            pltpu.VMEM((1, width), f32),
            pltpu.SemaphoreType.DMA((11,)),
        ],
        compiler_params=params(60),
        name="pack",
    )(
        w_query, w_key, w_value, frames.reshape(frame_rows, width),
        grad_frames.reshape(frame_rows, width), memory_in.reshape(segs, width),
        grad_memory.reshape(segs, width), ln_gain.reshape(1, width),
    )
    w_out, own_blocks = lax.optimization_barrier((w_out, own_blocks))

    far = swapped(tokens, "seg", 2)
    near = swapped(tokens, "seg", 1)
    cut = slice(queries - halo_rows, queries)
    tail = jnp.where(member == group - 1, tokens[cut], near[cut])
    if crossed:
        both = ("seg", "fsdp")
        straight, turned, beside, across = pairs(seg_size)
        mine = lax.ppermute(own_blocks[0], both, straight)
        other = lax.ppermute(own_blocks[1], both, straight)
        wo_near = lax.ppermute(w_out, both, beside)
        wqkv_parts = [
            own_blocks[0], mine, swapped(other, "seg", 1), lax.ppermute(mine, both, turned)
        ]
        wo_from = [w_out, wo_near, lax.ppermute(wo_near, both, across)]
    else:
        wqkv_parts = gathered(own_blocks[0])
        wo_from = [
            lax.dynamic_slice_in_dim(
                lax.all_gather(w_out, "fsdp", axis=0, tiled=True), member * block, block, 0
            )
        ]
    ahead = []
    for s in range(group, seg_size, group):
        ahead += [(s - 1, s), (s - 2, s + 2)]
    halo_even = lax.ppermute(tail, "seg", ahead)
    halo_odd = lax.ppermute(halo_even, "seg", [(s, s + 1) for s in range(0, seg_size, 2)])
    parts = [tokens, near, far, swapped(far, "seg", 1)]

    x_all, x_turned, u_all = pl.pallas_call(
        functools.partial(merge_kernel, group),
        in_specs=[vmem] * (group + 2),
        out_specs=[vmem] * 3,
        out_shape=[
            jax.ShapeDtypeStruct((all_rows, width), bf16),
            jax.ShapeDtypeStruct((width, all_rows), bf16),
            jax.ShapeDtypeStruct((group * queries, width), bf16),
        ],
        compiler_params=params(),
        name="merge",
    )(*parts, halo_even, halo_odd)

    soft, values = pl.pallas_call(
        functools.partial(weights_kernel, heads, frame_count, segs, crossed),
        in_specs=[vmem] * (1 + fsdp_size),
        out_specs=[vmem] * 2,
        out_shape=[
            jax.ShapeDtypeStruct((group, keys, heads * queries), bf16),
            jax.ShapeDtypeStruct((all_rows, block), bf16),
        ],
        scratch_shapes=[pltpu.VMEM((width, 3 * block), bf16)],
        compiler_params=params(),
        name="soft_weights",
    )(x_all, *wqkv_parts)

    if crossed:
        grad_shapes = [jax.ShapeDtypeStruct((2, rows, block), dtype) for dtype in (f32, bf16)]
    else:
        grad_shapes = [jax.ShapeDtypeStruct((rows, block), bf16)] * fsdp_size
    *grad_chunks, wo_mine = pl.pallas_call(
        functools.partial(grad_kernel, fsdp_size, heads, frame_count, segs, crossed),
        in_specs=[smem] + [vmem] * (3 + len(wo_from)),
        out_specs=[vmem] * (len(grad_shapes) + 1),
        out_shape=grad_shapes + [jax.ShapeDtypeStruct((block, width), bf16)],
        scratch_shapes=[
            pltpu.VMEM((all_rows, block), f32),
            pltpu.VMEM((width, block), f32),
        ],
        compiler_params=params(),
        name="value_grad",
    )(lengths, x_turned, u_all, soft, *wo_from)

    keep, send = pl.pallas_call(
        functools.partial(out_kernel, heads),
        in_specs=[vmem] * 3,
        out_specs=[vmem] * 2,
        out_shape=[
            jax.ShapeDtypeStruct((group // 2, queries, width), f32),
            jax.ShapeDtypeStruct((group // 2, queries, width), bf16),
        ],
        compiler_params=params(),
        name="attend_project",
    )(soft, values, wo_mine)
    near = swapped(send, "seg", 1)
    onward = (keep[1] + near[1].astype(f32)).astype(bf16)
    if crossed:
        kept, sent = grad_chunks
        came = lax.ppermute(sent, both, straight)
        came, _ = lax.optimization_barrier((came, send))
        passing = (kept[1] + came[1].astype(f32)).astype(bf16)
        grad_sum = kept[0] + came[0].astype(f32)
        grad_sum = grad_sum + lax.ppermute(passing, both, turned).astype(f32)
    else:
        grad_sum = grad_chunks[0].astype(f32)
        for j in range(1, fsdp_size):
            grad_sum = grad_sum + swapped(grad_chunks[j], "fsdp", j).astype(f32)
    bit = group
    while bit < seg_size:
        mine = grad_sum.astype(bf16)
        grad_sum = mine.astype(f32) + swapped(mine, "seg", bit).astype(f32)
        bit *= 2
    mine = grad_sum.astype(bf16)
    projected = keep[0] + near[0].astype(f32) + swapped(onward, "seg", 2).astype(f32)

    live = (seg * segs + jnp.arange(segs) < lengths[0]).astype(f32)
    frames_out = (
        frames.astype(f32)
        + live[None, :, None, None]
        * projected[:frame_rows].reshape(1, segs, frame_count, width)
    ).astype(bf16)
    memory_out = (live[None, :, None] * projected[None, frame_rows + segs :]).astype(bf16)

    far = swapped(mine, "seg", 2)
    high = (member & 2) > 0
    pair = jnp.stack([jnp.where(high, far, mine), jnp.where(high, mine, far)])
    near = swapped(pair, "seg", 1)
    odd = (member & 1) > 0
    value_grad = jnp.concatenate(
        [
            part[j]
            for j in range(2)
            for part in (jnp.where(odd, near, pair), jnp.where(odd, pair, near))
        ],
        axis=1,
    ).astype(f32)
    return (frames_out, memory_out, value_grad)


def solution(mesh):
    return jax.shard_map(
        on_device,
        mesh=mesh,
        in_specs=(
            P("fsdp", "seg", None, None),
            P("fsdp", "seg", None),
            P("fsdp"),
            P(),
            P("fsdp", None),
            P("fsdp", None),
            P("fsdp", None),
            P("fsdp", None),
            P("fsdp", "seg", None, None),
            P("fsdp", "seg", None),
        ),
        out_specs=(P("fsdp", "seg", None, None), P("fsdp", "seg", None), P("fsdp", None)),
        check_vma=False,
    )
```

time: 93.3 us -> 75 us (0.80)
  waiting for transfers between devices: 37.5 us -> 29.2 us
  local copies, waits for them, and re-layouts: 9.07 us -> 1.55 us
  starting transfers between devices: 31 us -> 29.3 us
  Pallas kernels: 10.5 us -> 9.23 us
    ppermute x29 -> x9, waiting for transfers between devices: 36.5 us -> 20.2 us  [swapped(): return lax.ppermute(array, axis, [(i, i ^ bit) for i in range(size)])]
    ppermute x29 -> x9, starting transfers between devices: 24 us -> 13.1 us  [swapped(): return lax.ppermute(array, axis, [(i, i ^ bit) for i in range(size)])]
    ppermute x2 -> x9, starting transfers between devices: 6.94 us -> 16.2 us  [the longest x1 4.33 us: on_device(): lax.ppermute(mine, both, turned)]
    ppermute x2 -> x9, waiting for transfers between devices: 1.03 us -> 8.95 us  [the longest x1 3.73 us: on_device(): grad_sum = grad_sum + lax.ppermute(passing, both, turned).astype(f32)]
    unnamed x20 -> x8, local copies, waits for them, and re-layouts: 8.19 us -> 1.48 us
    pallas_call x6 -> x4, Pallas kernels: 10 us -> 8.67 us  [the longest x1 3.05 us: on_device(): pl.pallas_call(functools.partial(weights_kernel, heads, frame_count, segs...]
  transfers between devices with their start and end apart: 31 -> 18, of which waited for: 19 -> 9; matrix products, arithmetic and copies ran while one was open for 2% -> 4% of each run, Pallas kernels for 11% -> 6%
where the time goes in v2:
time: 75 us; the launch traced here: 74.6 us
  starting transfers between devices  29.3 us (39%)
  waiting for transfers between devices  29.2 us (39%)
  Pallas kernels  9.23 us (12%)
  other arithmetic  3.82 us (5%)
  local copies, waits for them, and re-layouts  1.55 us (2%)
  between operations  1.51 us (2%)
    ppermute x9, waiting for transfers between devices, swapped(): return lax.ppermute(array, axis, [(i, i ^ bit) for i in range(size)])  20.2 us
    ppermute x9, starting transfers between devices, swapped(): return lax.ppermute(array, axis, [(i, i ^ bit) for i in range(size)])  13.1 us
    ppermute x1, starting transfers between devices, on_device(): lax.ppermute(mine, both, turned)  4.33 us
    ppermute x1, waiting for transfers between devices, on_device(): grad_sum = grad_sum + lax.ppermute(passing, both, turned).astype(f32)  3.73 us
    ppermute x1, starting transfers between devices, on_device(): wo_near = lax.ppermute(w_out, both, beside)  3.42 us
    ppermute x1, waiting for transfers between devices, on_device(): came = lax.ppermute(sent, both, straight)  3.3 us
    pallas_call x1, Pallas kernels, on_device(): pl.pallas_call(functools.partial(weights_kernel, heads, frame_count, segs...  3.05 us
    pallas_call x1, Pallas kernels, on_device(): pl.pallas_call(functools.partial(pack_kernel, frame_count), in_specs=[hbm...  2.56 us
  transfers between devices with their start and end apart: 18, of which 9 were waited for; matrix products, arithmetic and copies ran while one was open for 4% of the time, Pallas kernels for 6%

profile of v2, /device:TPU:0, one launch (start us, length us, event | category | flops | bytes accessed | tf_op | source)
XLA Modules:
  0.0 74.6 jit_solution(1497941274375763296)
XLA Ops:
  0.6 2.6 %pack.1 = (bf16[256,768]{1,0:T(8,128)(2,1)}, bf16[256,768]{1,0:T(8,128)(2,1)}, bf16[288,1024]{1,0:T(8,128)(2,1)}) custom-call(bf16[256,1024]{1,0:T(8,128)(2,1)} %wq.1, bf16[256,1024]{1,0:T(8,128)(2,1)} %wk.1, bf16[256,1024]{1,0:T(8,128)(2,1)} %wv.1, bf16[128,1024]{1,0:T(8,128)(2,1)} %bitcast.33, bf16[128,1024]{1,0:T(8,128)(2,1)} %bitcast.34, ...), custom_call_target="tpu_custom_call" | custom-call | tf_op jit(solution)/shard_map/pack/pallas_call | solution.py:274
  3.2 3.1 %collective-permute-start.1 = (bf16[288,1024]{1,0:T(8,128)(2,1)}, bf16[288,1024]{1,0:T(8,128)(2,1)S(1)}, u32[]{:S(2)}, u32[]{:S(2)}) collective-permute-start(bf16[288,1024]{1,0:T(8,128)(2,1)} %get-tuple-element.20.refs_0_), channel_id=1, source_target_pairs={{0,8},{4,12},{8,0},{12,4},{16,24},{20,28},{24,16},{28,20},{1,9},{5... | collective-permute-start | bytes 1769480 | tf_op jit(solution)/shard_map/ppermute | solution.py:34
  6.3 3.4 %collective-permute-start.9 = (bf16[256,1024]{1,0:T(8,128)(2,1)S(1)}, bf16[256,1024]{1,0:T(8,128)(2,1)S(1)}, u32[]{:S(2)}, u32[]{:S(2)}) collective-permute-start(bf16[256,1024]{1,0:T(8,128)(2,1)S(1)} %copy-done.1), channel_id=1, source_target_pairs={{0,1},{4,2},{5,4},{1,7},{10,11},{14,8},{15,14},{11,13},{16,17},{20... | collective-permute-start | bytes 1572872 | tf_op jit(solution)/shard_map/ppermute | solution.py:306
  9.7 0.2 collective-permute-start
  9.9 0.6 collective-permute-start.5
  10.5 1.4 %collective-permute-start.6 = (bf16[256,768]{1,0:T(8,128)(2,1)}, bf16[256,768]{1,0:T(8,128)(2,1)}, u32[]{:S(2)}, u32[]{:S(2)}) collective-permute-start(bf16[256,768]{1,0:T(8,128)(2,1)} %get-tuple-element.25), channel_id=1, source_target_pairs={{0,1},{1,0},{2,3},{3,2},{4,6},{5,7},{6,4},{7,5},{8,9},{9,8},{10,11... | collective-permute-start | bytes 1179656 | tf_op jit(solution)/shard_map/ppermute | solution.py:305
  11.9 7.9 %collective-permute-done.1.refs_2_ = bf16[288,1024]{1,0:T(8,128)(2,1)S(1)} collective-permute-done((bf16[288,1024]{1,0:T(8,128)(2,1)}, bf16[288,1024]{1,0:T(8,128)(2,1)S(1)}, u32[]{:S(2)}, u32[]{:S(2)}) %collective-permute-start.1) | collective-permute-done | bytes 589856 | tf_op jit(solution)/shard_map/ppermute | solution.py:34
  19.8 0.7 collective-permute-start.10
  20.7 4.3 %collective-permute-start.8 = (bf16[256,768]{1,0:T(8,128)(2,1)}, bf16[256,768]{1,0:T(8,128)(2,1)}, u32[]{:S(2)}, u32[]{:S(2)}) collective-permute-start(bf16[256,768]{1,0:T(8,128)(2,1)} %collective-permute-done.5.refs_1_), channel_id=1, source_target_pairs={{0,2},{1,3},{2,0},{3,1},{4,5},{5,4},{6,7},{7,6},{8,10},{9,11},{10,... | collective-permute-start | bytes 1179656 | tf_op jit(solution)/shard_map/ppermute | solution.py:308
  25.0 1.5 %collective-permute-done.6 = bf16[256,768]{1,0:T(8,128)(2,1)} collective-permute-done((bf16[256,768]{1,0:T(8,128)(2,1)}, bf16[256,768]{1,0:T(8,128)(2,1)}, u32[]{:S(2)}, u32[]{:S(2)}) %collective-permute-start.6) | collective-permute-done | bytes 393248 | tf_op jit(solution)/shard_map/ppermute | solution.py:305
  26.5 0.8 %slice_select_fusion = bf16[32,1024]{1,0:T(8,128)(2,1)S(1)} fusion(bf16[288,1024]{1,0:T(8,128)(2,1)S(1)} %collective-permute-done.refs_1_, bf16[288,1024]{1,0:T(8,128)(2,1)} %get-tuple-element.20.refs_0_, pred[]{:T(512)S(6)} %eq.5), kind=kLoop, calls=%fused_computation.19 | loop fusion | flops 32768 | bytes 196609 | tf_op jit(solution)/shard_map/jit(_where)/select_n | solution.py:300
  27.4 0.7 collective-permute-start.3
  28.1 2.4 %collective-permute-start.4 = (bf16[32,1024]{1,0:T(8,128)(2,1)S(1)}, bf16[32,1024]{1,0:T(8,128)(2,1)S(1)}, u32[]{:S(2)}, u32[]{:S(2)}) collective-permute-start(bf16[32,1024]{1,0:T(8,128)(2,1)S(1)} %collective-permute-done.3.refs_4_), channel_id=1, source_target_pairs={{0,4},{8,12},{16,20},{24,28},{1,5},{9,13},{17,21},{25,29},{2,6},{1... | collective-permute-start | bytes 196616 | tf_op jit(solution)/shard_map/ppermute | solution.py:322
  31.1 0.2 collective-permute-done.4.refs_5_
  31.4 1.1 %copy-done = bf16[288,1024]{1,0:T(8,128)(2,1)S(1)} copy-done((bf16[288,1024]{1,0:T(8,128)(2,1)S(1)}, bf16[288,1024]{1,0:T(8,128)(2,1)}, u32[]{:S(2)}) %copy-start) | copy-done | bytes 589848
  32.5 0.6 merge.1
  33.0 0.4 copy-done.2
  33.4 3.0 %soft_weights.1 = (bf16[4,176,576]{2,1,0:T(8,128)(2,1)S(1)}, bf16[608,256]{1,0:T(8,128)(2,1)S(1)}) custom-call(bf16[608,1024]{1,0:T(8,128)(2,1)S(1)} %get-tuple-element.21.x_all, bf16[256,768]{1,0:T(8,128)(2,1)S(1)} %copy-done.2, bf16[256,768]{1,0:T(8,128)(2,1)} %collective-permute-done.5.refs_1_, bf16[256,768]{1,0:T(8,128)(2,1)} %collective-permute-done.7.refs_2_, ...), custom_call_target="tpu_custom_call" | custom-call | tf_op jit(solution)/shard_map/soft_weights/pallas_call | solution.py:338
  36.5 2.0 %value_grad.1 = (f32[2,256,256]{2,1,0:T(8,128)S(1)}, bf16[2,256,256]{2,1,0:T(8,128)(2,1)S(1)}, bf16[256,1024]{1,0:T(8,128)(2,1)S(1)}) custom-call(s32[1]{0:T(128)} %copy.13.lengths, bf16[1024,608]{1,0:T(8,128)(2,1)S(1)} %get-tuple-element.28.x_turned, bf16[576,1024]{1,0:T(8,128)(2,1)S(1)} %get-tuple-element.29.u_all, ...), custom_call_target="tpu_custom_call" | custom-call | tf_op jit(solution)/shard_map/value_grad/pallas_call | solution.py:355
  38.5 2.5 %collective-permute-start.13 = (bf16[2,256,256]{2,1,0:T(8,128)(2,1)S(1)}, bf16[2,256,256]{2,1,0:T(8,128)(2,1)S(1)}, u32[]{:S(2)}, u32[]{:S(2)}) collective-permute-start(bf16[2,256,256]{2,1,0:T(8,128)(2,1)S(1)} %get-tuple-element.35), channel_id=1, source_target_pairs={{0,1},{1,0},{2,3},{3,2},{4,6},{5,7},{6,4},{7,5},{8,9},{9,8},{10,11... | collective-permute-start | bytes 786440 | tf_op jit(solution)/shard_map/ppermute | solution.py:383
  41.1 1.0 %attend_project.1 = (f32[2,144,1024]{2,1,0:T(8,128)S(1)}, bf16[2,144,1024]{2,1,0:T(8,128)(2,1)S(1)}) custom-call(bf16[4,176,576]{2,1,0:T(8,128)(2,1)S(1)} %get-tuple-element.26.soft, bf16[608,256]{1,0:T(8,128)(2,1)S(1)} %get-tuple-element.27.values, bf16[256,1024]{1,0:T(8,128)(2,1)S(1)} %get-tuple-element.31.wo), custom_call_target="tpu_custom_call" | custom-call | tf_op jit(solution)/shard_map/attend_project/pallas_call | solution.py:368
  42.1 3.3 %collective-permute-done.13 = bf16[2,256,256]{2,1,0:T(8,128)(2,1)S(1)} collective-permute-done((bf16[2,256,256]{2,1,0:T(8,128)(2,1)S(1)}, bf16[2,256,256]{2,1,0:T(8,128)(2,1)S(1)}, u32[]{:S(2)}, u32[]{:S(2)}) %collective-permute-start.13) | collective-permute-done | bytes 262176 | tf_op jit(solution)/shard_map/ppermute | solution.py:383
  45.6 1.2 %collective-permute-start.11 = (bf16[2,144,1024]{2,1,0:T(8,128)(2,1)S(1)}, bf16[2,144,1024]{2,1,0:T(8,128)(2,1)S(1)}, u32[]{:S(2)}, u32[]{:S(2)}) collective-permute-start(bf16[2,144,1024]{2,1,0:T(8,128)(2,1)S(1)} %get-tuple-element.33), channel_id=1, source_target_pairs={{0,4},{4,0},{8,12},{12,8},{16,20},{20,16},{24,28},{28,24},{1,5},{5... | collective-permute-start | bytes 1769480 | tf_op jit(solution)/shard_map/ppermute | solution.py:34
  46.8 3.7 %collective-permute-done.14 = bf16[256,256]{1,0:T(8,128)(2,1)S(1)} collective-permute-done((bf16[256,256]{1,0:T(8,128)(2,1)S(1)}, bf16[256,256]{1,0:T(8,128)(2,1)S(1)}, u32[]{:S(2)}, u32[]{:S(2)}) %collective-permute-start.14) | collective-permute-done | bytes 131104 | tf_op jit(solution)/shard_map/ppermute | solution.py:387
  50.6 6.4 %collective-permute-start.15 = (bf16[256,256]{1,0:T(8,128)(2,1)S(1)}, bf16[256,256]{1,0:T(8,128)(2,1)S(1)}, u32[]{:S(2)}, u32[]{:S(2)}) collective-permute-start(bf16[256,256]{1,0:T(8,128)(2,1)S(1)} %fusion.1), channel_id=1, source_target_pairs={{0,16},{4,20},{8,24},{12,28},{16,0},{20,4},{24,8},{28,12},{1,17},{... | collective-permute-start | bytes 393224 | tf_op jit(solution)/shard_map/ppermute | solution.py:34
  57.0 5.4 %collective-permute-done.15 = bf16[256,256]{1,0:T(8,128)(2,1)S(1)} collective-permute-done((bf16[256,256]{1,0:T(8,128)(2,1)S(1)}, bf16[256,256]{1,0:T(8,128)(2,1)S(1)}, u32[]{:S(2)}, u32[]{:S(2)}) %collective-permute-start.15) | collective-permute-done | bytes 131104 | tf_op jit(solution)/shard_map/ppermute | solution.py:34
  62.6 2.1 %collective-permute-start.12 = (bf16[144,1024]{1,0:T(8,128)(2,1)S(1)}, bf16[144,1024]{1,0:T(8,128)(2,1)S(1)}, u32[]{:S(2)}, u32[]{:S(2)}) collective-permute-start(bf16[144,1024]{1,0:T(8,128)(2,1)S(1)} %fusion), channel_id=1, source_target_pairs={{0,8},{4,12},{8,0},{12,4},{16,24},{20,28},{24,16},{28,20},{1,9},{5... | collective-permute-start | bytes 884744 | tf_op jit(solution)/shard_map/ppermute | solution.py:34
  64.6 3.9 %collective-permute-done.16 = bf16[256,256]{1,0:T(8,128)(2,1)S(1)} collective-permute-done((bf16[256,256]{1,0:T(8,128)(2,1)S(1)}, bf16[256,256]{1,0:T(8,128)(2,1)S(1)}, u32[]{:S(2)}, u32[]{:S(2)}) %collective-permute-start.16) | collective-permute-done | bytes 131104 | tf_op jit(solution)/shard_map/ppermute | solution.py:34
  68.7 3.0 %collective-permute-done.12 = bf16[144,1024]{1,0:T(8,128)(2,1)S(1)} collective-permute-done((bf16[144,1024]{1,0:T(8,128)(2,1)S(1)}, bf16[144,1024]{1,0:T(8,128)(2,1)S(1)}, u32[]{:S(2)}, u32[]{:S(2)}) %collective-permute-start.12) | collective-permute-done | bytes 294944 | tf_op jit(solution)/shard_map/ppermute | solution.py:34
  71.8 0.7 fusion.4
  72.6 0.8 %add_convert_fusion.1 = bf16[1,8,16,1024]{3,2,1,0:T(8,128)(2,1)} fusion(f32[1,8,16,1024]{3,2,1,0:T(8,128)S(1)} %bitcast.32, bf16[1,8,16,1024]{3,2,1,0:T(8,128)(2,1)S(1)} %copy-done.3, f32[8]{0:T(128)S(1)} %compare_convert_fusion), kind=kLoop, calls=%fused_computation.3 | loop fusion | flops 524288 | bytes 1048608 | tf_op jit(solution)/shard_map/convert_element_type | solution.py:405
  73.5 1.1 %maximum_convert_fusion = f32[256,1024]{1,0:T(8,128)} fusion(bf16[256,256]{1,0:T(8,128)(2,1)S(1)} %get-tuple-element.42, bf16[256,256]{1,0:T(8,128)(2,1)S(1)} %get-tuple-element.45, bf16[256,256]{1,0:T(8,128)(2,1)S(1)} %get-tuple-element.41, bf16[256,256]{1,0:T(8,128)(2,1)S(1)} %get-tuple-element.46), kind=kLoop, calls=%fused_computation.2 | loop fusion | flops 2097152 | bytes 1572864 | tf_op jit(solution)/shard_map/convert_element_type | solution.py:420
  (32 shorter events, 0.8 us)
Async XLA Ops:
  0.6 5.7 %copy-start.1 = (bf16[256,1024]{1,0:T(8,128)(2,1)S(1)}, bf16[256,1024]{1,0:T(8,128)(2,1)}, u32[]{:S(2)}) copy-start(bf16[256,1024]{1,0:T(8,128)(2,1)} %refs_0_) | copy-start | bytes 1572868
  3.2 16.6 %collective-permute-start.1 = (bf16[288,1024]{1,0:T(8,128)(2,1)}, bf16[288,1024]{1,0:T(8,128)(2,1)S(1)}, u32[]{:S(2)}, u32[]{:S(2)}) collective-permute-start(bf16[288,1024]{1,0:T(8,128)(2,1)} %get-tuple-element.20.refs_0_), channel_id=1, source_target_pairs={{0,8},{4,12},{8,0},{12,4},{16,24},{20,28},{24,16},{28,20},{1,9},{5... | collective-permute-start | bytes 1769480 | tf_op jit(solution)/shard_map/ppermute | solution.py:34
  6.3 13.5 %collective-permute-start.9 = (bf16[256,1024]{1,0:T(8,128)(2,1)S(1)}, bf16[256,1024]{1,0:T(8,128)(2,1)S(1)}, u32[]{:S(2)}, u32[]{:S(2)}) collective-permute-start(bf16[256,1024]{1,0:T(8,128)(2,1)S(1)} %copy-done.1), channel_id=1, source_target_pairs={{0,1},{4,2},{5,4},{1,7},{10,11},{14,8},{15,14},{11,13},{16,17},{20... | collective-permute-start | bytes 1572872 | tf_op jit(solution)/shard_map/ppermute | solution.py:306
  9.7 16.8 %collective-permute-start = (bf16[288,1024]{1,0:T(8,128)(2,1)}, bf16[288,1024]{1,0:T(8,128)(2,1)S(1)}, u32[]{:S(2)}, u32[]{:S(2)}) collective-permute-start(bf16[288,1024]{1,0:T(8,128)(2,1)} %get-tuple-element.20.refs_0_), channel_id=1, source_target_pairs={{0,4},{4,0},{8,12},{12,8},{16,20},{20,16},{24,28},{28,24},{1,5},{5... | collective-permute-start | bytes 1769480 | tf_op jit(solution)/shard_map/ppermute | solution.py:34
  9.9 10.8 %collective-permute-start.5 = (bf16[256,768]{1,0:T(8,128)(2,1)}, bf16[256,768]{1,0:T(8,128)(2,1)}, u32[]{:S(2)}, u32[]{:S(2)}) collective-permute-start(bf16[256,768]{1,0:T(8,128)(2,1)} %get-tuple-element.24.refs_0_), channel_id=1, source_target_pairs={{0,1},{1,0},{2,3},{3,2},{4,6},{5,7},{6,4},{7,5},{8,9},{9,8},{10,11... | collective-permute-start | bytes 1179656 | tf_op jit(solution)/shard_map/ppermute | solution.py:304
  10.5 16.0 %collective-permute-start.6 = (bf16[256,768]{1,0:T(8,128)(2,1)}, bf16[256,768]{1,0:T(8,128)(2,1)}, u32[]{:S(2)}, u32[]{:S(2)}) collective-permute-start(bf16[256,768]{1,0:T(8,128)(2,1)} %get-tuple-element.25), channel_id=1, source_target_pairs={{0,1},{1,0},{2,3},{3,2},{4,6},{5,7},{6,4},{7,5},{8,9},{9,8},{10,11... | collective-permute-start | bytes 1179656 | tf_op jit(solution)/shard_map/ppermute | solution.py:305
  19.8 11.5 %collective-permute-start.2 = (bf16[288,1024]{1,0:T(8,128)(2,1)S(1)}, bf16[288,1024]{1,0:T(8,128)(2,1)S(1)}, u32[]{:S(2)}, u32[]{:S(2)}) collective-permute-start(bf16[288,1024]{1,0:T(8,128)(2,1)S(1)} %collective-permute-done.1.refs_2_), channel_id=1, source_target_pairs={{0,4},{4,0},{8,12},{12,8},{16,20},{20,16},{24,28},{28,24},{1,5},{5... | collective-permute-start | bytes 1769480 | tf_op jit(solution)/shard_map/ppermute | solution.py:34
  19.8 16.7 %collective-permute-start.10 = (bf16[256,1024]{1,0:T(8,128)(2,1)S(1)}, bf16[256,1024]{1,0:T(8,128)(2,1)S(1)}, u32[]{:S(2)}, u32[]{:S(2)}) collective-permute-start(bf16[256,1024]{1,0:T(8,128)(2,1)S(1)} %collective-permute-done.9.refs_1_), channel_id=1, source_target_pairs={{2,3},{7,6},{8,9},{13,12},{18,19},{23,22},{24,25},{29,28}} | collective-permute-start | bytes 1572872 | tf_op jit(solution)/shard_map/ppermute | solution.py:310
  20.7 12.3 %collective-permute-start.8 = (bf16[256,768]{1,0:T(8,128)(2,1)}, bf16[256,768]{1,0:T(8,128)(2,1)}, u32[]{:S(2)}, u32[]{:S(2)}) collective-permute-start(bf16[256,768]{1,0:T(8,128)(2,1)} %collective-permute-done.5.refs_1_), channel_id=1, source_target_pairs={{0,2},{1,3},{2,0},{3,1},{4,5},{5,4},{6,7},{7,6},{8,10},{9,11},{10,... | collective-permute-start | bytes 1179656 | tf_op jit(solution)/shard_map/ppermute | solution.py:308
  26.5 6.5 %collective-permute-start.7 = (bf16[256,768]{1,0:T(8,128)(2,1)}, bf16[256,768]{1,0:T(8,128)(2,1)}, u32[]{:S(2)}, u32[]{:S(2)}) collective-permute-start(bf16[256,768]{1,0:T(8,128)(2,1)} %collective-permute-done.6), channel_id=1, source_target_pairs={{0,4},{4,0},{8,12},{12,8},{16,20},{20,16},{24,28},{28,24},{1,5},{5... | collective-permute-start | bytes 1179656 | tf_op jit(solution)/shard_map/ppermute | solution.py:34
  27.4 0.7 collective-permute-start.3
  28.1 3.3 %collective-permute-start.4 = (bf16[32,1024]{1,0:T(8,128)(2,1)S(1)}, bf16[32,1024]{1,0:T(8,128)(2,1)S(1)}, u32[]{:S(2)}, u32[]{:S(2)}) collective-permute-start(bf16[32,1024]{1,0:T(8,128)(2,1)S(1)} %collective-permute-done.3.refs_4_), channel_id=1, source_target_pairs={{0,4},{8,12},{16,20},{24,28},{1,5},{9,13},{17,21},{25,29},{2,6},{1... | collective-permute-start | bytes 196616 | tf_op jit(solution)/shard_map/ppermute | solution.py:322
  31.4 1.1 %copy-start = (bf16[288,1024]{1,0:T(8,128)(2,1)S(1)}, bf16[288,1024]{1,0:T(8,128)(2,1)}, u32[]{:S(2)}) copy-start(bf16[288,1024]{1,0:T(8,128)(2,1)} %get-tuple-element.20.refs_0_) | copy-start | bytes 1769476
  32.4 1.0 %copy-start.2 = (bf16[256,768]{1,0:T(8,128)(2,1)S(1)}, bf16[256,768]{1,0:T(8,128)(2,1)}, u32[]{:S(2)}) copy-start(bf16[256,768]{1,0:T(8,128)(2,1)} %get-tuple-element.24.refs_0_) | copy-start | bytes 1179652
  38.5 6.9 %collective-permute-start.13 = (bf16[2,256,256]{2,1,0:T(8,128)(2,1)S(1)}, bf16[2,256,256]{2,1,0:T(8,128)(2,1)S(1)}, u32[]{:S(2)}, u32[]{:S(2)}) collective-permute-start(bf16[2,256,256]{2,1,0:T(8,128)(2,1)S(1)} %get-tuple-element.35), channel_id=1, source_target_pairs={{0,1},{1,0},{2,3},{3,2},{4,6},{5,7},{6,4},{7,5},{8,9},{9,8},{10,11... | collective-permute-start | bytes 786440 | tf_op jit(solution)/shard_map/ppermute | solution.py:383
  45.5 5.0 %collective-permute-start.14 = (bf16[256,256]{1,0:T(8,128)(2,1)S(1)}, bf16[256,256]{1,0:T(8,128)(2,1)S(1)}, u32[]{:S(2)}, u32[]{:S(2)}) collective-permute-start(bf16[256,256]{1,0:T(8,128)(2,1)S(1)} %fusion.2), channel_id=1, source_target_pairs={{0,2},{1,3},{2,0},{3,1},{4,5},{5,4},{6,7},{7,6},{8,10},{9,11},{10,... | collective-permute-start | bytes 393224 | tf_op jit(solution)/shard_map/ppermute | solution.py:387
  45.6 16.9 %collective-permute-start.11 = (bf16[2,144,1024]{2,1,0:T(8,128)(2,1)S(1)}, bf16[2,144,1024]{2,1,0:T(8,128)(2,1)S(1)}, u32[]{:S(2)}, u32[]{:S(2)}) collective-permute-start(bf16[2,144,1024]{2,1,0:T(8,128)(2,1)S(1)} %get-tuple-element.33), channel_id=1, source_target_pairs={{0,4},{4,0},{8,12},{12,8},{16,20},{20,16},{24,28},{28,24},{1,5},{5... | collective-permute-start | bytes 1769480 | tf_op jit(solution)/shard_map/ppermute | solution.py:34
  50.6 11.8 %collective-permute-start.15 = (bf16[256,256]{1,0:T(8,128)(2,1)S(1)}, bf16[256,256]{1,0:T(8,128)(2,1)S(1)}, u32[]{:S(2)}, u32[]{:S(2)}) collective-permute-start(bf16[256,256]{1,0:T(8,128)(2,1)S(1)} %fusion.1), channel_id=1, source_target_pairs={{0,16},{4,20},{8,24},{12,28},{16,0},{20,4},{24,8},{28,12},{1,17},{... | collective-permute-start | bytes 393224 | tf_op jit(solution)/shard_map/ppermute | solution.py:34
  62.4 6.2 %collective-permute-start.16 = (bf16[256,256]{1,0:T(8,128)(2,1)S(1)}, bf16[256,256]{1,0:T(8,128)(2,1)S(1)}, u32[]{:S(2)}, u32[]{:S(2)}) collective-permute-start(bf16[256,256]{1,0:T(8,128)(2,1)S(1)} %add_convert_fusion.2), channel_id=1, source_target_pairs={{0,8},{4,12},{8,0},{12,4},{16,24},{20,28},{24,16},{28,20},{1,9},{5... | collective-permute-start | bytes 393224 | tf_op jit(solution)/shard_map/ppermute | solution.py:34
  62.6 9.2 %collective-permute-start.12 = (bf16[144,1024]{1,0:T(8,128)(2,1)S(1)}, bf16[144,1024]{1,0:T(8,128)(2,1)S(1)}, u32[]{:S(2)}, u32[]{:S(2)}) collective-permute-start(bf16[144,1024]{1,0:T(8,128)(2,1)S(1)} %fusion), channel_id=1, source_target_pairs={{0,8},{4,12},{8,0},{12,4},{16,24},{20,28},{24,16},{28,20},{1,9},{5... | collective-permute-start | bytes 884744 | tf_op jit(solution)/shard_map/ppermute | solution.py:34
  68.6 3.9 %copy-start.3 = (bf16[1,8,16,1024]{3,2,1,0:T(8,128)(2,1)S(1)}, bf16[1,8,16,1024]{3,2,1,0:T(8,128)(2,1)}, u32[]{:S(2)}) copy-start(bf16[1,8,16,1024]{3,2,1,0:T(8,128)(2,1)} %param.10) | copy-start | bytes 786436
  68.6 4.8 %collective-permute-start.17 = (bf16[2,256,256]{2,1,0:T(8,128)(2,1)S(1)}, bf16[2,256,256]{2,1,0:T(8,128)(2,1)S(1)}, u32[]{:S(2)}, u32[]{:S(2)}) collective-permute-start(bf16[2,256,256]{2,1,0:T(8,128)(2,1)S(1)} %pad_maximum_fusion), channel_id=1, source_target_pairs={{0,4},{4,0},{8,12},{12,8},{16,20},{20,16},{24,28},{28,24},{1,5},{5... | collective-permute-start | bytes 786440 | tf_op jit(solution)/shard_map/ppermute | solution.py:34

commit v3 on v2

--- a/solution.py
+++ b/solution.py
@@ -54,8 +54,8 @@
 
 
 def pack_kernel(frame_count, wq, wk, wv, frames, gf, mem, gm, gain, *refs):
-    blocks, (tokens, raw, few, one, sems) = refs[:-5], refs[-5:]
-    width = blocks[0].shape[1] // 3
+    blocks, tokens, raw, few, one, sems = refs
+    width = blocks.shape[2] // 3
     rows, model_width = gf.shape
     segs = mem.shape[0]
     half = tokens.shape[0] // 2
@@ -66,10 +66,10 @@
         pltpu.make_async_copy(gm, few.at[1], sems.at[3]),
         pltpu.make_async_copy(gf, tokens.at[pl.ds(half, rows)], sems.at[4]),
     ]
-    for i, block in enumerate(blocks):
+    for i in range(blocks.shape[0]):
         at = aligned(member_of() ^ i, width)
         for j, w in enumerate((wq, wk, wv)):
-            into = block.at[:, pl.ds(j * width, width)]
+            into = blocks.at[i, :, pl.ds(j * width, width)]
             sem = sems.at[5 + 3 * i + j]
             copies.append(pltpu.make_async_copy(w.at[:, pl.ds(at, width)], into, sem))
     for copy in copies:
@@ -87,8 +87,14 @@
         copy.wait()
 
 
+def split_kernel(both, mine, other):
+    mine[...] = both[0]
+    other[...] = both[1]
+
+
 def merge_kernel(group, *refs):
-    parts, halo_a, halo_b, x_all, x_turned, u_all = refs[:group], *refs[group:]
+    parts, halo_a, halo_b, wo_from = refs[:group], *refs[group : group + 2], refs[group + 2 : -4]
+    x_all, x_turned, u_all, wo = refs[-4:]
     half = parts[0].shape[0] // 2
     halo = halo_a.shape[0]
     odd = (member_of() & 1) > 0
@@ -98,15 +104,19 @@
         x_all[pl.ds(pl.multiple_of(halo + at, 16), half), :] = parts[i][:half, :]
         u_all[pl.ds(at, half), :] = parts[i][half:, :]
     x_turned[...] = x_all[...].T
+    wo[...] = wo_from[0][...]
+    if len(wo_from) > 1:
+        wo[...] = jnp.where(lax.axis_index("fsdp") == member_of(), wo[...], wo_from[1][...])
 
 
 def assemble(pieces, whole, crossed):
     own = lax.axis_index("fsdp")
-    rows = pieces[0].shape[0]
+    rows = pieces[0].shape[-2]
     flip = lax.axis_index("seg") & 1 if crossed else 0
     for j, piece in enumerate(pieces):
         apart = j ^ (3 * flip) if j in (1, 2) else j
-        whole[pl.ds(aligned(own ^ apart, rows), rows), :] = piece[...]
+        into = whole.at[pl.ds(aligned(own ^ apart, rows), rows), :]
+        into[...] = piece[0] if len(piece.shape) == 3 else piece[...]
 
 
 def head_stack(array, heads):
@@ -164,14 +174,11 @@
     blocks, keys, lanes = soft.shape
     queries = lanes // heads
     frames = segs * frame_count
-    chosen = wo_from[0][...]
+    wo[...] = wo_from[0][...]
     if len(wo_from) > 1:
-        apart = lax.axis_index("fsdp") ^ member_of()
-        chosen = jnp.where(
-            apart == 0, chosen, jnp.where(apart == 3, wo_from[2][...], wo_from[1][...])
-        )
-    wo[...] = chosen
-    back = lax.dot_general(u_all[...], chosen, NT, preferred_element_type=f32)
+        opposite = (lax.axis_index("fsdp") ^ member_of()) == 3
+        wo[...] = jnp.where(opposite, wo_from[1][...], wo[...])
+    back = lax.dot_general(u_all[...], wo[...], NT, preferred_element_type=f32)
     row = lax.broadcasted_iota(jnp.int32, (queries, wo.shape[0]), 0)
     seg_of = jnp.where(row < frames, row // frame_count, row - frames - segs)
     first = lax.axis_index("seg") - member_of()
@@ -238,17 +245,18 @@
 
 
 def pairs(seg_size):
-    straight, turned, beside, across = [], [], [], []
+    straight, turned, first, last = [], [], [], []
     for s in range(seg_size):
         along = 2 if s & 1 else 1
         for f in range(GROUP):
             straight.append((s * GROUP + f, s * GROUP + (f ^ along)))
             turned.append((s * GROUP + f, s * GROUP + (f ^ along ^ 3)))
         k = s % GROUP
-        beside.append((s * GROUP + k, s * GROUP + (k ^ 1)))
-        beside.append(((s ^ 1) * GROUP + k, s * GROUP + (k ^ 2)))
-        across.append((s * GROUP + (k ^ 2), s * GROUP + (k ^ 3)))
-    return straight, turned, beside, across
+        first.append((s * GROUP + k, s * GROUP + (k ^ 1)))
+        first.append(((s ^ 1) * GROUP + k, s * GROUP + (k ^ 2)))
+        first.append(((s ^ 3) * GROUP + k, (s ^ 3) * GROUP + (k ^ 3)))
+        last.append(((s ^ 3) * GROUP + (k ^ 3), s * GROUP + (k ^ 3)))
+    return straight, turned, first, last
 
 
 def on_device(
@@ -271,12 +279,12 @@
     member = seg % group
 
     crossed = fsdp_size == group
-    *own_blocks, tokens = pl.pallas_call(
+    own_blocks, tokens = pl.pallas_call(
         functools.partial(pack_kernel, frame_count),
         in_specs=[hbm] * 8,
-        out_specs=[vmem] * (2 + crossed),
-        out_shape=[jax.ShapeDtypeStruct((rows, 3 * block), bf16)] * (1 + crossed)
-        + [
+        out_specs=[vmem] * 2,
+        out_shape=[
+            jax.ShapeDtypeStruct((1 + crossed, rows, 3 * block), bf16),
             jax.ShapeDtypeStruct((2 * queries, width), bf16),
         ],
         scratch_shapes=[
@@ -298,42 +306,54 @@
     near = swapped(tokens, "seg", 1)
     cut = slice(queries - halo_rows, queries)
     tail = jnp.where(member == group - 1, tokens[cut], near[cut])
+    ahead = []
+    for s in range(group, seg_size, group):
+        ahead += [(s - 1, s), (s - 2, s + 2)]
+    halo_even = lax.ppermute(tail, "seg", ahead)
     if crossed:
         both = ("seg", "fsdp")
-        straight, turned, beside, across = pairs(seg_size)
-        mine = lax.ppermute(own_blocks[0], both, straight)
-        other = lax.ppermute(own_blocks[1], both, straight)
-        wo_near = lax.ppermute(w_out, both, beside)
+        straight, turned, first, last = pairs(seg_size)
+        came = lax.ppermute(own_blocks, both, straight)
+        wo_came = lax.ppermute(w_out, both, first)
+        came, far, near, halo_even, wo_came = lax.optimization_barrier(
+            (came, far, near, halo_even, wo_came)
+        )
+        mine, other = pl.pallas_call(
+            split_kernel,
+            in_specs=[vmem],
+            out_specs=[vmem] * 2,
+            out_shape=[jax.ShapeDtypeStruct(came.shape[1:], bf16)] * 2,
+            compiler_params=params(),
+            name="split",
+        )(came)
         wqkv_parts = [
-            own_blocks[0], mine, swapped(other, "seg", 1), lax.ppermute(mine, both, turned)
+            own_blocks, mine, swapped(other, "seg", 1), lax.ppermute(mine, both, turned)
         ]
-        wo_from = [w_out, wo_near, lax.ppermute(wo_near, both, across)]
+        wo_from, wo_last = [w_out, wo_came], [lax.ppermute(wo_came, both, last)]
     else:
-        wqkv_parts = gathered(own_blocks[0])
+        wqkv_parts = gathered(own_blocks)
         wo_from = [
             lax.dynamic_slice_in_dim(
                 lax.all_gather(w_out, "fsdp", axis=0, tiled=True), member * block, block, 0
             )
         ]
-    ahead = []
-    for s in range(group, seg_size, group):
-        ahead += [(s - 1, s), (s - 2, s + 2)]
-    halo_even = lax.ppermute(tail, "seg", ahead)
+        wo_last = []
     halo_odd = lax.ppermute(halo_even, "seg", [(s, s + 1) for s in range(0, seg_size, 2)])
     parts = [tokens, near, far, swapped(far, "seg", 1)]
 
-    x_all, x_turned, u_all = pl.pallas_call(
+    x_all, x_turned, u_all, wo_near = pl.pallas_call(
         functools.partial(merge_kernel, group),
-        in_specs=[vmem] * (group + 2),
-        out_specs=[vmem] * 3,
+        in_specs=[vmem] * (group + 2 + len(wo_from)),
+        out_specs=[vmem] * 4,
         out_shape=[
             jax.ShapeDtypeStruct((all_rows, width), bf16),
             jax.ShapeDtypeStruct((width, all_rows), bf16),
             jax.ShapeDtypeStruct((group * queries, width), bf16),
+            jax.ShapeDtypeStruct((block, width), bf16),
         ],
         compiler_params=params(),
         name="merge",
-    )(*parts, halo_even, halo_odd)
+    )(*parts, halo_even, halo_odd, *wo_from)
 
     soft, values = pl.pallas_call(
         functools.partial(weights_kernel, heads, frame_count, segs, crossed),
@@ -354,7 +374,7 @@
         grad_shapes = [jax.ShapeDtypeStruct((rows, block), bf16)] * fsdp_size
     *grad_chunks, wo_mine = pl.pallas_call(
         functools.partial(grad_kernel, fsdp_size, heads, frame_count, segs, crossed),
-        in_specs=[smem] + [vmem] * (3 + len(wo_from)),
+        in_specs=[smem] + [vmem] * (4 + len(wo_last)),
         out_specs=[vmem] * (len(grad_shapes) + 1),
         out_shape=grad_shapes + [jax.ShapeDtypeStruct((block, width), bf16)],
         scratch_shapes=[
@@ -363,7 +383,7 @@
         ],
         compiler_params=params(),
         name="value_grad",
-    )(lengths, x_turned, u_all, soft, *wo_from)
+    )(lengths, x_turned, u_all, soft, wo_near, *wo_last)
 
     keep, send = pl.pallas_call(
         functools.partial(out_kernel, heads),
@@ -378,13 +398,14 @@
     )(soft, values, wo_mine)
     near = swapped(send, "seg", 1)
     onward = (keep[1] + near[1].astype(f32)).astype(bf16)
+    back = swapped(onward, "seg", 2)
     if crossed:
         kept, sent = grad_chunks
-        came = lax.ppermute(sent, both, straight)
-        came, _ = lax.optimization_barrier((came, send))
+        came, _ = lax.optimization_barrier((lax.ppermute(sent, both, straight), send))
         passing = (kept[1] + came[1].astype(f32)).astype(bf16)
-        grad_sum = kept[0] + came[0].astype(f32)
-        grad_sum = grad_sum + lax.ppermute(passing, both, turned).astype(f32)
+        passing, onward = lax.optimization_barrier((passing, onward))
+        last = lax.ppermute(passing, both, turned)
+        grad_sum = kept[0] + came[0].astype(f32) + last.astype(f32)
     else:
         grad_sum = grad_chunks[0].astype(f32)
         for j in range(1, fsdp_size):
@@ -395,7 +416,7 @@
         grad_sum = mine.astype(f32) + swapped(mine, "seg", bit).astype(f32)
         bit *= 2
     mine = grad_sum.astype(bf16)
-    projected = keep[0] + near[0].astype(f32) + swapped(onward, "seg", 2).astype(f32)
+    projected = keep[0] + near[0].astype(f32) + back.astype(f32)
 
     live = (seg * segs + jnp.arange(segs) < lengths[0]).astype(f32)
     frames_out = (

time: 75 us -> 69.1 us (0.921)
  starting transfers between devices: 29.3 us -> 18.7 us
  waiting for transfers between devices: 29.2 us -> 35.4 us
  local copies, waits for them, and re-layouts: 1.55 us -> 0.09 us
    ppermute x6 -> x5, waiting for transfers between devices: 8.71 us -> 21.4 us  [the longest x1 11.8 us: on_device(): wo_came = lax.ppermute(w_out, both, first)]
    ppermute x9, waiting for transfers between devices: 20.2 us -> 12.1 us  [swapped(): return lax.ppermute(array, axis, [(i, i ^ bit) for i in range(size)])]
    ppermute x9, starting transfers between devices: 13.1 us -> 5.47 us  [swapped(): return lax.ppermute(array, axis, [(i, i ^ bit) for i in range(size)])]
    ppermute x1, starting transfers between devices: 4.33 us -> 0.07 us  [on_device(): lax.ppermute(mine, both, turned)]
    ppermute x1, waiting for transfers between devices: 0.01 us -> 1.71 us  [on_device(): lax.ppermute(mine, both, turned)]
    unnamed x8, local copies, waits for them, and re-layouts: 1.48 us -> 0.02 us
    pallas_call x1, Pallas kernels: 3.05 us -> 1.82 us  [on_device(): pl.pallas_call(functools.partial(weights_kernel, heads, frame_count, segs...]
    pallas_call x1, Pallas kernels: 0.56 us -> 1.69 us  [on_device(): pl.pallas_call(functools.partial(merge_kernel, group), in_specs=[vmem] *...]
  transfers between devices with their start and end apart: 18 -> 17, of which waited for: 9 -> 8; matrix products, arithmetic and copies ran while one was open for 4% -> 4% of each run, Pallas kernels for 6% -> 5%
where the time goes in v3:
time: 69.1 us; the launch traced here: 68.8 us
  waiting for transfers between devices  35.4 us (51%)
  starting transfers between devices  18.7 us (27%)
  Pallas kernels  9.2 us (13%)
  other arithmetic  3.82 us (6%)
  between operations  1.57 us (2%)
    ppermute x9, waiting for transfers between devices, swapped(): return lax.ppermute(array, axis, [(i, i ^ bit) for i in range(size)])  12.1 us
    ppermute x1, waiting for transfers between devices, on_device(): wo_came = lax.ppermute(w_out, both, first)  11.8 us
    ppermute x9, starting transfers between devices, swapped(): return lax.ppermute(array, axis, [(i, i ^ bit) for i in range(size)])  5.47 us
    ppermute x1, waiting for transfers between devices, on_device(): last = lax.ppermute(passing, both, turned)  4.95 us
    ppermute x1, waiting for transfers between devices, on_device(): lax.ppermute(sent, both, straight)  4.6 us
    ppermute x1, starting transfers between devices, on_device(): lax.ppermute(halo_even, 'seg', [(s, s + 1) for s in range(0, seg_size, 2)])  3.45 us
    pallas_call x1, Pallas kernels, on_device(): pl.pallas_call(functools.partial(pack_kernel, frame_count), in_specs=[hbm...  2.57 us
    ppermute x1, starting transfers between devices, on_device(): came = lax.ppermute(own_blocks, both, straight)  2.56 us
  transfers between devices with their start and end apart: 17, of which 8 were waited for; matrix products, arithmetic and copies ran while one was open for 4% of the time, Pallas kernels for 5%

profile of v3, /device:TPU:0, one launch (start us, length us, event | category | flops | bytes accessed | tf_op | source)
XLA Modules:
  0.0 68.8 jit_solution(17616908174538374800)
XLA Ops:
  0.6 2.6 %pack.1 = (bf16[2,256,768]{2,1,0:T(8,128)(2,1)}, bf16[288,1024]{1,0:T(8,128)(2,1)}) custom-call(bf16[256,1024]{1,0:T(8,128)(2,1)} %wq.1, bf16[256,1024]{1,0:T(8,128)(2,1)} %wk.1, bf16[256,1024]{1,0:T(8,128)(2,1)} %wv.1, bf16[128,1024]{1,0:T(8,128)(2,1)} %bitcast.33, bf16[128,1024]{1,0:T(8,128)(2,1)} %bitcast.34, bf16[8,1024]{1,0:T(8,128)(2,1)} %bitcast.35, ...), custom_call_target="tpu_custom_call" | custom-call | tf_op jit(solution)/shard_map/pack/pallas_call | solution.py:282
  3.2 0.5 collective-permute-start.2
  3.7 2.6 %collective-permute-start = (bf16[2,256,768]{2,1,0:T(8,128)(2,1)}, bf16[2,256,768]{2,1,0:T(8,128)(2,1)S(1)}, u32[]{:S(2)}, u32[]{:S(2)}) collective-permute-start(bf16[2,256,768]{2,1,0:T(8,128)(2,1)} %get-tuple-element.29.refs_0_), channel_id=1, source_target_pairs={{0,1},{1,0},{2,3},{3,2},{4,6},{5,7},{6,4},{7,5},{8,9},{9,8},{10,11... | collective-permute-start | bytes 2359304 | tf_op jit(solution)/shard_map/ppermute | solution.py:316
  6.3 1.6 %collective-permute-start.1 = (bf16[288,1024]{1,0:T(8,128)(2,1)}, bf16[288,1024]{1,0:T(8,128)(2,1)S(1)}, u32[]{:S(2)}, u32[]{:S(2)}) collective-permute-start(bf16[288,1024]{1,0:T(8,128)(2,1)} %get-tuple-element.27.refs_0_), channel_id=1, source_target_pairs={{0,8},{4,12},{8,0},{12,4},{16,24},{20,28},{24,16},{28,20},{1,9},{5... | collective-permute-start | bytes 1769480 | tf_op jit(solution)/shard_map/ppermute | solution.py:34
  7.9 2.4 %collective-permute-start.4 = (bf16[256,1024]{1,0:T(8,128)(2,1)S(1)}, bf16[256,1024]{1,0:T(8,128)(2,1)}, u32[]{:S(2)}, u32[]{:S(2)}) collective-permute-start(bf16[256,1024]{1,0:T(8,128)(2,1)S(1)} %copy-done.2), channel_id=1, source_target_pairs={{0,1},{4,2},{12,15},{5,4},{1,7},{9,10},{10,11},{14,8},{6,5},{15,14... | collective-permute-start | bytes 1572872 | tf_op jit(solution)/shard_map/ppermute | solution.py:317
  10.4 0.9 %slice_select_fusion = bf16[32,1024]{1,0:T(8,128)(2,1)S(1)} fusion(bf16[288,1024]{1,0:T(8,128)(2,1)S(1)} %collective-permute-done.2.refs_1_, bf16[288,1024]{1,0:T(8,128)(2,1)} %get-tuple-element.27.refs_0_, pred[]{:T(512)S(6)} %eq.5), kind=kLoop, calls=%fused_computation.19 | loop fusion | flops 32768 | bytes 196609 | tf_op jit(solution)/shard_map/jit(_where)/select_n | solution.py:308
  11.2 0.7 collective-permute-start.3
  11.9 11.8 %collective-permute-done.4.refs_7_ = bf16[256,1024]{1,0:T(8,128)(2,1)} collective-permute-done((bf16[256,1024]{1,0:T(8,128)(2,1)S(1)}, bf16[256,1024]{1,0:T(8,128)(2,1)}, u32[]{:S(2)}, u32[]{:S(2)}) %collective-permute-start.4) | collective-permute-done | bytes 524320 | tf_op jit(solution)/shard_map/ppermute | solution.py:317
  23.7 0.1 collective-permute-start.5
  23.8 2.1 %collective-permute-start.9 = (bf16[256,1024]{1,0:T(8,128)(2,1)}, bf16[256,1024]{1,0:T(8,128)(2,1)S(1)}, u32[]{:S(2)}, u32[]{:S(2)}) collective-permute-start(bf16[256,1024]{1,0:T(8,128)(2,1)} %collective-permute-done.4.refs_7_), channel_id=1, source_target_pairs={{15,3},{10,6},{5,9},{0,12},{31,19},{26,22},{21,25},{16,28}} | collective-permute-start | bytes 1572872 | tf_op jit(solution)/shard_map/ppermute | solution.py:332
  26.0 0.1 collective-permute-start.7
  26.0 0.1 collective-permute-start.8
  26.1 3.5 %collective-permute-start.6 = (bf16[32,1024]{1,0:T(8,128)(2,1)S(1)}, bf16[32,1024]{1,0:T(8,128)(2,1)S(1)}, u32[]{:S(2)}, u32[]{:S(2)}) collective-permute-start(bf16[32,1024]{1,0:T(8,128)(2,1)S(1)} %collective-permute-done.3.refs_4_), channel_id=1, source_target_pairs={{0,4},{8,12},{16,20},{24,28},{1,5},{9,13},{17,21},{25,29},{2,6},{1... | collective-permute-start | bytes 196616 | tf_op jit(solution)/shard_map/ppermute | solution.py:341
  30.2 0.2 collective-permute-done.6.refs_5_
  30.5 1.7 %merge.1 = (bf16[608,1024]{1,0:T(8,128)(2,1)S(1)}, bf16[1024,608]{1,0:T(8,128)(2,1)S(1)}, bf16[576,1024]{1,0:T(8,128)(2,1)S(1)}, bf16[256,1024]{1,0:T(8,128)(2,1)S(1)}) custom-call(bf16[288,1024]{1,0:T(8,128)(2,1)S(1)} %copy-done.1, bf16[288,1024]{1,0:T(8,128)(2,1)S(1)} %collective-permute-done.2.refs_1_, ...), custom_call_target="tpu_custom_call" | custom-call | tf_op jit(solution)/shard_map/merge/pallas_call | solution.py:344
  32.2 1.7 %collective-permute-done.8.refs_3_ = bf16[256,768]{1,0:T(8,128)(2,1)S(1)} collective-permute-done((bf16[256,768]{1,0:T(8,128)(2,1)S(1)}, bf16[256,768]{1,0:T(8,128)(2,1)S(1)}, u32[]{:S(2)}, u32[]{:S(2)}) %collective-permute-start.8) | collective-permute-done | bytes 393248 | tf_op jit(solution)/shard_map/ppermute | solution.py:330
  33.9 1.8 %soft_weights.1 = (bf16[4,176,576]{2,1,0:T(8,128)(2,1)S(1)}, bf16[608,256]{1,0:T(8,128)(2,1)S(1)}) custom-call(bf16[608,1024]{1,0:T(8,128)(2,1)S(1)} %get-tuple-element.35.x_all, bf16[2,256,768]{2,1,0:T(8,128)(2,1)S(1)} %copy-done, bf16[256,768]{1,0:T(8,128)(2,1)S(1)} %get-tuple-element.37.refs_1_, bf16[256,768]{1,0:T(8,128)(2,1)S(1)} %collective-permute-done.7.refs_2_, ...), custom_call_target="tpu_custom_call" | custom-call | tf_op jit(solution)/shard_map/soft_weights/pallas_call | solution.py:358
  35.7 2.0 %value_grad.1 = (f32[2,256,256]{2,1,0:T(8,128)S(1)}, bf16[2,256,256]{2,1,0:T(8,128)(2,1)S(1)}, bf16[256,1024]{1,0:T(8,128)(2,1)S(1)}) custom-call(s32[1]{0:T(128)} %copy.13.lengths, bf16[1024,608]{1,0:T(8,128)(2,1)S(1)} %get-tuple-element.41.x_turned, bf16[576,1024]{1,0:T(8,128)(2,1)S(1)} %get-tuple-element.42.u_all, ...), custom_call_target="tpu_custom_call" | custom-call | tf_op jit(solution)/shard_map/value_grad/pallas_call | solution.py:375
  37.8 1.1 %attend_project.1 = (f32[2,144,1024]{2,1,0:T(8,128)S(1)}, bf16[2,144,1024]{2,1,0:T(8,128)(2,1)S(1)}) custom-call(bf16[4,176,576]{2,1,0:T(8,128)(2,1)S(1)} %get-tuple-element.39.soft, bf16[608,256]{1,0:T(8,128)(2,1)S(1)} %get-tuple-element.40.values, bf16[256,1024]{1,0:T(8,128)(2,1)S(1)} %get-tuple-element.44.wo), custom_call_target="tpu_custom_call" | custom-call | tf_op jit(solution)/shard_map/attend_project/pallas_call | solution.py:388
  38.9 1.8 %collective-permute-start.12 = (bf16[2,256,256]{2,1,0:T(8,128)(2,1)S(1)}, bf16[2,256,256]{2,1,0:T(8,128)(2,1)S(1)}, u32[]{:S(2)}, u32[]{:S(2)}) collective-permute-start(bf16[2,256,256]{2,1,0:T(8,128)(2,1)S(1)} %get-tuple-element.48), channel_id=1, source_target_pairs={{0,1},{1,0},{2,3},{3,2},{4,6},{5,7},{6,4},{7,5},{8,9},{9,8},{10,11... | collective-permute-start | bytes 786440 | tf_op jit(solution)/shard_map/ppermute | solution.py:404
  40.7 4.6 %collective-permute-done.12 = bf16[2,256,256]{2,1,0:T(8,128)(2,1)S(1)} collective-permute-done((bf16[2,256,256]{2,1,0:T(8,128)(2,1)S(1)}, bf16[2,256,256]{2,1,0:T(8,128)(2,1)S(1)}, u32[]{:S(2)}, u32[]{:S(2)}) %collective-permute-start.12) | collective-permute-done | bytes 262176 | tf_op jit(solution)/shard_map/ppermute | solution.py:404
  45.4 0.1 collective-permute-start.13
  45.5 5.0 %collective-permute-done.13 = bf16[256,256]{1,0:T(8,128)(2,1)S(1)} collective-permute-done((bf16[256,256]{1,0:T(8,128)(2,1)S(1)}, bf16[256,256]{1,0:T(8,128)(2,1)S(1)}, u32[]{:S(2)}, u32[]{:S(2)}) %collective-permute-start.13) | collective-permute-done | bytes 131104 | tf_op jit(solution)/shard_map/ppermute | solution.py:407
  50.5 3.0 %collective-permute-start.14 = (bf16[256,256]{1,0:T(8,128)(2,1)S(1)}, bf16[256,256]{1,0:T(8,128)(2,1)S(1)}, u32[]{:S(2)}, u32[]{:S(2)}) collective-permute-start(bf16[256,256]{1,0:T(8,128)(2,1)S(1)} %fusion.1), channel_id=1, source_target_pairs={{0,16},{4,20},{8,24},{12,28},{16,0},{20,4},{24,8},{28,12},{1,17},{... | collective-permute-start | bytes 393224 | tf_op jit(solution)/shard_map/ppermute | solution.py:34
  53.6 4.6 %collective-permute-done.14 = bf16[256,256]{1,0:T(8,128)(2,1)S(1)} collective-permute-done((bf16[256,256]{1,0:T(8,128)(2,1)S(1)}, bf16[256,256]{1,0:T(8,128)(2,1)S(1)}, u32[]{:S(2)}, u32[]{:S(2)}) %collective-permute-start.14) | collective-permute-done | bytes 131104 | tf_op jit(solution)/shard_map/ppermute | solution.py:34
  58.2 0.1 collective-permute-start.15
  58.3 6.1 %collective-permute-done.11 = bf16[144,1024]{1,0:T(8,128)(2,1)S(1)} collective-permute-done((bf16[144,1024]{1,0:T(8,128)(2,1)S(1)}, bf16[144,1024]{1,0:T(8,128)(2,1)S(1)}, u32[]{:S(2)}, u32[]{:S(2)}) %collective-permute-start.11) | collective-permute-done | bytes 294944 | tf_op jit(solution)/shard_map/ppermute | solution.py:34
  64.4 0.1 bitcast_add_fusion
  64.5 1.4 %collective-permute-done.15 = bf16[256,256]{1,0:T(8,128)(2,1)S(1)} collective-permute-done((bf16[256,256]{1,0:T(8,128)(2,1)S(1)}, bf16[256,256]{1,0:T(8,128)(2,1)S(1)}, u32[]{:S(2)}, u32[]{:S(2)}) %collective-permute-start.15) | collective-permute-done | bytes 131104 | tf_op jit(solution)/shard_map/ppermute | solution.py:34
  66.0 0.7 fusion.4
  66.7 0.8 %add_convert_fusion.1 = bf16[1,8,16,1024]{3,2,1,0:T(8,128)(2,1)} fusion(f32[1,8,16,1024]{3,2,1,0:T(8,128)S(1)} %bitcast.32, bf16[1,8,16,1024]{3,2,1,0:T(8,128)(2,1)S(1)} %copy-done.3, f32[8]{0:T(128)S(1)} %compare_convert_fusion), kind=kLoop, calls=%fused_computation.3 | loop fusion | flops 524288 | bytes 1048608 | tf_op jit(solution)/shard_map/convert_element_type | solution.py:426
  67.7 1.1 %maximum_convert_fusion = f32[256,1024]{1,0:T(8,128)} fusion(bf16[256,256]{1,0:T(8,128)(2,1)S(1)} %get-tuple-element.56, bf16[256,256]{1,0:T(8,128)(2,1)S(1)} %get-tuple-element.59, bf16[256,256]{1,0:T(8,128)(2,1)S(1)} %get-tuple-element.55, bf16[256,256]{1,0:T(8,128)(2,1)S(1)} %get-tuple-element.60), kind=kLoop, calls=%fused_computation.2 | loop fusion | flops 2097152 | bytes 1572864 | tf_op jit(solution)/shard_map/convert_element_type | solution.py:441
  (31 shorter events, 0.6 us)
Async XLA Ops:
  0.6 7.3 %copy-start.2 = (bf16[256,1024]{1,0:T(8,128)(2,1)S(1)}, bf16[256,1024]{1,0:T(8,128)(2,1)}, u32[]{:S(2)}) copy-start(bf16[256,1024]{1,0:T(8,128)(2,1)} %refs_6_) | copy-start | bytes 1572868
  3.2 27.3 %copy-start.1 = (bf16[288,1024]{1,0:T(8,128)(2,1)S(1)}, bf16[288,1024]{1,0:T(8,128)(2,1)}, u32[]{:S(2)}) copy-start(bf16[288,1024]{1,0:T(8,128)(2,1)} %get-tuple-element.27.refs_0_) | copy-start | bytes 1769476
  3.2 7.1 %collective-permute-start.2 = (bf16[288,1024]{1,0:T(8,128)(2,1)}, bf16[288,1024]{1,0:T(8,128)(2,1)S(1)}, u32[]{:S(2)}, u32[]{:S(2)}) collective-permute-start(bf16[288,1024]{1,0:T(8,128)(2,1)} %get-tuple-element.27.refs_0_), channel_id=1, source_target_pairs={{0,4},{4,0},{8,12},{12,8},{16,20},{20,16},{24,28},{28,24},{1,5},{5... | collective-permute-start | bytes 1769480 | tf_op jit(solution)/shard_map/ppermute | solution.py:34
  3.7 20.0 %collective-permute-start = (bf16[2,256,768]{2,1,0:T(8,128)(2,1)}, bf16[2,256,768]{2,1,0:T(8,128)(2,1)S(1)}, u32[]{:S(2)}, u32[]{:S(2)}) collective-permute-start(bf16[2,256,768]{2,1,0:T(8,128)(2,1)} %get-tuple-element.29.refs_0_), channel_id=1, source_target_pairs={{0,1},{1,0},{2,3},{3,2},{4,6},{5,7},{6,4},{7,5},{8,9},{9,8},{10,11... | collective-permute-start | bytes 2359304 | tf_op jit(solution)/shard_map/ppermute | solution.py:316
  6.3 17.4 %collective-permute-start.1 = (bf16[288,1024]{1,0:T(8,128)(2,1)}, bf16[288,1024]{1,0:T(8,128)(2,1)S(1)}, u32[]{:S(2)}, u32[]{:S(2)}) collective-permute-start(bf16[288,1024]{1,0:T(8,128)(2,1)} %get-tuple-element.27.refs_0_), channel_id=1, source_target_pairs={{0,8},{4,12},{8,0},{12,4},{16,24},{20,28},{24,16},{28,20},{1,9},{5... | collective-permute-start | bytes 1769480 | tf_op jit(solution)/shard_map/ppermute | solution.py:34
  7.9 15.8 %collective-permute-start.4 = (bf16[256,1024]{1,0:T(8,128)(2,1)S(1)}, bf16[256,1024]{1,0:T(8,128)(2,1)}, u32[]{:S(2)}, u32[]{:S(2)}) collective-permute-start(bf16[256,1024]{1,0:T(8,128)(2,1)S(1)} %copy-done.2), channel_id=1, source_target_pairs={{0,1},{4,2},{12,15},{5,4},{1,7},{9,10},{10,11},{14,8},{6,5},{15,14... | collective-permute-start | bytes 1572872 | tf_op jit(solution)/shard_map/ppermute | solution.py:317
  11.2 12.5 %collective-permute-start.3 = (bf16[32,1024]{1,0:T(8,128)(2,1)S(1)}, bf16[32,1024]{1,0:T(8,128)(2,1)S(1)}, u32[]{:S(2)}, u32[]{:S(2)}) collective-permute-start(bf16[32,1024]{1,0:T(8,128)(2,1)S(1)} %slice_select_fusion), channel_id=1, source_target_pairs={{12,16},{8,24},{13,17},{9,25},{14,18},{10,26},{15,19},{11,27}} | collective-permute-start | bytes 196616 | tf_op jit(solution)/shard_map/ppermute | solution.py:312
  23.7 6.8 %collective-permute-start.5 = (bf16[288,1024]{1,0:T(8,128)(2,1)S(1)}, bf16[288,1024]{1,0:T(8,128)(2,1)S(1)}, u32[]{:S(2)}, u32[]{:S(2)}) collective-permute-start(bf16[288,1024]{1,0:T(8,128)(2,1)S(1)} %collective-permute-done.1.refs_2_), channel_id=1, source_target_pairs={{0,4},{4,0},{8,12},{12,8},{16,20},{20,16},{24,28},{28,24},{1,5},{5... | collective-permute-start | bytes 1769480 | tf_op jit(solution)/shard_map/ppermute | solution.py:34
  23.8 11.9 %collective-permute-start.9 = (bf16[256,1024]{1,0:T(8,128)(2,1)}, bf16[256,1024]{1,0:T(8,128)(2,1)S(1)}, u32[]{:S(2)}, u32[]{:S(2)}) collective-permute-start(bf16[256,1024]{1,0:T(8,128)(2,1)} %collective-permute-done.4.refs_7_), channel_id=1, source_target_pairs={{15,3},{10,6},{5,9},{0,12},{31,19},{26,22},{21,25},{16,28}} | collective-permute-start | bytes 1572872 | tf_op jit(solution)/shard_map/ppermute | solution.py:332
  26.0 6.2 %collective-permute-start.7 = (bf16[256,768]{1,0:T(8,128)(2,1)S(1)}, bf16[256,768]{1,0:T(8,128)(2,1)S(1)}, u32[]{:S(2)}, u32[]{:S(2)}) collective-permute-start(bf16[256,768]{1,0:T(8,128)(2,1)S(1)} %get-tuple-element.38), channel_id=1, source_target_pairs={{0,4},{4,0},{8,12},{12,8},{16,20},{20,16},{24,28},{28,24},{1,5},{5... | collective-permute-start | bytes 1179656 | tf_op jit(solution)/shard_map/ppermute | solution.py:34
  26.0 7.8 %collective-permute-start.8 = (bf16[256,768]{1,0:T(8,128)(2,1)S(1)}, bf16[256,768]{1,0:T(8,128)(2,1)S(1)}, u32[]{:S(2)}, u32[]{:S(2)}) collective-permute-start(bf16[256,768]{1,0:T(8,128)(2,1)S(1)} %get-tuple-element.37.refs_1_), channel_id=1, source_target_pairs={{0,2},{1,3},{2,0},{3,1},{4,5},{5,4},{6,7},{7,6},{8,10},{9,11},{10,... | collective-permute-start | bytes 1179656 | tf_op jit(solution)/shard_map/ppermute | solution.py:330
  26.1 4.3 %collective-permute-start.6 = (bf16[32,1024]{1,0:T(8,128)(2,1)S(1)}, bf16[32,1024]{1,0:T(8,128)(2,1)S(1)}, u32[]{:S(2)}, u32[]{:S(2)}) collective-permute-start(bf16[32,1024]{1,0:T(8,128)(2,1)S(1)} %collective-permute-done.3.refs_4_), channel_id=1, source_target_pairs={{0,4},{8,12},{16,20},{24,28},{1,5},{9,13},{17,21},{25,29},{2,6},{1... | collective-permute-start | bytes 196616 | tf_op jit(solution)/shard_map/ppermute | solution.py:341
  30.2 3.7 %copy-start = (bf16[2,256,768]{2,1,0:T(8,128)(2,1)S(1)}, bf16[2,256,768]{2,1,0:T(8,128)(2,1)}, u32[]{:S(2)}) copy-start(bf16[2,256,768]{2,1,0:T(8,128)(2,1)} %get-tuple-element.29.refs_0_) | copy-start | bytes 2359300
  38.8 6.5 %collective-permute-start.10 = (bf16[2,144,1024]{2,1,0:T(8,128)(2,1)S(1)}, bf16[2,144,1024]{2,1,0:T(8,128)(2,1)S(1)}, u32[]{:S(2)}, u32[]{:S(2)}) collective-permute-start(bf16[2,144,1024]{2,1,0:T(8,128)(2,1)S(1)} %get-tuple-element.46), channel_id=1, source_target_pairs={{0,4},{4,0},{8,12},{12,8},{16,20},{20,16},{24,28},{28,24},{1,5},{5... | collective-permute-start | bytes 1769480 | tf_op jit(solution)/shard_map/ppermute | solution.py:34
  38.9 6.4 %collective-permute-start.12 = (bf16[2,256,256]{2,1,0:T(8,128)(2,1)S(1)}, bf16[2,256,256]{2,1,0:T(8,128)(2,1)S(1)}, u32[]{:S(2)}, u32[]{:S(2)}) collective-permute-start(bf16[2,256,256]{2,1,0:T(8,128)(2,1)S(1)} %get-tuple-element.48), channel_id=1, source_target_pairs={{0,1},{1,0},{2,3},{3,2},{4,6},{5,7},{6,4},{7,5},{8,9},{9,8},{10,11... | collective-permute-start | bytes 786440 | tf_op jit(solution)/shard_map/ppermute | solution.py:404
  45.4 5.0 %collective-permute-start.13 = (bf16[256,256]{1,0:T(8,128)(2,1)S(1)}, bf16[256,256]{1,0:T(8,128)(2,1)S(1)}, u32[]{:S(2)}, u32[]{:S(2)}) collective-permute-start(bf16[256,256]{1,0:T(8,128)(2,1)S(1)} %fusion.2), channel_id=1, source_target_pairs={{0,2},{1,3},{2,0},{3,1},{4,5},{5,4},{6,7},{7,6},{8,10},{9,11},{10,... | collective-permute-start | bytes 393224 | tf_op jit(solution)/shard_map/ppermute | solution.py:407
  50.5 7.7 %collective-permute-start.14 = (bf16[256,256]{1,0:T(8,128)(2,1)S(1)}, bf16[256,256]{1,0:T(8,128)(2,1)S(1)}, u32[]{:S(2)}, u32[]{:S(2)}) collective-permute-start(bf16[256,256]{1,0:T(8,128)(2,1)S(1)} %fusion.1), channel_id=1, source_target_pairs={{0,16},{4,20},{8,24},{12,28},{16,0},{20,4},{24,8},{28,12},{1,17},{... | collective-permute-start | bytes 393224 | tf_op jit(solution)/shard_map/ppermute | solution.py:34
  53.5 10.8 %collective-permute-start.11 = (bf16[144,1024]{1,0:T(8,128)(2,1)S(1)}, bf16[144,1024]{1,0:T(8,128)(2,1)S(1)}, u32[]{:S(2)}, u32[]{:S(2)}) collective-permute-start(bf16[144,1024]{1,0:T(8,128)(2,1)S(1)} %fusion), channel_id=1, source_target_pairs={{0,8},{4,12},{8,0},{12,4},{16,24},{20,28},{24,16},{28,20},{1,9},{5... | collective-permute-start | bytes 884744 | tf_op jit(solution)/shard_map/ppermute | solution.py:34
  58.2 7.6 %collective-permute-start.15 = (bf16[256,256]{1,0:T(8,128)(2,1)S(1)}, bf16[256,256]{1,0:T(8,128)(2,1)S(1)}, u32[]{:S(2)}, u32[]{:S(2)}) collective-permute-start(bf16[256,256]{1,0:T(8,128)(2,1)S(1)} %add_convert_fusion.2), channel_id=1, source_target_pairs={{0,8},{4,12},{8,0},{12,4},{16,24},{20,28},{24,16},{28,20},{1,9},{5... | collective-permute-start | bytes 393224 | tf_op jit(solution)/shard_map/ppermute | solution.py:34
  64.5 2.2 %copy-start.3 = (bf16[1,8,16,1024]{3,2,1,0:T(8,128)(2,1)S(1)}, bf16[1,8,16,1024]{3,2,1,0:T(8,128)(2,1)}, u32[]{:S(2)}) copy-start(bf16[1,8,16,1024]{3,2,1,0:T(8,128)(2,1)} %param.10) | copy-start | bytes 786436
  65.9 1.6 %collective-permute-start.16 = (bf16[2,256,256]{2,1,0:T(8,128)(2,1)S(1)}, bf16[2,256,256]{2,1,0:T(8,128)(2,1)S(1)}, u32[]{:S(2)}, u32[]{:S(2)}) collective-permute-start(bf16[2,256,256]{2,1,0:T(8,128)(2,1)S(1)} %pad_maximum_fusion), channel_id=1, source_target_pairs={{0,4},{4,0},{8,12},{12,8},{16,20},{20,16},{24,28},{28,24},{1,5},{5... | collective-permute-start | bytes 786440 | tf_op jit(solution)/shard_map/ppermute | solution.py:34

commit v4 on v3

--- a/solution.py
+++ b/solution.py
@@ -12,6 +12,7 @@
 LEFT = 16
 MEMORY = 8
 GROUP = 4
+PIECES = 2
 
 
 epsilon = 1e-05
@@ -87,26 +88,35 @@
         copy.wait()
 
 
-def split_kernel(both, mine, other):
+def split_kernel(both, far, halo, mine, other, far_tokens, far_grads):
     mine[...] = both[0]
     other[...] = both[1]
-
-
-def merge_kernel(group, *refs):
-    parts, halo_a, halo_b, wo_from = refs[:group], *refs[group : group + 2], refs[group + 2 : -4]
-    x_all, x_turned, u_all, wo = refs[-4:]
-    half = parts[0].shape[0] // 2
-    halo = halo_a.shape[0]
+    half = far_grads.shape[0]
+    far_tokens[:half, :] = far[:half, :]
+    far_tokens[half:, :] = halo[...]
+    far_grads[...] = far[half:, :]
+
+
+def merge_kernel(tokens, near, far, far_grads, last, last_grads, x_all, x_turned, u_all):
+    half = far_grads.shape[0]
+    parts = [
+        (tokens[:half, :], tokens[half:, :]),
+        (near[:half, :], near[half:, :]),
+        (far[:half, :], far_grads[...]),
+        (last[:half, :], last_grads[...]),
+    ]
+    halo = far.shape[0] - half
     odd = (member_of() & 1) > 0
-    x_all[:halo, :] = jnp.where(odd, halo_b[...], halo_a[...])
-    for i in range(group):
+    x_all[:halo, :] = jnp.where(odd, last[half:, :], far[half:, :])
+    for i, (x_part, u_part) in enumerate(parts):
         at = aligned(member_of() ^ i, half)
-        x_all[pl.ds(pl.multiple_of(halo + at, 16), half), :] = parts[i][:half, :]
-        u_all[pl.ds(at, half), :] = parts[i][half:, :]
+        x_all[pl.ds(pl.multiple_of(halo + at, 16), half), :] = x_part
+        u_all[pl.ds(at, half), :] = u_part
     x_turned[...] = x_all[...].T
-    wo[...] = wo_from[0][...]
-    if len(wo_from) > 1:
-        wo[...] = jnp.where(lax.axis_index("fsdp") == member_of(), wo[...], wo_from[1][...])
+
+
+def pick_kernel(own, came, wo):
+    wo[...] = jnp.where(lax.axis_index("fsdp") == member_of(), own[...], came[...])
 
 
 def assemble(pieces, whole, crossed):
@@ -169,15 +179,11 @@
 
 def grad_kernel(count, heads, frame_count, segs, crossed, lengths, x_turned, u_all, soft, *refs):
     outputs = 2 if crossed else count
-    wo_from, outs = refs[: -outputs - 3], refs[-outputs - 3 : -3]
-    wo, values, whole = refs[-3:]
+    wo, outs = refs[0], refs[1 : 1 + outputs]
+    values, whole = refs[-2:]
     blocks, keys, lanes = soft.shape
     queries = lanes // heads
     frames = segs * frame_count
-    wo[...] = wo_from[0][...]
-    if len(wo_from) > 1:
-        opposite = (lax.axis_index("fsdp") ^ member_of()) == 3
-        wo[...] = jnp.where(opposite, wo_from[1][...], wo[...])
     back = lax.dot_general(u_all[...], wo[...], NT, preferred_element_type=f32)
     row = lax.broadcasted_iota(jnp.int32, (queries, wo.shape[0]), 0)
     seg_of = jnp.where(row < frames, row // frame_count, row - frames - segs)
@@ -212,12 +218,19 @@
             outs[j][...] = part(j, outs[j])
 
 
-def out_kernel(heads, soft, values, wo, keep, send):
+def out_kernel(heads, first, soft, values, *refs):
+    wo_from, (keep, *send) = refs[: -1 - PIECES], refs[-1 - PIECES :]
+    if len(wo_from) == 3:
+        wo_from, wo = wo_from[:2], wo_from[2]
+        opposite = (lax.axis_index("fsdp") ^ member_of()) == 3
+        wo[...] = jnp.where(opposite, wo_from[1][...], wo_from[0][...])
+    else:
+        wo = wo_from[0]
     blocks, keys, lanes = soft.shape
     queries = lanes // heads
     width = values.shape[1]
     head = lax.broadcasted_iota(jnp.int32, (queries, width), 1) // (width // heads)
-    for i in range(blocks):
+    for i in (first, first + 1):
         b = member_of() ^ i
         stacked = lax.dot_general(
             soft[b],
@@ -229,8 +242,46 @@
         for h in range(1, heads):
             attended = jnp.where(head == h, stacked[h * queries : (h + 1) * queries], attended)
         projected = jnp.dot(attended.astype(bf16), wo[...], preferred_element_type=f32)
-        into = send if i & 1 else keep
-        into[i // 2] = projected.astype(into.dtype)
+        if i == first:
+            keep[...] = projected
+        else:
+            start = 0
+            for into in send:
+                into[...] = projected[start : start + into.shape[0]].astype(into.dtype)
+                start += into.shape[0]
+
+
+def onward_kernel(keep, *refs):
+    pieces, onward = refs[:-1], refs[-1]
+    start = 0
+    for piece in pieces:
+        part = slice(start, start + piece.shape[0])
+        onward[part, :] = (keep[part, :] + piece[...].astype(f32)).astype(bf16)
+        start += piece.shape[0]
+
+
+def finish_kernel(frame_count, lengths, frames, keep, back, *refs):
+    pieces, frames_out, memory_out = refs[:-2], refs[-2], refs[-1]
+    segs = memory_out.shape[0]
+    count = frames.shape[0]
+    near = jnp.concatenate([piece[...].astype(f32) for piece in pieces], axis=0)
+    projected = keep[...] + near + back[...].astype(f32)
+    first = lax.axis_index("seg") * segs
+
+    def live(array, step):
+        at = lax.broadcasted_iota(jnp.int32, array.shape, 0) // step
+        return jnp.where(first + at < lengths[0], array, 0.0)
+
+    frames_out[...] = (
+        frames[...].astype(f32) + live(projected[:count], frame_count)
+    ).astype(bf16)
+    memory_out[...] = live(projected[count + segs :], 1).astype(bf16)
+
+
+def columns_kernel(mine, far, near_mine, near_far, out):
+    width = mine.shape[1]
+    for i, part in enumerate((mine, near_mine, far, near_far)):
+        out[:, pl.ds(aligned(member_of() ^ i, width), width)] = part[...].astype(f32)
 
 
 def gathered(piece):
@@ -309,51 +360,62 @@
     ahead = []
     for s in range(group, seg_size, group):
         ahead += [(s - 1, s), (s - 2, s + 2)]
-    halo_even = lax.ppermute(tail, "seg", ahead)
+    halo = lax.ppermute(tail, "seg", ahead)
     if crossed:
         both = ("seg", "fsdp")
         straight, turned, first, last = pairs(seg_size)
         came = lax.ppermute(own_blocks, both, straight)
         wo_came = lax.ppermute(w_out, both, first)
-        came, far, near, halo_even, wo_came = lax.optimization_barrier(
-            (came, far, near, halo_even, wo_came)
+        came, far, near, halo, wo_came = lax.optimization_barrier(
+            (came, far, near, halo, wo_came)
         )
-        mine, other = pl.pallas_call(
-            split_kernel,
-            in_specs=[vmem],
-            out_specs=[vmem] * 2,
-            out_shape=[jax.ShapeDtypeStruct(came.shape[1:], bf16)] * 2,
-            compiler_params=params(),
-            name="split",
-        )(came)
+        wo_last = lax.ppermute(wo_came, both, last)
+    else:
+        came = own_blocks
+        wo_near = lax.dynamic_slice_in_dim(
+            lax.all_gather(w_out, "fsdp", axis=0, tiled=True), member * block, block, 0
+        )
+    mine, other, far, far_grads = pl.pallas_call(
+        split_kernel,
+        in_specs=[vmem] * 3,
+        out_specs=[vmem] * 4,
+        out_shape=[jax.ShapeDtypeStruct(came.shape[1:], bf16)] * 2
+        + [
+            jax.ShapeDtypeStruct((queries + halo_rows, width), bf16),
+            jax.ShapeDtypeStruct((queries, width), bf16),
+        ],
+        compiler_params=params(),
+        name="split",
+    )(came, far, halo)
+    if crossed:
         wqkv_parts = [
             own_blocks, mine, swapped(other, "seg", 1), lax.ppermute(mine, both, turned)
         ]
-        wo_from, wo_last = [w_out, wo_came], [lax.ppermute(wo_came, both, last)]
+        wo_near = pl.pallas_call(
+            pick_kernel,
+            in_specs=[vmem] * 2,
+            out_specs=vmem,
+            out_shape=jax.ShapeDtypeStruct((block, width), bf16),
+            compiler_params=params(),
+            name="pick",
+        )(w_out, wo_came)
     else:
         wqkv_parts = gathered(own_blocks)
-        wo_from = [
-            lax.dynamic_slice_in_dim(
-                lax.all_gather(w_out, "fsdp", axis=0, tiled=True), member * block, block, 0
-            )
-        ]
-        wo_last = []
-    halo_odd = lax.ppermute(halo_even, "seg", [(s, s + 1) for s in range(0, seg_size, 2)])
-    parts = [tokens, near, far, swapped(far, "seg", 1)]
-
-    x_all, x_turned, u_all, wo_near = pl.pallas_call(
-        functools.partial(merge_kernel, group),
-        in_specs=[vmem] * (group + 2 + len(wo_from)),
-        out_specs=[vmem] * 4,
+    parts = [tokens, near, far, far_grads, swapped(far, "seg", 1), swapped(far_grads, "seg", 1)]
+
+    x_all, x_turned, u_all = pl.pallas_call(
+        merge_kernel,
+        in_specs=[vmem] * len(parts),
+        out_specs=[vmem] * 3,
         out_shape=[
             jax.ShapeDtypeStruct((all_rows, width), bf16),
             jax.ShapeDtypeStruct((width, all_rows), bf16),
             jax.ShapeDtypeStruct((group * queries, width), bf16),
-            jax.ShapeDtypeStruct((block, width), bf16),
         ],
         compiler_params=params(),
         name="merge",
-    )(*parts, halo_even, halo_odd, *wo_from)
+    )(*parts)
+    x_all, wo_near = lax.optimization_barrier((x_all, wo_near))
 
     soft, values = pl.pallas_call(
         functools.partial(weights_kernel, heads, frame_count, segs, crossed),
@@ -368,40 +430,55 @@
         name="soft_weights",
     )(x_all, *wqkv_parts)
 
+    def attend(start, wo_from, name):
+        wo_shape = [jax.ShapeDtypeStruct((block, width), bf16)] * (len(wo_from) - 1)
+        cut = queries // PIECES // 16 * 16
+        sizes = [cut] * (PIECES - 1) + [queries - cut * (PIECES - 1)]
+        outs = pl.pallas_call(
+            functools.partial(out_kernel, heads, start),
+            in_specs=[vmem] * (2 + len(wo_from)),
+            out_specs=[vmem] * (len(wo_shape) + 1 + PIECES),
+            out_shape=wo_shape
+            + [jax.ShapeDtypeStruct((queries, width), f32)]
+            + [jax.ShapeDtypeStruct((size, width), bf16) for size in sizes],
+            compiler_params=params(),
+            name=name,
+        )(soft, values, *wo_from)
+        return outs[: len(wo_shape)], outs[len(wo_shape)], outs[len(wo_shape) + 1 :]
+
+    picked, keep_far, send_far = attend(2, [wo_near] + ([wo_last] if crossed else []), "attend_far")
+    wo_mine = picked[0] if crossed else wo_near
     if crossed:
         grad_shapes = [jax.ShapeDtypeStruct((2, rows, block), dtype) for dtype in (f32, bf16)]
     else:
         grad_shapes = [jax.ShapeDtypeStruct((rows, block), bf16)] * fsdp_size
-    *grad_chunks, wo_mine = pl.pallas_call(
+    grad_chunks = pl.pallas_call(
         functools.partial(grad_kernel, fsdp_size, heads, frame_count, segs, crossed),
-        in_specs=[smem] + [vmem] * (4 + len(wo_last)),
-        out_specs=[vmem] * (len(grad_shapes) + 1),
-        out_shape=grad_shapes + [jax.ShapeDtypeStruct((block, width), bf16)],
+        in_specs=[smem] + [vmem] * 4,
+        out_specs=[vmem] * len(grad_shapes),
+        out_shape=grad_shapes,
         scratch_shapes=[
             pltpu.VMEM((all_rows, block), f32),
             pltpu.VMEM((width, block), f32),
         ],
         compiler_params=params(),
         name="value_grad",
-    )(lengths, x_turned, u_all, soft, wo_near, *wo_last)
-
-    keep, send = pl.pallas_call(
-        functools.partial(out_kernel, heads),
-        in_specs=[vmem] * 3,
-        out_specs=[vmem] * 2,
-        out_shape=[
-            jax.ShapeDtypeStruct((group // 2, queries, width), f32),
-            jax.ShapeDtypeStruct((group // 2, queries, width), bf16),
-        ],
-        compiler_params=params(),
-        name="attend_project",
-    )(soft, values, wo_mine)
-    near = swapped(send, "seg", 1)
-    onward = (keep[1] + near[1].astype(f32)).astype(bf16)
-    back = swapped(onward, "seg", 2)
+    )(lengths, x_turned, u_all, soft, wo_mine)
+
+    _, keep, send = attend(0, [wo_mine], "attend_near")
+    near = [swapped(piece, "seg", 1) for piece in send]
+    near_far = [swapped(piece, "seg", 1) for piece in send_far]
+    onward = pl.pallas_call(
+        onward_kernel,
+        in_specs=[vmem] * (1 + PIECES),
+        out_specs=vmem,
+        out_shape=jax.ShapeDtypeStruct((queries, width), bf16),
+        compiler_params=params(),
+        name="onward",
+    )(keep_far, *near_far)
     if crossed:
         kept, sent = grad_chunks
-        came, _ = lax.optimization_barrier((lax.ppermute(sent, both, straight), send))
+        came = lax.ppermute(sent, both, straight)
         passing = (kept[1] + came[1].astype(f32)).astype(bf16)
         passing, onward = lax.optimization_barrier((passing, onward))
         last = lax.ppermute(passing, both, turned)
@@ -410,35 +487,37 @@
         grad_sum = grad_chunks[0].astype(f32)
         for j in range(1, fsdp_size):
             grad_sum = grad_sum + swapped(grad_chunks[j], "fsdp", j).astype(f32)
+    back = swapped(onward, "seg", 2)
+    back = swapped(onward, "seg", 2)
     bit = group
     while bit < seg_size:
         mine = grad_sum.astype(bf16)
-        grad_sum = mine.astype(f32) + swapped(mine, "seg", bit).astype(f32)
+        other, back = lax.optimization_barrier((swapped(mine, "seg", bit), back))
+        grad_sum = mine.astype(f32) + other.astype(f32)
         bit *= 2
-    mine = grad_sum.astype(bf16)
-    projected = keep[0] + near[0].astype(f32) + back.astype(f32)
-
-    live = (seg * segs + jnp.arange(segs) < lengths[0]).astype(f32)
-    frames_out = (
-        frames.astype(f32)
-        + live[None, :, None, None]
-        * projected[:frame_rows].reshape(1, segs, frame_count, width)
-    ).astype(bf16)
-    memory_out = (live[None, :, None] * projected[None, frame_rows + segs :]).astype(bf16)
-
+    mine, near = lax.optimization_barrier((grad_sum.astype(bf16), near))
+    frames_out, memory_out = pl.pallas_call(
+        functools.partial(finish_kernel, frame_count),
+        in_specs=[smem] + [vmem] * (3 + PIECES),
+        out_specs=[vmem] * 2,
+        out_shape=[
+            jax.ShapeDtypeStruct((frame_rows, width), bf16),
+            jax.ShapeDtypeStruct((segs, width), bf16),
+        ],
+        compiler_params=params(),
+        name="finish",
+    )(lengths, frames.reshape(frame_rows, width), keep, back, *near)
     far = swapped(mine, "seg", 2)
-    high = (member & 2) > 0
-    pair = jnp.stack([jnp.where(high, far, mine), jnp.where(high, mine, far)])
-    near = swapped(pair, "seg", 1)
-    odd = (member & 1) > 0
-    value_grad = jnp.concatenate(
-        [
-            part[j]
-            for j in range(2)
-            for part in (jnp.where(odd, near, pair), jnp.where(odd, pair, near))
-        ],
-        axis=1,
-    ).astype(f32)
+    value_grad = pl.pallas_call(
+        columns_kernel,
+        in_specs=[vmem] * 4,
+        out_specs=vmem,
+        out_shape=jax.ShapeDtypeStruct((rows, width), f32),
+        compiler_params=params(),
+        name="columns",
+    )(mine, far, swapped(mine, "seg", 1), swapped(far, "seg", 1))
+    frames_out = frames_out.reshape(frames.shape)
+    memory_out = memory_out.reshape(memory_in.shape)
     return (frames_out, memory_out, value_grad)
 
 

time: 69.1 us -> 65.2 us (0.944)
  waiting for transfers between devices: 35.4 us -> 29.1 us
  starting transfers between devices: 18.7 us -> 22.8 us
  other arithmetic: 3.82 us -> 0.95 us
  Pallas kernels: 9.2 us -> 10.6 us
    ppermute x9 -> x14, starting transfers between devices: 5.47 us -> 12.7 us  [swapped(): return lax.ppermute(array, axis, [(i, i ^ bit) for i in range(size)])]
    ppermute x9 -> x14, waiting for transfers between devices: 12.1 us -> 8.38 us  [swapped(): return lax.ppermute(array, axis, [(i, i ^ bit) for i in range(size)])]
    ppermute x4 -> x3, starting transfers between devices: 8.06 us -> 4.92 us  [the longest x1 2.8 us: on_device(): came = lax.ppermute(sent, both, straight)]
    convert_element_type x5 -> x1, other arithmetic: 2.67 us -> 0.03 us  [on_device(): mine, near = lax.optimization_barrier((grad_sum.astype(bf16), near))]
    ppermute x4 -> x3, waiting for transfers between devices: 4.82 us -> 2.71 us  [the longest x1 2.71 us: on_device(): came = lax.ppermute(sent, both, straight)]
    pallas_call x3 -> x8, Pallas kernels: 2.8 us -> 4.2 us  [the longest x2 1.46 us: attend(): pl.pallas_call(functools.partial(out_kernel, heads, start), in_specs=[vme...]
    ppermute x1, waiting for transfers between devices: 4.95 us -> 3.57 us  [on_device(): last = lax.ppermute(passing, both, turned)]
    ppermute x1, waiting for transfers between devices: 1.71 us -> 2.86 us  [on_device(): lax.ppermute(mine, both, turned)]
  transfers between devices with their start and end apart: 17 -> 21, of which waited for: 8 -> 10; matrix products, arithmetic and copies ran while one was open for 4% -> 1% of each run, Pallas kernels for 5% -> 7%
where the time goes in v4:
time: 65.2 us; the launch traced here: 64.9 us
  waiting for transfers between devices  29.1 us (45%)
  starting transfers between devices  22.8 us (35%)
  Pallas kernels  10.6 us (16%)
  between operations  1.51 us (2%)
  other arithmetic  0.95 us (1%)
    ppermute x14, starting transfers between devices, swapped(): return lax.ppermute(array, axis, [(i, i ^ bit) for i in range(size)])  12.7 us
    ppermute x1, waiting for transfers between devices, on_device(): wo_came = lax.ppermute(w_out, both, first)  11.6 us
    ppermute x14, waiting for transfers between devices, swapped(): return lax.ppermute(array, axis, [(i, i ^ bit) for i in range(size)])  8.38 us
    ppermute x1, waiting for transfers between devices, on_device(): last = lax.ppermute(passing, both, turned)  3.57 us
    ppermute x1, waiting for transfers between devices, on_device(): lax.ppermute(mine, both, turned)  2.86 us
    ppermute x1, starting transfers between devices, on_device(): came = lax.ppermute(sent, both, straight)  2.8 us
    ppermute x1, waiting for transfers between devices, on_device(): came = lax.ppermute(sent, both, straight)  2.71 us
    pallas_call x1, Pallas kernels, on_device(): pl.pallas_call(functools.partial(pack_kernel, frame_count), in_specs=[hbm...  2.57 us
  transfers between devices with their start and end apart: 21, of which 10 were waited for; matrix products, arithmetic and copies ran while one was open for 1% of the time, Pallas kernels for 7%

profile of v4, /device:TPU:0, one launch (start us, length us, event | category | flops | bytes accessed | tf_op | source)
XLA Modules:
  0.0 64.9 jit_solution(14494067054044906215)
XLA Ops:
  0.6 2.6 %pack.1 = (bf16[2,256,768]{2,1,0:T(8,128)(2,1)}, bf16[288,1024]{1,0:T(8,128)(2,1)}) custom-call(bf16[256,1024]{1,0:T(8,128)(2,1)} %wq.1, bf16[256,1024]{1,0:T(8,128)(2,1)} %wk.1, bf16[256,1024]{1,0:T(8,128)(2,1)} %wv.1, bf16[128,1024]{1,0:T(8,128)(2,1)} %bitcast.13, bf16[128,1024]{1,0:T(8,128)(2,1)} %bitcast.15, bf16[8,1024]{1,0:T(8,128)(2,1)} %bitcast.16, ...), custom_call_target="tpu_custom_call" | custom-call | tf_op jit(solution)/shard_map/pack/pallas_call | solution.py:333
  3.2 0.5 collective-permute-start.2
  3.7 2.6 %collective-permute-start = (bf16[2,256,768]{2,1,0:T(8,128)(2,1)}, bf16[2,256,768]{2,1,0:T(8,128)(2,1)S(1)}, u32[]{:S(2)}, u32[]{:S(2)}) collective-permute-start(bf16[2,256,768]{2,1,0:T(8,128)(2,1)} %get-tuple-element.43.refs_0_), channel_id=1, source_target_pairs={{0,1},{1,0},{2,3},{3,2},{4,6},{5,7},{6,4},{7,5},{8,9},{9,8},{10,11... | collective-permute-start | bytes 2359304 | tf_op jit(solution)/shard_map/ppermute | solution.py:367
  6.3 1.6 %collective-permute-start.1 = (bf16[288,1024]{1,0:T(8,128)(2,1)}, bf16[288,1024]{1,0:T(8,128)(2,1)S(1)}, u32[]{:S(2)}, u32[]{:S(2)}) collective-permute-start(bf16[288,1024]{1,0:T(8,128)(2,1)} %get-tuple-element.41.tokens), channel_id=1, source_target_pairs={{0,8},{4,12},{8,0},{12,4},{16,24},{20,28},{24,16},{28,20},{1,9},{5... | collective-permute-start | bytes 1769480 | tf_op jit(solution)/shard_map/ppermute | solution.py:35
  7.9 2.4 %collective-permute-start.4 = (bf16[256,1024]{1,0:T(8,128)(2,1)S(1)}, bf16[256,1024]{1,0:T(8,128)(2,1)S(1)}, u32[]{:S(2)}, u32[]{:S(2)}) collective-permute-start(bf16[256,1024]{1,0:T(8,128)(2,1)S(1)} %copy-done.3), channel_id=1, source_target_pairs={{0,1},{4,2},{12,15},{5,4},{1,7},{9,10},{10,11},{14,8},{6,5},{15,14... | collective-permute-start | bytes 1572872 | tf_op jit(solution)/shard_map/ppermute | solution.py:368
  10.3 0.9 %slice_select_fusion = bf16[32,1024]{1,0:T(8,128)(2,1)S(1)} fusion(bf16[288,1024]{1,0:T(8,128)(2,1)S(1)} %collective-permute-done.2.near, bf16[288,1024]{1,0:T(8,128)(2,1)} %get-tuple-element.41.tokens, pred[]{:T(512)S(6)} %eq.5), kind=kLoop, calls=%fused_computation.5 | loop fusion | flops 32768 | bytes 196609 | tf_op jit(solution)/shard_map/jit(_where)/select_n | solution.py:359
  11.2 0.8 %collective-permute-start.3 = (bf16[32,1024]{1,0:T(8,128)(2,1)S(1)}, bf16[32,1024]{1,0:T(8,128)(2,1)S(1)}, u32[]{:S(2)}, u32[]{:S(2)}) collective-permute-start(bf16[32,1024]{1,0:T(8,128)(2,1)S(1)} %slice_select_fusion), channel_id=1, source_target_pairs={{12,16},{8,24},{13,17},{9,25},{14,18},{10,26},{15,19},{11,27}} | collective-permute-start | bytes 196616 | tf_op jit(solution)/shard_map/ppermute | solution.py:363
  12.0 11.6 %collective-permute-done.4.came = bf16[256,1024]{1,0:T(8,128)(2,1)S(1)} collective-permute-done((bf16[256,1024]{1,0:T(8,128)(2,1)S(1)}, bf16[256,1024]{1,0:T(8,128)(2,1)S(1)}, u32[]{:S(2)}, u32[]{:S(2)}) %collective-permute-start.4) | collective-permute-done | bytes 524320 | tf_op jit(solution)/shard_map/ppermute | solution.py:368
  23.6 1.3 %collective-permute-start.9 = (bf16[256,1024]{1,0:T(8,128)(2,1)S(1)}, bf16[256,1024]{1,0:T(8,128)(2,1)S(1)}, u32[]{:S(2)}, u32[]{:S(2)}) collective-permute-start(bf16[256,1024]{1,0:T(8,128)(2,1)S(1)} %collective-permute-done.4.came), channel_id=1, source_target_pairs={{15,3},{10,6},{5,9},{0,12},{31,19},{26,22},{21,25},{16,28}} | collective-permute-start | bytes 1572872 | tf_op jit(solution)/shard_map/ppermute | solution.py:372
  25.2 2.5 %collective-permute-start.5 = (bf16[176,1024]{1,0:T(8,128)(2,1)S(1)}, bf16[176,1024]{1,0:T(8,128)(2,1)S(1)}, u32[]{:S(2)}, u32[]{:S(2)}) collective-permute-start(bf16[176,1024]{1,0:T(8,128)(2,1)S(1)} %get-tuple-element.49.far), channel_id=1, source_target_pairs={{0,4},{4,0},{8,12},{12,8},{16,20},{20,16},{24,28},{28,24},{1,5},{5... | collective-permute-start | bytes 1081352 | tf_op jit(solution)/shard_map/ppermute | solution.py:35
  28.5 1.0 %collective-permute-done.6.last_grads = bf16[144,1024]{1,0:T(8,128)(2,1)S(1)} collective-permute-done((bf16[144,1024]{1,0:T(8,128)(2,1)S(1)}, bf16[144,1024]{1,0:T(8,128)(2,1)S(1)}, u32[]{:S(2)}, u32[]{:S(2)}) %collective-permute-start.6) | collective-permute-done | bytes 294944 | tf_op jit(solution)/shard_map/ppermute | solution.py:35
  29.4 0.6 merge.1
  30.1 2.9 %collective-permute-done.8.refs_3_ = bf16[256,768]{1,0:T(8,128)(2,1)S(1)} collective-permute-done((bf16[256,768]{1,0:T(8,128)(2,1)S(1)}, bf16[256,768]{1,0:T(8,128)(2,1)S(1)}, u32[]{:S(2)}, u32[]{:S(2)}) %collective-permute-start.8) | collective-permute-done | bytes 393248 | tf_op jit(solution)/shard_map/ppermute | solution.py:392
  33.0 1.8 %soft_weights.1 = (bf16[4,176,576]{2,1,0:T(8,128)(2,1)S(1)}, bf16[608,256]{1,0:T(8,128)(2,1)S(1)}) custom-call(bf16[608,1024]{1,0:T(8,128)(2,1)S(1)} %get-tuple-element.53.x_all, bf16[2,256,768]{2,1,0:T(8,128)(2,1)S(1)} %copy-done.1, bf16[256,768]{1,0:T(8,128)(2,1)S(1)} %get-tuple-element.54.refs_1_, bf16[256,768]{1,0:T(8,128)(2,1)S(1)} %collective-permute-done.7.refs_2_, ...), custom_call_target="tpu_custom_call" | custom-call | tf_op jit(solution)/shard_map/soft_weights/pallas_call | solution.py:420
  34.8 0.7 %attend_far.1 = (bf16[256,1024]{1,0:T(8,128)(2,1)S(1)}, f32[144,1024]{1,0:T(8,128)S(1)}, bf16[64,1024]{1,0:T(8,128)(2,1)S(1)}, bf16[80,1024]{1,0:T(8,128)(2,1)S(1)}) custom-call(bf16[4,176,576]{2,1,0:T(8,128)(2,1)S(1)} %get-tuple-element.56.soft, bf16[608,256]{1,0:T(8,128)(2,1)S(1)} %get-tuple-element.57.values, bf16[256,1024]{1,0:T(8,128)(2,1)S(1)} %pick.1.refs_0_, ...), custom_call_target="tpu_custom_call" | custom-call | tf_op jit(solution)/shard_map/attend_far/pallas_call | solution.py:437
  35.5 2.0 %value_grad.1 = (f32[2,256,256]{2,1,0:T(8,128)S(1)}, bf16[2,256,256]{2,1,0:T(8,128)(2,1)S(1)}) custom-call(s32[1]{0:T(128)S(6)} %copy.13.lengths, bf16[1024,608]{1,0:T(8,128)(2,1)S(1)} %get-tuple-element.61.x_turned, bf16[576,1024]{1,0:T(8,128)(2,1)S(1)} %get-tuple-element.62.u_all, bf16[4,176,576]{2,1,0:T(8,128)(2,1)S(1)} %get-tuple-element.56.soft, ...), custom_call_target="tpu_custom_call" | custom-call | tf_op jit(solution)/shard_map/value_grad/pallas_call | solution.py:455
  37.5 2.8 %collective-permute-start.10 = (bf16[2,256,256]{2,1,0:T(8,128)(2,1)S(1)}, bf16[2,256,256]{2,1,0:T(8,128)(2,1)S(1)}, u32[]{:S(2)}, u32[]{:S(2)}) collective-permute-start(bf16[2,256,256]{2,1,0:T(8,128)(2,1)S(1)} %get-tuple-element.64), channel_id=1, source_target_pairs={{0,1},{1,0},{2,3},{3,2},{4,6},{5,7},{6,4},{7,5},{8,9},{9,8},{10,11... | collective-permute-start | bytes 786440 | tf_op jit(solution)/shard_map/ppermute | solution.py:481
  40.3 0.5 collective-permute-start.11
  40.9 1.1 %collective-permute-done.11.refs_0_ = bf16[64,1024]{1,0:T(8,128)(2,1)S(1)} collective-permute-done((bf16[64,1024]{1,0:T(8,128)(2,1)S(1)}, bf16[64,1024]{1,0:T(8,128)(2,1)S(1)}, u32[]{:S(2)}, u32[]{:S(2)}) %collective-permute-start.11) | collective-permute-done | bytes 131104 | tf_op jit(solution)/shard_map/ppermute | solution.py:35
  42.0 2.7 %collective-permute-done.10 = bf16[2,256,256]{2,1,0:T(8,128)(2,1)S(1)} collective-permute-done((bf16[2,256,256]{2,1,0:T(8,128)(2,1)S(1)}, bf16[2,256,256]{2,1,0:T(8,128)(2,1)S(1)}, u32[]{:S(2)}, u32[]{:S(2)}) %collective-permute-start.10) | collective-permute-done | bytes 262176 | tf_op jit(solution)/shard_map/ppermute | solution.py:481
  44.7 0.1 collective-permute-start.13
  44.8 1.4 %collective-permute-start.15 = (bf16[144,1024]{1,0:T(8,128)(2,1)S(1)}, bf16[144,1024]{1,0:T(8,128)(2,1)S(1)}, u32[]{:S(2)}, u32[]{:S(2)}) collective-permute-start(bf16[144,1024]{1,0:T(8,128)(2,1)S(1)} %onward.1), channel_id=1, source_target_pairs={{0,8},{4,12},{8,0},{12,4},{16,24},{20,28},{24,16},{28,20},{1,9},{5... | collective-permute-start | bytes 884744 | tf_op jit(solution)/shard_map/ppermute | solution.py:35
  46.2 3.6 %collective-permute-done.13 = bf16[256,256]{1,0:T(8,128)(2,1)S(1)} collective-permute-done((bf16[256,256]{1,0:T(8,128)(2,1)S(1)}, bf16[256,256]{1,0:T(8,128)(2,1)S(1)}, u32[]{:S(2)}, u32[]{:S(2)}) %collective-permute-start.13) | collective-permute-done | bytes 131104 | tf_op jit(solution)/shard_map/ppermute | solution.py:484
  49.8 2.7 %collective-permute-start.14 = (bf16[256,256]{1,0:T(8,128)(2,1)S(1)}, bf16[256,256]{1,0:T(8,128)(2,1)S(1)}, u32[]{:S(2)}, u32[]{:S(2)}) collective-permute-start(bf16[256,256]{1,0:T(8,128)(2,1)S(1)} %fusion), channel_id=1, source_target_pairs={{0,16},{4,20},{8,24},{12,28},{16,0},{20,4},{24,8},{28,12},{1,17},{... | collective-permute-start | bytes 393224 | tf_op jit(solution)/shard_map/ppermute | solution.py:35
  52.5 0.7 %attend_near.1 = (f32[144,1024]{1,0:T(8,128)S(1)}, bf16[64,1024]{1,0:T(8,128)(2,1)S(1)}, bf16[80,1024]{1,0:T(8,128)(2,1)S(1)}) custom-call(bf16[4,176,576]{2,1,0:T(8,128)(2,1)S(1)} %get-tuple-element.56.soft, bf16[608,256]{1,0:T(8,128)(2,1)S(1)} %get-tuple-element.57.values, bf16[256,1024]{1,0:T(8,128)(2,1)S(1)} %get-tuple-element.59.refs_0_), custom_call_target="tpu_custom_call" | custom-call | tf_op jit(solution)/shard_map/attend_near/pallas_call | solution.py:437
  53.3 0.5 collective-permute-start.16
  53.8 2.8 %collective-permute-done.14 = bf16[256,256]{1,0:T(8,128)(2,1)S(1)} collective-permute-done((bf16[256,256]{1,0:T(8,128)(2,1)S(1)}, bf16[256,256]{1,0:T(8,128)(2,1)S(1)}, u32[]{:S(2)}, u32[]{:S(2)}) %collective-permute-start.14) | collective-permute-done | bytes 131104 | tf_op jit(solution)/shard_map/ppermute | solution.py:35
  56.7 2.9 %collective-permute-start.18 = (bf16[256,256]{1,0:T(8,128)(2,1)S(1)}, bf16[256,256]{1,0:T(8,128)(2,1)S(1)}, u32[]{:S(2)}, u32[]{:S(2)}) collective-permute-start(bf16[256,256]{1,0:T(8,128)(2,1)S(1)} %add_convert_fusion.mine), channel_id=1, source_target_pairs={{0,8},{4,12},{8,0},{12,4},{16,24},{20,28},{24,16},{28,20},{1,9},{5... | collective-permute-start | bytes 393224 | tf_op jit(solution)/shard_map/ppermute | solution.py:35
  59.6 2.9 %collective-permute-done.18.far = bf16[256,256]{1,0:T(8,128)(2,1)S(1)} collective-permute-done((bf16[256,256]{1,0:T(8,128)(2,1)S(1)}, bf16[256,256]{1,0:T(8,128)(2,1)S(1)}, u32[]{:S(2)}, u32[]{:S(2)}) %collective-permute-start.18) | collective-permute-done | bytes 131104 | tf_op jit(solution)/shard_map/ppermute | solution.py:35
  62.5 0.8 %finish.1 = (bf16[128,1024]{1,0:T(8,128)(2,1)}, bf16[8,1024]{1,0:T(8,128)(2,1)}) custom-call(s32[1]{0:T(128)S(6)} %copy.13.lengths, bf16[128,1024]{1,0:T(8,128)(2,1)S(1)} %bitcast.14, f32[144,1024]{1,0:T(8,128)S(1)} %get-tuple-element.60.keep, bf16[144,1024]{1,0:T(8,128)(2,1)S(1)} %collective-permute-done.15.back, ...), custom_call_target="tpu_custom_call" | custom-call | tf_op jit(solution)/shard_map/finish/pallas_call | solution.py:499
  63.4 0.5 collective-permute-done.20.near_far
  63.9 1.1 %columns.1 = f32[256,1024]{1,0:T(8,128)} custom-call(bf16[256,256]{1,0:T(8,128)(2,1)S(1)} %add_convert_fusion.mine, bf16[256,256]{1,0:T(8,128)(2,1)S(1)} %collective-permute-done.18.far, bf16[256,256]{1,0:T(8,128)(2,1)S(1)} %collective-permute-done.19.near_mine, bf16[256,256]{1,0:T(8,128)(2,1)S(1)} %collective-permute-done.20.near_far), custom_call_target="tpu_custom_call" | custom-call | tf_op jit(solution)/shard_map/columns/pallas_call | solution.py:511
  (33 shorter events, 0.6 us)
Async XLA Ops:
  0.6 7.2 %copy-start.3 = (bf16[256,1024]{1,0:T(8,128)(2,1)S(1)}, bf16[256,1024]{1,0:T(8,128)(2,1)}, u32[]{:S(2)}) copy-start(bf16[256,1024]{1,0:T(8,128)(2,1)} %own) | copy-start | bytes 1572868
  3.2 7.1 %collective-permute-start.2 = (bf16[288,1024]{1,0:T(8,128)(2,1)}, bf16[288,1024]{1,0:T(8,128)(2,1)S(1)}, u32[]{:S(2)}, u32[]{:S(2)}) collective-permute-start(bf16[288,1024]{1,0:T(8,128)(2,1)} %get-tuple-element.41.tokens), channel_id=1, source_target_pairs={{0,4},{4,0},{8,12},{12,8},{16,20},{20,16},{24,28},{28,24},{1,5},{5... | collective-permute-start | bytes 1769480 | tf_op jit(solution)/shard_map/ppermute | solution.py:35
  3.7 19.9 %collective-permute-start = (bf16[2,256,768]{2,1,0:T(8,128)(2,1)}, bf16[2,256,768]{2,1,0:T(8,128)(2,1)S(1)}, u32[]{:S(2)}, u32[]{:S(2)}) collective-permute-start(bf16[2,256,768]{2,1,0:T(8,128)(2,1)} %get-tuple-element.43.refs_0_), channel_id=1, source_target_pairs={{0,1},{1,0},{2,3},{3,2},{4,6},{5,7},{6,4},{7,5},{8,9},{9,8},{10,11... | collective-permute-start | bytes 2359304 | tf_op jit(solution)/shard_map/ppermute | solution.py:367
  6.3 17.3 %collective-permute-start.1 = (bf16[288,1024]{1,0:T(8,128)(2,1)}, bf16[288,1024]{1,0:T(8,128)(2,1)S(1)}, u32[]{:S(2)}, u32[]{:S(2)}) collective-permute-start(bf16[288,1024]{1,0:T(8,128)(2,1)} %get-tuple-element.41.tokens), channel_id=1, source_target_pairs={{0,8},{4,12},{8,0},{12,4},{16,24},{20,28},{24,16},{28,20},{1,9},{5... | collective-permute-start | bytes 1769480 | tf_op jit(solution)/shard_map/ppermute | solution.py:35
  7.9 15.7 %collective-permute-start.4 = (bf16[256,1024]{1,0:T(8,128)(2,1)S(1)}, bf16[256,1024]{1,0:T(8,128)(2,1)S(1)}, u32[]{:S(2)}, u32[]{:S(2)}) collective-permute-start(bf16[256,1024]{1,0:T(8,128)(2,1)S(1)} %copy-done.3), channel_id=1, source_target_pairs={{0,1},{4,2},{12,15},{5,4},{1,7},{9,10},{10,11},{14,8},{6,5},{15,14... | collective-permute-start | bytes 1572872 | tf_op jit(solution)/shard_map/ppermute | solution.py:368
  11.2 18.2 %copy-start.2 = (bf16[288,1024]{1,0:T(8,128)(2,1)S(1)}, bf16[288,1024]{1,0:T(8,128)(2,1)}, u32[]{:S(2)}) copy-start(bf16[288,1024]{1,0:T(8,128)(2,1)} %get-tuple-element.41.tokens) | copy-start | bytes 1769476
  11.2 12.4 %collective-permute-start.3 = (bf16[32,1024]{1,0:T(8,128)(2,1)S(1)}, bf16[32,1024]{1,0:T(8,128)(2,1)S(1)}, u32[]{:S(2)}, u32[]{:S(2)}) collective-permute-start(bf16[32,1024]{1,0:T(8,128)(2,1)S(1)} %slice_select_fusion), channel_id=1, source_target_pairs={{12,16},{8,24},{13,17},{9,25},{14,18},{10,26},{15,19},{11,27}} | collective-permute-start | bytes 196616 | tf_op jit(solution)/shard_map/ppermute | solution.py:363
  23.6 11.2 %collective-permute-start.9 = (bf16[256,1024]{1,0:T(8,128)(2,1)S(1)}, bf16[256,1024]{1,0:T(8,128)(2,1)S(1)}, u32[]{:S(2)}, u32[]{:S(2)}) collective-permute-start(bf16[256,1024]{1,0:T(8,128)(2,1)S(1)} %collective-permute-done.4.came), channel_id=1, source_target_pairs={{15,3},{10,6},{5,9},{0,12},{31,19},{26,22},{21,25},{16,28}} | collective-permute-start | bytes 1572872 | tf_op jit(solution)/shard_map/ppermute | solution.py:372
  25.0 5.1 %collective-permute-start.7 = (bf16[256,768]{1,0:T(8,128)(2,1)S(1)}, bf16[256,768]{1,0:T(8,128)(2,1)S(1)}, u32[]{:S(2)}, u32[]{:S(2)}) collective-permute-start(bf16[256,768]{1,0:T(8,128)(2,1)S(1)} %get-tuple-element.55), channel_id=1, source_target_pairs={{0,4},{4,0},{8,12},{12,8},{16,20},{20,16},{24,28},{28,24},{1,5},{5... | collective-permute-start | bytes 1179656 | tf_op jit(solution)/shard_map/ppermute | solution.py:35
  25.1 7.8 %collective-permute-start.8 = (bf16[256,768]{1,0:T(8,128)(2,1)S(1)}, bf16[256,768]{1,0:T(8,128)(2,1)S(1)}, u32[]{:S(2)}, u32[]{:S(2)}) collective-permute-start(bf16[256,768]{1,0:T(8,128)(2,1)S(1)} %get-tuple-element.54.refs_1_), channel_id=1, source_target_pairs={{0,2},{1,3},{2,0},{3,1},{4,5},{5,4},{6,7},{7,6},{8,10},{9,11},{10,... | collective-permute-start | bytes 1179656 | tf_op jit(solution)/shard_map/ppermute | solution.py:392
  25.2 4.3 %collective-permute-start.5 = (bf16[176,1024]{1,0:T(8,128)(2,1)S(1)}, bf16[176,1024]{1,0:T(8,128)(2,1)S(1)}, u32[]{:S(2)}, u32[]{:S(2)}) collective-permute-start(bf16[176,1024]{1,0:T(8,128)(2,1)S(1)} %get-tuple-element.49.far), channel_id=1, source_target_pairs={{0,4},{4,0},{8,12},{12,8},{16,20},{20,16},{24,28},{28,24},{1,5},{5... | collective-permute-start | bytes 1081352 | tf_op jit(solution)/shard_map/ppermute | solution.py:35
  27.7 1.7 %collective-permute-start.6 = (bf16[144,1024]{1,0:T(8,128)(2,1)S(1)}, bf16[144,1024]{1,0:T(8,128)(2,1)S(1)}, u32[]{:S(2)}, u32[]{:S(2)}) collective-permute-start(bf16[144,1024]{1,0:T(8,128)(2,1)S(1)} %get-tuple-element.50.far_grads), channel_id=1, source_target_pairs={{0,4},{4,0},{8,12},{12,8},{16,20},{20,16},{24,28},{28,24},{1,5},{5... | collective-permute-start | bytes 884744 | tf_op jit(solution)/shard_map/ppermute | solution.py:35
  28.4 4.5 %copy-start.1 = (bf16[2,256,768]{2,1,0:T(8,128)(2,1)S(1)}, bf16[2,256,768]{2,1,0:T(8,128)(2,1)}, u32[]{:S(2)}) copy-start(bf16[2,256,768]{2,1,0:T(8,128)(2,1)} %get-tuple-element.43.refs_0_) | copy-start | bytes 2359300
  37.5 7.2 %collective-permute-start.10 = (bf16[2,256,256]{2,1,0:T(8,128)(2,1)S(1)}, bf16[2,256,256]{2,1,0:T(8,128)(2,1)S(1)}, u32[]{:S(2)}, u32[]{:S(2)}) collective-permute-start(bf16[2,256,256]{2,1,0:T(8,128)(2,1)S(1)} %get-tuple-element.64), channel_id=1, source_target_pairs={{0,1},{1,0},{2,3},{3,2},{4,6},{5,7},{6,4},{7,5},{8,9},{9,8},{10,11... | collective-permute-start | bytes 786440 | tf_op jit(solution)/shard_map/ppermute | solution.py:481
  40.3 1.6 %collective-permute-start.12 = (bf16[80,1024]{1,0:T(8,128)(2,1)S(1)}, bf16[80,1024]{1,0:T(8,128)(2,1)S(1)}, u32[]{:S(2)}, u32[]{:S(2)}) collective-permute-start(bf16[80,1024]{1,0:T(8,128)(2,1)S(1)} %get-tuple-element.67), channel_id=1, source_target_pairs={{0,4},{4,0},{8,12},{12,8},{16,20},{20,16},{24,28},{28,24},{1,5},{5... | collective-permute-start | bytes 491528 | tf_op jit(solution)/shard_map/ppermute | solution.py:35
  40.3 1.6 %collective-permute-start.11 = (bf16[64,1024]{1,0:T(8,128)(2,1)S(1)}, bf16[64,1024]{1,0:T(8,128)(2,1)S(1)}, u32[]{:S(2)}, u32[]{:S(2)}) collective-permute-start(bf16[64,1024]{1,0:T(8,128)(2,1)S(1)} %get-tuple-element.66), channel_id=1, source_target_pairs={{0,4},{4,0},{8,12},{12,8},{16,20},{20,16},{24,28},{28,24},{1,5},{5... | collective-permute-start | bytes 393224 | tf_op jit(solution)/shard_map/ppermute | solution.py:35
  44.7 17.8 %copy-start = (bf16[1,8,16,1024]{3,2,1,0:T(8,128)(2,1)S(1)}, bf16[1,8,16,1024]{3,2,1,0:T(8,128)(2,1)}, u32[]{:S(2)}) copy-start(bf16[1,8,16,1024]{3,2,1,0:T(8,128)(2,1)} %param.10) | copy-start | bytes 786436
  44.7 5.0 %collective-permute-start.13 = (bf16[256,256]{1,0:T(8,128)(2,1)S(1)}, bf16[256,256]{1,0:T(8,128)(2,1)S(1)}, u32[]{:S(2)}, u32[]{:S(2)}) collective-permute-start(bf16[256,256]{1,0:T(8,128)(2,1)S(1)} %fusion.1), channel_id=1, source_target_pairs={{0,2},{1,3},{2,0},{3,1},{4,5},{5,4},{6,7},{7,6},{8,10},{9,11},{10,... | collective-permute-start | bytes 393224 | tf_op jit(solution)/shard_map/ppermute | solution.py:484
  44.8 11.8 %collective-permute-start.15 = (bf16[144,1024]{1,0:T(8,128)(2,1)S(1)}, bf16[144,1024]{1,0:T(8,128)(2,1)S(1)}, u32[]{:S(2)}, u32[]{:S(2)}) collective-permute-start(bf16[144,1024]{1,0:T(8,128)(2,1)S(1)} %onward.1), channel_id=1, source_target_pairs={{0,8},{4,12},{8,0},{12,4},{16,24},{20,28},{24,16},{28,20},{1,9},{5... | collective-permute-start | bytes 884744 | tf_op jit(solution)/shard_map/ppermute | solution.py:35
  49.8 6.8 %collective-permute-start.14 = (bf16[256,256]{1,0:T(8,128)(2,1)S(1)}, bf16[256,256]{1,0:T(8,128)(2,1)S(1)}, u32[]{:S(2)}, u32[]{:S(2)}) collective-permute-start(bf16[256,256]{1,0:T(8,128)(2,1)S(1)} %fusion), channel_id=1, source_target_pairs={{0,16},{4,20},{8,24},{12,28},{16,0},{20,4},{24,8},{28,12},{1,17},{... | collective-permute-start | bytes 393224 | tf_op jit(solution)/shard_map/ppermute | solution.py:35
  53.2 3.5 %collective-permute-start.17 = (bf16[80,1024]{1,0:T(8,128)(2,1)S(1)}, bf16[80,1024]{1,0:T(8,128)(2,1)S(1)}, u32[]{:S(2)}, u32[]{:S(2)}) collective-permute-start(bf16[80,1024]{1,0:T(8,128)(2,1)S(1)} %get-tuple-element.73), channel_id=1, source_target_pairs={{0,4},{4,0},{8,12},{12,8},{16,20},{20,16},{24,28},{28,24},{1,5},{5... | collective-permute-start | bytes 491528 | tf_op jit(solution)/shard_map/ppermute | solution.py:35
  53.3 3.4 %collective-permute-start.16 = (bf16[64,1024]{1,0:T(8,128)(2,1)S(1)}, bf16[64,1024]{1,0:T(8,128)(2,1)S(1)}, u32[]{:S(2)}, u32[]{:S(2)}) collective-permute-start(bf16[64,1024]{1,0:T(8,128)(2,1)S(1)} %get-tuple-element.72), channel_id=1, source_target_pairs={{0,4},{4,0},{8,12},{12,8},{16,20},{20,16},{24,28},{28,24},{1,5},{5... | collective-permute-start | bytes 393224 | tf_op jit(solution)/shard_map/ppermute | solution.py:35
  56.7 5.8 %collective-permute-start.18 = (bf16[256,256]{1,0:T(8,128)(2,1)S(1)}, bf16[256,256]{1,0:T(8,128)(2,1)S(1)}, u32[]{:S(2)}, u32[]{:S(2)}) collective-permute-start(bf16[256,256]{1,0:T(8,128)(2,1)S(1)} %add_convert_fusion.mine), channel_id=1, source_target_pairs={{0,8},{4,12},{8,0},{12,4},{16,24},{20,28},{24,16},{28,20},{1,9},{5... | collective-permute-start | bytes 393224 | tf_op jit(solution)/shard_map/ppermute | solution.py:35
  59.6 3.8 %collective-permute-start.19 = (bf16[256,256]{1,0:T(8,128)(2,1)S(1)}, bf16[256,256]{1,0:T(8,128)(2,1)S(1)}, u32[]{:S(2)}, u32[]{:S(2)}) collective-permute-start(bf16[256,256]{1,0:T(8,128)(2,1)S(1)} %add_convert_fusion.mine), channel_id=1, source_target_pairs={{0,4},{4,0},{8,12},{12,8},{16,20},{20,16},{24,28},{28,24},{1,5},{5... | collective-permute-start | bytes 393224 | tf_op jit(solution)/shard_map/ppermute | solution.py:35
  62.5 1.3 %collective-permute-start.20 = (bf16[256,256]{1,0:T(8,128)(2,1)S(1)}, bf16[256,256]{1,0:T(8,128)(2,1)S(1)}, u32[]{:S(2)}, u32[]{:S(2)}) collective-permute-start(bf16[256,256]{1,0:T(8,128)(2,1)S(1)} %collective-permute-done.18.far), channel_id=1, source_target_pairs={{0,4},{4,0},{8,12},{12,8},{16,20},{20,16},{24,28},{28,24},{1,5},{5... | collective-permute-start | bytes 393224 | tf_op jit(solution)/shard_map/ppermute | solution.py:35

commit v5 on v4

--- a/solution.py
+++ b/solution.py
@@ -119,13 +119,11 @@
     wo[...] = jnp.where(lax.axis_index("fsdp") == member_of(), own[...], came[...])
 
 
-def assemble(pieces, whole, crossed):
+def assemble(pieces, whole):
     own = lax.axis_index("fsdp")
     rows = pieces[0].shape[-2]
-    flip = lax.axis_index("seg") & 1 if crossed else 0
     for j, piece in enumerate(pieces):
-        apart = j ^ (3 * flip) if j in (1, 2) else j
-        into = whole.at[pl.ds(aligned(own ^ apart, rows), rows), :]
+        into = whole.at[pl.ds(aligned(own ^ j, rows), rows), :]
         into[...] = piece[0] if len(piece.shape) == 3 else piece[...]
 
 
@@ -136,15 +134,36 @@
     return jnp.concatenate([jnp.where(head == h, array, zero) for h in range(heads)], axis=0)
 
 
+def early_kernel(x_all, mine, beside, swapped_in, total):
+    own = lax.axis_index("fsdp")
+    along = 1 + (lax.axis_index("seg") & 1)
+    rows = beside.shape[0]
+    columns = lambda j: x_all[:, pl.ds(aligned(own ^ j, rows), rows)]
+    total[...] = (
+        jnp.dot(columns(0), mine[0], preferred_element_type=f32)
+        + jnp.dot(columns(along), beside[...], preferred_element_type=f32)
+        + jnp.dot(columns(along ^ 3), swapped_in[...], preferred_element_type=f32)
+    )
+
+
 def weights_kernel(heads, frame_count, segs, crossed, x_all, *refs):
-    soft, values, wqkv = refs[-3:]
-    assemble(refs[:-3], wqkv, crossed)
+    soft, values = refs[-3:-1] if not crossed else refs[-2:]
+    if crossed:
+        total, last = refs[:2]
+        rows = last.shape[0]
+        at = aligned(lax.axis_index("fsdp") ^ 3, rows)
+        product = total[...] + jnp.dot(
+            x_all[:, pl.ds(at, rows)], last[...], preferred_element_type=f32
+        )
+    else:
+        assemble(refs[:-3], refs[-1])
+        product = jnp.dot(x_all[...], refs[-1][...], preferred_element_type=f32)
+    projected = product.astype(bf16)
     blocks, keys, lanes = soft.shape
     queries = lanes // heads
     halo = keys - queries
     frames = segs * frame_count
     block = values.shape[1]
-    projected = jnp.dot(x_all[...], wqkv[...], preferred_element_type=f32).astype(bf16)
     q_all, k_all = projected[:, :block], projected[:, block : 2 * block]
     values[...] = projected[:, 2 * block :]
     key = lax.broadcasted_iota(jnp.int32, (keys, lanes), 0)
@@ -177,55 +196,50 @@
         soft[b] = (exponent / jnp.sum(exponent, axis=0, keepdims=True)).astype(bf16)
 
 
-def grad_kernel(count, heads, frame_count, segs, crossed, lengths, x_turned, u_all, soft, *refs):
-    outputs = 2 if crossed else count
-    wo, outs = refs[0], refs[1 : 1 + outputs]
-    values, whole = refs[-2:]
+def grad_kernel(heads, frame_count, segs, lengths, u_all, soft, *refs):
+    wo_from, (wo, values, total) = refs[:-3], refs[-3:]
     blocks, keys, lanes = soft.shape
     queries = lanes // heads
     frames = segs * frame_count
+    wo[...] = wo_from[0][...]
+    if len(wo_from) > 1:
+        opposite = (lax.axis_index("fsdp") ^ member_of()) == 3
+        wo[...] = jnp.where(opposite, wo_from[1][...], wo[...])
     back = lax.dot_general(u_all[...], wo[...], NT, preferred_element_type=f32)
     row = lax.broadcasted_iota(jnp.int32, (queries, wo.shape[0]), 0)
     seg_of = jnp.where(row < frames, row // frame_count, row - frames - segs)
     first = lax.axis_index("seg") - member_of()
-    values[: keys - queries, :] = jnp.zeros((keys - queries, values.shape[1]), f32)
+    split = keys - queries
+    total[:split, :] = jnp.zeros((split, total.shape[1]), f32)
     for b in range(blocks):
         start = b * queries
         live = ((first + b) * segs + seg_of < lengths[0]).astype(f32)
         grad_attended = head_stack((live * back[start : start + queries]).astype(bf16), heads)
         term = jnp.dot(soft[b], grad_attended, preferred_element_type=f32)
-        split = keys - queries
-        values[start : start + split, :] += term[:split]
-        values[start + split : start + keys, :] = term[split:]
-    whole[...] = jnp.dot(
-        x_turned[...], values[...].astype(bf16), preferred_element_type=f32
-    )
+        total[start : start + split, :] += term[:split]
+        total[start + split : start + keys, :] = term[split:]
+    values[...] = total[...].astype(bf16)
+
+
+def rows_kernel(which, x_turned, values, *outs):
     own = lax.axis_index("fsdp")
-    rows = whole.shape[0] // count
-
-    def part(apart, into):
-        return whole[pl.ds(aligned(own ^ apart, rows), rows), :].astype(into.dtype)
-
-    if crossed:
-        keep, send = outs
-        along = 1 + (lax.axis_index("seg") & 1)
-        keep[0] = part(0, keep)
-        keep[1] = part(along ^ 3, keep)
-        send[0] = part(along, send)
-        send[1] = part(3, send)
+    along = 1 + (lax.axis_index("seg") & 1)
+    parts = {"kept": (0, along ^ 3), "sent": (along, 3)}
+    if which in parts:
+        into = [outs[0].at[i] for i in range(2)]
+        apart = parts[which]
     else:
-        for j in range(count):
-            outs[j][...] = part(j, outs[j])
+        into, apart = outs, range(len(outs))
+    rows = into[0].shape[0]
+    for out, j in zip(into, apart, strict=True):
+        at = pl.ds(aligned(own ^ j, rows), rows)
+        out[...] = jnp.dot(
+            x_turned[at, :], values[...], preferred_element_type=f32
+        ).astype(out.dtype)
 
 
 def out_kernel(heads, first, soft, values, *refs):
-    wo_from, (keep, *send) = refs[: -1 - PIECES], refs[-1 - PIECES :]
-    if len(wo_from) == 3:
-        wo_from, wo = wo_from[:2], wo_from[2]
-        opposite = (lax.axis_index("fsdp") ^ member_of()) == 3
-        wo[...] = jnp.where(opposite, wo_from[1][...], wo_from[0][...])
-    else:
-        wo = wo_from[0]
+    wo, keep, *send = refs
     blocks, keys, lanes = soft.shape
     queries = lanes // heads
     width = values.shape[1]
@@ -388,9 +402,8 @@
         name="split",
     )(came, far, halo)
     if crossed:
-        wqkv_parts = [
-            own_blocks, mine, swapped(other, "seg", 1), lax.ppermute(mine, both, turned)
-        ]
+        other = swapped(other, "seg", 1)
+        forwarded = lax.ppermute(mine, both, turned)
         wo_near = pl.pallas_call(
             pick_kernel,
             in_specs=[vmem] * 2,
@@ -417,55 +430,75 @@
     )(*parts)
     x_all, wo_near = lax.optimization_barrier((x_all, wo_near))
 
+    if crossed:
+        early = pl.pallas_call(
+            early_kernel,
+            in_specs=[vmem] * 4,
+            out_specs=vmem,
+            out_shape=jax.ShapeDtypeStruct((all_rows, 3 * block), f32),
+            compiler_params=params(),
+            name="early",
+        )(x_all, own_blocks, mine, other)
+        wqkv_parts = [early, forwarded]
     soft, values = pl.pallas_call(
         functools.partial(weights_kernel, heads, frame_count, segs, crossed),
-        in_specs=[vmem] * (1 + fsdp_size),
+        in_specs=[vmem] * (1 + len(wqkv_parts)),
         out_specs=[vmem] * 2,
         out_shape=[
             jax.ShapeDtypeStruct((group, keys, heads * queries), bf16),
             jax.ShapeDtypeStruct((all_rows, block), bf16),
         ],
-        scratch_shapes=[pltpu.VMEM((width, 3 * block), bf16)],
+        scratch_shapes=[] if crossed else [pltpu.VMEM((width, 3 * block), bf16)],
         compiler_params=params(),
         name="soft_weights",
     )(x_all, *wqkv_parts)
 
-    def attend(start, wo_from, name):
-        wo_shape = [jax.ShapeDtypeStruct((block, width), bf16)] * (len(wo_from) - 1)
+    values_grad_shape = jax.ShapeDtypeStruct((all_rows, block), bf16)
+    wo_from = [wo_near] + ([wo_last] if crossed else [])
+    wo_mine, values_grad = pl.pallas_call(
+        functools.partial(grad_kernel, heads, frame_count, segs),
+        in_specs=[smem] + [vmem] * (2 + len(wo_from)),
+        out_specs=[vmem] * 2,
+        out_shape=[jax.ShapeDtypeStruct((block, width), bf16), values_grad_shape],
+        scratch_shapes=[pltpu.VMEM((all_rows, block), f32)],
+        compiler_params=params(),
+        name="values_grad",
+    )(lengths, u_all, soft, *wo_from)
+
+    def grad_rows(which, shapes):
+        return pl.pallas_call(
+            functools.partial(rows_kernel, which),
+            in_specs=[vmem] * 2,
+            out_specs=[vmem] * len(shapes),
+            out_shape=shapes,
+            compiler_params=params(),
+            name="grad_rows_" + which,
+        )(x_turned, values_grad)
+
+    if crossed:
+        (sent,) = grad_rows("sent", [jax.ShapeDtypeStruct((2, rows, block), bf16)])
+        (kept,) = grad_rows("kept", [jax.ShapeDtypeStruct((2, rows, block), f32)])
+    else:
+        grad_chunks = grad_rows(
+            "all", [jax.ShapeDtypeStruct((rows, block), bf16)] * fsdp_size
+        )
+
+    def attend(start, name):
         cut = queries // PIECES // 16 * 16
         sizes = [cut] * (PIECES - 1) + [queries - cut * (PIECES - 1)]
-        outs = pl.pallas_call(
+        keep, *send = pl.pallas_call(
             functools.partial(out_kernel, heads, start),
-            in_specs=[vmem] * (2 + len(wo_from)),
-            out_specs=[vmem] * (len(wo_shape) + 1 + PIECES),
-            out_shape=wo_shape
-            + [jax.ShapeDtypeStruct((queries, width), f32)]
+            in_specs=[vmem] * 3,
+            out_specs=[vmem] * (1 + PIECES),
+            out_shape=[jax.ShapeDtypeStruct((queries, width), f32)]
             + [jax.ShapeDtypeStruct((size, width), bf16) for size in sizes],
             compiler_params=params(),
             name=name,
-        )(soft, values, *wo_from)
-        return outs[: len(wo_shape)], outs[len(wo_shape)], outs[len(wo_shape) + 1 :]
-
-    picked, keep_far, send_far = attend(2, [wo_near] + ([wo_last] if crossed else []), "attend_far")
-    wo_mine = picked[0] if crossed else wo_near
-    if crossed:
-        grad_shapes = [jax.ShapeDtypeStruct((2, rows, block), dtype) for dtype in (f32, bf16)]
-    else:
-        grad_shapes = [jax.ShapeDtypeStruct((rows, block), bf16)] * fsdp_size
-    grad_chunks = pl.pallas_call(
-        functools.partial(grad_kernel, fsdp_size, heads, frame_count, segs, crossed),
-        in_specs=[smem] + [vmem] * 4,
-        out_specs=[vmem] * len(grad_shapes),
-        out_shape=grad_shapes,
-        scratch_shapes=[
-            pltpu.VMEM((all_rows, block), f32),
-            pltpu.VMEM((width, block), f32),
-        ],
-        compiler_params=params(),
-        name="value_grad",
-    )(lengths, x_turned, u_all, soft, wo_mine)
-
-    _, keep, send = attend(0, [wo_mine], "attend_near")
+        )(soft, values, wo_mine)
+        return keep, send
+
+    keep_far, send_far = attend(2, "attend_far")
+    keep, send = attend(0, "attend_near")
     near = [swapped(piece, "seg", 1) for piece in send]
     near_far = [swapped(piece, "seg", 1) for piece in send_far]
     onward = pl.pallas_call(
@@ -477,7 +510,6 @@
         name="onward",
     )(keep_far, *near_far)
     if crossed:
-        kept, sent = grad_chunks
         came = lax.ppermute(sent, both, straight)
         passing = (kept[1] + came[1].astype(f32)).astype(bf16)
         passing, onward = lax.optimization_barrier((passing, onward))

time: 65.2 us -> 63.6 us (0.975)
  waiting for transfers between devices: 29.1 us -> 27 us
    pallas_call x1 -> x4, Pallas kernels: 1.99 us -> 3.02 us  [the longest x1 1.39 us: on_device(): pl.pallas_call(functools.partial(grad_kernel, heads, frame_count, segs),...]
    ppermute x1, waiting for transfers between devices: 2.86 us -> 1.94 us  [on_device(): forwarded = lax.ppermute(mine, both, turned)]
    ppermute x1, waiting for transfers between devices: 2.71 us -> 1.92 us  [on_device(): came = lax.ppermute(sent, both, straight)]
  transfers between devices with their start and end apart: 21 -> 21, of which waited for: 10 -> 10; matrix products, arithmetic and copies ran while one was open for 1% -> 1% of each run, Pallas kernels for 7% -> 9%
where the time goes in v5:
time: 63.6 us; the launch traced here: 63.3 us
  waiting for transfers between devices  27 us (42%)
  starting transfers between devices  22.8 us (36%)
  Pallas kernels  10.9 us (17%)
  between operations  1.55 us (2%)
  other arithmetic  0.95 us (1%)
    ppermute x14, starting transfers between devices, swapped(): return lax.ppermute(array, axis, [(i, i ^ bit) for i in range(size)])  12.7 us
    ppermute x1, waiting for transfers between devices, on_device(): wo_came = lax.ppermute(w_out, both, first)  11.6 us
    ppermute x14, waiting for transfers between devices, swapped(): return lax.ppermute(array, axis, [(i, i ^ bit) for i in range(size)])  8.01 us
    ppermute x1, waiting for transfers between devices, on_device(): last = lax.ppermute(passing, both, turned)  3.57 us
    ppermute x1, starting transfers between devices, on_device(): came = lax.ppermute(sent, both, straight)  2.81 us
    pallas_call x1, Pallas kernels, on_device(): pl.pallas_call(functools.partial(pack_kernel, frame_count), in_specs=[hbm...  2.57 us
    ppermute x1, starting transfers between devices, on_device(): came = lax.ppermute(own_blocks, both, straight)  2.56 us
    ppermute x1, starting transfers between devices, on_device(): wo_came = lax.ppermute(w_out, both, first)  2.43 us
  transfers between devices with their start and end apart: 21, of which 10 were waited for; matrix products, arithmetic and copies ran while one was open for 1% of the time, Pallas kernels for 9%

profile of v5, /device:TPU:0, one launch (start us, length us, event | category | flops | bytes accessed | tf_op | source)
XLA Modules:
  0.0 63.3 jit_solution(7196098690030746110)
XLA Ops:
  0.6 2.6 %pack.1 = (bf16[2,256,768]{2,1,0:T(8,128)(2,1)}, bf16[288,1024]{1,0:T(8,128)(2,1)}) custom-call(bf16[256,1024]{1,0:T(8,128)(2,1)} %wq.1, bf16[256,1024]{1,0:T(8,128)(2,1)} %wk.1, bf16[256,1024]{1,0:T(8,128)(2,1)} %wv.1, bf16[128,1024]{1,0:T(8,128)(2,1)} %bitcast.15, bf16[128,1024]{1,0:T(8,128)(2,1)} %bitcast.17, bf16[8,1024]{1,0:T(8,128)(2,1)} %bitcast.18, ...), custom_call_target="tpu_custom_call" | custom-call | tf_op jit(solution)/shard_map/pack/pallas_call | solution.py:347
  3.2 0.5 collective-permute-start.2
  3.7 2.6 %collective-permute-start = (bf16[2,256,768]{2,1,0:T(8,128)(2,1)}, bf16[2,256,768]{2,1,0:T(8,128)(2,1)S(1)}, u32[]{:S(2)}, u32[]{:S(2)}) collective-permute-start(bf16[2,256,768]{2,1,0:T(8,128)(2,1)} %get-tuple-element.42.mine), channel_id=1, source_target_pairs={{0,1},{1,0},{2,3},{3,2},{4,6},{5,7},{6,4},{7,5},{8,9},{9,8},{10,11... | collective-permute-start | bytes 2359304 | tf_op jit(solution)/shard_map/ppermute | solution.py:381
  6.3 1.6 %collective-permute-start.1 = (bf16[288,1024]{1,0:T(8,128)(2,1)}, bf16[288,1024]{1,0:T(8,128)(2,1)S(1)}, u32[]{:S(2)}, u32[]{:S(2)}) collective-permute-start(bf16[288,1024]{1,0:T(8,128)(2,1)} %get-tuple-element.40.tokens), channel_id=1, source_target_pairs={{0,8},{4,12},{8,0},{12,4},{16,24},{20,28},{24,16},{28,20},{1,9},{5... | collective-permute-start | bytes 1769480 | tf_op jit(solution)/shard_map/ppermute | solution.py:35
  7.9 2.4 %collective-permute-start.4 = (bf16[256,1024]{1,0:T(8,128)(2,1)S(1)}, bf16[256,1024]{1,0:T(8,128)(2,1)S(1)}, u32[]{:S(2)}, u32[]{:S(2)}) collective-permute-start(bf16[256,1024]{1,0:T(8,128)(2,1)S(1)} %copy-done.3), channel_id=1, source_target_pairs={{0,1},{4,2},{12,15},{5,4},{1,7},{9,10},{10,11},{14,8},{6,5},{15,14... | collective-permute-start | bytes 1572872 | tf_op jit(solution)/shard_map/ppermute | solution.py:382
  10.3 0.9 %slice_select_fusion = bf16[32,1024]{1,0:T(8,128)(2,1)S(1)} fusion(bf16[288,1024]{1,0:T(8,128)(2,1)S(1)} %collective-permute-done.2.near, bf16[288,1024]{1,0:T(8,128)(2,1)} %get-tuple-element.40.tokens, pred[]{:T(512)S(6)} %eq.5), kind=kLoop, calls=%fused_computation.8 | loop fusion | flops 32768 | bytes 196609 | tf_op jit(solution)/shard_map/jit(_where)/select_n | solution.py:373
  11.2 0.8 %collective-permute-start.3 = (bf16[32,1024]{1,0:T(8,128)(2,1)S(1)}, bf16[32,1024]{1,0:T(8,128)(2,1)S(1)}, u32[]{:S(2)}, u32[]{:S(2)}) collective-permute-start(bf16[32,1024]{1,0:T(8,128)(2,1)S(1)} %slice_select_fusion), channel_id=1, source_target_pairs={{12,16},{8,24},{13,17},{9,25},{14,18},{10,26},{15,19},{11,27}} | collective-permute-start | bytes 196616 | tf_op jit(solution)/shard_map/ppermute | solution.py:377
  12.0 11.6 %collective-permute-done.4.came = bf16[256,1024]{1,0:T(8,128)(2,1)S(1)} collective-permute-done((bf16[256,1024]{1,0:T(8,128)(2,1)S(1)}, bf16[256,1024]{1,0:T(8,128)(2,1)S(1)}, u32[]{:S(2)}, u32[]{:S(2)}) %collective-permute-start.4) | collective-permute-done | bytes 524320 | tf_op jit(solution)/shard_map/ppermute | solution.py:382
  23.6 1.3 %collective-permute-start.9 = (bf16[256,1024]{1,0:T(8,128)(2,1)S(1)}, bf16[256,1024]{1,0:T(8,128)(2,1)S(1)}, u32[]{:S(2)}, u32[]{:S(2)}) collective-permute-start(bf16[256,1024]{1,0:T(8,128)(2,1)S(1)} %collective-permute-done.4.came), channel_id=1, source_target_pairs={{15,3},{10,6},{5,9},{0,12},{31,19},{26,22},{21,25},{16,28}} | collective-permute-start | bytes 1572872 | tf_op jit(solution)/shard_map/ppermute | solution.py:386
  25.2 2.5 %collective-permute-start.5 = (bf16[176,1024]{1,0:T(8,128)(2,1)S(1)}, bf16[176,1024]{1,0:T(8,128)(2,1)S(1)}, u32[]{:S(2)}, u32[]{:S(2)}) collective-permute-start(bf16[176,1024]{1,0:T(8,128)(2,1)S(1)} %get-tuple-element.48.far), channel_id=1, source_target_pairs={{0,4},{4,0},{8,12},{12,8},{16,20},{20,16},{24,28},{28,24},{1,5},{5... | collective-permute-start | bytes 1081352 | tf_op jit(solution)/shard_map/ppermute | solution.py:35
  28.5 1.0 %collective-permute-done.6.last_grads = bf16[144,1024]{1,0:T(8,128)(2,1)S(1)} collective-permute-done((bf16[144,1024]{1,0:T(8,128)(2,1)S(1)}, bf16[144,1024]{1,0:T(8,128)(2,1)S(1)}, u32[]{:S(2)}, u32[]{:S(2)}) %collective-permute-start.6) | collective-permute-done | bytes 294944 | tf_op jit(solution)/shard_map/ppermute | solution.py:35
  29.4 0.6 %merge.1 = (bf16[608,1024]{1,0:T(8,128)(2,1)S(1)}, bf16[1024,608]{1,0:T(8,128)(2,1)S(1)}, bf16[576,1024]{1,0:T(8,128)(2,1)S(1)}) custom-call(bf16[288,1024]{1,0:T(8,128)(2,1)S(1)} %copy-done.2, bf16[288,1024]{1,0:T(8,128)(2,1)S(1)} %collective-permute-done.2.near, bf16[176,1024]{1,0:T(8,128)(2,1)S(1)} %get-tuple-element.48.far, ...), custom_call_target="tpu_custom_call" | custom-call | tf_op jit(solution)/shard_map/merge/pallas_call | solution.py:419
  30.1 0.9 %early.1.refs_0_ = f32[608,768]{1,0:T(8,128)S(1)} custom-call(bf16[608,1024]{1,0:T(8,128)(2,1)S(1)} %get-tuple-element.52.x_all, bf16[2,256,768]{2,1,0:T(8,128)(2,1)S(1)} %copy-done.1, bf16[256,768]{1,0:T(8,128)(2,1)S(1)} %get-tuple-element.53.beside, bf16[256,768]{1,0:T(8,128)(2,1)S(1)} %collective-permute-done.7.swapped_in), custom_call_target="tpu_custom_call" | custom-call | tf_op jit(solution)/shard_map/early/pallas_call | solution.py:434
  31.0 1.9 %collective-permute-done.8.refs_1_ = bf16[256,768]{1,0:T(8,128)(2,1)S(1)} collective-permute-done((bf16[256,768]{1,0:T(8,128)(2,1)S(1)}, bf16[256,768]{1,0:T(8,128)(2,1)S(1)}, u32[]{:S(2)}, u32[]{:S(2)}) %collective-permute-start.8) | collective-permute-done | bytes 393248 | tf_op jit(solution)/shard_map/ppermute | solution.py:406
  33.0 1.2 %soft_weights.1 = (bf16[4,176,576]{2,1,0:T(8,128)(2,1)S(1)}, bf16[608,256]{1,0:T(8,128)(2,1)S(1)}) custom-call(bf16[608,1024]{1,0:T(8,128)(2,1)S(1)} %get-tuple-element.52.x_all, f32[608,768]{1,0:T(8,128)S(1)} %early.1.refs_0_, bf16[256,768]{1,0:T(8,128)(2,1)S(1)} %collective-permute-done.8.refs_1_), custom_call_target="tpu_custom_call" | custom-call | tf_op jit(solution)/shard_map/soft_weights/pallas_call | solution.py:443
  34.1 1.4 %values_grad.1 = (bf16[256,1024]{1,0:T(8,128)(2,1)S(1)}, bf16[608,256]{1,0:T(8,128)(2,1)S(1)}) custom-call(s32[1]{0:T(128)S(6)} %copy.13.lengths, bf16[576,1024]{1,0:T(8,128)(2,1)S(1)} %get-tuple-element.57.u_all, bf16[4,176,576]{2,1,0:T(8,128)(2,1)S(1)} %get-tuple-element.55.soft, bf16[256,1024]{1,0:T(8,128)(2,1)S(1)} %pick.1.refs_0_, ...), custom_call_target="tpu_custom_call" | custom-call | tf_op jit(solution)/shard_map/values_grad/pallas_call | solution.py:458
  35.9 2.8 %collective-permute-start.10 = (bf16[2,256,256]{2,1,0:T(8,128)(2,1)S(1)}, bf16[2,256,256]{2,1,0:T(8,128)(2,1)S(1)}, u32[]{:S(2)}, u32[]{:S(2)}) collective-permute-start(bf16[2,256,256]{2,1,0:T(8,128)(2,1)S(1)} %grad_rows_sent.1), channel_id=1, source_target_pairs={{0,1},{1,0},{2,3},{3,2},{4,6},{5,7},{6,4},{7,5},{8,9},{9,8},{10,11... | collective-permute-start | bytes 786440 | tf_op jit(solution)/shard_map/ppermute | solution.py:513
  38.7 0.7 %attend_far.1 = (f32[144,1024]{1,0:T(8,128)S(1)}, bf16[64,1024]{1,0:T(8,128)(2,1)S(1)}, bf16[80,1024]{1,0:T(8,128)(2,1)S(1)}) custom-call(bf16[4,176,576]{2,1,0:T(8,128)(2,1)S(1)} %get-tuple-element.55.soft, bf16[608,256]{1,0:T(8,128)(2,1)S(1)} %get-tuple-element.56.values, bf16[256,1024]{1,0:T(8,128)(2,1)S(1)} %get-tuple-element.59.refs_0_), custom_call_target="tpu_custom_call" | custom-call | tf_op jit(solution)/shard_map/attend_far/pallas_call | solution.py:489
  39.5 0.5 collective-permute-start.11
  40.4 0.7 %collective-permute-done.11.refs_0_ = bf16[64,1024]{1,0:T(8,128)(2,1)S(1)} collective-permute-done((bf16[64,1024]{1,0:T(8,128)(2,1)S(1)}, bf16[64,1024]{1,0:T(8,128)(2,1)S(1)}, u32[]{:S(2)}, u32[]{:S(2)}) %collective-permute-start.11) | collective-permute-done | bytes 131104 | tf_op jit(solution)/shard_map/ppermute | solution.py:35
  41.2 1.9 %collective-permute-done.10 = bf16[2,256,256]{2,1,0:T(8,128)(2,1)S(1)} collective-permute-done((bf16[2,256,256]{2,1,0:T(8,128)(2,1)S(1)}, bf16[2,256,256]{2,1,0:T(8,128)(2,1)S(1)}, u32[]{:S(2)}, u32[]{:S(2)}) %collective-permute-start.10) | collective-permute-done | bytes 262176 | tf_op jit(solution)/shard_map/ppermute | solution.py:513
  43.2 1.4 %collective-permute-start.15 = (bf16[144,1024]{1,0:T(8,128)(2,1)S(1)}, bf16[144,1024]{1,0:T(8,128)(2,1)S(1)}, u32[]{:S(2)}, u32[]{:S(2)}) collective-permute-start(bf16[144,1024]{1,0:T(8,128)(2,1)S(1)} %onward.1), channel_id=1, source_target_pairs={{0,8},{4,12},{8,0},{12,4},{16,24},{20,28},{24,16},{28,20},{1,9},{5... | collective-permute-start | bytes 884744 | tf_op jit(solution)/shard_map/ppermute | solution.py:35
  44.6 3.6 %collective-permute-done.13 = bf16[256,256]{1,0:T(8,128)(2,1)S(1)} collective-permute-done((bf16[256,256]{1,0:T(8,128)(2,1)S(1)}, bf16[256,256]{1,0:T(8,128)(2,1)S(1)}, u32[]{:S(2)}, u32[]{:S(2)}) %collective-permute-start.13) | collective-permute-done | bytes 131104 | tf_op jit(solution)/shard_map/ppermute | solution.py:516
  48.2 2.7 %collective-permute-start.14 = (bf16[256,256]{1,0:T(8,128)(2,1)S(1)}, bf16[256,256]{1,0:T(8,128)(2,1)S(1)}, u32[]{:S(2)}, u32[]{:S(2)}) collective-permute-start(bf16[256,256]{1,0:T(8,128)(2,1)S(1)} %fusion.3), channel_id=1, source_target_pairs={{0,16},{4,20},{8,24},{12,28},{16,0},{20,4},{24,8},{28,12},{1,17},{... | collective-permute-start | bytes 393224 | tf_op jit(solution)/shard_map/ppermute | solution.py:35
  50.9 0.7 %attend_near.1 = (f32[144,1024]{1,0:T(8,128)S(1)}, bf16[64,1024]{1,0:T(8,128)(2,1)S(1)}, bf16[80,1024]{1,0:T(8,128)(2,1)S(1)}) custom-call(bf16[4,176,576]{2,1,0:T(8,128)(2,1)S(1)} %get-tuple-element.55.soft, bf16[608,256]{1,0:T(8,128)(2,1)S(1)} %get-tuple-element.56.values, bf16[256,1024]{1,0:T(8,128)(2,1)S(1)} %get-tuple-element.59.refs_0_), custom_call_target="tpu_custom_call" | custom-call | tf_op jit(solution)/shard_map/attend_near/pallas_call | solution.py:489
  51.7 0.5 collective-permute-start.16
  52.2 2.8 %collective-permute-done.14 = bf16[256,256]{1,0:T(8,128)(2,1)S(1)} collective-permute-done((bf16[256,256]{1,0:T(8,128)(2,1)S(1)}, bf16[256,256]{1,0:T(8,128)(2,1)S(1)}, u32[]{:S(2)}, u32[]{:S(2)}) %collective-permute-start.14) | collective-permute-done | bytes 131104 | tf_op jit(solution)/shard_map/ppermute | solution.py:35
  55.1 2.9 %collective-permute-start.18 = (bf16[256,256]{1,0:T(8,128)(2,1)S(1)}, bf16[256,256]{1,0:T(8,128)(2,1)S(1)}, u32[]{:S(2)}, u32[]{:S(2)}) collective-permute-start(bf16[256,256]{1,0:T(8,128)(2,1)S(1)} %add_convert_fusion.mine), channel_id=1, source_target_pairs={{0,8},{4,12},{8,0},{12,4},{16,24},{20,28},{24,16},{28,20},{1,9},{5... | collective-permute-start | bytes 393224 | tf_op jit(solution)/shard_map/ppermute | solution.py:35
  58.0 2.9 %collective-permute-done.18.far = bf16[256,256]{1,0:T(8,128)(2,1)S(1)} collective-permute-done((bf16[256,256]{1,0:T(8,128)(2,1)S(1)}, bf16[256,256]{1,0:T(8,128)(2,1)S(1)}, u32[]{:S(2)}, u32[]{:S(2)}) %collective-permute-start.18) | collective-permute-done | bytes 131104 | tf_op jit(solution)/shard_map/ppermute | solution.py:35
  60.9 0.8 %finish.1 = (bf16[128,1024]{1,0:T(8,128)(2,1)}, bf16[8,1024]{1,0:T(8,128)(2,1)}) custom-call(s32[1]{0:T(128)S(6)} %copy.13.lengths, bf16[128,1024]{1,0:T(8,128)(2,1)S(1)} %bitcast.16, f32[144,1024]{1,0:T(8,128)S(1)} %get-tuple-element.60.keep, bf16[144,1024]{1,0:T(8,128)(2,1)S(1)} %collective-permute-done.15.back, ...), custom_call_target="tpu_custom_call" | custom-call | tf_op jit(solution)/shard_map/finish/pallas_call | solution.py:531
  61.8 0.5 collective-permute-done.20.near_far
  62.2 1.1 %columns.1 = f32[256,1024]{1,0:T(8,128)} custom-call(bf16[256,256]{1,0:T(8,128)(2,1)S(1)} %add_convert_fusion.mine, bf16[256,256]{1,0:T(8,128)(2,1)S(1)} %collective-permute-done.18.far, bf16[256,256]{1,0:T(8,128)(2,1)S(1)} %collective-permute-done.19.near_mine, bf16[256,256]{1,0:T(8,128)(2,1)S(1)} %collective-permute-done.20.near_far), custom_call_target="tpu_custom_call" | custom-call | tf_op jit(solution)/shard_map/columns/pallas_call | solution.py:543
  (36 shorter events, 1.5 us)
Async XLA Ops:
  0.6 7.2 %copy-start.3 = (bf16[256,1024]{1,0:T(8,128)(2,1)S(1)}, bf16[256,1024]{1,0:T(8,128)(2,1)}, u32[]{:S(2)}) copy-start(bf16[256,1024]{1,0:T(8,128)(2,1)} %own) | copy-start | bytes 1572868
  3.2 7.1 %collective-permute-start.2 = (bf16[288,1024]{1,0:T(8,128)(2,1)}, bf16[288,1024]{1,0:T(8,128)(2,1)S(1)}, u32[]{:S(2)}, u32[]{:S(2)}) collective-permute-start(bf16[288,1024]{1,0:T(8,128)(2,1)} %get-tuple-element.40.tokens), channel_id=1, source_target_pairs={{0,4},{4,0},{8,12},{12,8},{16,20},{20,16},{24,28},{28,24},{1,5},{5... | collective-permute-start | bytes 1769480 | tf_op jit(solution)/shard_map/ppermute | solution.py:35
  3.7 19.9 %collective-permute-start = (bf16[2,256,768]{2,1,0:T(8,128)(2,1)}, bf16[2,256,768]{2,1,0:T(8,128)(2,1)S(1)}, u32[]{:S(2)}, u32[]{:S(2)}) collective-permute-start(bf16[2,256,768]{2,1,0:T(8,128)(2,1)} %get-tuple-element.42.mine), channel_id=1, source_target_pairs={{0,1},{1,0},{2,3},{3,2},{4,6},{5,7},{6,4},{7,5},{8,9},{9,8},{10,11... | collective-permute-start | bytes 2359304 | tf_op jit(solution)/shard_map/ppermute | solution.py:381
  6.3 17.3 %collective-permute-start.1 = (bf16[288,1024]{1,0:T(8,128)(2,1)}, bf16[288,1024]{1,0:T(8,128)(2,1)S(1)}, u32[]{:S(2)}, u32[]{:S(2)}) collective-permute-start(bf16[288,1024]{1,0:T(8,128)(2,1)} %get-tuple-element.40.tokens), channel_id=1, source_target_pairs={{0,8},{4,12},{8,0},{12,4},{16,24},{20,28},{24,16},{28,20},{1,9},{5... | collective-permute-start | bytes 1769480 | tf_op jit(solution)/shard_map/ppermute | solution.py:35
  7.9 15.7 %collective-permute-start.4 = (bf16[256,1024]{1,0:T(8,128)(2,1)S(1)}, bf16[256,1024]{1,0:T(8,128)(2,1)S(1)}, u32[]{:S(2)}, u32[]{:S(2)}) collective-permute-start(bf16[256,1024]{1,0:T(8,128)(2,1)S(1)} %copy-done.3), channel_id=1, source_target_pairs={{0,1},{4,2},{12,15},{5,4},{1,7},{9,10},{10,11},{14,8},{6,5},{15,14... | collective-permute-start | bytes 1572872 | tf_op jit(solution)/shard_map/ppermute | solution.py:382
  11.2 18.2 %copy-start.2 = (bf16[288,1024]{1,0:T(8,128)(2,1)S(1)}, bf16[288,1024]{1,0:T(8,128)(2,1)}, u32[]{:S(2)}) copy-start(bf16[288,1024]{1,0:T(8,128)(2,1)} %get-tuple-element.40.tokens) | copy-start | bytes 1769476
  11.2 12.4 %collective-permute-start.3 = (bf16[32,1024]{1,0:T(8,128)(2,1)S(1)}, bf16[32,1024]{1,0:T(8,128)(2,1)S(1)}, u32[]{:S(2)}, u32[]{:S(2)}) collective-permute-start(bf16[32,1024]{1,0:T(8,128)(2,1)S(1)} %slice_select_fusion), channel_id=1, source_target_pairs={{12,16},{8,24},{13,17},{9,25},{14,18},{10,26},{15,19},{11,27}} | collective-permute-start | bytes 196616 | tf_op jit(solution)/shard_map/ppermute | solution.py:377
  23.6 10.5 %collective-permute-start.9 = (bf16[256,1024]{1,0:T(8,128)(2,1)S(1)}, bf16[256,1024]{1,0:T(8,128)(2,1)S(1)}, u32[]{:S(2)}, u32[]{:S(2)}) collective-permute-start(bf16[256,1024]{1,0:T(8,128)(2,1)S(1)} %collective-permute-done.4.came), channel_id=1, source_target_pairs={{15,3},{10,6},{5,9},{0,12},{31,19},{26,22},{21,25},{16,28}} | collective-permute-start | bytes 1572872 | tf_op jit(solution)/shard_map/ppermute | solution.py:386
  25.0 5.1 %collective-permute-start.7 = (bf16[256,768]{1,0:T(8,128)(2,1)S(1)}, bf16[256,768]{1,0:T(8,128)(2,1)S(1)}, u32[]{:S(2)}, u32[]{:S(2)}) collective-permute-start(bf16[256,768]{1,0:T(8,128)(2,1)S(1)} %get-tuple-element.54), channel_id=1, source_target_pairs={{0,4},{4,0},{8,12},{12,8},{16,20},{20,16},{24,28},{28,24},{1,5},{5... | collective-permute-start | bytes 1179656 | tf_op jit(solution)/shard_map/ppermute | solution.py:35
  25.1 7.8 %collective-permute-start.8 = (bf16[256,768]{1,0:T(8,128)(2,1)S(1)}, bf16[256,768]{1,0:T(8,128)(2,1)S(1)}, u32[]{:S(2)}, u32[]{:S(2)}) collective-permute-start(bf16[256,768]{1,0:T(8,128)(2,1)S(1)} %get-tuple-element.53.beside), channel_id=1, source_target_pairs={{0,2},{1,3},{2,0},{3,1},{4,5},{5,4},{6,7},{7,6},{8,10},{9,11},{10,... | collective-permute-start | bytes 1179656 | tf_op jit(solution)/shard_map/ppermute | solution.py:406
  25.2 4.3 %collective-permute-start.5 = (bf16[176,1024]{1,0:T(8,128)(2,1)S(1)}, bf16[176,1024]{1,0:T(8,128)(2,1)S(1)}, u32[]{:S(2)}, u32[]{:S(2)}) collective-permute-start(bf16[176,1024]{1,0:T(8,128)(2,1)S(1)} %get-tuple-element.48.far), channel_id=1, source_target_pairs={{0,4},{4,0},{8,12},{12,8},{16,20},{20,16},{24,28},{28,24},{1,5},{5... | collective-permute-start | bytes 1081352 | tf_op jit(solution)/shard_map/ppermute | solution.py:35
  27.7 1.7 %collective-permute-start.6 = (bf16[144,1024]{1,0:T(8,128)(2,1)S(1)}, bf16[144,1024]{1,0:T(8,128)(2,1)S(1)}, u32[]{:S(2)}, u32[]{:S(2)}) collective-permute-start(bf16[144,1024]{1,0:T(8,128)(2,1)S(1)} %get-tuple-element.49.far_grads), channel_id=1, source_target_pairs={{0,4},{4,0},{8,12},{12,8},{16,20},{20,16},{24,28},{28,24},{1,5},{5... | collective-permute-start | bytes 884744 | tf_op jit(solution)/shard_map/ppermute | solution.py:35
  28.4 1.7 %copy-start.1 = (bf16[2,256,768]{2,1,0:T(8,128)(2,1)S(1)}, bf16[2,256,768]{2,1,0:T(8,128)(2,1)}, u32[]{:S(2)}) copy-start(bf16[2,256,768]{2,1,0:T(8,128)(2,1)} %get-tuple-element.42.mine) | copy-start | bytes 2359300
  35.9 7.2 %collective-permute-start.10 = (bf16[2,256,256]{2,1,0:T(8,128)(2,1)S(1)}, bf16[2,256,256]{2,1,0:T(8,128)(2,1)S(1)}, u32[]{:S(2)}, u32[]{:S(2)}) collective-permute-start(bf16[2,256,256]{2,1,0:T(8,128)(2,1)S(1)} %grad_rows_sent.1), channel_id=1, source_target_pairs={{0,1},{1,0},{2,3},{3,2},{4,6},{5,7},{6,4},{7,5},{8,9},{9,8},{10,11... | collective-permute-start | bytes 786440 | tf_op jit(solution)/shard_map/ppermute | solution.py:513
  39.5 1.7 %collective-permute-start.12 = (bf16[80,1024]{1,0:T(8,128)(2,1)S(1)}, bf16[80,1024]{1,0:T(8,128)(2,1)S(1)}, u32[]{:S(2)}, u32[]{:S(2)}) collective-permute-start(bf16[80,1024]{1,0:T(8,128)(2,1)S(1)} %get-tuple-element.65), channel_id=1, source_target_pairs={{0,4},{4,0},{8,12},{12,8},{16,20},{20,16},{24,28},{28,24},{1,5},{5... | collective-permute-start | bytes 491528 | tf_op jit(solution)/shard_map/ppermute | solution.py:35
  39.5 1.6 %collective-permute-start.11 = (bf16[64,1024]{1,0:T(8,128)(2,1)S(1)}, bf16[64,1024]{1,0:T(8,128)(2,1)S(1)}, u32[]{:S(2)}, u32[]{:S(2)}) collective-permute-start(bf16[64,1024]{1,0:T(8,128)(2,1)S(1)} %get-tuple-element.64), channel_id=1, source_target_pairs={{0,4},{4,0},{8,12},{12,8},{16,20},{20,16},{24,28},{28,24},{1,5},{5... | collective-permute-start | bytes 393224 | tf_op jit(solution)/shard_map/ppermute | solution.py:35
  43.1 17.8 %copy-start = (bf16[1,8,16,1024]{3,2,1,0:T(8,128)(2,1)S(1)}, bf16[1,8,16,1024]{3,2,1,0:T(8,128)(2,1)}, u32[]{:S(2)}) copy-start(bf16[1,8,16,1024]{3,2,1,0:T(8,128)(2,1)} %param.10) | copy-start | bytes 786436
  43.1 5.0 %collective-permute-start.13 = (bf16[256,256]{1,0:T(8,128)(2,1)S(1)}, bf16[256,256]{1,0:T(8,128)(2,1)S(1)}, u32[]{:S(2)}, u32[]{:S(2)}) collective-permute-start(bf16[256,256]{1,0:T(8,128)(2,1)S(1)} %fusion.4), channel_id=1, source_target_pairs={{0,2},{1,3},{2,0},{3,1},{4,5},{5,4},{6,7},{7,6},{8,10},{9,11},{10,... | collective-permute-start | bytes 393224 | tf_op jit(solution)/shard_map/ppermute | solution.py:516
  43.2 11.8 %collective-permute-start.15 = (bf16[144,1024]{1,0:T(8,128)(2,1)S(1)}, bf16[144,1024]{1,0:T(8,128)(2,1)S(1)}, u32[]{:S(2)}, u32[]{:S(2)}) collective-permute-start(bf16[144,1024]{1,0:T(8,128)(2,1)S(1)} %onward.1), channel_id=1, source_target_pairs={{0,8},{4,12},{8,0},{12,4},{16,24},{20,28},{24,16},{28,20},{1,9},{5... | collective-permute-start | bytes 884744 | tf_op jit(solution)/shard_map/ppermute | solution.py:35
  48.2 6.7 %collective-permute-start.14 = (bf16[256,256]{1,0:T(8,128)(2,1)S(1)}, bf16[256,256]{1,0:T(8,128)(2,1)S(1)}, u32[]{:S(2)}, u32[]{:S(2)}) collective-permute-start(bf16[256,256]{1,0:T(8,128)(2,1)S(1)} %fusion.3), channel_id=1, source_target_pairs={{0,16},{4,20},{8,24},{12,28},{16,0},{20,4},{24,8},{28,12},{1,17},{... | collective-permute-start | bytes 393224 | tf_op jit(solution)/shard_map/ppermute | solution.py:35
  51.6 3.5 %collective-permute-start.17 = (bf16[80,1024]{1,0:T(8,128)(2,1)S(1)}, bf16[80,1024]{1,0:T(8,128)(2,1)S(1)}, u32[]{:S(2)}, u32[]{:S(2)}) collective-permute-start(bf16[80,1024]{1,0:T(8,128)(2,1)S(1)} %get-tuple-element.71), channel_id=1, source_target_pairs={{0,4},{4,0},{8,12},{12,8},{16,20},{20,16},{24,28},{28,24},{1,5},{5... | collective-permute-start | bytes 491528 | tf_op jit(solution)/shard_map/ppermute | solution.py:35
  51.7 3.4 %collective-permute-start.16 = (bf16[64,1024]{1,0:T(8,128)(2,1)S(1)}, bf16[64,1024]{1,0:T(8,128)(2,1)S(1)}, u32[]{:S(2)}, u32[]{:S(2)}) collective-permute-start(bf16[64,1024]{1,0:T(8,128)(2,1)S(1)} %get-tuple-element.70), channel_id=1, source_target_pairs={{0,4},{4,0},{8,12},{12,8},{16,20},{20,16},{24,28},{28,24},{1,5},{5... | collective-permute-start | bytes 393224 | tf_op jit(solution)/shard_map/ppermute | solution.py:35
  55.1 5.8 %collective-permute-start.18 = (bf16[256,256]{1,0:T(8,128)(2,1)S(1)}, bf16[256,256]{1,0:T(8,128)(2,1)S(1)}, u32[]{:S(2)}, u32[]{:S(2)}) collective-permute-start(bf16[256,256]{1,0:T(8,128)(2,1)S(1)} %add_convert_fusion.mine), channel_id=1, source_target_pairs={{0,8},{4,12},{8,0},{12,4},{16,24},{20,28},{24,16},{28,20},{1,9},{5... | collective-permute-start | bytes 393224 | tf_op jit(solution)/shard_map/ppermute | solution.py:35
  58.0 3.8 %collective-permute-start.19 = (bf16[256,256]{1,0:T(8,128)(2,1)S(1)}, bf16[256,256]{1,0:T(8,128)(2,1)S(1)}, u32[]{:S(2)}, u32[]{:S(2)}) collective-permute-start(bf16[256,256]{1,0:T(8,128)(2,1)S(1)} %add_convert_fusion.mine), channel_id=1, source_target_pairs={{0,4},{4,0},{8,12},{12,8},{16,20},{20,16},{24,28},{28,24},{1,5},{5... | collective-permute-start | bytes 393224 | tf_op jit(solution)/shard_map/ppermute | solution.py:35
  60.9 1.3 %collective-permute-start.20 = (bf16[256,256]{1,0:T(8,128)(2,1)S(1)}, bf16[256,256]{1,0:T(8,128)(2,1)S(1)}, u32[]{:S(2)}, u32[]{:S(2)}) collective-permute-start(bf16[256,256]{1,0:T(8,128)(2,1)S(1)} %collective-permute-done.18.far), channel_id=1, source_target_pairs={{0,4},{4,0},{8,12},{12,8},{16,20},{20,16},{24,28},{28,24},{1,5},{5... | collective-permute-start | bytes 393224 | tf_op jit(solution)/shard_map/ppermute | solution.py:35

commit v6 on v5

--- a/solution.py
+++ b/solution.py
@@ -55,7 +55,7 @@
 
 
 def pack_kernel(frame_count, wq, wk, wv, frames, gf, mem, gm, gain, *refs):
-    blocks, tokens, raw, few, one, sems = refs
+    blocks, tokens, tail, raw, few, one, sems = refs
     width = blocks.shape[2] // 3
     rows, model_width = gf.shape
     segs = mem.shape[0]
@@ -84,16 +84,19 @@
         [few[0], (summary / frame_count).astype(bf16)], axis=0
     )
     tokens[half + rows :, :] = jnp.concatenate([jnp.zeros_like(few[1]), few[1]], axis=0)
+    tail[...] = tokens[half - tail.shape[0] : half, :]
     for copy in copies[4:]:
         copy.wait()
 
 
-def split_kernel(both, far, halo, mine, other, far_tokens, far_grads):
-    mine[...] = both[0]
+def split_kernel(both, far, halo_first, halo_third, mine, mine_values, other, far_tokens, far_grads):
+    width = mine.shape[1]
+    mine[...] = both[0, :, :width]
+    mine_values[...] = both[0, :, width:]
     other[...] = both[1]
     half = far_grads.shape[0]
     far_tokens[:half, :] = far[:half, :]
-    far_tokens[half:, :] = halo[...]
+    far_tokens[half:, :] = jnp.where(member_of() == 0, halo_first[...], halo_third[...])
     far_grads[...] = far[half:, :]
 
 
@@ -134,38 +137,52 @@
     return jnp.concatenate([jnp.where(head == h, array, zero) for h in range(heads)], axis=0)
 
 
-def early_kernel(x_all, mine, beside, swapped_in, total):
+def early_kernel(x_all, mine, beside, beside_values, swapped_in, total, total_values):
     own = lax.axis_index("fsdp")
     along = 1 + (lax.axis_index("seg") & 1)
-    rows = beside.shape[0]
+    rows, width = beside.shape
     columns = lambda j: x_all[:, pl.ds(aligned(own ^ j, rows), rows)]
-    total[...] = (
-        jnp.dot(columns(0), mine[0], preferred_element_type=f32)
-        + jnp.dot(columns(along), beside[...], preferred_element_type=f32)
-        + jnp.dot(columns(along ^ 3), swapped_in[...], preferred_element_type=f32)
-    )
+    product = jnp.dot(columns(0), mine[0], preferred_element_type=f32) + jnp.dot(
+        columns(along ^ 3), swapped_in[...], preferred_element_type=f32
+    )
+    total[...] = product[:, :width] + jnp.dot(
+        columns(along), beside[...], preferred_element_type=f32
+    )
+    total_values[...] = product[:, width:] + jnp.dot(
+        columns(along), beside_values[...], preferred_element_type=f32
+    )
+
+
+def values_kernel(x_all, total, last, values):
+    rows = last.shape[0]
+    at = aligned(lax.axis_index("fsdp") ^ 3, rows)
+    columns = x_all[:, pl.ds(at, rows)]
+    values[...] = (
+        total[...] + jnp.dot(columns, last[...], preferred_element_type=f32)
+    ).astype(bf16)
 
 
 def weights_kernel(heads, frame_count, segs, crossed, x_all, *refs):
-    soft, values = refs[-3:-1] if not crossed else refs[-2:]
-    if crossed:
-        total, last = refs[:2]
+    if crossed:
+        total, last, soft = refs
         rows = last.shape[0]
         at = aligned(lax.axis_index("fsdp") ^ 3, rows)
         product = total[...] + jnp.dot(
             x_all[:, pl.ds(at, rows)], last[...], preferred_element_type=f32
         )
     else:
-        assemble(refs[:-3], refs[-1])
-        product = jnp.dot(x_all[...], refs[-1][...], preferred_element_type=f32)
+        soft, values, whole = refs[-3:]
+        assemble(refs[:-3], whole)
+        product = jnp.dot(x_all[...], whole[...], preferred_element_type=f32)
     projected = product.astype(bf16)
     blocks, keys, lanes = soft.shape
     queries = lanes // heads
     halo = keys - queries
     frames = segs * frame_count
-    block = values.shape[1]
+    block = projected.shape[1] // (2 if crossed else 3)
     q_all, k_all = projected[:, :block], projected[:, block : 2 * block]
-    values[...] = projected[:, 2 * block :]
+    if not crossed:
+        values[...] = projected[:, 2 * block :]
     key = lax.broadcasted_iota(jnp.int32, (keys, lanes), 0)
     row = lax.broadcasted_iota(jnp.int32, (keys, lanes), 1)
     for h in range(1, heads):
@@ -344,13 +361,14 @@
     member = seg % group
 
     crossed = fsdp_size == group
-    own_blocks, tokens = pl.pallas_call(
+    own_blocks, tokens, tail = pl.pallas_call(
         functools.partial(pack_kernel, frame_count),
         in_specs=[hbm] * 8,
-        out_specs=[vmem] * 2,
+        out_specs=[vmem] * 3,
         out_shape=[
             jax.ShapeDtypeStruct((1 + crossed, rows, 3 * block), bf16),
             jax.ShapeDtypeStruct((2 * queries, width), bf16),
+            jax.ShapeDtypeStruct((halo_rows, width), bf16),
         ],
         scratch_shapes=[
             pltpu.VMEM((frame_rows, width), bf16),
@@ -369,12 +387,10 @@
 
     far = swapped(tokens, "seg", 2)
     near = swapped(tokens, "seg", 1)
-    cut = slice(queries - halo_rows, queries)
-    tail = jnp.where(member == group - 1, tokens[cut], near[cut])
-    ahead = []
-    for s in range(group, seg_size, group):
-        ahead += [(s - 1, s), (s - 2, s + 2)]
-    halo = lax.ppermute(tail, "seg", ahead)
+    starts = range(group, seg_size, group)
+    halo = [
+        lax.ppermute(tail, "seg", [(s - 1, s + ahead) for s in starts]) for ahead in (0, 2)
+    ]
     if crossed:
         both = ("seg", "fsdp")
         straight, turned, first, last = pairs(seg_size)
@@ -385,22 +401,24 @@
         )
         wo_last = lax.ppermute(wo_came, both, last)
     else:
-        came = own_blocks
+        came = jnp.concatenate([own_blocks, own_blocks])
         wo_near = lax.dynamic_slice_in_dim(
             lax.all_gather(w_out, "fsdp", axis=0, tiled=True), member * block, block, 0
         )
-    mine, other, far, far_grads = pl.pallas_call(
+    mine, mine_values, other, far, far_grads = pl.pallas_call(
         split_kernel,
-        in_specs=[vmem] * 3,
-        out_specs=[vmem] * 4,
-        out_shape=[jax.ShapeDtypeStruct(came.shape[1:], bf16)] * 2
+        in_specs=[vmem] * 4,
+        out_specs=[vmem] * 5,
+        out_shape=[jax.ShapeDtypeStruct((rows, 2 * block), bf16)]
+        + [jax.ShapeDtypeStruct((rows, block), bf16)]
+        + [jax.ShapeDtypeStruct(came.shape[1:], bf16)]
         + [
             jax.ShapeDtypeStruct((queries + halo_rows, width), bf16),
             jax.ShapeDtypeStruct((queries, width), bf16),
         ],
         compiler_params=params(),
         name="split",
-    )(came, far, halo)
+    )(came, far, *halo)
     if crossed:
         other = swapped(other, "seg", 1)
         forwarded = lax.ppermute(mine, both, turned)
@@ -428,30 +446,45 @@
         compiler_params=params(),
         name="merge",
     )(*parts)
-    x_all, wo_near = lax.optimization_barrier((x_all, wo_near))
-
-    if crossed:
-        early = pl.pallas_call(
+    x_all, wo_near, mine_values = lax.optimization_barrier((x_all, wo_near, mine_values))
+    if crossed:
+        forwarded_values = lax.ppermute(mine_values, both, turned)
+
+    soft_shape = jax.ShapeDtypeStruct((group, keys, heads * queries), bf16)
+    values_shape = jax.ShapeDtypeStruct((all_rows, block), bf16)
+    if crossed:
+        early, early_values = pl.pallas_call(
             early_kernel,
-            in_specs=[vmem] * 4,
-            out_specs=vmem,
-            out_shape=jax.ShapeDtypeStruct((all_rows, 3 * block), f32),
+            in_specs=[vmem] * 5,
+            out_specs=[vmem] * 2,
+            out_shape=[
+                jax.ShapeDtypeStruct((all_rows, 2 * block), f32),
+                jax.ShapeDtypeStruct((all_rows, block), f32),
+            ],
             compiler_params=params(),
             name="early",
-        )(x_all, own_blocks, mine, other)
+        )(x_all, own_blocks, mine, mine_values, other)
         wqkv_parts = [early, forwarded]
-    soft, values = pl.pallas_call(
+    soft, *values = pl.pallas_call(
         functools.partial(weights_kernel, heads, frame_count, segs, crossed),
         in_specs=[vmem] * (1 + len(wqkv_parts)),
-        out_specs=[vmem] * 2,
-        out_shape=[
-            jax.ShapeDtypeStruct((group, keys, heads * queries), bf16),
-            jax.ShapeDtypeStruct((all_rows, block), bf16),
-        ],
+        out_specs=[vmem] * (2 - crossed),
+        out_shape=[soft_shape] + [values_shape] * (1 - crossed),
         scratch_shapes=[] if crossed else [pltpu.VMEM((width, 3 * block), bf16)],
         compiler_params=params(),
         name="soft_weights",
     )(x_all, *wqkv_parts)
+    if crossed:
+        values = pl.pallas_call(
+            values_kernel,
+            in_specs=[vmem] * 3,
+            out_specs=vmem,
+            out_shape=values_shape,
+            compiler_params=params(),
+            name="values",
+        )(x_all, early_values, forwarded_values)
+    else:
+        (values,) = values
 
     values_grad_shape = jax.ShapeDtypeStruct((all_rows, block), bf16)
     wo_from = [wo_near] + ([wo_last] if crossed else [])

time: 63.6 us -> 62 us (0.975)
  starting transfers between devices: 22.8 us -> 21.7 us
  other arithmetic: 0.95 us -> 0.1 us
    ppermute x14, starting transfers between devices: 12.7 us -> 10.6 us  [swapped(): return lax.ppermute(array, axis, [(i, i ^ bit) for i in range(size)])]
    ppermute x14, waiting for transfers between devices: 8.01 us -> 9.02 us  [swapped(): return lax.ppermute(array, axis, [(i, i ^ bit) for i in range(size)])]
    select_n x1 -> x0, other arithmetic: 0.85 us -> none  [on_device(): tail = jnp.where(member == group - 1, tokens[cut], near[cut])]
    ppermute x1 -> x3, starting transfers between devices: 0.8 us -> 1.58 us  [the longest x2 1.46 us: on_device(): lax.ppermute(tail, 'seg', [(s - 1, s + ahead) for s in starts])]
  transfers between devices with their start and end apart: 21 -> 23, of which waited for: 10 -> 10; matrix products, arithmetic and copies ran while one was open for 1% -> 0% of each run, Pallas kernels for 9% -> 12%
where the time goes in v6:
time: 62 us; the launch traced here: 61.8 us
  waiting for transfers between devices  27.2 us (44%)
  starting transfers between devices  21.7 us (35%)
  Pallas kernels  11.2 us (18%)
  between operations  1.55 us (2%)
    ppermute x1, waiting for transfers between devices, on_device(): wo_came = lax.ppermute(w_out, both, first)  11.5 us
    ppermute x14, starting transfers between devices, swapped(): return lax.ppermute(array, axis, [(i, i ^ bit) for i in range(size)])  10.6 us
    ppermute x14, waiting for transfers between devices, swapped(): return lax.ppermute(array, axis, [(i, i ^ bit) for i in range(size)])  9.02 us
    ppermute x1, waiting for transfers between devices, on_device(): last = lax.ppermute(passing, both, turned)  3.11 us
    ppermute x1, starting transfers between devices, on_device(): came = lax.ppermute(own_blocks, both, straight)  3 us
    ppermute x1, starting transfers between devices, on_device(): wo_came = lax.ppermute(w_out, both, first)  2.69 us
    pallas_call x1, Pallas kernels, on_device(): pl.pallas_call(functools.partial(pack_kernel, frame_count), in_specs=[hbm...  2.57 us
    ppermute x1, starting transfers between devices, on_device(): came = lax.ppermute(sent, both, straight)  2.39 us
  transfers between devices with their start and end apart: 23, of which 10 were waited for; matrix products, arithmetic and copies ran while one was open for 0% of the time, Pallas kernels for 12%

profile of v6, /device:TPU:0, one launch (start us, length us, event | category | flops | bytes accessed | tf_op | source)
XLA Modules:
  0.0 61.8 jit_solution(16128899306624058442)
XLA Ops:
  0.6 2.6 %pack.1 = (bf16[2,256,768]{2,1,0:T(8,128)(2,1)}, bf16[288,1024]{1,0:T(8,128)(2,1)}, bf16[32,1024]{1,0:T(8,128)(2,1)}) custom-call(bf16[256,1024]{1,0:T(8,128)(2,1)} %wq.1, bf16[256,1024]{1,0:T(8,128)(2,1)} %wk.1, bf16[256,1024]{1,0:T(8,128)(2,1)} %wv.1, bf16[128,1024]{1,0:T(8,128)(2,1)} %bitcast.15, bf16[128,1024]{1,0:T(8,128)(2,1)} %bitcast.17, ...), custom_call_target="tpu_custom_call" | custom-call | tf_op jit(solution)/shard_map/pack/pallas_call | solution.py:364
  3.2 3.0 %collective-permute-start = (bf16[2,256,768]{2,1,0:T(8,128)(2,1)}, bf16[2,256,768]{2,1,0:T(8,128)(2,1)S(1)}, u32[]{:S(2)}, u32[]{:S(2)}) collective-permute-start(bf16[2,256,768]{2,1,0:T(8,128)(2,1)} %get-tuple-element.46.mine), channel_id=1, source_target_pairs={{0,1},{1,0},{2,3},{3,2},{4,6},{5,7},{6,4},{7,5},{8,9},{9,8},{10,11... | collective-permute-start | bytes 2359304 | tf_op jit(solution)/shard_map/ppermute | solution.py:397
  6.2 1.6 %collective-permute-start.1 = (bf16[288,1024]{1,0:T(8,128)(2,1)}, bf16[288,1024]{1,0:T(8,128)(2,1)S(1)}, u32[]{:S(2)}, u32[]{:S(2)}) collective-permute-start(bf16[288,1024]{1,0:T(8,128)(2,1)} %get-tuple-element.44.tokens), channel_id=1, source_target_pairs={{0,8},{4,12},{8,0},{12,4},{16,24},{20,28},{24,16},{28,20},{1,9},{5... | collective-permute-start | bytes 1769480 | tf_op jit(solution)/shard_map/ppermute | solution.py:35
  7.8 2.7 %collective-permute-start.5 = (bf16[256,1024]{1,0:T(8,128)(2,1)S(1)}, bf16[256,1024]{1,0:T(8,128)(2,1)S(1)}, u32[]{:S(2)}, u32[]{:S(2)}) collective-permute-start(bf16[256,1024]{1,0:T(8,128)(2,1)S(1)} %copy-done.3), channel_id=1, source_target_pairs={{0,1},{4,2},{12,15},{5,4},{1,7},{9,10},{10,11},{14,8},{6,5},{15,14... | collective-permute-start | bytes 1572872 | tf_op jit(solution)/shard_map/ppermute | solution.py:398
  10.5 0.8 %collective-permute-start.3 = (bf16[32,1024]{1,0:T(8,128)(2,1)}, bf16[32,1024]{1,0:T(8,128)(2,1)S(1)}, u32[]{:S(2)}, u32[]{:S(2)}) collective-permute-start(bf16[32,1024]{1,0:T(8,128)(2,1)} %get-tuple-element.47), channel_id=1, source_target_pairs={{12,16},{13,17},{14,18},{15,19}} | collective-permute-start | bytes 196616 | tf_op jit(solution)/shard_map/ppermute | solution.py:392
  11.3 0.7 %collective-permute-start.4 = (bf16[32,1024]{1,0:T(8,128)(2,1)}, bf16[32,1024]{1,0:T(8,128)(2,1)S(1)}, u32[]{:S(2)}, u32[]{:S(2)}) collective-permute-start(bf16[32,1024]{1,0:T(8,128)(2,1)} %get-tuple-element.47), channel_id=1, source_target_pairs={{12,24},{13,25},{14,26},{15,27}} | collective-permute-start | bytes 196616 | tf_op jit(solution)/shard_map/ppermute | solution.py:392
  12.0 11.5 %collective-permute-done.5.came = bf16[256,1024]{1,0:T(8,128)(2,1)S(1)} collective-permute-done((bf16[256,1024]{1,0:T(8,128)(2,1)S(1)}, bf16[256,1024]{1,0:T(8,128)(2,1)S(1)}, u32[]{:S(2)}, u32[]{:S(2)}) %collective-permute-start.5) | collective-permute-done | bytes 524320 | tf_op jit(solution)/shard_map/ppermute | solution.py:398
  23.5 1.3 %collective-permute-start.11 = (bf16[256,1024]{1,0:T(8,128)(2,1)S(1)}, bf16[256,1024]{1,0:T(8,128)(2,1)S(1)}, u32[]{:S(2)}, u32[]{:S(2)}) collective-permute-start(bf16[256,1024]{1,0:T(8,128)(2,1)S(1)} %collective-permute-done.5.came), channel_id=1, source_target_pairs={{15,3},{10,6},{5,9},{0,12},{31,19},{26,22},{21,25},{16,28}} | collective-permute-start | bytes 1572872 | tf_op jit(solution)/shard_map/ppermute | solution.py:402
  25.0 0.5 collective-permute-start.8
  25.7 2.0 %collective-permute-done.7.last_grads = bf16[144,1024]{1,0:T(8,128)(2,1)S(1)} collective-permute-done((bf16[144,1024]{1,0:T(8,128)(2,1)S(1)}, bf16[144,1024]{1,0:T(8,128)(2,1)S(1)}, u32[]{:S(2)}, u32[]{:S(2)}) %collective-permute-start.7) | collective-permute-done | bytes 294944 | tf_op jit(solution)/shard_map/ppermute | solution.py:35
  27.7 0.6 %merge.1 = (bf16[608,1024]{1,0:T(8,128)(2,1)S(1)}, bf16[1024,608]{1,0:T(8,128)(2,1)S(1)}, bf16[576,1024]{1,0:T(8,128)(2,1)S(1)}) custom-call(bf16[288,1024]{1,0:T(8,128)(2,1)S(1)} %copy-done.2, bf16[288,1024]{1,0:T(8,128)(2,1)S(1)} %collective-permute-done.2.near, bf16[176,1024]{1,0:T(8,128)(2,1)S(1)} %get-tuple-element.54.far, ...), custom_call_target="tpu_custom_call" | custom-call | tf_op jit(solution)/shard_map/merge/pallas_call | solution.py:437
  29.1 0.9 %early.1 = (f32[608,512]{1,0:T(8,128)S(1)}, f32[608,256]{1,0:T(8,128)S(1)}) custom-call(bf16[608,1024]{1,0:T(8,128)(2,1)S(1)} %get-tuple-element.59.x_all, bf16[2,256,768]{2,1,0:T(8,128)(2,1)S(1)} %copy-done.1, bf16[256,512]{1,0:T(8,128)(2,1)S(1)} %get-tuple-element.60.beside, bf16[256,256]{1,0:T(8,128)(2,1)S(1)} %get-tuple-element.61.beside_values, ...), custom_call_target="tpu_custom_call" | custom-call | tf_op jit(solution)/shard_map/early/pallas_call | solution.py:456
  30.0 1.9 %collective-permute-done.9.refs_1_ = bf16[256,512]{1,0:T(8,128)(2,1)S(1)} collective-permute-done((bf16[256,512]{1,0:T(8,128)(2,1)S(1)}, bf16[256,512]{1,0:T(8,128)(2,1)S(1)}, u32[]{:S(2)}, u32[]{:S(2)}) %collective-permute-start.9) | collective-permute-done | bytes 262176 | tf_op jit(solution)/shard_map/ppermute | solution.py:424
  32.0 1.2 %soft_weights.1.soft = bf16[4,176,576]{2,1,0:T(8,128)(2,1)S(1)} custom-call(bf16[608,1024]{1,0:T(8,128)(2,1)S(1)} %get-tuple-element.59.x_all, f32[608,512]{1,0:T(8,128)S(1)} %get-tuple-element.63.refs_0_, bf16[256,512]{1,0:T(8,128)(2,1)S(1)} %collective-permute-done.9.refs_1_), custom_call_target="tpu_custom_call" | custom-call | tf_op jit(solution)/shard_map/soft_weights/pallas_call | solution.py:468
  33.2 1.4 %values_grad.1 = (bf16[256,1024]{1,0:T(8,128)(2,1)S(1)}, bf16[608,256]{1,0:T(8,128)(2,1)S(1)}) custom-call(s32[1]{0:T(128)S(6)} %copy.13.lengths, bf16[576,1024]{1,0:T(8,128)(2,1)S(1)} %get-tuple-element.65.u_all, bf16[4,176,576]{2,1,0:T(8,128)(2,1)S(1)} %soft_weights.1.soft, bf16[256,1024]{1,0:T(8,128)(2,1)S(1)} %pick.1.refs_0_, ...), custom_call_target="tpu_custom_call" | custom-call | tf_op jit(solution)/shard_map/values_grad/pallas_call | solution.py:491
  34.6 0.4 grad_rows_sent.1
  34.9 2.4 %collective-permute-start.12 = (bf16[2,256,256]{2,1,0:T(8,128)(2,1)S(1)}, bf16[2,256,256]{2,1,0:T(8,128)(2,1)S(1)}, u32[]{:S(2)}, u32[]{:S(2)}) collective-permute-start(bf16[2,256,256]{2,1,0:T(8,128)(2,1)S(1)} %grad_rows_sent.1), channel_id=1, source_target_pairs={{0,1},{1,0},{2,3},{3,2},{4,6},{5,7},{6,4},{7,5},{8,9},{9,8},{10,11... | collective-permute-start | bytes 786440 | tf_op jit(solution)/shard_map/ppermute | solution.py:546
  37.6 0.7 %attend_far.1 = (f32[144,1024]{1,0:T(8,128)S(1)}, bf16[64,1024]{1,0:T(8,128)(2,1)S(1)}, bf16[80,1024]{1,0:T(8,128)(2,1)S(1)}) custom-call(bf16[4,176,576]{2,1,0:T(8,128)(2,1)S(1)} %soft_weights.1.soft, bf16[608,256]{1,0:T(8,128)(2,1)S(1)} %values.1, bf16[256,1024]{1,0:T(8,128)(2,1)S(1)} %get-tuple-element.67.refs_0_), custom_call_target="tpu_custom_call" | custom-call | tf_op jit(solution)/shard_map/attend_far/pallas_call | solution.py:522
  38.4 0.5 collective-permute-start.13
  39.3 0.7 %collective-permute-done.13.refs_0_ = bf16[64,1024]{1,0:T(8,128)(2,1)S(1)} collective-permute-done((bf16[64,1024]{1,0:T(8,128)(2,1)S(1)}, bf16[64,1024]{1,0:T(8,128)(2,1)S(1)}, u32[]{:S(2)}, u32[]{:S(2)}) %collective-permute-start.13) | collective-permute-done | bytes 131104 | tf_op jit(solution)/shard_map/ppermute | solution.py:35
  40.0 1.7 %collective-permute-done.12 = bf16[2,256,256]{2,1,0:T(8,128)(2,1)S(1)} collective-permute-done((bf16[2,256,256]{2,1,0:T(8,128)(2,1)S(1)}, bf16[2,256,256]{2,1,0:T(8,128)(2,1)S(1)}, u32[]{:S(2)}, u32[]{:S(2)}) %collective-permute-start.12) | collective-permute-done | bytes 262176 | tf_op jit(solution)/shard_map/ppermute | solution.py:546
  41.8 1.8 %collective-permute-start.17 = (bf16[144,1024]{1,0:T(8,128)(2,1)S(1)}, bf16[144,1024]{1,0:T(8,128)(2,1)S(1)}, u32[]{:S(2)}, u32[]{:S(2)}) collective-permute-start(bf16[144,1024]{1,0:T(8,128)(2,1)S(1)} %onward.1), channel_id=1, source_target_pairs={{0,8},{4,12},{8,0},{12,4},{16,24},{20,28},{24,16},{28,20},{1,9},{5... | collective-permute-start | bytes 884744 | tf_op jit(solution)/shard_map/ppermute | solution.py:35
  43.6 3.1 %collective-permute-done.15 = bf16[256,256]{1,0:T(8,128)(2,1)S(1)} collective-permute-done((bf16[256,256]{1,0:T(8,128)(2,1)S(1)}, bf16[256,256]{1,0:T(8,128)(2,1)S(1)}, u32[]{:S(2)}, u32[]{:S(2)}) %collective-permute-start.15) | collective-permute-done | bytes 131104 | tf_op jit(solution)/shard_map/ppermute | solution.py:549
  46.8 2.6 %collective-permute-start.16 = (bf16[256,256]{1,0:T(8,128)(2,1)S(1)}, bf16[256,256]{1,0:T(8,128)(2,1)S(1)}, u32[]{:S(2)}, u32[]{:S(2)}) collective-permute-start(bf16[256,256]{1,0:T(8,128)(2,1)S(1)} %fusion.3), channel_id=1, source_target_pairs={{0,16},{4,20},{8,24},{12,28},{16,0},{20,4},{24,8},{28,12},{1,17},{... | collective-permute-start | bytes 393224 | tf_op jit(solution)/shard_map/ppermute | solution.py:35
  49.4 0.7 %attend_near.1 = (f32[144,1024]{1,0:T(8,128)S(1)}, bf16[64,1024]{1,0:T(8,128)(2,1)S(1)}, bf16[80,1024]{1,0:T(8,128)(2,1)S(1)}) custom-call(bf16[4,176,576]{2,1,0:T(8,128)(2,1)S(1)} %soft_weights.1.soft, bf16[608,256]{1,0:T(8,128)(2,1)S(1)} %values.1, bf16[256,1024]{1,0:T(8,128)(2,1)S(1)} %get-tuple-element.67.refs_0_), custom_call_target="tpu_custom_call" | custom-call | tf_op jit(solution)/shard_map/attend_near/pallas_call | solution.py:522
  50.2 0.5 collective-permute-start.18
  50.7 2.8 %collective-permute-done.16 = bf16[256,256]{1,0:T(8,128)(2,1)S(1)} collective-permute-done((bf16[256,256]{1,0:T(8,128)(2,1)S(1)}, bf16[256,256]{1,0:T(8,128)(2,1)S(1)}, u32[]{:S(2)}, u32[]{:S(2)}) %collective-permute-start.16) | collective-permute-done | bytes 131104 | tf_op jit(solution)/shard_map/ppermute | solution.py:35
  53.7 2.8 %collective-permute-start.20 = (bf16[256,256]{1,0:T(8,128)(2,1)S(1)}, bf16[256,256]{1,0:T(8,128)(2,1)S(1)}, u32[]{:S(2)}, u32[]{:S(2)}) collective-permute-start(bf16[256,256]{1,0:T(8,128)(2,1)S(1)} %add_convert_fusion.mine), channel_id=1, source_target_pairs={{0,8},{4,12},{8,0},{12,4},{16,24},{20,28},{24,16},{28,20},{1,9},{5... | collective-permute-start | bytes 393224 | tf_op jit(solution)/shard_map/ppermute | solution.py:35
  56.4 2.9 %collective-permute-done.20.far = bf16[256,256]{1,0:T(8,128)(2,1)S(1)} collective-permute-done((bf16[256,256]{1,0:T(8,128)(2,1)S(1)}, bf16[256,256]{1,0:T(8,128)(2,1)S(1)}, u32[]{:S(2)}, u32[]{:S(2)}) %collective-permute-start.20) | collective-permute-done | bytes 131104 | tf_op jit(solution)/shard_map/ppermute | solution.py:35
  59.4 0.8 %finish.1 = (bf16[128,1024]{1,0:T(8,128)(2,1)}, bf16[8,1024]{1,0:T(8,128)(2,1)}) custom-call(s32[1]{0:T(128)S(6)} %copy.13.lengths, bf16[128,1024]{1,0:T(8,128)(2,1)S(1)} %bitcast.16, f32[144,1024]{1,0:T(8,128)S(1)} %get-tuple-element.68.keep, bf16[144,1024]{1,0:T(8,128)(2,1)S(1)} %collective-permute-done.17.back, ...), custom_call_target="tpu_custom_call" | custom-call | tf_op jit(solution)/shard_map/finish/pallas_call | solution.py:564
  60.2 0.5 collective-permute-done.22.near_far
  60.7 1.1 %columns.1 = f32[256,1024]{1,0:T(8,128)} custom-call(bf16[256,256]{1,0:T(8,128)(2,1)S(1)} %add_convert_fusion.mine, bf16[256,256]{1,0:T(8,128)(2,1)S(1)} %collective-permute-done.20.far, bf16[256,256]{1,0:T(8,128)(2,1)S(1)} %collective-permute-done.21.near_mine, bf16[256,256]{1,0:T(8,128)(2,1)S(1)} %collective-permute-done.22.near_far), custom_call_target="tpu_custom_call" | custom-call | tf_op jit(solution)/shard_map/columns/pallas_call | solution.py:576
  (40 shorter events, 1.6 us)
Async XLA Ops:
  0.6 7.2 %copy-start.3 = (bf16[256,1024]{1,0:T(8,128)(2,1)S(1)}, bf16[256,1024]{1,0:T(8,128)(2,1)}, u32[]{:S(2)}) copy-start(bf16[256,1024]{1,0:T(8,128)(2,1)} %own) | copy-start | bytes 1572868
  3.2 20.3 %collective-permute-start = (bf16[2,256,768]{2,1,0:T(8,128)(2,1)}, bf16[2,256,768]{2,1,0:T(8,128)(2,1)S(1)}, u32[]{:S(2)}, u32[]{:S(2)}) collective-permute-start(bf16[2,256,768]{2,1,0:T(8,128)(2,1)} %get-tuple-element.46.mine), channel_id=1, source_target_pairs={{0,1},{1,0},{2,3},{3,2},{4,6},{5,7},{6,4},{7,5},{8,9},{9,8},{10,11... | collective-permute-start | bytes 2359304 | tf_op jit(solution)/shard_map/ppermute | solution.py:397
  6.2 17.3 %collective-permute-start.1 = (bf16[288,1024]{1,0:T(8,128)(2,1)}, bf16[288,1024]{1,0:T(8,128)(2,1)S(1)}, u32[]{:S(2)}, u32[]{:S(2)}) collective-permute-start(bf16[288,1024]{1,0:T(8,128)(2,1)} %get-tuple-element.44.tokens), channel_id=1, source_target_pairs={{0,8},{4,12},{8,0},{12,4},{16,24},{20,28},{24,16},{28,20},{1,9},{5... | collective-permute-start | bytes 1769480 | tf_op jit(solution)/shard_map/ppermute | solution.py:35
  7.8 15.7 %collective-permute-start.2 = (bf16[288,1024]{1,0:T(8,128)(2,1)}, bf16[288,1024]{1,0:T(8,128)(2,1)S(1)}, u32[]{:S(2)}, u32[]{:S(2)}) collective-permute-start(bf16[288,1024]{1,0:T(8,128)(2,1)} %get-tuple-element.44.tokens), channel_id=1, source_target_pairs={{0,4},{4,0},{8,12},{12,8},{16,20},{20,16},{24,28},{28,24},{1,5},{5... | collective-permute-start | bytes 1769480 | tf_op jit(solution)/shard_map/ppermute | solution.py:35
  7.8 15.7 %collective-permute-start.5 = (bf16[256,1024]{1,0:T(8,128)(2,1)S(1)}, bf16[256,1024]{1,0:T(8,128)(2,1)S(1)}, u32[]{:S(2)}, u32[]{:S(2)}) collective-permute-start(bf16[256,1024]{1,0:T(8,128)(2,1)S(1)} %copy-done.3), channel_id=1, source_target_pairs={{0,1},{4,2},{12,15},{5,4},{1,7},{9,10},{10,11},{14,8},{6,5},{15,14... | collective-permute-start | bytes 1572872 | tf_op jit(solution)/shard_map/ppermute | solution.py:398
  10.5 17.2 %copy-start.2 = (bf16[288,1024]{1,0:T(8,128)(2,1)S(1)}, bf16[288,1024]{1,0:T(8,128)(2,1)}, u32[]{:S(2)}) copy-start(bf16[288,1024]{1,0:T(8,128)(2,1)} %get-tuple-element.44.tokens) | copy-start | bytes 1769476
  10.5 0.8 %collective-permute-start.3 = (bf16[32,1024]{1,0:T(8,128)(2,1)}, bf16[32,1024]{1,0:T(8,128)(2,1)S(1)}, u32[]{:S(2)}, u32[]{:S(2)}) collective-permute-start(bf16[32,1024]{1,0:T(8,128)(2,1)} %get-tuple-element.47), channel_id=1, source_target_pairs={{12,16},{13,17},{14,18},{15,19}} | collective-permute-start | bytes 196616 | tf_op jit(solution)/shard_map/ppermute | solution.py:392
  11.3 0.7 %collective-permute-start.4 = (bf16[32,1024]{1,0:T(8,128)(2,1)}, bf16[32,1024]{1,0:T(8,128)(2,1)S(1)}, u32[]{:S(2)}, u32[]{:S(2)}) collective-permute-start(bf16[32,1024]{1,0:T(8,128)(2,1)} %get-tuple-element.47), channel_id=1, source_target_pairs={{12,24},{13,25},{14,26},{15,27}} | collective-permute-start | bytes 196616 | tf_op jit(solution)/shard_map/ppermute | solution.py:392
  23.5 9.6 %collective-permute-start.11 = (bf16[256,1024]{1,0:T(8,128)(2,1)S(1)}, bf16[256,1024]{1,0:T(8,128)(2,1)S(1)}, u32[]{:S(2)}, u32[]{:S(2)}) collective-permute-start(bf16[256,1024]{1,0:T(8,128)(2,1)S(1)} %collective-permute-done.5.came), channel_id=1, source_target_pairs={{15,3},{10,6},{5,9},{0,12},{31,19},{26,22},{21,25},{16,28}} | collective-permute-start | bytes 1572872 | tf_op jit(solution)/shard_map/ppermute | solution.py:402
  25.0 2.7 %collective-permute-start.6 = (bf16[176,1024]{1,0:T(8,128)(2,1)S(1)}, bf16[176,1024]{1,0:T(8,128)(2,1)S(1)}, u32[]{:S(2)}, u32[]{:S(2)}) collective-permute-start(bf16[176,1024]{1,0:T(8,128)(2,1)S(1)} %get-tuple-element.54.far), channel_id=1, source_target_pairs={{0,4},{4,0},{8,12},{12,8},{16,20},{20,16},{24,28},{28,24},{1,5},{5... | collective-permute-start | bytes 1081352 | tf_op jit(solution)/shard_map/ppermute | solution.py:35
  25.0 4.1 %collective-permute-start.8 = (bf16[256,768]{1,0:T(8,128)(2,1)S(1)}, bf16[256,768]{1,0:T(8,128)(2,1)S(1)}, u32[]{:S(2)}, u32[]{:S(2)}) collective-permute-start(bf16[256,768]{1,0:T(8,128)(2,1)S(1)} %get-tuple-element.62), channel_id=1, source_target_pairs={{0,4},{4,0},{8,12},{12,8},{16,20},{20,16},{24,28},{28,24},{1,5},{5... | collective-permute-start | bytes 1179656 | tf_op jit(solution)/shard_map/ppermute | solution.py:35
  25.5 2.1 %collective-permute-start.7 = (bf16[144,1024]{1,0:T(8,128)(2,1)S(1)}, bf16[144,1024]{1,0:T(8,128)(2,1)S(1)}, u32[]{:S(2)}, u32[]{:S(2)}) collective-permute-start(bf16[144,1024]{1,0:T(8,128)(2,1)S(1)} %get-tuple-element.55.far_grads), channel_id=1, source_target_pairs={{0,4},{4,0},{8,12},{12,8},{16,20},{20,16},{24,28},{28,24},{1,5},{5... | collective-permute-start | bytes 884744 | tf_op jit(solution)/shard_map/ppermute | solution.py:35
  25.6 6.4 %collective-permute-start.9 = (bf16[256,512]{1,0:T(8,128)(2,1)S(1)}, bf16[256,512]{1,0:T(8,128)(2,1)S(1)}, u32[]{:S(2)}, u32[]{:S(2)}) collective-permute-start(bf16[256,512]{1,0:T(8,128)(2,1)S(1)} %get-tuple-element.60.beside), channel_id=1, source_target_pairs={{0,2},{1,3},{2,0},{3,1},{4,5},{5,4},{6,7},{7,6},{8,10},{9,11},{10,... | collective-permute-start | bytes 786440 | tf_op jit(solution)/shard_map/ppermute | solution.py:424
  25.7 3.4 %copy-start.1 = (bf16[2,256,768]{2,1,0:T(8,128)(2,1)S(1)}, bf16[2,256,768]{2,1,0:T(8,128)(2,1)}, u32[]{:S(2)}) copy-start(bf16[2,256,768]{2,1,0:T(8,128)(2,1)} %get-tuple-element.46.mine) | copy-start | bytes 2359300
  28.3 9.0 %collective-permute-start.10 = (bf16[256,256]{1,0:T(8,128)(2,1)S(1)}, bf16[256,256]{1,0:T(8,128)(2,1)S(1)}, u32[]{:S(2)}, u32[]{:S(2)}) collective-permute-start(bf16[256,256]{1,0:T(8,128)(2,1)S(1)} %get-tuple-element.61.beside_values), channel_id=1, source_target_pairs={{0,2},{1,3},{2,0},{3,1},{4,5},{5,4},{6,7},{7,6},{8,10},{9,11},{10,... | collective-permute-start | bytes 393224 | tf_op jit(solution)/shard_map/ppermute | solution.py:451
  34.9 6.7 %collective-permute-start.12 = (bf16[2,256,256]{2,1,0:T(8,128)(2,1)S(1)}, bf16[2,256,256]{2,1,0:T(8,128)(2,1)S(1)}, u32[]{:S(2)}, u32[]{:S(2)}) collective-permute-start(bf16[2,256,256]{2,1,0:T(8,128)(2,1)S(1)} %grad_rows_sent.1), channel_id=1, source_target_pairs={{0,1},{1,0},{2,3},{3,2},{4,6},{5,7},{6,4},{7,5},{8,9},{9,8},{10,11... | collective-permute-start | bytes 786440 | tf_op jit(solution)/shard_map/ppermute | solution.py:546
  38.3 1.7 %collective-permute-start.14 = (bf16[80,1024]{1,0:T(8,128)(2,1)S(1)}, bf16[80,1024]{1,0:T(8,128)(2,1)S(1)}, u32[]{:S(2)}, u32[]{:S(2)}) collective-permute-start(bf16[80,1024]{1,0:T(8,128)(2,1)S(1)} %get-tuple-element.73), channel_id=1, source_target_pairs={{0,4},{4,0},{8,12},{12,8},{16,20},{20,16},{24,28},{28,24},{1,5},{5... | collective-permute-start | bytes 491528 | tf_op jit(solution)/shard_map/ppermute | solution.py:35
  38.4 1.6 %collective-permute-start.13 = (bf16[64,1024]{1,0:T(8,128)(2,1)S(1)}, bf16[64,1024]{1,0:T(8,128)(2,1)S(1)}, u32[]{:S(2)}, u32[]{:S(2)}) collective-permute-start(bf16[64,1024]{1,0:T(8,128)(2,1)S(1)} %get-tuple-element.72), channel_id=1, source_target_pairs={{0,4},{4,0},{8,12},{12,8},{16,20},{20,16},{24,28},{28,24},{1,5},{5... | collective-permute-start | bytes 393224 | tf_op jit(solution)/shard_map/ppermute | solution.py:35
  41.7 17.7 %copy-start = (bf16[1,8,16,1024]{3,2,1,0:T(8,128)(2,1)S(1)}, bf16[1,8,16,1024]{3,2,1,0:T(8,128)(2,1)}, u32[]{:S(2)}) copy-start(bf16[1,8,16,1024]{3,2,1,0:T(8,128)(2,1)} %param.10) | copy-start | bytes 786436
  41.7 5.0 %collective-permute-start.15 = (bf16[256,256]{1,0:T(8,128)(2,1)S(1)}, bf16[256,256]{1,0:T(8,128)(2,1)S(1)}, u32[]{:S(2)}, u32[]{:S(2)}) collective-permute-start(bf16[256,256]{1,0:T(8,128)(2,1)S(1)} %fusion.4), channel_id=1, source_target_pairs={{0,2},{1,3},{2,0},{3,1},{4,5},{5,4},{6,7},{7,6},{8,10},{9,11},{10,... | collective-permute-start | bytes 393224 | tf_op jit(solution)/shard_map/ppermute | solution.py:549
  41.8 11.8 %collective-permute-start.17 = (bf16[144,1024]{1,0:T(8,128)(2,1)S(1)}, bf16[144,1024]{1,0:T(8,128)(2,1)S(1)}, u32[]{:S(2)}, u32[]{:S(2)}) collective-permute-start(bf16[144,1024]{1,0:T(8,128)(2,1)S(1)} %onward.1), channel_id=1, source_target_pairs={{0,8},{4,12},{8,0},{12,4},{16,24},{20,28},{24,16},{28,20},{1,9},{5... | collective-permute-start | bytes 884744 | tf_op jit(solution)/shard_map/ppermute | solution.py:35
  46.8 6.7 %collective-permute-start.16 = (bf16[256,256]{1,0:T(8,128)(2,1)S(1)}, bf16[256,256]{1,0:T(8,128)(2,1)S(1)}, u32[]{:S(2)}, u32[]{:S(2)}) collective-permute-start(bf16[256,256]{1,0:T(8,128)(2,1)S(1)} %fusion.3), channel_id=1, source_target_pairs={{0,16},{4,20},{8,24},{12,28},{16,0},{20,4},{24,8},{28,12},{1,17},{... | collective-permute-start | bytes 393224 | tf_op jit(solution)/shard_map/ppermute | solution.py:35
  50.2 3.5 %collective-permute-start.19 = (bf16[80,1024]{1,0:T(8,128)(2,1)S(1)}, bf16[80,1024]{1,0:T(8,128)(2,1)S(1)}, u32[]{:S(2)}, u32[]{:S(2)}) collective-permute-start(bf16[80,1024]{1,0:T(8,128)(2,1)S(1)} %get-tuple-element.79), channel_id=1, source_target_pairs={{0,4},{4,0},{8,12},{12,8},{16,20},{20,16},{24,28},{28,24},{1,5},{5... | collective-permute-start | bytes 491528 | tf_op jit(solution)/shard_map/ppermute | solution.py:35
  50.2 3.4 %collective-permute-start.18 = (bf16[64,1024]{1,0:T(8,128)(2,1)S(1)}, bf16[64,1024]{1,0:T(8,128)(2,1)S(1)}, u32[]{:S(2)}, u32[]{:S(2)}) collective-permute-start(bf16[64,1024]{1,0:T(8,128)(2,1)S(1)} %get-tuple-element.78), channel_id=1, source_target_pairs={{0,4},{4,0},{8,12},{12,8},{16,20},{20,16},{24,28},{28,24},{1,5},{5... | collective-permute-start | bytes 393224 | tf_op jit(solution)/shard_map/ppermute | solution.py:35
  53.7 5.7 %collective-permute-start.20 = (bf16[256,256]{1,0:T(8,128)(2,1)S(1)}, bf16[256,256]{1,0:T(8,128)(2,1)S(1)}, u32[]{:S(2)}, u32[]{:S(2)}) collective-permute-start(bf16[256,256]{1,0:T(8,128)(2,1)S(1)} %add_convert_fusion.mine), channel_id=1, source_target_pairs={{0,8},{4,12},{8,0},{12,4},{16,24},{20,28},{24,16},{28,20},{1,9},{5... | collective-permute-start | bytes 393224 | tf_op jit(solution)/shard_map/ppermute | solution.py:35
  56.4 3.8 %collective-permute-start.21 = (bf16[256,256]{1,0:T(8,128)(2,1)S(1)}, bf16[256,256]{1,0:T(8,128)(2,1)S(1)}, u32[]{:S(2)}, u32[]{:S(2)}) collective-permute-start(bf16[256,256]{1,0:T(8,128)(2,1)S(1)} %add_convert_fusion.mine), channel_id=1, source_target_pairs={{0,4},{4,0},{8,12},{12,8},{16,20},{20,16},{24,28},{28,24},{1,5},{5... | collective-permute-start | bytes 393224 | tf_op jit(solution)/shard_map/ppermute | solution.py:35
  59.4 1.3 %collective-permute-start.22 = (bf16[256,256]{1,0:T(8,128)(2,1)S(1)}, bf16[256,256]{1,0:T(8,128)(2,1)S(1)}, u32[]{:S(2)}, u32[]{:S(2)}) collective-permute-start(bf16[256,256]{1,0:T(8,128)(2,1)S(1)} %collective-permute-done.20.far), channel_id=1, source_target_pairs={{0,4},{4,0},{8,12},{12,8},{16,20},{20,16},{24,28},{28,24},{1,5},{5... | collective-permute-start | bytes 393224 | tf_op jit(solution)/shard_map/ppermute | solution.py:35

commit v7 on v6

--- a/solution.py
+++ b/solution.py
@@ -213,8 +213,9 @@
         soft[b] = (exponent / jnp.sum(exponent, axis=0, keepdims=True)).astype(bf16)
 
 
-def grad_kernel(heads, frame_count, segs, lengths, u_all, soft, *refs):
-    wo_from, (wo, values, total) = refs[:-3], refs[-3:]
+def grad_kernel(heads, frame_count, segs, crossed, lengths, u_all, soft, x_turned, *refs):
+    outputs = 3 + crossed
+    wo_from, (wo, values, *sent, total) = refs[:-outputs], refs[-outputs:]
     blocks, keys, lanes = soft.shape
     queries = lanes // heads
     frames = segs * frame_count
@@ -236,6 +237,8 @@
         total[start : start + split, :] += term[:split]
         total[start + split : start + keys, :] = term[split:]
     values[...] = total[...].astype(bf16)
+    if crossed:
+        rows_kernel("sent", x_turned, values, *sent)
 
 
 def rows_kernel(which, x_turned, values, *outs):
@@ -309,10 +312,18 @@
     memory_out[...] = live(projected[count + segs :], 1).astype(bf16)
 
 
-def columns_kernel(mine, far, near_mine, near_far, out):
-    width = mine.shape[1]
-    for i, part in enumerate((mine, near_mine, far, near_far)):
-        out[:, pl.ds(aligned(member_of() ^ i, width), width)] = part[...].astype(f32)
+def columns_kernel(apart, *refs):
+    count = len(apart)
+    blocks, (out, wide, sems) = refs[:count], refs[-3:]
+    width = blocks[0].shape[1]
+    copies = []
+    for i, block in enumerate(blocks):
+        wide[i] = block[...].astype(f32)
+        at = pl.ds(aligned(member_of() ^ apart[i], width), width)
+        copies.append(pltpu.make_async_copy(wide.at[i], out.at[:, at], sems.at[i]))
+        copies[-1].start()
+    for copy in copies:
+        copy.wait()
 
 
 def gathered(piece):
@@ -488,15 +499,16 @@
 
     values_grad_shape = jax.ShapeDtypeStruct((all_rows, block), bf16)
     wo_from = [wo_near] + ([wo_last] if crossed else [])
-    wo_mine, values_grad = pl.pallas_call(
-        functools.partial(grad_kernel, heads, frame_count, segs),
-        in_specs=[smem] + [vmem] * (2 + len(wo_from)),
-        out_specs=[vmem] * 2,
-        out_shape=[jax.ShapeDtypeStruct((block, width), bf16), values_grad_shape],
+    sent_shape = [jax.ShapeDtypeStruct((2, rows, block), bf16)] * crossed
+    wo_mine, values_grad, *sent = pl.pallas_call(
+        functools.partial(grad_kernel, heads, frame_count, segs, crossed),
+        in_specs=[smem] + [vmem] * (3 + len(wo_from)),
+        out_specs=[vmem] * (2 + crossed),
+        out_shape=[jax.ShapeDtypeStruct((block, width), bf16), values_grad_shape] + sent_shape,
         scratch_shapes=[pltpu.VMEM((all_rows, block), f32)],
         compiler_params=params(),
         name="values_grad",
-    )(lengths, u_all, soft, *wo_from)
+    )(lengths, u_all, soft, x_turned, *wo_from)
 
     def grad_rows(which, shapes):
         return pl.pallas_call(
@@ -509,20 +521,20 @@
         )(x_turned, values_grad)
 
     if crossed:
-        (sent,) = grad_rows("sent", [jax.ShapeDtypeStruct((2, rows, block), bf16)])
+        (sent,) = sent
         (kept,) = grad_rows("kept", [jax.ShapeDtypeStruct((2, rows, block), f32)])
     else:
         grad_chunks = grad_rows(
             "all", [jax.ShapeDtypeStruct((rows, block), bf16)] * fsdp_size
         )
 
-    def attend(start, name):
-        cut = queries // PIECES // 16 * 16
-        sizes = [cut] * (PIECES - 1) + [queries - cut * (PIECES - 1)]
+    def attend(start, name, pieces):
+        cut = queries // pieces // 16 * 16
+        sizes = [cut] * (pieces - 1) + [queries - cut * (pieces - 1)]
         keep, *send = pl.pallas_call(
             functools.partial(out_kernel, heads, start),
             in_specs=[vmem] * 3,
-            out_specs=[vmem] * (1 + PIECES),
+            out_specs=[vmem] * (1 + pieces),
             out_shape=[jax.ShapeDtypeStruct((queries, width), f32)]
             + [jax.ShapeDtypeStruct((size, width), bf16) for size in sizes],
             compiler_params=params(),
@@ -530,8 +542,8 @@
         )(soft, values, wo_mine)
         return keep, send
 
-    keep_far, send_far = attend(2, "attend_far")
-    keep, send = attend(0, "attend_near")
+    keep_far, send_far = attend(2, "attend_far", PIECES)
+    keep, send = attend(0, "attend_near", 1)
     near = [swapped(piece, "seg", 1) for piece in send]
     near_far = [swapped(piece, "seg", 1) for piece in send_far]
     onward = pl.pallas_call(
@@ -560,10 +572,10 @@
         other, back = lax.optimization_barrier((swapped(mine, "seg", bit), back))
         grad_sum = mine.astype(f32) + other.astype(f32)
         bit *= 2
-    mine, near = lax.optimization_barrier((grad_sum.astype(bf16), near))
+    mine = grad_sum.astype(bf16)
     frames_out, memory_out = pl.pallas_call(
         functools.partial(finish_kernel, frame_count),
-        in_specs=[smem] + [vmem] * (3 + PIECES),
+        in_specs=[smem] + [vmem] * 4,
         out_specs=[vmem] * 2,
         out_shape=[
             jax.ShapeDtypeStruct((frame_rows, width), bf16),
@@ -572,15 +584,28 @@
         compiler_params=params(),
         name="finish",
     )(lengths, frames.reshape(frame_rows, width), keep, back, *near)
-    far = swapped(mine, "seg", 2)
-    value_grad = pl.pallas_call(
-        columns_kernel,
-        in_specs=[vmem] * 4,
-        out_specs=vmem,
-        out_shape=jax.ShapeDtypeStruct((rows, width), f32),
-        compiler_params=params(),
-        name="columns",
-    )(mine, far, swapped(mine, "seg", 1), swapped(far, "seg", 1))
+    far, frames_out, memory_out = lax.optimization_barrier(
+        (swapped(mine, "seg", 2), frames_out, memory_out)
+    )
+
+    def columns(apart, blocks, *onto):
+        count = len(blocks)
+        return pl.pallas_call(
+            functools.partial(columns_kernel, apart),
+            in_specs=[vmem] * count + [hbm] * len(onto),
+            out_specs=hbm,
+            out_shape=jax.ShapeDtypeStruct((rows, width), f32),
+            scratch_shapes=[
+                pltpu.VMEM((count, rows, block), f32),
+                pltpu.SemaphoreType.DMA((count,)),
+            ],
+            input_output_aliases={count: 0} if onto else {},
+            compiler_params=params(),
+            name="columns" + "_rest" * len(onto),
+        )(*blocks, *onto)
+
+    begun = columns((0, 2, 1), (mine, far, swapped(mine, "seg", 1)))
+    value_grad = columns((3,), (swapped(far, "seg", 1),), begun)
     frames_out = frames_out.reshape(frames.shape)
     memory_out = memory_out.reshape(memory_in.shape)
     return (frames_out, memory_out, value_grad)

time: 62 us -> 61.6 us (level)
    pallas_call x2 -> x3, Pallas kernels: 2.44 us -> 3.33 us  [the longest x1 1.68 us: on_device(): pl.pallas_call(functools.partial(grad_kernel, heads, frame_count, segs, c...]
    ppermute x14 -> x13, starting transfers between devices: 10.6 us -> 10.1 us  [swapped(): return lax.ppermute(array, axis, [(i, i ^ bit) for i in range(size)])]
    ppermute x14 -> x13, waiting for transfers between devices: 9.02 us -> 8.58 us  [swapped(): return lax.ppermute(array, axis, [(i, i ^ bit) for i in range(size)])]
  transfers between devices with their start and end apart: 23 -> 22, of which waited for: 10 -> 10; matrix products, arithmetic and copies ran while one was open for 0% -> 0% of each run, Pallas kernels for 12% -> 14%
where the time goes in v7:
time: 61.6 us; the launch traced here: 61.4 us
  waiting for transfers between devices  26.8 us (44%)
  starting transfers between devices  21.2 us (34%)
  Pallas kernels  11.7 us (19%)
  between operations  1.53 us (2%)
    ppermute x1, waiting for transfers between devices, on_device(): wo_came = lax.ppermute(w_out, both, first)  11.5 us
    ppermute x13, starting transfers between devices, swapped(): return lax.ppermute(array, axis, [(i, i ^ bit) for i in range(size)])  10.1 us
    ppermute x13, waiting for transfers between devices, swapped(): return lax.ppermute(array, axis, [(i, i ^ bit) for i in range(size)])  8.58 us
    ppermute x1, waiting for transfers between devices, on_device(): last = lax.ppermute(passing, both, turned)  3.11 us
    ppermute x1, starting transfers between devices, on_device(): came = lax.ppermute(own_blocks, both, straight)  3 us
    ppermute x1, starting transfers between devices, on_device(): wo_came = lax.ppermute(w_out, both, first)  2.69 us
    pallas_call x1, Pallas kernels, on_device(): pl.pallas_call(functools.partial(pack_kernel, frame_count), in_specs=[hbm...  2.57 us
    ppermute x1, starting transfers between devices, on_device(): came = lax.ppermute(sent, both, straight)  2.39 us
  transfers between devices with their start and end apart: 22, of which 10 were waited for; matrix products, arithmetic and copies ran while one was open for 0% of the time, Pallas kernels for 14%

profile of v7, /device:TPU:0, one launch (start us, length us, event | category | flops | bytes accessed | tf_op | source)
XLA Modules:
  0.0 61.4 jit_solution(7023967537287557017)
XLA Ops:
  0.6 2.6 %pack.1 = (bf16[2,256,768]{2,1,0:T(8,128)(2,1)}, bf16[288,1024]{1,0:T(8,128)(2,1)}, bf16[32,1024]{1,0:T(8,128)(2,1)}) custom-call(bf16[256,1024]{1,0:T(8,128)(2,1)} %wq.1, bf16[256,1024]{1,0:T(8,128)(2,1)} %wk.1, bf16[256,1024]{1,0:T(8,128)(2,1)} %wv.1, bf16[128,1024]{1,0:T(8,128)(2,1)} %bitcast.15, bf16[128,1024]{1,0:T(8,128)(2,1)} %bitcast.17, ...), custom_call_target="tpu_custom_call" | custom-call | tf_op jit(solution)/shard_map/pack/pallas_call | solution.py:375
  3.2 3.0 %collective-permute-start = (bf16[2,256,768]{2,1,0:T(8,128)(2,1)}, bf16[2,256,768]{2,1,0:T(8,128)(2,1)S(1)}, u32[]{:S(2)}, u32[]{:S(2)}) collective-permute-start(bf16[2,256,768]{2,1,0:T(8,128)(2,1)} %get-tuple-element.46.mine), channel_id=1, source_target_pairs={{0,1},{1,0},{2,3},{3,2},{4,6},{5,7},{6,4},{7,5},{8,9},{9,8},{10,11... | collective-permute-start | bytes 2359304 | tf_op jit(solution)/shard_map/ppermute | solution.py:408
  6.2 1.6 %collective-permute-start.1 = (bf16[288,1024]{1,0:T(8,128)(2,1)}, bf16[288,1024]{1,0:T(8,128)(2,1)S(1)}, u32[]{:S(2)}, u32[]{:S(2)}) collective-permute-start(bf16[288,1024]{1,0:T(8,128)(2,1)} %get-tuple-element.44.tokens), channel_id=1, source_target_pairs={{0,8},{4,12},{8,0},{12,4},{16,24},{20,28},{24,16},{28,20},{1,9},{5... | collective-permute-start | bytes 1769480 | tf_op jit(solution)/shard_map/ppermute | solution.py:35
  7.8 2.7 %collective-permute-start.5 = (bf16[256,1024]{1,0:T(8,128)(2,1)S(1)}, bf16[256,1024]{1,0:T(8,128)(2,1)S(1)}, u32[]{:S(2)}, u32[]{:S(2)}) collective-permute-start(bf16[256,1024]{1,0:T(8,128)(2,1)S(1)} %copy-done.3), channel_id=1, source_target_pairs={{0,1},{4,2},{12,15},{5,4},{1,7},{9,10},{10,11},{14,8},{6,5},{15,14... | collective-permute-start | bytes 1572872 | tf_op jit(solution)/shard_map/ppermute | solution.py:409
  10.5 0.8 %collective-permute-start.3 = (bf16[32,1024]{1,0:T(8,128)(2,1)}, bf16[32,1024]{1,0:T(8,128)(2,1)S(1)}, u32[]{:S(2)}, u32[]{:S(2)}) collective-permute-start(bf16[32,1024]{1,0:T(8,128)(2,1)} %get-tuple-element.47), channel_id=1, source_target_pairs={{12,16},{13,17},{14,18},{15,19}} | collective-permute-start | bytes 196616 | tf_op jit(solution)/shard_map/ppermute | solution.py:403
  11.3 0.7 %collective-permute-start.4 = (bf16[32,1024]{1,0:T(8,128)(2,1)}, bf16[32,1024]{1,0:T(8,128)(2,1)S(1)}, u32[]{:S(2)}, u32[]{:S(2)}) collective-permute-start(bf16[32,1024]{1,0:T(8,128)(2,1)} %get-tuple-element.47), channel_id=1, source_target_pairs={{12,24},{13,25},{14,26},{15,27}} | collective-permute-start | bytes 196616 | tf_op jit(solution)/shard_map/ppermute | solution.py:403
  12.0 11.5 %collective-permute-done.5.came = bf16[256,1024]{1,0:T(8,128)(2,1)S(1)} collective-permute-done((bf16[256,1024]{1,0:T(8,128)(2,1)S(1)}, bf16[256,1024]{1,0:T(8,128)(2,1)S(1)}, u32[]{:S(2)}, u32[]{:S(2)}) %collective-permute-start.5) | collective-permute-done | bytes 524320 | tf_op jit(solution)/shard_map/ppermute | solution.py:409
  23.5 1.3 %collective-permute-start.10 = (bf16[256,1024]{1,0:T(8,128)(2,1)S(1)}, bf16[256,1024]{1,0:T(8,128)(2,1)S(1)}, u32[]{:S(2)}, u32[]{:S(2)}) collective-permute-start(bf16[256,1024]{1,0:T(8,128)(2,1)S(1)} %collective-permute-done.5.came), channel_id=1, source_target_pairs={{15,3},{10,6},{5,9},{0,12},{31,19},{26,22},{21,25},{16,28}} | collective-permute-start | bytes 1572872 | tf_op jit(solution)/shard_map/ppermute | solution.py:413
  25.0 0.5 collective-permute-start.8
  25.7 2.0 %collective-permute-done.7.last_grads = bf16[144,1024]{1,0:T(8,128)(2,1)S(1)} collective-permute-done((bf16[144,1024]{1,0:T(8,128)(2,1)S(1)}, bf16[144,1024]{1,0:T(8,128)(2,1)S(1)}, u32[]{:S(2)}, u32[]{:S(2)}) %collective-permute-start.7) | collective-permute-done | bytes 294944 | tf_op jit(solution)/shard_map/ppermute | solution.py:35
  27.7 0.6 %merge.1 = (bf16[608,1024]{1,0:T(8,128)(2,1)S(1)}, bf16[1024,608]{1,0:T(8,128)(2,1)S(1)}, bf16[576,1024]{1,0:T(8,128)(2,1)S(1)}) custom-call(bf16[288,1024]{1,0:T(8,128)(2,1)S(1)} %copy-done.2, bf16[288,1024]{1,0:T(8,128)(2,1)S(1)} %collective-permute-done.2.near, bf16[176,1024]{1,0:T(8,128)(2,1)S(1)} %get-tuple-element.54.far, ...), custom_call_target="tpu_custom_call" | custom-call | tf_op jit(solution)/shard_map/merge/pallas_call | solution.py:448
  29.1 0.9 %early.1 = (f32[608,512]{1,0:T(8,128)S(1)}, f32[608,256]{1,0:T(8,128)S(1)}) custom-call(bf16[608,1024]{1,0:T(8,128)(2,1)S(1)} %get-tuple-element.61.x_all, bf16[2,256,768]{2,1,0:T(8,128)(2,1)S(1)} %copy-done.1, bf16[256,512]{1,0:T(8,128)(2,1)S(1)} %get-tuple-element.62.beside, bf16[256,256]{1,0:T(8,128)(2,1)S(1)} %get-tuple-element.63.beside_values, ...), custom_call_target="tpu_custom_call" | custom-call | tf_op jit(solution)/shard_map/early/pallas_call | solution.py:467
  30.0 1.9 %collective-permute-done.9.refs_1_ = bf16[256,512]{1,0:T(8,128)(2,1)S(1)} collective-permute-done((bf16[256,512]{1,0:T(8,128)(2,1)S(1)}, bf16[256,512]{1,0:T(8,128)(2,1)S(1)}, u32[]{:S(2)}, u32[]{:S(2)}) %collective-permute-start.9) | collective-permute-done | bytes 262176 | tf_op jit(solution)/shard_map/ppermute | solution.py:435
  32.0 1.2 %soft_weights.1.soft = bf16[4,176,576]{2,1,0:T(8,128)(2,1)S(1)} custom-call(bf16[608,1024]{1,0:T(8,128)(2,1)S(1)} %get-tuple-element.61.x_all, f32[608,512]{1,0:T(8,128)S(1)} %get-tuple-element.65.refs_0_, bf16[256,512]{1,0:T(8,128)(2,1)S(1)} %collective-permute-done.9.refs_1_), custom_call_target="tpu_custom_call" | custom-call | tf_op jit(solution)/shard_map/soft_weights/pallas_call | solution.py:479
  33.2 1.7 %values_grad.1 = (bf16[256,1024]{1,0:T(8,128)(2,1)S(1)}, bf16[608,256]{1,0:T(8,128)(2,1)S(1)}, bf16[2,256,256]{2,1,0:T(8,128)(2,1)S(1)}) custom-call(s32[1]{0:T(128)S(6)} %copy.15.lengths, bf16[576,1024]{1,0:T(8,128)(2,1)S(1)} %get-tuple-element.57.u_all, bf16[4,176,576]{2,1,0:T(8,128)(2,1)S(1)} %soft_weights.1.soft, ...), custom_call_target="tpu_custom_call" | custom-call | tf_op jit(solution)/shard_map/values_grad/pallas_call | solution.py:503
  34.9 2.4 %collective-permute-start.11 = (bf16[2,256,256]{2,1,0:T(8,128)(2,1)S(1)}, bf16[2,256,256]{2,1,0:T(8,128)(2,1)S(1)}, u32[]{:S(2)}, u32[]{:S(2)}) collective-permute-start(bf16[2,256,256]{2,1,0:T(8,128)(2,1)S(1)} %get-tuple-element.68), channel_id=1, source_target_pairs={{0,1},{1,0},{2,3},{3,2},{4,6},{5,7},{6,4},{7,5},{8,9},{9,8},{10,11... | collective-permute-start | bytes 786440 | tf_op jit(solution)/shard_map/ppermute | solution.py:558
  37.5 0.7 %attend_far.1 = (f32[144,1024]{1,0:T(8,128)S(1)}, bf16[64,1024]{1,0:T(8,128)(2,1)S(1)}, bf16[80,1024]{1,0:T(8,128)(2,1)S(1)}) custom-call(bf16[4,176,576]{2,1,0:T(8,128)(2,1)S(1)} %soft_weights.1.soft, bf16[608,256]{1,0:T(8,128)(2,1)S(1)} %values.1, bf16[256,1024]{1,0:T(8,128)(2,1)S(1)} %get-tuple-element.70.refs_0_), custom_call_target="tpu_custom_call" | custom-call | tf_op jit(solution)/shard_map/attend_far/pallas_call | solution.py:534
  38.3 0.5 collective-permute-start.13
  38.8 0.4 grad_rows_kept.1
  39.2 0.7 %collective-permute-done.13.refs_0_ = bf16[64,1024]{1,0:T(8,128)(2,1)S(1)} collective-permute-done((bf16[64,1024]{1,0:T(8,128)(2,1)S(1)}, bf16[64,1024]{1,0:T(8,128)(2,1)S(1)}, u32[]{:S(2)}, u32[]{:S(2)}) %collective-permute-start.13) | collective-permute-done | bytes 131104 | tf_op jit(solution)/shard_map/ppermute | solution.py:35
  39.9 1.6 %collective-permute-done.11 = bf16[2,256,256]{2,1,0:T(8,128)(2,1)S(1)} collective-permute-done((bf16[2,256,256]{2,1,0:T(8,128)(2,1)S(1)}, bf16[2,256,256]{2,1,0:T(8,128)(2,1)S(1)}, u32[]{:S(2)}, u32[]{:S(2)}) %collective-permute-start.11) | collective-permute-done | bytes 262176 | tf_op jit(solution)/shard_map/ppermute | solution.py:558
  41.7 1.8 %collective-permute-start.17 = (bf16[144,1024]{1,0:T(8,128)(2,1)S(1)}, bf16[144,1024]{1,0:T(8,128)(2,1)S(1)}, u32[]{:S(2)}, u32[]{:S(2)}) collective-permute-start(bf16[144,1024]{1,0:T(8,128)(2,1)S(1)} %onward.1), channel_id=1, source_target_pairs={{0,8},{4,12},{8,0},{12,4},{16,24},{20,28},{24,16},{28,20},{1,9},{5... | collective-permute-start | bytes 884744 | tf_op jit(solution)/shard_map/ppermute | solution.py:35
  43.6 3.1 %collective-permute-done.15 = bf16[256,256]{1,0:T(8,128)(2,1)S(1)} collective-permute-done((bf16[256,256]{1,0:T(8,128)(2,1)S(1)}, bf16[256,256]{1,0:T(8,128)(2,1)S(1)}, u32[]{:S(2)}, u32[]{:S(2)}) %collective-permute-start.15) | collective-permute-done | bytes 131104 | tf_op jit(solution)/shard_map/ppermute | solution.py:561
  46.7 2.6 %collective-permute-start.16 = (bf16[256,256]{1,0:T(8,128)(2,1)S(1)}, bf16[256,256]{1,0:T(8,128)(2,1)S(1)}, u32[]{:S(2)}, u32[]{:S(2)}) collective-permute-start(bf16[256,256]{1,0:T(8,128)(2,1)S(1)} %fusion.3), channel_id=1, source_target_pairs={{0,16},{4,20},{8,24},{12,28},{16,0},{20,4},{24,8},{28,12},{1,17},{... | collective-permute-start | bytes 393224 | tf_op jit(solution)/shard_map/ppermute | solution.py:35
  49.4 0.7 %attend_near.1 = (f32[144,1024]{1,0:T(8,128)S(1)}, bf16[144,1024]{1,0:T(8,128)(2,1)S(1)}) custom-call(bf16[4,176,576]{2,1,0:T(8,128)(2,1)S(1)} %soft_weights.1.soft, bf16[608,256]{1,0:T(8,128)(2,1)S(1)} %values.1, bf16[256,1024]{1,0:T(8,128)(2,1)S(1)} %get-tuple-element.70.refs_0_), custom_call_target="tpu_custom_call" | custom-call | tf_op jit(solution)/shard_map/attend_near/pallas_call | solution.py:534
  50.2 3.3 %collective-permute-done.16 = bf16[256,256]{1,0:T(8,128)(2,1)S(1)} collective-permute-done((bf16[256,256]{1,0:T(8,128)(2,1)S(1)}, bf16[256,256]{1,0:T(8,128)(2,1)S(1)}, u32[]{:S(2)}, u32[]{:S(2)}) %collective-permute-start.16) | collective-permute-done | bytes 131104 | tf_op jit(solution)/shard_map/ppermute | solution.py:35
  53.6 2.8 %collective-permute-start.18 = (bf16[256,256]{1,0:T(8,128)(2,1)S(1)}, bf16[256,256]{1,0:T(8,128)(2,1)S(1)}, u32[]{:S(2)}, u32[]{:S(2)}) collective-permute-start(bf16[256,256]{1,0:T(8,128)(2,1)S(1)} %add_convert_fusion.refs_0_), channel_id=1, source_target_pairs={{0,8},{4,12},{8,0},{12,4},{16,24},{20,28},{24,16},{28,20},{1,9},{5... | collective-permute-start | bytes 393224 | tf_op jit(solution)/shard_map/ppermute | solution.py:35
  56.4 0.8 %finish.1 = (bf16[128,1024]{1,0:T(8,128)(2,1)}, bf16[8,1024]{1,0:T(8,128)(2,1)}) custom-call(s32[1]{0:T(128)S(6)} %copy.15.lengths, bf16[128,1024]{1,0:T(8,128)(2,1)S(1)} %bitcast.16, f32[144,1024]{1,0:T(8,128)S(1)} %get-tuple-element.77.keep, bf16[144,1024]{1,0:T(8,128)(2,1)S(1)} %collective-permute-done.17.back, ...), custom_call_target="tpu_custom_call" | custom-call | tf_op jit(solution)/shard_map/finish/pallas_call | solution.py:576
  57.2 2.1 %collective-permute-done.18.refs_1_ = bf16[256,256]{1,0:T(8,128)(2,1)S(1)} collective-permute-done((bf16[256,256]{1,0:T(8,128)(2,1)S(1)}, bf16[256,256]{1,0:T(8,128)(2,1)S(1)}, u32[]{:S(2)}, u32[]{:S(2)}) %collective-permute-start.18) | collective-permute-done | bytes 131104 | tf_op jit(solution)/shard_map/ppermute | solution.py:35
  59.3 0.9 %columns.1.refs_1_ = f32[256,1024]{1,0:T(8,128)} custom-call(bf16[256,256]{1,0:T(8,128)(2,1)S(1)} %add_convert_fusion.refs_0_, bf16[256,256]{1,0:T(8,128)(2,1)S(1)} %collective-permute-done.18.refs_1_, bf16[256,256]{1,0:T(8,128)(2,1)S(1)} %collective-permute-done.21.refs_2_), custom_call_target="tpu_custom_call" | custom-call | tf_op jit(solution)/shard_map/columns/pallas_call | solution.py:593
  60.2 0.4 collective-permute-done.20.refs_0_
  60.6 0.7 %columns_rest.1 = f32[256,1024]{1,0:T(8,128)} custom-call(bf16[256,256]{1,0:T(8,128)(2,1)S(1)} %collective-permute-done.20.refs_0_, f32[256,1024]{1,0:T(8,128)} %columns.1.refs_1_), custom_call_target="tpu_custom_call", output_to_operand_aliasing={{}: (1, {})} | custom-call | tf_op jit(solution)/shard_map/columns_rest/pallas_call | solution.py:593
  (38 shorter events, 1.2 us)
Async XLA Ops:
  0.6 7.2 %copy-start.3 = (bf16[256,1024]{1,0:T(8,128)(2,1)S(1)}, bf16[256,1024]{1,0:T(8,128)(2,1)}, u32[]{:S(2)}) copy-start(bf16[256,1024]{1,0:T(8,128)(2,1)} %own) | copy-start | bytes 1572868
  3.2 20.3 %collective-permute-start = (bf16[2,256,768]{2,1,0:T(8,128)(2,1)}, bf16[2,256,768]{2,1,0:T(8,128)(2,1)S(1)}, u32[]{:S(2)}, u32[]{:S(2)}) collective-permute-start(bf16[2,256,768]{2,1,0:T(8,128)(2,1)} %get-tuple-element.46.mine), channel_id=1, source_target_pairs={{0,1},{1,0},{2,3},{3,2},{4,6},{5,7},{6,4},{7,5},{8,9},{9,8},{10,11... | collective-permute-start | bytes 2359304 | tf_op jit(solution)/shard_map/ppermute | solution.py:408
  6.2 17.3 %collective-permute-start.1 = (bf16[288,1024]{1,0:T(8,128)(2,1)}, bf16[288,1024]{1,0:T(8,128)(2,1)S(1)}, u32[]{:S(2)}, u32[]{:S(2)}) collective-permute-start(bf16[288,1024]{1,0:T(8,128)(2,1)} %get-tuple-element.44.tokens), channel_id=1, source_target_pairs={{0,8},{4,12},{8,0},{12,4},{16,24},{20,28},{24,16},{28,20},{1,9},{5... | collective-permute-start | bytes 1769480 | tf_op jit(solution)/shard_map/ppermute | solution.py:35
  7.8 15.7 %collective-permute-start.2 = (bf16[288,1024]{1,0:T(8,128)(2,1)}, bf16[288,1024]{1,0:T(8,128)(2,1)S(1)}, u32[]{:S(2)}, u32[]{:S(2)}) collective-permute-start(bf16[288,1024]{1,0:T(8,128)(2,1)} %get-tuple-element.44.tokens), channel_id=1, source_target_pairs={{0,4},{4,0},{8,12},{12,8},{16,20},{20,16},{24,28},{28,24},{1,5},{5... | collective-permute-start | bytes 1769480 | tf_op jit(solution)/shard_map/ppermute | solution.py:35
  7.8 15.7 %collective-permute-start.5 = (bf16[256,1024]{1,0:T(8,128)(2,1)S(1)}, bf16[256,1024]{1,0:T(8,128)(2,1)S(1)}, u32[]{:S(2)}, u32[]{:S(2)}) collective-permute-start(bf16[256,1024]{1,0:T(8,128)(2,1)S(1)} %copy-done.3), channel_id=1, source_target_pairs={{0,1},{4,2},{12,15},{5,4},{1,7},{9,10},{10,11},{14,8},{6,5},{15,14... | collective-permute-start | bytes 1572872 | tf_op jit(solution)/shard_map/ppermute | solution.py:409
  10.5 17.2 %copy-start.2 = (bf16[288,1024]{1,0:T(8,128)(2,1)S(1)}, bf16[288,1024]{1,0:T(8,128)(2,1)}, u32[]{:S(2)}) copy-start(bf16[288,1024]{1,0:T(8,128)(2,1)} %get-tuple-element.44.tokens) | copy-start | bytes 1769476
  10.5 0.8 %collective-permute-start.3 = (bf16[32,1024]{1,0:T(8,128)(2,1)}, bf16[32,1024]{1,0:T(8,128)(2,1)S(1)}, u32[]{:S(2)}, u32[]{:S(2)}) collective-permute-start(bf16[32,1024]{1,0:T(8,128)(2,1)} %get-tuple-element.47), channel_id=1, source_target_pairs={{12,16},{13,17},{14,18},{15,19}} | collective-permute-start | bytes 196616 | tf_op jit(solution)/shard_map/ppermute | solution.py:403
  11.3 0.7 %collective-permute-start.4 = (bf16[32,1024]{1,0:T(8,128)(2,1)}, bf16[32,1024]{1,0:T(8,128)(2,1)S(1)}, u32[]{:S(2)}, u32[]{:S(2)}) collective-permute-start(bf16[32,1024]{1,0:T(8,128)(2,1)} %get-tuple-element.47), channel_id=1, source_target_pairs={{12,24},{13,25},{14,26},{15,27}} | collective-permute-start | bytes 196616 | tf_op jit(solution)/shard_map/ppermute | solution.py:403
  23.5 9.6 %collective-permute-start.10 = (bf16[256,1024]{1,0:T(8,128)(2,1)S(1)}, bf16[256,1024]{1,0:T(8,128)(2,1)S(1)}, u32[]{:S(2)}, u32[]{:S(2)}) collective-permute-start(bf16[256,1024]{1,0:T(8,128)(2,1)S(1)} %collective-permute-done.5.came), channel_id=1, source_target_pairs={{15,3},{10,6},{5,9},{0,12},{31,19},{26,22},{21,25},{16,28}} | collective-permute-start | bytes 1572872 | tf_op jit(solution)/shard_map/ppermute | solution.py:413
  25.0 2.7 %collective-permute-start.6 = (bf16[176,1024]{1,0:T(8,128)(2,1)S(1)}, bf16[176,1024]{1,0:T(8,128)(2,1)S(1)}, u32[]{:S(2)}, u32[]{:S(2)}) collective-permute-start(bf16[176,1024]{1,0:T(8,128)(2,1)S(1)} %get-tuple-element.54.far), channel_id=1, source_target_pairs={{0,4},{4,0},{8,12},{12,8},{16,20},{20,16},{24,28},{28,24},{1,5},{5... | collective-permute-start | bytes 1081352 | tf_op jit(solution)/shard_map/ppermute | solution.py:35
  25.0 4.1 %collective-permute-start.8 = (bf16[256,768]{1,0:T(8,128)(2,1)S(1)}, bf16[256,768]{1,0:T(8,128)(2,1)S(1)}, u32[]{:S(2)}, u32[]{:S(2)}) collective-permute-start(bf16[256,768]{1,0:T(8,128)(2,1)S(1)} %get-tuple-element.64), channel_id=1, source_target_pairs={{0,4},{4,0},{8,12},{12,8},{16,20},{20,16},{24,28},{28,24},{1,5},{5... | collective-permute-start | bytes 1179656 | tf_op jit(solution)/shard_map/ppermute | solution.py:35
  25.5 2.1 %collective-permute-start.7 = (bf16[144,1024]{1,0:T(8,128)(2,1)S(1)}, bf16[144,1024]{1,0:T(8,128)(2,1)S(1)}, u32[]{:S(2)}, u32[]{:S(2)}) collective-permute-start(bf16[144,1024]{1,0:T(8,128)(2,1)S(1)} %get-tuple-element.55.far_grads), channel_id=1, source_target_pairs={{0,4},{4,0},{8,12},{12,8},{16,20},{20,16},{24,28},{28,24},{1,5},{5... | collective-permute-start | bytes 884744 | tf_op jit(solution)/shard_map/ppermute | solution.py:35
  25.6 6.4 %collective-permute-start.9 = (bf16[256,512]{1,0:T(8,128)(2,1)S(1)}, bf16[256,512]{1,0:T(8,128)(2,1)S(1)}, u32[]{:S(2)}, u32[]{:S(2)}) collective-permute-start(bf16[256,512]{1,0:T(8,128)(2,1)S(1)} %get-tuple-element.62.beside), channel_id=1, source_target_pairs={{0,2},{1,3},{2,0},{3,1},{4,5},{5,4},{6,7},{7,6},{8,10},{9,11},{10,... | collective-permute-start | bytes 786440 | tf_op jit(solution)/shard_map/ppermute | solution.py:435
  25.7 3.4 %copy-start.1 = (bf16[2,256,768]{2,1,0:T(8,128)(2,1)S(1)}, bf16[2,256,768]{2,1,0:T(8,128)(2,1)}, u32[]{:S(2)}) copy-start(bf16[2,256,768]{2,1,0:T(8,128)(2,1)} %get-tuple-element.46.mine) | copy-start | bytes 2359300
  28.3 8.9 %collective-permute-start.12 = (bf16[256,256]{1,0:T(8,128)(2,1)S(1)}, bf16[256,256]{1,0:T(8,128)(2,1)S(1)}, u32[]{:S(2)}, u32[]{:S(2)}) collective-permute-start(bf16[256,256]{1,0:T(8,128)(2,1)S(1)} %get-tuple-element.63.beside_values), channel_id=1, source_target_pairs={{0,2},{1,3},{2,0},{3,1},{4,5},{5,4},{6,7},{7,6},{8,10},{9,11},{10,... | collective-permute-start | bytes 393224 | tf_op jit(solution)/shard_map/ppermute | solution.py:462
  34.9 6.7 %collective-permute-start.11 = (bf16[2,256,256]{2,1,0:T(8,128)(2,1)S(1)}, bf16[2,256,256]{2,1,0:T(8,128)(2,1)S(1)}, u32[]{:S(2)}, u32[]{:S(2)}) collective-permute-start(bf16[2,256,256]{2,1,0:T(8,128)(2,1)S(1)} %get-tuple-element.68), channel_id=1, source_target_pairs={{0,1},{1,0},{2,3},{3,2},{4,6},{5,7},{6,4},{7,5},{8,9},{9,8},{10,11... | collective-permute-start | bytes 786440 | tf_op jit(solution)/shard_map/ppermute | solution.py:558
  38.2 1.7 %collective-permute-start.14 = (bf16[80,1024]{1,0:T(8,128)(2,1)S(1)}, bf16[80,1024]{1,0:T(8,128)(2,1)S(1)}, u32[]{:S(2)}, u32[]{:S(2)}) collective-permute-start(bf16[80,1024]{1,0:T(8,128)(2,1)S(1)} %get-tuple-element.73), channel_id=1, source_target_pairs={{0,4},{4,0},{8,12},{12,8},{16,20},{20,16},{24,28},{28,24},{1,5},{5... | collective-permute-start | bytes 491528 | tf_op jit(solution)/shard_map/ppermute | solution.py:35
  38.3 1.6 %collective-permute-start.13 = (bf16[64,1024]{1,0:T(8,128)(2,1)S(1)}, bf16[64,1024]{1,0:T(8,128)(2,1)S(1)}, u32[]{:S(2)}, u32[]{:S(2)}) collective-permute-start(bf16[64,1024]{1,0:T(8,128)(2,1)S(1)} %get-tuple-element.72), channel_id=1, source_target_pairs={{0,4},{4,0},{8,12},{12,8},{16,20},{20,16},{24,28},{28,24},{1,5},{5... | collective-permute-start | bytes 393224 | tf_op jit(solution)/shard_map/ppermute | solution.py:35
  41.6 14.7 %copy-start = (bf16[1,8,16,1024]{3,2,1,0:T(8,128)(2,1)S(1)}, bf16[1,8,16,1024]{3,2,1,0:T(8,128)(2,1)}, u32[]{:S(2)}) copy-start(bf16[1,8,16,1024]{3,2,1,0:T(8,128)(2,1)} %param.10) | copy-start | bytes 786436
  41.6 5.0 %collective-permute-start.15 = (bf16[256,256]{1,0:T(8,128)(2,1)S(1)}, bf16[256,256]{1,0:T(8,128)(2,1)S(1)}, u32[]{:S(2)}, u32[]{:S(2)}) collective-permute-start(bf16[256,256]{1,0:T(8,128)(2,1)S(1)} %fusion.4), channel_id=1, source_target_pairs={{0,2},{1,3},{2,0},{3,1},{4,5},{5,4},{6,7},{7,6},{8,10},{9,11},{10,... | collective-permute-start | bytes 393224 | tf_op jit(solution)/shard_map/ppermute | solution.py:561
  41.7 11.8 %collective-permute-start.17 = (bf16[144,1024]{1,0:T(8,128)(2,1)S(1)}, bf16[144,1024]{1,0:T(8,128)(2,1)S(1)}, u32[]{:S(2)}, u32[]{:S(2)}) collective-permute-start(bf16[144,1024]{1,0:T(8,128)(2,1)S(1)} %onward.1), channel_id=1, source_target_pairs={{0,8},{4,12},{8,0},{12,4},{16,24},{20,28},{24,16},{28,20},{1,9},{5... | collective-permute-start | bytes 884744 | tf_op jit(solution)/shard_map/ppermute | solution.py:35
  46.7 6.8 %collective-permute-start.16 = (bf16[256,256]{1,0:T(8,128)(2,1)S(1)}, bf16[256,256]{1,0:T(8,128)(2,1)S(1)}, u32[]{:S(2)}, u32[]{:S(2)}) collective-permute-start(bf16[256,256]{1,0:T(8,128)(2,1)S(1)} %fusion.3), channel_id=1, source_target_pairs={{0,16},{4,20},{8,24},{12,28},{16,0},{20,4},{24,8},{28,12},{1,17},{... | collective-permute-start | bytes 393224 | tf_op jit(solution)/shard_map/ppermute | solution.py:35
  50.1 6.3 %collective-permute-start.19 = (bf16[144,1024]{1,0:T(8,128)(2,1)S(1)}, bf16[144,1024]{1,0:T(8,128)(2,1)S(1)}, u32[]{:S(2)}, u32[]{:S(2)}) collective-permute-start(bf16[144,1024]{1,0:T(8,128)(2,1)S(1)} %get-tuple-element.79), channel_id=1, source_target_pairs={{0,4},{4,0},{8,12},{12,8},{16,20},{20,16},{24,28},{28,24},{1,5},{5... | collective-permute-start | bytes 884744 | tf_op jit(solution)/shard_map/ppermute | solution.py:35
  53.6 5.7 %collective-permute-start.18 = (bf16[256,256]{1,0:T(8,128)(2,1)S(1)}, bf16[256,256]{1,0:T(8,128)(2,1)S(1)}, u32[]{:S(2)}, u32[]{:S(2)}) collective-permute-start(bf16[256,256]{1,0:T(8,128)(2,1)S(1)} %add_convert_fusion.refs_0_), channel_id=1, source_target_pairs={{0,8},{4,12},{8,0},{12,4},{16,24},{20,28},{24,16},{28,20},{1,9},{5... | collective-permute-start | bytes 393224 | tf_op jit(solution)/shard_map/ppermute | solution.py:35
  56.3 3.0 %collective-permute-start.21 = (bf16[256,256]{1,0:T(8,128)(2,1)S(1)}, bf16[256,256]{1,0:T(8,128)(2,1)S(1)}, u32[]{:S(2)}, u32[]{:S(2)}) collective-permute-start(bf16[256,256]{1,0:T(8,128)(2,1)S(1)} %add_convert_fusion.refs_0_), channel_id=1, source_target_pairs={{0,4},{4,0},{8,12},{12,8},{16,20},{20,16},{24,28},{28,24},{1,5},{5... | collective-permute-start | bytes 393224 | tf_op jit(solution)/shard_map/ppermute | solution.py:35
  59.3 1.3 %collective-permute-start.20 = (bf16[256,256]{1,0:T(8,128)(2,1)S(1)}, bf16[256,256]{1,0:T(8,128)(2,1)S(1)}, u32[]{:S(2)}, u32[]{:S(2)}) collective-permute-start(bf16[256,256]{1,0:T(8,128)(2,1)S(1)} %collective-permute-done.18.refs_1_), channel_id=1, source_target_pairs={{0,4},{4,0},{8,12},{12,8},{16,20},{20,16},{24,28},{28,24},{1,5},{5... | collective-permute-start | bytes 393224 | tf_op jit(solution)/shard_map/ppermute | solution.py:35

commit v8 on v7

--- a/solution.py
+++ b/solution.py
@@ -162,7 +162,7 @@
     ).astype(bf16)
 
 
-def weights_kernel(heads, frame_count, segs, crossed, x_all, *refs):
+def weights_kernel(heads, crossed, x_all, bias, *refs):
     if crossed:
         total, last, soft = refs
         rows = last.shape[0]
@@ -178,11 +178,29 @@
     blocks, keys, lanes = soft.shape
     queries = lanes // heads
     halo = keys - queries
-    frames = segs * frame_count
     block = projected.shape[1] // (2 if crossed else 3)
     q_all, k_all = projected[:, :block], projected[:, block : 2 * block]
     if not crossed:
         values[...] = projected[:, 2 * block :]
+    scale = 1.0 / math.sqrt(block // heads)
+    for b in range(blocks):
+        start = b * queries
+        q_b = head_stack(q_all[halo + start : halo + start + queries], heads)
+        scores = (
+            lax.dot_general(k_all[start : start + keys], q_b, NT, preferred_element_type=f32)
+            * scale
+            + bias[min(b, 1)]
+        )
+        exponent = jnp.exp(scores - jnp.max(scores, axis=0, keepdims=True))
+        inverse = 1.0 / jnp.sum(exponent, axis=0, keepdims=True)
+        soft[b] = (exponent * inverse).astype(bf16)
+
+
+def mask_kernel(heads, frame_count, segs, group, bias):
+    _, keys, lanes = bias.shape
+    queries = lanes // heads
+    halo = keys - queries
+    frames = segs * frame_count
     key = lax.broadcasted_iota(jnp.int32, (keys, lanes), 0)
     row = lax.broadcasted_iota(jnp.int32, (keys, lanes), 1)
     for h in range(1, heads):
@@ -198,32 +216,30 @@
     valid_halo = ((key < LEFT) & (at == 0)) | (
         (halo_mem >= 0) & (halo_mem < MEMORY) & (halo_mem >= at)
     )
-    inside = lax.axis_index("seg") >= blocks
-    scale = 1.0 / math.sqrt(block // heads)
-    for b in range(blocks):
-        valid = valid_own | (valid_halo & inside if b == 0 else valid_halo)
-        start = b * queries
-        q_b = head_stack(q_all[halo + start : halo + start + queries], heads)
-        scores = (
-            lax.dot_general(k_all[start : start + keys], q_b, NT, preferred_element_type=f32)
-            * scale
-        )
-        scores = jnp.where(valid, scores, masked_score)
-        exponent = jnp.exp(scores - jnp.max(scores, axis=0, keepdims=True))
-        soft[b] = (exponent / jnp.sum(exponent, axis=0, keepdims=True)).astype(bf16)
-
-
-def grad_kernel(heads, frame_count, segs, crossed, lengths, u_all, soft, x_turned, *refs):
-    outputs = 3 + crossed
-    wo_from, (wo, values, *sent, total) = refs[:-outputs], refs[-outputs:]
+    inside = lax.axis_index("seg") >= group
+    bias[0] = jnp.where(valid_own | (valid_halo & inside), 0.0, masked_score)
+    bias[1] = jnp.where(valid_own | valid_halo, 0.0, masked_score)
+
+
+def back_kernel(u_all, wo, back):
+    back[...] = lax.dot_general(u_all[...], wo[...], NT, preferred_element_type=f32)
+
+
+def grad_kernel(heads, frame_count, segs, crossed, lengths, u_all, soft, x_turned, early, *refs):
+    outputs = 4 + crossed
+    wo_from, (wo, values, *sent, total, back) = refs[:-outputs], refs[-outputs:]
     blocks, keys, lanes = soft.shape
     queries = lanes // heads
     frames = segs * frame_count
     wo[...] = wo_from[0][...]
+    back[...] = early[...]
     if len(wo_from) > 1:
-        opposite = (lax.axis_index("fsdp") ^ member_of()) == 3
-        wo[...] = jnp.where(opposite, wo_from[1][...], wo[...])
-    back = lax.dot_general(u_all[...], wo[...], NT, preferred_element_type=f32)
+
+        @pl.when((lax.axis_index("fsdp") ^ member_of()) == 3)
+        def _():
+            wo[...] = wo_from[1][...]
+            back[...] = lax.dot_general(u_all[...], wo[...], NT, preferred_element_type=f32)
+
     row = lax.broadcasted_iota(jnp.int32, (queries, wo.shape[0]), 0)
     seg_of = jnp.where(row < frames, row // frame_count, row - frames - segs)
     first = lax.axis_index("seg") - member_of()
@@ -461,6 +477,22 @@
     if crossed:
         forwarded_values = lax.ppermute(mine_values, both, turned)
 
+    back = pl.pallas_call(
+        back_kernel,
+        in_specs=[vmem] * 2,
+        out_specs=vmem,
+        out_shape=jax.ShapeDtypeStruct((group * queries, block), f32),
+        compiler_params=params(),
+        name="back",
+    )(u_all, wo_near)
+    bias = pl.pallas_call(
+        functools.partial(mask_kernel, heads, frame_count, segs, group),
+        out_specs=vmem,
+        out_shape=jax.ShapeDtypeStruct((2, keys, heads * queries), f32),
+        compiler_params=params(),
+        name="mask",
+    )()
+    back, bias, x_all = lax.optimization_barrier((back, bias, x_all))
     soft_shape = jax.ShapeDtypeStruct((group, keys, heads * queries), bf16)
     values_shape = jax.ShapeDtypeStruct((all_rows, block), bf16)
     if crossed:
@@ -477,14 +509,14 @@
         )(x_all, own_blocks, mine, mine_values, other)
         wqkv_parts = [early, forwarded]
     soft, *values = pl.pallas_call(
-        functools.partial(weights_kernel, heads, frame_count, segs, crossed),
-        in_specs=[vmem] * (1 + len(wqkv_parts)),
+        functools.partial(weights_kernel, heads, crossed),
+        in_specs=[vmem] * (2 + len(wqkv_parts)),
         out_specs=[vmem] * (2 - crossed),
         out_shape=[soft_shape] + [values_shape] * (1 - crossed),
         scratch_shapes=[] if crossed else [pltpu.VMEM((width, 3 * block), bf16)],
         compiler_params=params(),
         name="soft_weights",
-    )(x_all, *wqkv_parts)
+    )(x_all, bias, *wqkv_parts)
     if crossed:
         values = pl.pallas_call(
             values_kernel,
@@ -502,13 +534,16 @@
     sent_shape = [jax.ShapeDtypeStruct((2, rows, block), bf16)] * crossed
     wo_mine, values_grad, *sent = pl.pallas_call(
         functools.partial(grad_kernel, heads, frame_count, segs, crossed),
-        in_specs=[smem] + [vmem] * (3 + len(wo_from)),
+        in_specs=[smem] + [vmem] * (4 + len(wo_from)),
         out_specs=[vmem] * (2 + crossed),
         out_shape=[jax.ShapeDtypeStruct((block, width), bf16), values_grad_shape] + sent_shape,
-        scratch_shapes=[pltpu.VMEM((all_rows, block), f32)],
+        scratch_shapes=[
+            pltpu.VMEM((all_rows, block), f32),
+            pltpu.VMEM((group * queries, block), f32),
+        ],
         compiler_params=params(),
         name="values_grad",
-    )(lengths, u_all, soft, x_turned, *wo_from)
+    )(lengths, u_all, soft, x_turned, back, *wo_from)
 
     def grad_rows(which, shapes):
         return pl.pallas_call(

time: 61.6 us -> 61.1 us (level)
    ppermute x13, starting transfers between devices: 10.1 us -> 8.96 us  [swapped(): return lax.ppermute(array, axis, [(i, i ^ bit) for i in range(size)])]
    ppermute x1, starting transfers between devices: 0.1 us -> 1.01 us  [on_device(): last = lax.ppermute(passing, both, turned)]
    ppermute x1, waiting for transfers between devices: 1.95 us -> 1.27 us  [on_device(): forwarded = lax.ppermute(mine, both, turned)]
    pallas_call x1 -> x3, Pallas kernels: 1.16 us -> 1.69 us  [the longest x1 1.1 us: on_device(): pl.pallas_call(functools.partial(weights_kernel, heads, crossed), in_spec...]
  transfers between devices with their start and end apart: 22 -> 22, of which waited for: 10 -> 9; matrix products, arithmetic and copies ran while one was open for 0% -> 0% of each run, Pallas kernels for 14% -> 14%
where the time goes in v8:
time: 61.1 us; the launch traced here: 60.9 us
  waiting for transfers between devices  26.5 us (43%)
  starting transfers between devices  20.9 us (34%)
  Pallas kernels  11.7 us (19%)
  between operations  1.61 us (3%)
    ppermute x1, waiting for transfers between devices, on_device(): wo_came = lax.ppermute(w_out, both, first)  11.5 us
    ppermute x13, starting transfers between devices, swapped(): return lax.ppermute(array, axis, [(i, i ^ bit) for i in range(size)])  8.96 us
    ppermute x13, waiting for transfers between devices, swapped(): return lax.ppermute(array, axis, [(i, i ^ bit) for i in range(size)])  8.93 us
    ppermute x1, waiting for transfers between devices, on_device(): last = lax.ppermute(passing, both, turned)  3.1 us
    ppermute x1, starting transfers between devices, on_device(): came = lax.ppermute(own_blocks, both, straight)  3 us
    ppermute x1, starting transfers between devices, on_device(): wo_came = lax.ppermute(w_out, both, first)  2.69 us
    pallas_call x1, Pallas kernels, on_device(): pl.pallas_call(functools.partial(pack_kernel, frame_count), in_specs=[hbm...  2.57 us
    ppermute x1, starting transfers between devices, on_device(): came = lax.ppermute(sent, both, straight)  2.38 us
  transfers between devices with their start and end apart: 22, of which 9 were waited for; matrix products, arithmetic and copies ran while one was open for 0% of the time, Pallas kernels for 14%

profile of v8, /device:TPU:0, one launch (start us, length us, event | category | flops | bytes accessed | tf_op | source)
XLA Modules:
  0.0 60.9 jit_solution(15118203316457847226)
XLA Ops:
  0.6 2.6 %pack.1 = (bf16[2,256,768]{2,1,0:T(8,128)(2,1)}, bf16[288,1024]{1,0:T(8,128)(2,1)}, bf16[32,1024]{1,0:T(8,128)(2,1)}) custom-call(bf16[256,1024]{1,0:T(8,128)(2,1)} %wq.1, bf16[256,1024]{1,0:T(8,128)(2,1)} %wk.1, bf16[256,1024]{1,0:T(8,128)(2,1)} %wv.1, bf16[128,1024]{1,0:T(8,128)(2,1)} %bitcast.15, bf16[128,1024]{1,0:T(8,128)(2,1)} %bitcast.17, ...), custom_call_target="tpu_custom_call" | custom-call | tf_op jit(solution)/shard_map/pack/pallas_call | solution.py:391
  3.2 3.0 %collective-permute-start = (bf16[2,256,768]{2,1,0:T(8,128)(2,1)}, bf16[2,256,768]{2,1,0:T(8,128)(2,1)S(1)}, u32[]{:S(2)}, u32[]{:S(2)}) collective-permute-start(bf16[2,256,768]{2,1,0:T(8,128)(2,1)} %get-tuple-element.49.mine), channel_id=1, source_target_pairs={{0,1},{1,0},{2,3},{3,2},{4,6},{5,7},{6,4},{7,5},{8,9},{9,8},{10,11... | collective-permute-start | bytes 2359304 | tf_op jit(solution)/shard_map/ppermute | solution.py:424
  6.2 1.6 %collective-permute-start.1 = (bf16[288,1024]{1,0:T(8,128)(2,1)}, bf16[288,1024]{1,0:T(8,128)(2,1)S(1)}, u32[]{:S(2)}, u32[]{:S(2)}) collective-permute-start(bf16[288,1024]{1,0:T(8,128)(2,1)} %get-tuple-element.47.tokens), channel_id=1, source_target_pairs={{0,8},{4,12},{8,0},{12,4},{16,24},{20,28},{24,16},{28,20},{1,9},{5... | collective-permute-start | bytes 1769480 | tf_op jit(solution)/shard_map/ppermute | solution.py:35
  7.8 2.7 %collective-permute-start.5 = (bf16[256,1024]{1,0:T(8,128)(2,1)S(1)}, bf16[256,1024]{1,0:T(8,128)(2,1)S(1)}, u32[]{:S(2)}, u32[]{:S(2)}) collective-permute-start(bf16[256,1024]{1,0:T(8,128)(2,1)S(1)} %copy-done.3), channel_id=1, source_target_pairs={{0,1},{4,2},{12,15},{5,4},{1,7},{9,10},{10,11},{14,8},{6,5},{15,14... | collective-permute-start | bytes 1572872 | tf_op jit(solution)/shard_map/ppermute | solution.py:425
  10.5 0.8 %collective-permute-start.3 = (bf16[32,1024]{1,0:T(8,128)(2,1)}, bf16[32,1024]{1,0:T(8,128)(2,1)S(1)}, u32[]{:S(2)}, u32[]{:S(2)}) collective-permute-start(bf16[32,1024]{1,0:T(8,128)(2,1)} %get-tuple-element.50), channel_id=1, source_target_pairs={{12,16},{13,17},{14,18},{15,19}} | collective-permute-start | bytes 196616 | tf_op jit(solution)/shard_map/ppermute | solution.py:419
  11.3 0.7 %collective-permute-start.4 = (bf16[32,1024]{1,0:T(8,128)(2,1)}, bf16[32,1024]{1,0:T(8,128)(2,1)S(1)}, u32[]{:S(2)}, u32[]{:S(2)}) collective-permute-start(bf16[32,1024]{1,0:T(8,128)(2,1)} %get-tuple-element.50), channel_id=1, source_target_pairs={{12,24},{13,25},{14,26},{15,27}} | collective-permute-start | bytes 196616 | tf_op jit(solution)/shard_map/ppermute | solution.py:419
  12.0 11.5 %collective-permute-done.5.came = bf16[256,1024]{1,0:T(8,128)(2,1)S(1)} collective-permute-done((bf16[256,1024]{1,0:T(8,128)(2,1)S(1)}, bf16[256,1024]{1,0:T(8,128)(2,1)S(1)}, u32[]{:S(2)}, u32[]{:S(2)}) %collective-permute-start.5) | collective-permute-done | bytes 524320 | tf_op jit(solution)/shard_map/ppermute | solution.py:425
  23.5 1.3 %collective-permute-start.10 = (bf16[256,1024]{1,0:T(8,128)(2,1)S(1)}, bf16[256,1024]{1,0:T(8,128)(2,1)S(1)}, u32[]{:S(2)}, u32[]{:S(2)}) collective-permute-start(bf16[256,1024]{1,0:T(8,128)(2,1)S(1)} %collective-permute-done.5.came), channel_id=1, source_target_pairs={{15,3},{10,6},{5,9},{0,12},{31,19},{26,22},{21,25},{16,28}} | collective-permute-start | bytes 1572872 | tf_op jit(solution)/shard_map/ppermute | solution.py:429
  25.0 0.5 collective-permute-start.8
  25.7 2.0 %collective-permute-done.7.last_grads = bf16[144,1024]{1,0:T(8,128)(2,1)S(1)} collective-permute-done((bf16[144,1024]{1,0:T(8,128)(2,1)S(1)}, bf16[144,1024]{1,0:T(8,128)(2,1)S(1)}, u32[]{:S(2)}, u32[]{:S(2)}) %collective-permute-start.7) | collective-permute-done | bytes 294944 | tf_op jit(solution)/shard_map/ppermute | solution.py:35
  27.7 0.6 %merge.1 = (bf16[608,1024]{1,0:T(8,128)(2,1)S(1)}, bf16[1024,608]{1,0:T(8,128)(2,1)S(1)}, bf16[576,1024]{1,0:T(8,128)(2,1)S(1)}) custom-call(bf16[288,1024]{1,0:T(8,128)(2,1)S(1)} %copy-done.2, bf16[288,1024]{1,0:T(8,128)(2,1)S(1)} %collective-permute-done.2.near, bf16[176,1024]{1,0:T(8,128)(2,1)S(1)} %get-tuple-element.57.far, ...), custom_call_target="tpu_custom_call" | custom-call | tf_op jit(solution)/shard_map/merge/pallas_call | solution.py:464
  29.3 0.5 back.1.early
  29.8 0.9 %early.1 = (f32[608,512]{1,0:T(8,128)S(1)}, f32[608,256]{1,0:T(8,128)S(1)}) custom-call(bf16[608,1024]{1,0:T(8,128)(2,1)S(1)} %get-tuple-element.66.x_all, bf16[2,256,768]{2,1,0:T(8,128)(2,1)S(1)} %copy-done.1, bf16[256,512]{1,0:T(8,128)(2,1)S(1)} %get-tuple-element.68.beside, bf16[256,256]{1,0:T(8,128)(2,1)S(1)} %get-tuple-element.69.beside_values, ...), custom_call_target="tpu_custom_call" | custom-call | tf_op jit(solution)/shard_map/early/pallas_call | solution.py:499
  30.7 1.3 %collective-permute-done.9.refs_1_ = bf16[256,512]{1,0:T(8,128)(2,1)S(1)} collective-permute-done((bf16[256,512]{1,0:T(8,128)(2,1)S(1)}, bf16[256,512]{1,0:T(8,128)(2,1)S(1)}, u32[]{:S(2)}, u32[]{:S(2)}) %collective-permute-start.9) | collective-permute-done | bytes 262176 | tf_op jit(solution)/shard_map/ppermute | solution.py:451
  32.0 1.1 %soft_weights.1.soft = bf16[4,176,576]{2,1,0:T(8,128)(2,1)S(1)} custom-call(bf16[608,1024]{1,0:T(8,128)(2,1)S(1)} %get-tuple-element.66.x_all, f32[2,176,576]{2,1,0:T(8,128)S(1)} %mask.1.bias, f32[608,512]{1,0:T(8,128)S(1)} %get-tuple-element.71.refs_0_, bf16[256,512]{1,0:T(8,128)(2,1)S(1)} %collective-permute-done.9.refs_1_), custom_call_target="tpu_custom_call" | custom-call | tf_op jit(solution)/shard_map/soft_weights/pallas_call | solution.py:511
  33.1 1.2 %values_grad.1 = (bf16[256,1024]{1,0:T(8,128)(2,1)S(1)}, bf16[608,256]{1,0:T(8,128)(2,1)S(1)}, bf16[2,256,256]{2,1,0:T(8,128)(2,1)S(1)}) custom-call(s32[1]{0:T(128)S(6)} %copy.15.lengths, bf16[576,1024]{1,0:T(8,128)(2,1)S(1)} %get-tuple-element.60.u_all, bf16[4,176,576]{2,1,0:T(8,128)(2,1)S(1)} %soft_weights.1.soft, ...), custom_call_target="tpu_custom_call" | custom-call | tf_op jit(solution)/shard_map/values_grad/pallas_call | solution.py:535
  34.3 2.4 %collective-permute-start.11 = (bf16[2,256,256]{2,1,0:T(8,128)(2,1)S(1)}, bf16[2,256,256]{2,1,0:T(8,128)(2,1)S(1)}, u32[]{:S(2)}, u32[]{:S(2)}) collective-permute-start(bf16[2,256,256]{2,1,0:T(8,128)(2,1)S(1)} %get-tuple-element.74), channel_id=1, source_target_pairs={{0,1},{1,0},{2,3},{3,2},{4,6},{5,7},{6,4},{7,5},{8,9},{9,8},{10,11... | collective-permute-start | bytes 786440 | tf_op jit(solution)/shard_map/ppermute | solution.py:593
  36.9 0.7 %attend_far.1 = (f32[144,1024]{1,0:T(8,128)S(1)}, bf16[64,1024]{1,0:T(8,128)(2,1)S(1)}, bf16[80,1024]{1,0:T(8,128)(2,1)S(1)}) custom-call(bf16[4,176,576]{2,1,0:T(8,128)(2,1)S(1)} %soft_weights.1.soft, bf16[608,256]{1,0:T(8,128)(2,1)S(1)} %values.1, bf16[256,1024]{1,0:T(8,128)(2,1)S(1)} %get-tuple-element.76.refs_0_), custom_call_target="tpu_custom_call" | custom-call | tf_op jit(solution)/shard_map/attend_far/pallas_call | solution.py:569
  37.7 0.5 collective-permute-start.13
  38.6 0.7 %collective-permute-done.13.refs_0_ = bf16[64,1024]{1,0:T(8,128)(2,1)S(1)} collective-permute-done((bf16[64,1024]{1,0:T(8,128)(2,1)S(1)}, bf16[64,1024]{1,0:T(8,128)(2,1)S(1)}, u32[]{:S(2)}, u32[]{:S(2)}) %collective-permute-start.13) | collective-permute-done | bytes 131104 | tf_op jit(solution)/shard_map/ppermute | solution.py:35
  39.4 1.7 %collective-permute-done.11 = bf16[2,256,256]{2,1,0:T(8,128)(2,1)S(1)} collective-permute-done((bf16[2,256,256]{2,1,0:T(8,128)(2,1)S(1)}, bf16[2,256,256]{2,1,0:T(8,128)(2,1)S(1)}, u32[]{:S(2)}, u32[]{:S(2)}) %collective-permute-start.11) | collective-permute-done | bytes 262176 | tf_op jit(solution)/shard_map/ppermute | solution.py:593
  41.1 1.0 %collective-permute-start.15 = (bf16[256,256]{1,0:T(8,128)(2,1)S(1)}, bf16[256,256]{1,0:T(8,128)(2,1)S(1)}, u32[]{:S(2)}, u32[]{:S(2)}) collective-permute-start(bf16[256,256]{1,0:T(8,128)(2,1)S(1)} %fusion.4), channel_id=1, source_target_pairs={{0,2},{1,3},{2,0},{3,1},{4,5},{5,4},{6,7},{7,6},{8,10},{9,11},{10,... | collective-permute-start | bytes 393224 | tf_op jit(solution)/shard_map/ppermute | solution.py:596
  42.1 0.9 %collective-permute-start.17 = (bf16[144,1024]{1,0:T(8,128)(2,1)S(1)}, bf16[144,1024]{1,0:T(8,128)(2,1)S(1)}, u32[]{:S(2)}, u32[]{:S(2)}) collective-permute-start(bf16[144,1024]{1,0:T(8,128)(2,1)S(1)} %onward.1), channel_id=1, source_target_pairs={{0,8},{4,12},{8,0},{12,4},{16,24},{20,28},{24,16},{28,20},{1,9},{5... | collective-permute-start | bytes 884744 | tf_op jit(solution)/shard_map/ppermute | solution.py:35
  43.0 3.1 %collective-permute-done.15 = bf16[256,256]{1,0:T(8,128)(2,1)S(1)} collective-permute-done((bf16[256,256]{1,0:T(8,128)(2,1)S(1)}, bf16[256,256]{1,0:T(8,128)(2,1)S(1)}, u32[]{:S(2)}, u32[]{:S(2)}) %collective-permute-start.15) | collective-permute-done | bytes 131104 | tf_op jit(solution)/shard_map/ppermute | solution.py:596
  46.1 2.7 %collective-permute-start.16 = (bf16[256,256]{1,0:T(8,128)(2,1)S(1)}, bf16[256,256]{1,0:T(8,128)(2,1)S(1)}, u32[]{:S(2)}, u32[]{:S(2)}) collective-permute-start(bf16[256,256]{1,0:T(8,128)(2,1)S(1)} %fusion.3), channel_id=1, source_target_pairs={{0,16},{4,20},{8,24},{12,28},{16,0},{20,4},{24,8},{28,12},{1,17},{... | collective-permute-start | bytes 393224 | tf_op jit(solution)/shard_map/ppermute | solution.py:35
  48.8 0.7 %attend_near.1 = (f32[144,1024]{1,0:T(8,128)S(1)}, bf16[144,1024]{1,0:T(8,128)(2,1)S(1)}) custom-call(bf16[4,176,576]{2,1,0:T(8,128)(2,1)S(1)} %soft_weights.1.soft, bf16[608,256]{1,0:T(8,128)(2,1)S(1)} %values.1, bf16[256,1024]{1,0:T(8,128)(2,1)S(1)} %get-tuple-element.76.refs_0_), custom_call_target="tpu_custom_call" | custom-call | tf_op jit(solution)/shard_map/attend_near/pallas_call | solution.py:569
  49.6 3.7 %collective-permute-done.16 = bf16[256,256]{1,0:T(8,128)(2,1)S(1)} collective-permute-done((bf16[256,256]{1,0:T(8,128)(2,1)S(1)}, bf16[256,256]{1,0:T(8,128)(2,1)S(1)}, u32[]{:S(2)}, u32[]{:S(2)}) %collective-permute-start.16) | collective-permute-done | bytes 131104 | tf_op jit(solution)/shard_map/ppermute | solution.py:35
  53.3 2.5 %collective-permute-start.18 = (bf16[256,256]{1,0:T(8,128)(2,1)S(1)}, bf16[256,256]{1,0:T(8,128)(2,1)S(1)}, u32[]{:S(2)}, u32[]{:S(2)}) collective-permute-start(bf16[256,256]{1,0:T(8,128)(2,1)S(1)} %add_convert_fusion.refs_0_), channel_id=1, source_target_pairs={{0,8},{4,12},{8,0},{12,4},{16,24},{20,28},{24,16},{28,20},{1,9},{5... | collective-permute-start | bytes 393224 | tf_op jit(solution)/shard_map/ppermute | solution.py:35
  55.9 0.8 %finish.1 = (bf16[128,1024]{1,0:T(8,128)(2,1)}, bf16[8,1024]{1,0:T(8,128)(2,1)}) custom-call(s32[1]{0:T(128)S(6)} %copy.15.lengths, bf16[128,1024]{1,0:T(8,128)(2,1)S(1)} %bitcast.16, f32[144,1024]{1,0:T(8,128)S(1)} %get-tuple-element.83.keep, bf16[144,1024]{1,0:T(8,128)(2,1)S(1)} %collective-permute-done.17.back, ...), custom_call_target="tpu_custom_call" | custom-call | tf_op jit(solution)/shard_map/finish/pallas_call | solution.py:611
  56.7 2.1 %collective-permute-done.18.refs_1_ = bf16[256,256]{1,0:T(8,128)(2,1)S(1)} collective-permute-done((bf16[256,256]{1,0:T(8,128)(2,1)S(1)}, bf16[256,256]{1,0:T(8,128)(2,1)S(1)}, u32[]{:S(2)}, u32[]{:S(2)}) %collective-permute-start.18) | collective-permute-done | bytes 131104 | tf_op jit(solution)/shard_map/ppermute | solution.py:35
  58.8 0.9 %columns.1.refs_1_ = f32[256,1024]{1,0:T(8,128)} custom-call(bf16[256,256]{1,0:T(8,128)(2,1)S(1)} %add_convert_fusion.refs_0_, bf16[256,256]{1,0:T(8,128)(2,1)S(1)} %collective-permute-done.18.refs_1_, bf16[256,256]{1,0:T(8,128)(2,1)S(1)} %collective-permute-done.21.refs_2_), custom_call_target="tpu_custom_call" | custom-call | tf_op jit(solution)/shard_map/columns/pallas_call | solution.py:628
  60.1 0.7 %columns_rest.1 = f32[256,1024]{1,0:T(8,128)} custom-call(bf16[256,256]{1,0:T(8,128)(2,1)S(1)} %collective-permute-done.20.refs_0_, f32[256,1024]{1,0:T(8,128)} %columns.1.refs_1_), custom_call_target="tpu_custom_call", output_to_operand_aliasing={{}: (1, {})} | custom-call | tf_op jit(solution)/shard_map/columns_rest/pallas_call | solution.py:628
  (40 shorter events, 1.9 us)
Async XLA Ops:
  0.6 7.2 %copy-start.3 = (bf16[256,1024]{1,0:T(8,128)(2,1)S(1)}, bf16[256,1024]{1,0:T(8,128)(2,1)}, u32[]{:S(2)}) copy-start(bf16[256,1024]{1,0:T(8,128)(2,1)} %own) | copy-start | bytes 1572868
  3.2 20.3 %collective-permute-start = (bf16[2,256,768]{2,1,0:T(8,128)(2,1)}, bf16[2,256,768]{2,1,0:T(8,128)(2,1)S(1)}, u32[]{:S(2)}, u32[]{:S(2)}) collective-permute-start(bf16[2,256,768]{2,1,0:T(8,128)(2,1)} %get-tuple-element.49.mine), channel_id=1, source_target_pairs={{0,1},{1,0},{2,3},{3,2},{4,6},{5,7},{6,4},{7,5},{8,9},{9,8},{10,11... | collective-permute-start | bytes 2359304 | tf_op jit(solution)/shard_map/ppermute | solution.py:424
  6.2 17.3 %collective-permute-start.1 = (bf16[288,1024]{1,0:T(8,128)(2,1)}, bf16[288,1024]{1,0:T(8,128)(2,1)S(1)}, u32[]{:S(2)}, u32[]{:S(2)}) collective-permute-start(bf16[288,1024]{1,0:T(8,128)(2,1)} %get-tuple-element.47.tokens), channel_id=1, source_target_pairs={{0,8},{4,12},{8,0},{12,4},{16,24},{20,28},{24,16},{28,20},{1,9},{5... | collective-permute-start | bytes 1769480 | tf_op jit(solution)/shard_map/ppermute | solution.py:35
  7.8 15.7 %collective-permute-start.2 = (bf16[288,1024]{1,0:T(8,128)(2,1)}, bf16[288,1024]{1,0:T(8,128)(2,1)S(1)}, u32[]{:S(2)}, u32[]{:S(2)}) collective-permute-start(bf16[288,1024]{1,0:T(8,128)(2,1)} %get-tuple-element.47.tokens), channel_id=1, source_target_pairs={{0,4},{4,0},{8,12},{12,8},{16,20},{20,16},{24,28},{28,24},{1,5},{5... | collective-permute-start | bytes 1769480 | tf_op jit(solution)/shard_map/ppermute | solution.py:35
  7.8 15.7 %collective-permute-start.5 = (bf16[256,1024]{1,0:T(8,128)(2,1)S(1)}, bf16[256,1024]{1,0:T(8,128)(2,1)S(1)}, u32[]{:S(2)}, u32[]{:S(2)}) collective-permute-start(bf16[256,1024]{1,0:T(8,128)(2,1)S(1)} %copy-done.3), channel_id=1, source_target_pairs={{0,1},{4,2},{12,15},{5,4},{1,7},{9,10},{10,11},{14,8},{6,5},{15,14... | collective-permute-start | bytes 1572872 | tf_op jit(solution)/shard_map/ppermute | solution.py:425
  10.5 17.2 %copy-start.2 = (bf16[288,1024]{1,0:T(8,128)(2,1)S(1)}, bf16[288,1024]{1,0:T(8,128)(2,1)}, u32[]{:S(2)}) copy-start(bf16[288,1024]{1,0:T(8,128)(2,1)} %get-tuple-element.47.tokens) | copy-start | bytes 1769476
  10.5 0.8 %collective-permute-start.3 = (bf16[32,1024]{1,0:T(8,128)(2,1)}, bf16[32,1024]{1,0:T(8,128)(2,1)S(1)}, u32[]{:S(2)}, u32[]{:S(2)}) collective-permute-start(bf16[32,1024]{1,0:T(8,128)(2,1)} %get-tuple-element.50), channel_id=1, source_target_pairs={{12,16},{13,17},{14,18},{15,19}} | collective-permute-start | bytes 196616 | tf_op jit(solution)/shard_map/ppermute | solution.py:419
  11.3 0.7 %collective-permute-start.4 = (bf16[32,1024]{1,0:T(8,128)(2,1)}, bf16[32,1024]{1,0:T(8,128)(2,1)S(1)}, u32[]{:S(2)}, u32[]{:S(2)}) collective-permute-start(bf16[32,1024]{1,0:T(8,128)(2,1)} %get-tuple-element.50), channel_id=1, source_target_pairs={{12,24},{13,25},{14,26},{15,27}} | collective-permute-start | bytes 196616 | tf_op jit(solution)/shard_map/ppermute | solution.py:419
  23.5 9.6 %collective-permute-start.10 = (bf16[256,1024]{1,0:T(8,128)(2,1)S(1)}, bf16[256,1024]{1,0:T(8,128)(2,1)S(1)}, u32[]{:S(2)}, u32[]{:S(2)}) collective-permute-start(bf16[256,1024]{1,0:T(8,128)(2,1)S(1)} %collective-permute-done.5.came), channel_id=1, source_target_pairs={{15,3},{10,6},{5,9},{0,12},{31,19},{26,22},{21,25},{16,28}} | collective-permute-start | bytes 1572872 | tf_op jit(solution)/shard_map/ppermute | solution.py:429
  25.0 2.7 %collective-permute-start.6 = (bf16[176,1024]{1,0:T(8,128)(2,1)S(1)}, bf16[176,1024]{1,0:T(8,128)(2,1)S(1)}, u32[]{:S(2)}, u32[]{:S(2)}) collective-permute-start(bf16[176,1024]{1,0:T(8,128)(2,1)S(1)} %get-tuple-element.57.far), channel_id=1, source_target_pairs={{0,4},{4,0},{8,12},{12,8},{16,20},{20,16},{24,28},{28,24},{1,5},{5... | collective-permute-start | bytes 1081352 | tf_op jit(solution)/shard_map/ppermute | solution.py:35
  25.0 4.7 %collective-permute-start.8 = (bf16[256,768]{1,0:T(8,128)(2,1)S(1)}, bf16[256,768]{1,0:T(8,128)(2,1)S(1)}, u32[]{:S(2)}, u32[]{:S(2)}) collective-permute-start(bf16[256,768]{1,0:T(8,128)(2,1)S(1)} %get-tuple-element.70), channel_id=1, source_target_pairs={{0,4},{4,0},{8,12},{12,8},{16,20},{20,16},{24,28},{28,24},{1,5},{5... | collective-permute-start | bytes 1179656 | tf_op jit(solution)/shard_map/ppermute | solution.py:35
  25.5 2.1 %collective-permute-start.7 = (bf16[144,1024]{1,0:T(8,128)(2,1)S(1)}, bf16[144,1024]{1,0:T(8,128)(2,1)S(1)}, u32[]{:S(2)}, u32[]{:S(2)}) collective-permute-start(bf16[144,1024]{1,0:T(8,128)(2,1)S(1)} %get-tuple-element.58.far_grads), channel_id=1, source_target_pairs={{0,4},{4,0},{8,12},{12,8},{16,20},{20,16},{24,28},{28,24},{1,5},{5... | collective-permute-start | bytes 884744 | tf_op jit(solution)/shard_map/ppermute | solution.py:35
  25.6 6.4 %collective-permute-start.9 = (bf16[256,512]{1,0:T(8,128)(2,1)S(1)}, bf16[256,512]{1,0:T(8,128)(2,1)S(1)}, u32[]{:S(2)}, u32[]{:S(2)}) collective-permute-start(bf16[256,512]{1,0:T(8,128)(2,1)S(1)} %get-tuple-element.68.beside), channel_id=1, source_target_pairs={{0,2},{1,3},{2,0},{3,1},{4,5},{5,4},{6,7},{7,6},{8,10},{9,11},{10,... | collective-permute-start | bytes 786440 | tf_op jit(solution)/shard_map/ppermute | solution.py:451
  28.3 8.3 %collective-permute-start.12 = (bf16[256,256]{1,0:T(8,128)(2,1)S(1)}, bf16[256,256]{1,0:T(8,128)(2,1)S(1)}, u32[]{:S(2)}, u32[]{:S(2)}) collective-permute-start(bf16[256,256]{1,0:T(8,128)(2,1)S(1)} %get-tuple-element.69.beside_values), channel_id=1, source_target_pairs={{0,2},{1,3},{2,0},{3,1},{4,5},{5,4},{6,7},{7,6},{8,10},{9,11},{10,... | collective-permute-start | bytes 393224 | tf_op jit(solution)/shard_map/ppermute | solution.py:478
  28.5 1.2 %copy-start.1 = (bf16[2,256,768]{2,1,0:T(8,128)(2,1)S(1)}, bf16[2,256,768]{2,1,0:T(8,128)(2,1)}, u32[]{:S(2)}) copy-start(bf16[2,256,768]{2,1,0:T(8,128)(2,1)} %get-tuple-element.49.mine) | copy-start | bytes 2359300
  34.3 6.7 %collective-permute-start.11 = (bf16[2,256,256]{2,1,0:T(8,128)(2,1)S(1)}, bf16[2,256,256]{2,1,0:T(8,128)(2,1)S(1)}, u32[]{:S(2)}, u32[]{:S(2)}) collective-permute-start(bf16[2,256,256]{2,1,0:T(8,128)(2,1)S(1)} %get-tuple-element.74), channel_id=1, source_target_pairs={{0,1},{1,0},{2,3},{3,2},{4,6},{5,7},{6,4},{7,5},{8,9},{9,8},{10,11... | collective-permute-start | bytes 786440 | tf_op jit(solution)/shard_map/ppermute | solution.py:593
  37.6 1.7 %collective-permute-start.14 = (bf16[80,1024]{1,0:T(8,128)(2,1)S(1)}, bf16[80,1024]{1,0:T(8,128)(2,1)S(1)}, u32[]{:S(2)}, u32[]{:S(2)}) collective-permute-start(bf16[80,1024]{1,0:T(8,128)(2,1)S(1)} %get-tuple-element.79), channel_id=1, source_target_pairs={{0,4},{4,0},{8,12},{12,8},{16,20},{20,16},{24,28},{28,24},{1,5},{5... | collective-permute-start | bytes 491528 | tf_op jit(solution)/shard_map/ppermute | solution.py:35
  37.7 1.6 %collective-permute-start.13 = (bf16[64,1024]{1,0:T(8,128)(2,1)S(1)}, bf16[64,1024]{1,0:T(8,128)(2,1)S(1)}, u32[]{:S(2)}, u32[]{:S(2)}) collective-permute-start(bf16[64,1024]{1,0:T(8,128)(2,1)S(1)} %get-tuple-element.78), channel_id=1, source_target_pairs={{0,4},{4,0},{8,12},{12,8},{16,20},{20,16},{24,28},{28,24},{1,5},{5... | collective-permute-start | bytes 393224 | tf_op jit(solution)/shard_map/ppermute | solution.py:35
  41.0 14.8 %copy-start = (bf16[1,8,16,1024]{3,2,1,0:T(8,128)(2,1)S(1)}, bf16[1,8,16,1024]{3,2,1,0:T(8,128)(2,1)}, u32[]{:S(2)}) copy-start(bf16[1,8,16,1024]{3,2,1,0:T(8,128)(2,1)} %param.10) | copy-start | bytes 786436
  41.1 5.0 %collective-permute-start.15 = (bf16[256,256]{1,0:T(8,128)(2,1)S(1)}, bf16[256,256]{1,0:T(8,128)(2,1)S(1)}, u32[]{:S(2)}, u32[]{:S(2)}) collective-permute-start(bf16[256,256]{1,0:T(8,128)(2,1)S(1)} %fusion.4), channel_id=1, source_target_pairs={{0,2},{1,3},{2,0},{3,1},{4,5},{5,4},{6,7},{7,6},{8,10},{9,11},{10,... | collective-permute-start | bytes 393224 | tf_op jit(solution)/shard_map/ppermute | solution.py:596
  42.1 11.2 %collective-permute-start.17 = (bf16[144,1024]{1,0:T(8,128)(2,1)S(1)}, bf16[144,1024]{1,0:T(8,128)(2,1)S(1)}, u32[]{:S(2)}, u32[]{:S(2)}) collective-permute-start(bf16[144,1024]{1,0:T(8,128)(2,1)S(1)} %onward.1), channel_id=1, source_target_pairs={{0,8},{4,12},{8,0},{12,4},{16,24},{20,28},{24,16},{28,20},{1,9},{5... | collective-permute-start | bytes 884744 | tf_op jit(solution)/shard_map/ppermute | solution.py:35
  46.1 7.2 %collective-permute-start.16 = (bf16[256,256]{1,0:T(8,128)(2,1)S(1)}, bf16[256,256]{1,0:T(8,128)(2,1)S(1)}, u32[]{:S(2)}, u32[]{:S(2)}) collective-permute-start(bf16[256,256]{1,0:T(8,128)(2,1)S(1)} %fusion.3), channel_id=1, source_target_pairs={{0,16},{4,20},{8,24},{12,28},{16,0},{20,4},{24,8},{28,12},{1,17},{... | collective-permute-start | bytes 393224 | tf_op jit(solution)/shard_map/ppermute | solution.py:35
  49.5 6.3 %collective-permute-start.19 = (bf16[144,1024]{1,0:T(8,128)(2,1)S(1)}, bf16[144,1024]{1,0:T(8,128)(2,1)S(1)}, u32[]{:S(2)}, u32[]{:S(2)}) collective-permute-start(bf16[144,1024]{1,0:T(8,128)(2,1)S(1)} %get-tuple-element.85), channel_id=1, source_target_pairs={{0,4},{4,0},{8,12},{12,8},{16,20},{20,16},{24,28},{28,24},{1,5},{5... | collective-permute-start | bytes 884744 | tf_op jit(solution)/shard_map/ppermute | solution.py:35
  53.3 5.5 %collective-permute-start.18 = (bf16[256,256]{1,0:T(8,128)(2,1)S(1)}, bf16[256,256]{1,0:T(8,128)(2,1)S(1)}, u32[]{:S(2)}, u32[]{:S(2)}) collective-permute-start(bf16[256,256]{1,0:T(8,128)(2,1)S(1)} %add_convert_fusion.refs_0_), channel_id=1, source_target_pairs={{0,8},{4,12},{8,0},{12,4},{16,24},{20,28},{24,16},{28,20},{1,9},{5... | collective-permute-start | bytes 393224 | tf_op jit(solution)/shard_map/ppermute | solution.py:35
  55.8 3.0 %collective-permute-start.21 = (bf16[256,256]{1,0:T(8,128)(2,1)S(1)}, bf16[256,256]{1,0:T(8,128)(2,1)S(1)}, u32[]{:S(2)}, u32[]{:S(2)}) collective-permute-start(bf16[256,256]{1,0:T(8,128)(2,1)S(1)} %add_convert_fusion.refs_0_), channel_id=1, source_target_pairs={{0,4},{4,0},{8,12},{12,8},{16,20},{20,16},{24,28},{28,24},{1,5},{5... | collective-permute-start | bytes 393224 | tf_op jit(solution)/shard_map/ppermute | solution.py:35
  58.8 1.3 %collective-permute-start.20 = (bf16[256,256]{1,0:T(8,128)(2,1)S(1)}, bf16[256,256]{1,0:T(8,128)(2,1)S(1)}, u32[]{:S(2)}, u32[]{:S(2)}) collective-permute-start(bf16[256,256]{1,0:T(8,128)(2,1)S(1)} %collective-permute-done.18.refs_1_), channel_id=1, source_target_pairs={{0,4},{4,0},{8,12},{12,8},{16,20},{20,16},{24,28},{28,24},{1,5},{5... | collective-permute-start | bytes 393224 | tf_op jit(solution)/shard_map/ppermute | solution.py:35

commit v9 on v8

--- a/solution.py
+++ b/solution.py
@@ -137,29 +137,27 @@
     return jnp.concatenate([jnp.where(head == h, array, zero) for h in range(heads)], axis=0)
 
 
-def early_kernel(x_all, mine, beside, beside_values, swapped_in, total, total_values):
+def early_kernel(x_all, mine, beside, swapped_in, total):
     own = lax.axis_index("fsdp")
-    along = 1 + (lax.axis_index("seg") & 1)
+    along = 2 - (lax.axis_index("seg") & 1)
     rows, width = beside.shape
-    columns = lambda j: x_all[:, pl.ds(aligned(own ^ j, rows), rows)]
-    product = jnp.dot(columns(0), mine[0], preferred_element_type=f32) + jnp.dot(
-        columns(along ^ 3), swapped_in[...], preferred_element_type=f32
-    )
-    total[...] = product[:, :width] + jnp.dot(
-        columns(along), beside[...], preferred_element_type=f32
-    )
-    total_values[...] = product[:, width:] + jnp.dot(
-        columns(along), beside_values[...], preferred_element_type=f32
-    )
-
-
-def values_kernel(x_all, total, last, values):
-    rows = last.shape[0]
-    at = aligned(lax.axis_index("fsdp") ^ 3, rows)
-    columns = x_all[:, pl.ds(at, rows)]
-    values[...] = (
-        total[...] + jnp.dot(columns, last[...], preferred_element_type=f32)
-    ).astype(bf16)
+    product = 0.0
+    for j, piece in ((0, mine.at[0]), (along, beside), (along ^ 3, swapped_in)):
+        columns = x_all[:, pl.ds(aligned(own ^ j, rows), rows)]
+        product = product + jnp.dot(columns, piece[:, :width], preferred_element_type=f32)
+    total[...] = product
+
+
+def values_kernel(x_all, mine, beside, swapped_in, across, values):
+    own = lax.axis_index("fsdp")
+    along = 2 - (lax.axis_index("seg") & 1)
+    rows, width = beside.shape
+    total = 0.0
+    for j, piece in ((0, mine.at[0]), (along, beside), (along ^ 3, swapped_in), (3, across)):
+        columns = x_all[:, pl.ds(aligned(own ^ j, rows), rows)]
+        start = piece.shape[1] - width
+        total = total + jnp.dot(columns, piece[:, start:], preferred_element_type=f32)
+    values[...] = total.astype(bf16)
 
 
 def weights_kernel(heads, crossed, x_all, bias, *refs):
@@ -231,15 +229,21 @@
     blocks, keys, lanes = soft.shape
     queries = lanes // heads
     frames = segs * frame_count
-    wo[...] = wo_from[0][...]
-    back[...] = early[...]
+
+    def here():
+        wo[...] = wo_from[0][...]
+        back[...] = early[...]
+
+    def late():
+        wo[...] = wo_from[1][...]
+        back[...] = lax.dot_general(u_all[...], wo[...], NT, preferred_element_type=f32)
+
     if len(wo_from) > 1:
-
-        @pl.when((lax.axis_index("fsdp") ^ member_of()) == 3)
-        def _():
-            wo[...] = wo_from[1][...]
-            back[...] = lax.dot_general(u_all[...], wo[...], NT, preferred_element_type=f32)
-
+        opposite = (lax.axis_index("fsdp") ^ member_of()) == 3
+        pl.when(opposite)(late)
+        pl.when(jnp.logical_not(opposite))(here)
+    else:
+        here()
     row = lax.broadcasted_iota(jnp.int32, (queries, wo.shape[0]), 0)
     seg_of = jnp.where(row < frames, row // frame_count, row - frames - segs)
     first = lax.axis_index("seg") - member_of()
@@ -259,7 +263,7 @@
 
 def rows_kernel(which, x_turned, values, *outs):
     own = lax.axis_index("fsdp")
-    along = 1 + (lax.axis_index("seg") & 1)
+    along = 2 - (lax.axis_index("seg") & 1)
     parts = {"kept": (0, along ^ 3), "sent": (along, 3)}
     if which in parts:
         into = [outs[0].at[i] for i in range(2)]
@@ -356,7 +360,7 @@
 def pairs(seg_size):
     straight, turned, first, last = [], [], [], []
     for s in range(seg_size):
-        along = 2 if s & 1 else 1
+        along = 1 if s & 1 else 2
         for f in range(GROUP):
             straight.append((s * GROUP + f, s * GROUP + (f ^ along)))
             turned.append((s * GROUP + f, s * GROUP + (f ^ along ^ 3)))
@@ -418,13 +422,20 @@
     halo = [
         lax.ppermute(tail, "seg", [(s - 1, s + ahead) for s in starts]) for ahead in (0, 2)
     ]
+    bias = pl.pallas_call(
+        functools.partial(mask_kernel, heads, frame_count, segs, group),
+        out_specs=vmem,
+        out_shape=jax.ShapeDtypeStruct((2, keys, heads * queries), f32),
+        compiler_params=params(),
+        name="mask",
+    )()
     if crossed:
         both = ("seg", "fsdp")
         straight, turned, first, last = pairs(seg_size)
         came = lax.ppermute(own_blocks, both, straight)
         wo_came = lax.ppermute(w_out, both, first)
-        came, far, near, halo, wo_came = lax.optimization_barrier(
-            (came, far, near, halo, wo_came)
+        came, far, near, halo, wo_came, bias = lax.optimization_barrier(
+            (came, far, near, halo, wo_came, bias)
         )
         wo_last = lax.ppermute(wo_came, both, last)
     else:
@@ -473,9 +484,7 @@
         compiler_params=params(),
         name="merge",
     )(*parts)
-    x_all, wo_near, mine_values = lax.optimization_barrier((x_all, wo_near, mine_values))
-    if crossed:
-        forwarded_values = lax.ppermute(mine_values, both, turned)
+    x_all, wo_near = lax.optimization_barrier((x_all, wo_near))
 
     back = pl.pallas_call(
         back_kernel,
@@ -485,28 +494,20 @@
         compiler_params=params(),
         name="back",
     )(u_all, wo_near)
-    bias = pl.pallas_call(
-        functools.partial(mask_kernel, heads, frame_count, segs, group),
-        out_specs=vmem,
-        out_shape=jax.ShapeDtypeStruct((2, keys, heads * queries), f32),
-        compiler_params=params(),
-        name="mask",
-    )()
-    back, bias, x_all = lax.optimization_barrier((back, bias, x_all))
+    back, x_all = lax.optimization_barrier((back, x_all))
     soft_shape = jax.ShapeDtypeStruct((group, keys, heads * queries), bf16)
     values_shape = jax.ShapeDtypeStruct((all_rows, block), bf16)
     if crossed:
-        early, early_values = pl.pallas_call(
+        early = pl.pallas_call(
             early_kernel,
-            in_specs=[vmem] * 5,
-            out_specs=[vmem] * 2,
-            out_shape=[
-                jax.ShapeDtypeStruct((all_rows, 2 * block), f32),
-                jax.ShapeDtypeStruct((all_rows, block), f32),
-            ],
+            in_specs=[vmem] * 4,
+            out_specs=vmem,
+            out_shape=jax.ShapeDtypeStruct((all_rows, 2 * block), f32),
             compiler_params=params(),
             name="early",
-        )(x_all, own_blocks, mine, mine_values, other)
+        )(x_all, own_blocks, mine, other)
+        early, waiting = lax.optimization_barrier((early, mine_values))
+        forwarded_values = lax.ppermute(waiting, both, turned)
         wqkv_parts = [early, forwarded]
     soft, *values = pl.pallas_call(
         functools.partial(weights_kernel, heads, crossed),
@@ -520,12 +521,12 @@
     if crossed:
         values = pl.pallas_call(
             values_kernel,
-            in_specs=[vmem] * 3,
+            in_specs=[vmem] * 5,
             out_specs=vmem,
             out_shape=values_shape,
             compiler_params=params(),
             name="values",
-        )(x_all, early_values, forwarded_values)
+        )(x_all, own_blocks, mine_values, other, forwarded_values)
     else:
         (values,) = values
 
@@ -599,12 +600,11 @@
         grad_sum = grad_chunks[0].astype(f32)
         for j in range(1, fsdp_size):
             grad_sum = grad_sum + swapped(grad_chunks[j], "fsdp", j).astype(f32)
-    back = swapped(onward, "seg", 2)
-    back = swapped(onward, "seg", 2)
+    returned = swapped(onward, "seg", 2)
     bit = group
     while bit < seg_size:
         mine = grad_sum.astype(bf16)
-        other, back = lax.optimization_barrier((swapped(mine, "seg", bit), back))
+        other, returned = lax.optimization_barrier((swapped(mine, "seg", bit), returned))
         grad_sum = mine.astype(f32) + other.astype(f32)
         bit *= 2
     mine = grad_sum.astype(bf16)
@@ -618,7 +618,7 @@
         ],
         compiler_params=params(),
         name="finish",
-    )(lengths, frames.reshape(frame_rows, width), keep, back, *near)
+    )(lengths, frames.reshape(frame_rows, width), keep, returned, *near)
     far, frames_out, memory_out = lax.optimization_barrier(
         (swapped(mine, "seg", 2), frames_out, memory_out)
     )

time: 61.1 us -> 60.8 us (level)
  waiting for transfers between devices: 26.5 us -> 22.3 us
  starting transfers between devices: 20.9 us -> 24.2 us
    ppermute x1, starting transfers between devices: 0.01 us -> 3.01 us  [on_device(): forwarded = lax.ppermute(mine, both, turned)]
    ppermute x13, waiting for transfers between devices: 8.93 us -> 6.42 us  [swapped(): return lax.ppermute(array, axis, [(i, i ^ bit) for i in range(size)])]
    ppermute x1, starting transfers between devices: 2.38 us -> 0.07 us  [on_device(): came = lax.ppermute(sent, both, straight)]
    ppermute x1, waiting for transfers between devices: 11.5 us -> 9.66 us  [on_device(): wo_came = lax.ppermute(w_out, both, first)]
    ppermute x1, starting transfers between devices: 0.11 us -> 1.75 us  [on_device(): forwarded_values = lax.ppermute(waiting, both, turned)]
    ppermute x1, waiting for transfers between devices: 1.65 us -> 3.17 us  [on_device(): came = lax.ppermute(sent, both, straight)]
    ppermute x1, waiting for transfers between devices: 1.27 us -> 0.01 us  [on_device(): forwarded = lax.ppermute(mine, both, turned)]
    ppermute x1, starting transfers between devices: 2.69 us -> 3.39 us  [on_device(): wo_came = lax.ppermute(w_out, both, first)]
  transfers between devices with their start and end apart: 22 -> 22, of which waited for: 9 -> 8; matrix products, arithmetic and copies ran while one was open for 0% -> 0% of each run, Pallas kernels for 14% -> 14%
where the time goes in v9:
time: 60.8 us; the launch traced here: 60.6 us
  starting transfers between devices  24.2 us (40%)
  waiting for transfers between devices  22.3 us (37%)
  Pallas kernels  11.8 us (19%)
  between operations  1.57 us (3%)
  local copies, waits for them, and re-layouts  0.62 us (1%)
    ppermute x1, waiting for transfers between devices, on_device(): wo_came = lax.ppermute(w_out, both, first)  9.66 us
    ppermute x13, starting transfers between devices, swapped(): return lax.ppermute(array, axis, [(i, i ^ bit) for i in range(size)])  8.78 us
    ppermute x13, waiting for transfers between devices, swapped(): return lax.ppermute(array, axis, [(i, i ^ bit) for i in range(size)])  6.42 us
    ppermute x1, starting transfers between devices, on_device(): wo_came = lax.ppermute(w_out, both, first)  3.39 us
    ppermute x1, waiting for transfers between devices, on_device(): came = lax.ppermute(sent, both, straight)  3.17 us
    ppermute x1, starting transfers between devices, on_device(): came = lax.ppermute(own_blocks, both, straight)  3.03 us
    ppermute x1, starting transfers between devices, on_device(): forwarded = lax.ppermute(mine, both, turned)  3.01 us
    ppermute x1, waiting for transfers between devices, on_device(): last = lax.ppermute(passing, both, turned)  2.85 us
  transfers between devices with their start and end apart: 22, of which 8 were waited for; matrix products, arithmetic and copies ran while one was open for 0% of the time, Pallas kernels for 14%

profile of v9, /device:TPU:0, one launch (start us, length us, event | category | flops | bytes accessed | tf_op | source)
XLA Modules:
  0.0 60.6 jit_solution(8048100350597291745)
XLA Ops:
  0.6 2.6 %pack.1 = (bf16[2,256,768]{2,1,0:T(8,128)(2,1)}, bf16[288,1024]{1,0:T(8,128)(2,1)}, bf16[32,1024]{1,0:T(8,128)(2,1)}) custom-call(bf16[256,1024]{1,0:T(8,128)(2,1)} %wq.1, bf16[256,1024]{1,0:T(8,128)(2,1)} %wk.1, bf16[256,1024]{1,0:T(8,128)(2,1)} %wv.1, bf16[128,1024]{1,0:T(8,128)(2,1)} %bitcast.15, bf16[128,1024]{1,0:T(8,128)(2,1)} %bitcast.17, ...), custom_call_target="tpu_custom_call" | custom-call | tf_op jit(solution)/shard_map/pack/pallas_call | solution.py:395
  3.2 3.0 %collective-permute-start = (bf16[2,256,768]{2,1,0:T(8,128)(2,1)}, bf16[2,256,768]{2,1,0:T(8,128)(2,1)S(1)}, u32[]{:S(2)}, u32[]{:S(2)}) collective-permute-start(bf16[2,256,768]{2,1,0:T(8,128)(2,1)} %get-tuple-element.48.mine), channel_id=1, source_target_pairs={{0,2},{1,3},{2,0},{3,1},{4,5},{5,4},{6,7},{7,6},{8,10},{9,11},{10,... | collective-permute-start | bytes 2359304 | tf_op jit(solution)/shard_map/ppermute | solution.py:435
  6.3 1.6 %collective-permute-start.1 = (bf16[288,1024]{1,0:T(8,128)(2,1)}, bf16[288,1024]{1,0:T(8,128)(2,1)S(1)}, u32[]{:S(2)}, u32[]{:S(2)}) collective-permute-start(bf16[288,1024]{1,0:T(8,128)(2,1)} %get-tuple-element.46.tokens), channel_id=1, source_target_pairs={{0,8},{4,12},{8,0},{12,4},{16,24},{20,28},{24,16},{28,20},{1,9},{5... | collective-permute-start | bytes 1769480 | tf_op jit(solution)/shard_map/ppermute | solution.py:35
  7.8 3.4 %collective-permute-start.5 = (bf16[256,1024]{1,0:T(8,128)(2,1)S(1)}, bf16[256,1024]{1,0:T(8,128)(2,1)S(1)}, u32[]{:S(2)}, u32[]{:S(2)}) collective-permute-start(bf16[256,1024]{1,0:T(8,128)(2,1)S(1)} %copy-done.3), channel_id=1, source_target_pairs={{0,1},{4,2},{12,15},{5,4},{1,7},{9,10},{10,11},{14,8},{6,5},{15,14... | collective-permute-start | bytes 1572872 | tf_op jit(solution)/shard_map/ppermute | solution.py:436
  11.2 0.7 %collective-permute-start.3 = (bf16[32,1024]{1,0:T(8,128)(2,1)}, bf16[32,1024]{1,0:T(8,128)(2,1)S(1)}, u32[]{:S(2)}, u32[]{:S(2)}) collective-permute-start(bf16[32,1024]{1,0:T(8,128)(2,1)} %get-tuple-element.49), channel_id=1, source_target_pairs={{12,16},{13,17},{14,18},{15,19}} | collective-permute-start | bytes 196616 | tf_op jit(solution)/shard_map/ppermute | solution.py:423
  11.9 0.7 %collective-permute-start.4 = (bf16[32,1024]{1,0:T(8,128)(2,1)}, bf16[32,1024]{1,0:T(8,128)(2,1)S(1)}, u32[]{:S(2)}, u32[]{:S(2)}) collective-permute-start(bf16[32,1024]{1,0:T(8,128)(2,1)} %get-tuple-element.49), channel_id=1, source_target_pairs={{12,24},{13,25},{14,26},{15,27}} | collective-permute-start | bytes 196616 | tf_op jit(solution)/shard_map/ppermute | solution.py:423
  12.7 9.7 %collective-permute-done.5.came = bf16[256,1024]{1,0:T(8,128)(2,1)S(1)} collective-permute-done((bf16[256,1024]{1,0:T(8,128)(2,1)S(1)}, bf16[256,1024]{1,0:T(8,128)(2,1)S(1)}, u32[]{:S(2)}, u32[]{:S(2)}) %collective-permute-start.5) | collective-permute-done | bytes 524320 | tf_op jit(solution)/shard_map/ppermute | solution.py:436
  22.4 1.3 %collective-permute-start.10 = (bf16[256,1024]{1,0:T(8,128)(2,1)S(1)}, bf16[256,1024]{1,0:T(8,128)(2,1)S(1)}, u32[]{:S(2)}, u32[]{:S(2)}) collective-permute-start(bf16[256,1024]{1,0:T(8,128)(2,1)S(1)} %collective-permute-done.5.came), channel_id=1, source_target_pairs={{15,3},{10,6},{5,9},{0,12},{31,19},{26,22},{21,25},{16,28}} | collective-permute-start | bytes 1572872 | tf_op jit(solution)/shard_map/ppermute | solution.py:440
  23.9 0.5 collective-permute-start.6
  24.5 3.0 %collective-permute-start.9 = (bf16[256,512]{1,0:T(8,128)(2,1)S(1)}, bf16[256,512]{1,0:T(8,128)(2,1)S(1)}, u32[]{:S(2)}, u32[]{:S(2)}) collective-permute-start(bf16[256,512]{1,0:T(8,128)(2,1)S(1)} %get-tuple-element.66.beside), channel_id=1, source_target_pairs={{0,1},{1,0},{2,3},{3,2},{4,6},{5,7},{6,4},{7,5},{8,9},{9,8},{10,11... | collective-permute-start | bytes 786440 | tf_op jit(solution)/shard_map/ppermute | solution.py:462
  27.6 0.6 %merge.1 = (bf16[608,1024]{1,0:T(8,128)(2,1)S(1)}, bf16[1024,608]{1,0:T(8,128)(2,1)S(1)}, bf16[576,1024]{1,0:T(8,128)(2,1)S(1)}) custom-call(bf16[288,1024]{1,0:T(8,128)(2,1)S(1)} %copy-done.2, bf16[288,1024]{1,0:T(8,128)(2,1)S(1)} %collective-permute-done.2.near, bf16[176,1024]{1,0:T(8,128)(2,1)S(1)} %get-tuple-element.56.far, ...), custom_call_target="tpu_custom_call" | custom-call | tf_op jit(solution)/shard_map/merge/pallas_call | solution.py:475
  28.2 0.5 back.1.early
  28.8 0.6 copy-done
  29.4 0.6 %early.1.refs_0_ = f32[608,512]{1,0:T(8,128)S(1)} custom-call(bf16[608,1024]{1,0:T(8,128)(2,1)S(1)} %get-tuple-element.64.x_all, bf16[2,256,768]{2,1,0:T(8,128)(2,1)S(1)} %copy-done, bf16[256,512]{1,0:T(8,128)(2,1)S(1)} %get-tuple-element.66.beside, bf16[256,768]{1,0:T(8,128)(2,1)S(1)} %collective-permute-done.8.swapped_in), custom_call_target="tpu_custom_call" | custom-call | tf_op jit(solution)/shard_map/early/pallas_call | solution.py:501
  30.0 1.7 %collective-permute-start.12 = (bf16[256,256]{1,0:T(8,128)(2,1)S(1)}, bf16[256,256]{1,0:T(8,128)(2,1)S(1)}, u32[]{:S(2)}, u32[]{:S(2)}) collective-permute-start(bf16[256,256]{1,0:T(8,128)(2,1)S(1)} %get-tuple-element.73.beside), channel_id=1, source_target_pairs={{0,1},{1,0},{2,3},{3,2},{4,6},{5,7},{6,4},{7,5},{8,9},{9,8},{10,11... | collective-permute-start | bytes 393224 | tf_op jit(solution)/shard_map/ppermute | solution.py:510
  32.4 1.1 %soft_weights.1.soft = bf16[4,176,576]{2,1,0:T(8,128)(2,1)S(1)} custom-call(bf16[608,1024]{1,0:T(8,128)(2,1)S(1)} %get-tuple-element.64.x_all, f32[2,176,576]{2,1,0:T(8,128)S(1)} %mask.1.bias, f32[608,512]{1,0:T(8,128)S(1)} %early.1.refs_0_, bf16[256,512]{1,0:T(8,128)(2,1)S(1)} %collective-permute-done.9.refs_1_), custom_call_target="tpu_custom_call" | custom-call | tf_op jit(solution)/shard_map/soft_weights/pallas_call | solution.py:512
  33.5 1.2 %values_grad.1 = (bf16[256,1024]{1,0:T(8,128)(2,1)S(1)}, bf16[608,256]{1,0:T(8,128)(2,1)S(1)}, bf16[2,256,256]{2,1,0:T(8,128)(2,1)S(1)}) custom-call(s32[1]{0:T(128)S(6)} %copy.15.lengths, bf16[576,1024]{1,0:T(8,128)(2,1)S(1)} %get-tuple-element.59.u_all, bf16[4,176,576]{2,1,0:T(8,128)(2,1)S(1)} %soft_weights.1.soft, ...), custom_call_target="tpu_custom_call" | custom-call | tf_op jit(solution)/shard_map/values_grad/pallas_call | solution.py:536
  35.0 0.5 values.1
  35.6 0.7 %attend_far.1 = (f32[144,1024]{1,0:T(8,128)S(1)}, bf16[64,1024]{1,0:T(8,128)(2,1)S(1)}, bf16[80,1024]{1,0:T(8,128)(2,1)S(1)}) custom-call(bf16[4,176,576]{2,1,0:T(8,128)(2,1)S(1)} %soft_weights.1.soft, bf16[608,256]{1,0:T(8,128)(2,1)S(1)} %values.1, bf16[256,1024]{1,0:T(8,128)(2,1)S(1)} %get-tuple-element.74.refs_0_), custom_call_target="tpu_custom_call" | custom-call | tf_op jit(solution)/shard_map/attend_far/pallas_call | solution.py:570
  37.2 0.7 %collective-permute-done.13.refs_0_ = bf16[64,1024]{1,0:T(8,128)(2,1)S(1)} collective-permute-done((bf16[64,1024]{1,0:T(8,128)(2,1)S(1)}, bf16[64,1024]{1,0:T(8,128)(2,1)S(1)}, u32[]{:S(2)}, u32[]{:S(2)}) %collective-permute-start.13) | collective-permute-done | bytes 131104 | tf_op jit(solution)/shard_map/ppermute | solution.py:35
  38.0 3.2 %collective-permute-done.11 = bf16[2,256,256]{2,1,0:T(8,128)(2,1)S(1)} collective-permute-done((bf16[2,256,256]{2,1,0:T(8,128)(2,1)S(1)}, bf16[2,256,256]{2,1,0:T(8,128)(2,1)S(1)}, u32[]{:S(2)}, u32[]{:S(2)}) %collective-permute-start.11) | collective-permute-done | bytes 262176 | tf_op jit(solution)/shard_map/ppermute | solution.py:594
  41.2 1.5 %collective-permute-start.15 = (bf16[256,256]{1,0:T(8,128)(2,1)S(1)}, bf16[256,256]{1,0:T(8,128)(2,1)S(1)}, u32[]{:S(2)}, u32[]{:S(2)}) collective-permute-start(bf16[256,256]{1,0:T(8,128)(2,1)S(1)} %fusion.4), channel_id=1, source_target_pairs={{0,1},{1,0},{2,3},{3,2},{4,6},{5,7},{6,4},{7,5},{8,9},{9,8},{10,11... | collective-permute-start | bytes 393224 | tf_op jit(solution)/shard_map/ppermute | solution.py:597
  42.7 0.7 %collective-permute-start.17 = (bf16[144,1024]{1,0:T(8,128)(2,1)S(1)}, bf16[144,1024]{1,0:T(8,128)(2,1)S(1)}, u32[]{:S(2)}, u32[]{:S(2)}) collective-permute-start(bf16[144,1024]{1,0:T(8,128)(2,1)S(1)} %onward.1), channel_id=1, source_target_pairs={{0,8},{4,12},{8,0},{12,4},{16,24},{20,28},{24,16},{28,20},{1,9},{5... | collective-permute-start | bytes 884744 | tf_op jit(solution)/shard_map/ppermute | solution.py:35
  43.4 2.8 %collective-permute-done.15 = bf16[256,256]{1,0:T(8,128)(2,1)S(1)} collective-permute-done((bf16[256,256]{1,0:T(8,128)(2,1)S(1)}, bf16[256,256]{1,0:T(8,128)(2,1)S(1)}, u32[]{:S(2)}, u32[]{:S(2)}) %collective-permute-start.15) | collective-permute-done | bytes 131104 | tf_op jit(solution)/shard_map/ppermute | solution.py:597
  46.3 2.7 %collective-permute-start.16 = (bf16[256,256]{1,0:T(8,128)(2,1)S(1)}, bf16[256,256]{1,0:T(8,128)(2,1)S(1)}, u32[]{:S(2)}, u32[]{:S(2)}) collective-permute-start(bf16[256,256]{1,0:T(8,128)(2,1)S(1)} %fusion.3), channel_id=1, source_target_pairs={{0,16},{4,20},{8,24},{12,28},{16,0},{20,4},{24,8},{28,12},{1,17},{... | collective-permute-start | bytes 393224 | tf_op jit(solution)/shard_map/ppermute | solution.py:35
  48.9 0.7 %attend_near.1 = (f32[144,1024]{1,0:T(8,128)S(1)}, bf16[144,1024]{1,0:T(8,128)(2,1)S(1)}) custom-call(bf16[4,176,576]{2,1,0:T(8,128)(2,1)S(1)} %soft_weights.1.soft, bf16[608,256]{1,0:T(8,128)(2,1)S(1)} %values.1, bf16[256,1024]{1,0:T(8,128)(2,1)S(1)} %get-tuple-element.74.refs_0_), custom_call_target="tpu_custom_call" | custom-call | tf_op jit(solution)/shard_map/attend_near/pallas_call | solution.py:570
  49.7 3.2 %collective-permute-done.16 = bf16[256,256]{1,0:T(8,128)(2,1)S(1)} collective-permute-done((bf16[256,256]{1,0:T(8,128)(2,1)S(1)}, bf16[256,256]{1,0:T(8,128)(2,1)S(1)}, u32[]{:S(2)}, u32[]{:S(2)}) %collective-permute-start.16) | collective-permute-done | bytes 131104 | tf_op jit(solution)/shard_map/ppermute | solution.py:35
  53.0 2.6 %collective-permute-start.18 = (bf16[256,256]{1,0:T(8,128)(2,1)S(1)}, bf16[256,256]{1,0:T(8,128)(2,1)S(1)}, u32[]{:S(2)}, u32[]{:S(2)}) collective-permute-start(bf16[256,256]{1,0:T(8,128)(2,1)S(1)} %add_convert_fusion.refs_0_), channel_id=1, source_target_pairs={{0,8},{4,12},{8,0},{12,4},{16,24},{20,28},{24,16},{28,20},{1,9},{5... | collective-permute-start | bytes 393224 | tf_op jit(solution)/shard_map/ppermute | solution.py:35
  55.5 0.8 %finish.1 = (bf16[128,1024]{1,0:T(8,128)(2,1)}, bf16[8,1024]{1,0:T(8,128)(2,1)}) custom-call(s32[1]{0:T(128)S(6)} %copy.15.lengths, bf16[128,1024]{1,0:T(8,128)(2,1)S(1)} %bitcast.16, f32[144,1024]{1,0:T(8,128)S(1)} %get-tuple-element.81.keep, bf16[144,1024]{1,0:T(8,128)(2,1)S(1)} %collective-permute-done.17.back, ...), custom_call_target="tpu_custom_call" | custom-call | tf_op jit(solution)/shard_map/finish/pallas_call | solution.py:611
  56.4 2.1 %collective-permute-done.18.refs_1_ = bf16[256,256]{1,0:T(8,128)(2,1)S(1)} collective-permute-done((bf16[256,256]{1,0:T(8,128)(2,1)S(1)}, bf16[256,256]{1,0:T(8,128)(2,1)S(1)}, u32[]{:S(2)}, u32[]{:S(2)}) %collective-permute-start.18) | collective-permute-done | bytes 131104 | tf_op jit(solution)/shard_map/ppermute | solution.py:35
  58.5 0.9 %columns.1.refs_1_ = f32[256,1024]{1,0:T(8,128)} custom-call(bf16[256,256]{1,0:T(8,128)(2,1)S(1)} %add_convert_fusion.refs_0_, bf16[256,256]{1,0:T(8,128)(2,1)S(1)} %collective-permute-done.18.refs_1_, bf16[256,256]{1,0:T(8,128)(2,1)S(1)} %collective-permute-done.21.refs_2_), custom_call_target="tpu_custom_call" | custom-call | tf_op jit(solution)/shard_map/columns/pallas_call | solution.py:628
  59.8 0.7 %columns_rest.1 = f32[256,1024]{1,0:T(8,128)} custom-call(bf16[256,256]{1,0:T(8,128)(2,1)S(1)} %collective-permute-done.20.refs_0_, f32[256,1024]{1,0:T(8,128)} %columns.1.refs_1_), custom_call_target="tpu_custom_call", output_to_operand_aliasing={{}: (1, {})} | custom-call | tf_op jit(solution)/shard_map/columns_rest/pallas_call | solution.py:628
  (40 shorter events, 2.4 us)
Async XLA Ops:
  0.6 7.2 %copy-start.3 = (bf16[256,1024]{1,0:T(8,128)(2,1)S(1)}, bf16[256,1024]{1,0:T(8,128)(2,1)}, u32[]{:S(2)}) copy-start(bf16[256,1024]{1,0:T(8,128)(2,1)} %own) | copy-start | bytes 1572868
  3.2 19.2 %collective-permute-start = (bf16[2,256,768]{2,1,0:T(8,128)(2,1)}, bf16[2,256,768]{2,1,0:T(8,128)(2,1)S(1)}, u32[]{:S(2)}, u32[]{:S(2)}) collective-permute-start(bf16[2,256,768]{2,1,0:T(8,128)(2,1)} %get-tuple-element.48.mine), channel_id=1, source_target_pairs={{0,2},{1,3},{2,0},{3,1},{4,5},{5,4},{6,7},{7,6},{8,10},{9,11},{10,... | collective-permute-start | bytes 2359304 | tf_op jit(solution)/shard_map/ppermute | solution.py:435
  6.3 16.1 %collective-permute-start.1 = (bf16[288,1024]{1,0:T(8,128)(2,1)}, bf16[288,1024]{1,0:T(8,128)(2,1)S(1)}, u32[]{:S(2)}, u32[]{:S(2)}) collective-permute-start(bf16[288,1024]{1,0:T(8,128)(2,1)} %get-tuple-element.46.tokens), channel_id=1, source_target_pairs={{0,8},{4,12},{8,0},{12,4},{16,24},{20,28},{24,16},{28,20},{1,9},{5... | collective-permute-start | bytes 1769480 | tf_op jit(solution)/shard_map/ppermute | solution.py:35
  7.8 14.5 %collective-permute-start.2 = (bf16[288,1024]{1,0:T(8,128)(2,1)}, bf16[288,1024]{1,0:T(8,128)(2,1)S(1)}, u32[]{:S(2)}, u32[]{:S(2)}) collective-permute-start(bf16[288,1024]{1,0:T(8,128)(2,1)} %get-tuple-element.46.tokens), channel_id=1, source_target_pairs={{0,4},{4,0},{8,12},{12,8},{16,20},{20,16},{24,28},{28,24},{1,5},{5... | collective-permute-start | bytes 1769480 | tf_op jit(solution)/shard_map/ppermute | solution.py:35
  7.8 14.5 %collective-permute-start.5 = (bf16[256,1024]{1,0:T(8,128)(2,1)S(1)}, bf16[256,1024]{1,0:T(8,128)(2,1)S(1)}, u32[]{:S(2)}, u32[]{:S(2)}) collective-permute-start(bf16[256,1024]{1,0:T(8,128)(2,1)S(1)} %copy-done.3), channel_id=1, source_target_pairs={{0,1},{4,2},{12,15},{5,4},{1,7},{9,10},{10,11},{14,8},{6,5},{15,14... | collective-permute-start | bytes 1572872 | tf_op jit(solution)/shard_map/ppermute | solution.py:436
  11.2 0.7 %collective-permute-start.3 = (bf16[32,1024]{1,0:T(8,128)(2,1)}, bf16[32,1024]{1,0:T(8,128)(2,1)S(1)}, u32[]{:S(2)}, u32[]{:S(2)}) collective-permute-start(bf16[32,1024]{1,0:T(8,128)(2,1)} %get-tuple-element.49), channel_id=1, source_target_pairs={{12,16},{13,17},{14,18},{15,19}} | collective-permute-start | bytes 196616 | tf_op jit(solution)/shard_map/ppermute | solution.py:423
  11.9 0.8 %collective-permute-start.4 = (bf16[32,1024]{1,0:T(8,128)(2,1)}, bf16[32,1024]{1,0:T(8,128)(2,1)S(1)}, u32[]{:S(2)}, u32[]{:S(2)}) collective-permute-start(bf16[32,1024]{1,0:T(8,128)(2,1)} %get-tuple-element.49), channel_id=1, source_target_pairs={{12,24},{13,25},{14,26},{15,27}} | collective-permute-start | bytes 196616 | tf_op jit(solution)/shard_map/ppermute | solution.py:423
  12.7 14.9 %copy-start.2 = (bf16[288,1024]{1,0:T(8,128)(2,1)S(1)}, bf16[288,1024]{1,0:T(8,128)(2,1)}, u32[]{:S(2)}) copy-start(bf16[288,1024]{1,0:T(8,128)(2,1)} %get-tuple-element.46.tokens) | copy-start | bytes 1769476
  22.4 11.2 %collective-permute-start.10 = (bf16[256,1024]{1,0:T(8,128)(2,1)S(1)}, bf16[256,1024]{1,0:T(8,128)(2,1)S(1)}, u32[]{:S(2)}, u32[]{:S(2)}) collective-permute-start(bf16[256,1024]{1,0:T(8,128)(2,1)S(1)} %collective-permute-done.5.came), channel_id=1, source_target_pairs={{15,3},{10,6},{5,9},{0,12},{31,19},{26,22},{21,25},{16,28}} | collective-permute-start | bytes 1572872 | tf_op jit(solution)/shard_map/ppermute | solution.py:440
  23.8 4.9 %collective-permute-start.8 = (bf16[256,768]{1,0:T(8,128)(2,1)S(1)}, bf16[256,768]{1,0:T(8,128)(2,1)S(1)}, u32[]{:S(2)}, u32[]{:S(2)}) collective-permute-start(bf16[256,768]{1,0:T(8,128)(2,1)S(1)} %get-tuple-element.67), channel_id=1, source_target_pairs={{0,4},{4,0},{8,12},{12,8},{16,20},{20,16},{24,28},{28,24},{1,5},{5... | collective-permute-start | bytes 1179656 | tf_op jit(solution)/shard_map/ppermute | solution.py:35
  23.9 3.7 %collective-permute-start.6 = (bf16[176,1024]{1,0:T(8,128)(2,1)S(1)}, bf16[176,1024]{1,0:T(8,128)(2,1)S(1)}, u32[]{:S(2)}, u32[]{:S(2)}) collective-permute-start(bf16[176,1024]{1,0:T(8,128)(2,1)S(1)} %get-tuple-element.56.far), channel_id=1, source_target_pairs={{0,4},{4,0},{8,12},{12,8},{16,20},{20,16},{24,28},{28,24},{1,5},{5... | collective-permute-start | bytes 1081352 | tf_op jit(solution)/shard_map/ppermute | solution.py:35
  24.4 3.2 %collective-permute-start.7 = (bf16[144,1024]{1,0:T(8,128)(2,1)S(1)}, bf16[144,1024]{1,0:T(8,128)(2,1)S(1)}, u32[]{:S(2)}, u32[]{:S(2)}) collective-permute-start(bf16[144,1024]{1,0:T(8,128)(2,1)S(1)} %get-tuple-element.57.far_grads), channel_id=1, source_target_pairs={{0,4},{4,0},{8,12},{12,8},{16,20},{20,16},{24,28},{28,24},{1,5},{5... | collective-permute-start | bytes 884744 | tf_op jit(solution)/shard_map/ppermute | solution.py:35
  24.5 7.9 %collective-permute-start.9 = (bf16[256,512]{1,0:T(8,128)(2,1)S(1)}, bf16[256,512]{1,0:T(8,128)(2,1)S(1)}, u32[]{:S(2)}, u32[]{:S(2)}) collective-permute-start(bf16[256,512]{1,0:T(8,128)(2,1)S(1)} %get-tuple-element.66.beside), channel_id=1, source_target_pairs={{0,1},{1,0},{2,3},{3,2},{4,6},{5,7},{6,4},{7,5},{8,9},{9,8},{10,11... | collective-permute-start | bytes 786440 | tf_op jit(solution)/shard_map/ppermute | solution.py:462
  28.2 1.1 %copy-start = (bf16[2,256,768]{2,1,0:T(8,128)(2,1)S(1)}, bf16[2,256,768]{2,1,0:T(8,128)(2,1)}, u32[]{:S(2)}) copy-start(bf16[2,256,768]{2,1,0:T(8,128)(2,1)} %get-tuple-element.48.mine) | copy-start | bytes 2359300
  30.0 5.0 %collective-permute-start.12 = (bf16[256,256]{1,0:T(8,128)(2,1)S(1)}, bf16[256,256]{1,0:T(8,128)(2,1)S(1)}, u32[]{:S(2)}, u32[]{:S(2)}) collective-permute-start(bf16[256,256]{1,0:T(8,128)(2,1)S(1)} %get-tuple-element.73.beside), channel_id=1, source_target_pairs={{0,1},{1,0},{2,3},{3,2},{4,6},{5,7},{6,4},{7,5},{8,9},{9,8},{10,11... | collective-permute-start | bytes 393224 | tf_op jit(solution)/shard_map/ppermute | solution.py:510
  34.7 6.4 %collective-permute-start.11 = (bf16[2,256,256]{2,1,0:T(8,128)(2,1)S(1)}, bf16[2,256,256]{2,1,0:T(8,128)(2,1)S(1)}, u32[]{:S(2)}, u32[]{:S(2)}) collective-permute-start(bf16[2,256,256]{2,1,0:T(8,128)(2,1)S(1)} %get-tuple-element.72), channel_id=1, source_target_pairs={{0,2},{1,3},{2,0},{3,1},{4,5},{5,4},{6,7},{7,6},{8,10},{9,11},{10,... | collective-permute-start | bytes 786440 | tf_op jit(solution)/shard_map/ppermute | solution.py:594
  36.3 1.7 %collective-permute-start.14 = (bf16[80,1024]{1,0:T(8,128)(2,1)S(1)}, bf16[80,1024]{1,0:T(8,128)(2,1)S(1)}, u32[]{:S(2)}, u32[]{:S(2)}) collective-permute-start(bf16[80,1024]{1,0:T(8,128)(2,1)S(1)} %get-tuple-element.77), channel_id=1, source_target_pairs={{0,4},{4,0},{8,12},{12,8},{16,20},{20,16},{24,28},{28,24},{1,5},{5... | collective-permute-start | bytes 491528 | tf_op jit(solution)/shard_map/ppermute | solution.py:35
  36.5 1.4 %collective-permute-start.13 = (bf16[64,1024]{1,0:T(8,128)(2,1)S(1)}, bf16[64,1024]{1,0:T(8,128)(2,1)S(1)}, u32[]{:S(2)}, u32[]{:S(2)}) collective-permute-start(bf16[64,1024]{1,0:T(8,128)(2,1)S(1)} %get-tuple-element.76), channel_id=1, source_target_pairs={{0,4},{4,0},{8,12},{12,8},{16,20},{20,16},{24,28},{28,24},{1,5},{5... | collective-permute-start | bytes 393224 | tf_op jit(solution)/shard_map/ppermute | solution.py:35
  41.2 14.3 %copy-start.1 = (bf16[1,8,16,1024]{3,2,1,0:T(8,128)(2,1)S(1)}, bf16[1,8,16,1024]{3,2,1,0:T(8,128)(2,1)}, u32[]{:S(2)}) copy-start(bf16[1,8,16,1024]{3,2,1,0:T(8,128)(2,1)} %param.10) | copy-start | bytes 786436
  41.2 5.0 %collective-permute-start.15 = (bf16[256,256]{1,0:T(8,128)(2,1)S(1)}, bf16[256,256]{1,0:T(8,128)(2,1)S(1)}, u32[]{:S(2)}, u32[]{:S(2)}) collective-permute-start(bf16[256,256]{1,0:T(8,128)(2,1)S(1)} %fusion.4), channel_id=1, source_target_pairs={{0,1},{1,0},{2,3},{3,2},{4,6},{5,7},{6,4},{7,5},{8,9},{9,8},{10,11... | collective-permute-start | bytes 393224 | tf_op jit(solution)/shard_map/ppermute | solution.py:597
  42.7 10.2 %collective-permute-start.17 = (bf16[144,1024]{1,0:T(8,128)(2,1)S(1)}, bf16[144,1024]{1,0:T(8,128)(2,1)S(1)}, u32[]{:S(2)}, u32[]{:S(2)}) collective-permute-start(bf16[144,1024]{1,0:T(8,128)(2,1)S(1)} %onward.1), channel_id=1, source_target_pairs={{0,8},{4,12},{8,0},{12,4},{16,24},{20,28},{24,16},{28,20},{1,9},{5... | collective-permute-start | bytes 884744 | tf_op jit(solution)/shard_map/ppermute | solution.py:35
  46.3 6.6 %collective-permute-start.16 = (bf16[256,256]{1,0:T(8,128)(2,1)S(1)}, bf16[256,256]{1,0:T(8,128)(2,1)S(1)}, u32[]{:S(2)}, u32[]{:S(2)}) collective-permute-start(bf16[256,256]{1,0:T(8,128)(2,1)S(1)} %fusion.3), channel_id=1, source_target_pairs={{0,16},{4,20},{8,24},{12,28},{16,0},{20,4},{24,8},{28,12},{1,17},{... | collective-permute-start | bytes 393224 | tf_op jit(solution)/shard_map/ppermute | solution.py:35
  49.7 5.9 %collective-permute-start.19 = (bf16[144,1024]{1,0:T(8,128)(2,1)S(1)}, bf16[144,1024]{1,0:T(8,128)(2,1)S(1)}, u32[]{:S(2)}, u32[]{:S(2)}) collective-permute-start(bf16[144,1024]{1,0:T(8,128)(2,1)S(1)} %get-tuple-element.83), channel_id=1, source_target_pairs={{0,4},{4,0},{8,12},{12,8},{16,20},{20,16},{24,28},{28,24},{1,5},{5... | collective-permute-start | bytes 884744 | tf_op jit(solution)/shard_map/ppermute | solution.py:35
  53.0 5.5 %collective-permute-start.18 = (bf16[256,256]{1,0:T(8,128)(2,1)S(1)}, bf16[256,256]{1,0:T(8,128)(2,1)S(1)}, u32[]{:S(2)}, u32[]{:S(2)}) collective-permute-start(bf16[256,256]{1,0:T(8,128)(2,1)S(1)} %add_convert_fusion.refs_0_), channel_id=1, source_target_pairs={{0,8},{4,12},{8,0},{12,4},{16,24},{20,28},{24,16},{28,20},{1,9},{5... | collective-permute-start | bytes 393224 | tf_op jit(solution)/shard_map/ppermute | solution.py:35
  55.5 3.0 %collective-permute-start.21 = (bf16[256,256]{1,0:T(8,128)(2,1)S(1)}, bf16[256,256]{1,0:T(8,128)(2,1)S(1)}, u32[]{:S(2)}, u32[]{:S(2)}) collective-permute-start(bf16[256,256]{1,0:T(8,128)(2,1)S(1)} %add_convert_fusion.refs_0_), channel_id=1, source_target_pairs={{0,4},{4,0},{8,12},{12,8},{16,20},{20,16},{24,28},{28,24},{1,5},{5... | collective-permute-start | bytes 393224 | tf_op jit(solution)/shard_map/ppermute | solution.py:35
  58.5 1.3 %collective-permute-start.20 = (bf16[256,256]{1,0:T(8,128)(2,1)S(1)}, bf16[256,256]{1,0:T(8,128)(2,1)S(1)}, u32[]{:S(2)}, u32[]{:S(2)}) collective-permute-start(bf16[256,256]{1,0:T(8,128)(2,1)S(1)} %collective-permute-done.18.refs_1_), channel_id=1, source_target_pairs={{0,4},{4,0},{8,12},{12,8},{16,20},{20,16},{24,28},{28,24},{1,5},{5... | collective-permute-start | bytes 393224 | tf_op jit(solution)/shard_map/ppermute | solution.py:35

commit v10 on v9

--- a/solution.py
+++ b/solution.py
@@ -219,8 +219,14 @@
     bias[1] = jnp.where(valid_own | valid_halo, 0.0, masked_score)
 
 
-def back_kernel(u_all, wo, back):
-    back[...] = lax.dot_general(u_all[...], wo[...], NT, preferred_element_type=f32)
+def back_kernel(crossed, u_all, wo, back):
+    def product():
+        back[...] = lax.dot_general(u_all[...], wo[...], NT, preferred_element_type=f32)
+
+    if crossed:
+        pl.when((lax.axis_index("fsdp") ^ member_of()) != 3)(product)
+    else:
+        product()
 
 
 def grad_kernel(heads, frame_count, segs, crossed, lengths, u_all, soft, x_turned, early, *refs):
@@ -487,7 +493,7 @@
     x_all, wo_near = lax.optimization_barrier((x_all, wo_near))
 
     back = pl.pallas_call(
-        back_kernel,
+        functools.partial(back_kernel, crossed),
         in_specs=[vmem] * 2,
         out_specs=vmem,
         out_shape=jax.ShapeDtypeStruct((group * queries, block), f32),

time: 60.8 us -> 60.8 us (level)
  no operation moved by 1% of the time
where the time goes in v10:
time: 60.8 us; the launch traced here: 60.6 us
  starting transfers between devices  24.2 us (40%)
  waiting for transfers between devices  22.3 us (37%)
  Pallas kernels  11.8 us (19%)
  between operations  1.57 us (3%)
  local copies, waits for them, and re-layouts  0.61 us (1%)
    ppermute x1, waiting for transfers between devices, on_device(): wo_came = lax.ppermute(w_out, both, first)  9.66 us
    ppermute x13, starting transfers between devices, swapped(): return lax.ppermute(array, axis, [(i, i ^ bit) for i in range(size)])  8.78 us
    ppermute x13, waiting for transfers between devices, swapped(): return lax.ppermute(array, axis, [(i, i ^ bit) for i in range(size)])  6.42 us
    ppermute x1, starting transfers between devices, on_device(): wo_came = lax.ppermute(w_out, both, first)  3.39 us
    ppermute x1, waiting for transfers between devices, on_device(): came = lax.ppermute(sent, both, straight)  3.17 us
    ppermute x1, starting transfers between devices, on_device(): came = lax.ppermute(own_blocks, both, straight)  3.03 us
    ppermute x1, starting transfers between devices, on_device(): forwarded = lax.ppermute(mine, both, turned)  3.01 us
    ppermute x1, waiting for transfers between devices, on_device(): last = lax.ppermute(passing, both, turned)  2.85 us
  transfers between devices with their start and end apart: 22, of which 8 were waited for; matrix products, arithmetic and copies ran while one was open for 0% of the time, Pallas kernels for 14%

profile of v10, /device:TPU:0, one launch (start us, length us, event | category | flops | bytes accessed | tf_op | source)
XLA Modules:
  0.0 60.6 jit_solution(10797428988754123105)
XLA Ops:
  0.6 2.6 %pack.1 = (bf16[2,256,768]{2,1,0:T(8,128)(2,1)}, bf16[288,1024]{1,0:T(8,128)(2,1)}, bf16[32,1024]{1,0:T(8,128)(2,1)}) custom-call(bf16[256,1024]{1,0:T(8,128)(2,1)} %wq.1, bf16[256,1024]{1,0:T(8,128)(2,1)} %wk.1, bf16[256,1024]{1,0:T(8,128)(2,1)} %wv.1, bf16[128,1024]{1,0:T(8,128)(2,1)} %bitcast.15, bf16[128,1024]{1,0:T(8,128)(2,1)} %bitcast.17, ...), custom_call_target="tpu_custom_call" | custom-call | tf_op jit(solution)/shard_map/pack/pallas_call | solution.py:401
  3.2 3.0 %collective-permute-start = (bf16[2,256,768]{2,1,0:T(8,128)(2,1)}, bf16[2,256,768]{2,1,0:T(8,128)(2,1)S(1)}, u32[]{:S(2)}, u32[]{:S(2)}) collective-permute-start(bf16[2,256,768]{2,1,0:T(8,128)(2,1)} %get-tuple-element.48.mine), channel_id=1, source_target_pairs={{0,2},{1,3},{2,0},{3,1},{4,5},{5,4},{6,7},{7,6},{8,10},{9,11},{10,... | collective-permute-start | bytes 2359304 | tf_op jit(solution)/shard_map/ppermute | solution.py:441
  6.3 1.6 %collective-permute-start.1 = (bf16[288,1024]{1,0:T(8,128)(2,1)}, bf16[288,1024]{1,0:T(8,128)(2,1)S(1)}, u32[]{:S(2)}, u32[]{:S(2)}) collective-permute-start(bf16[288,1024]{1,0:T(8,128)(2,1)} %get-tuple-element.46.tokens), channel_id=1, source_target_pairs={{0,8},{4,12},{8,0},{12,4},{16,24},{20,28},{24,16},{28,20},{1,9},{5... | collective-permute-start | bytes 1769480 | tf_op jit(solution)/shard_map/ppermute | solution.py:35
  7.8 3.4 %collective-permute-start.5 = (bf16[256,1024]{1,0:T(8,128)(2,1)S(1)}, bf16[256,1024]{1,0:T(8,128)(2,1)S(1)}, u32[]{:S(2)}, u32[]{:S(2)}) collective-permute-start(bf16[256,1024]{1,0:T(8,128)(2,1)S(1)} %copy-done.3), channel_id=1, source_target_pairs={{0,1},{4,2},{12,15},{5,4},{1,7},{9,10},{10,11},{14,8},{6,5},{15,14... | collective-permute-start | bytes 1572872 | tf_op jit(solution)/shard_map/ppermute | solution.py:442
  11.2 0.7 %collective-permute-start.3 = (bf16[32,1024]{1,0:T(8,128)(2,1)}, bf16[32,1024]{1,0:T(8,128)(2,1)S(1)}, u32[]{:S(2)}, u32[]{:S(2)}) collective-permute-start(bf16[32,1024]{1,0:T(8,128)(2,1)} %get-tuple-element.49), channel_id=1, source_target_pairs={{12,16},{13,17},{14,18},{15,19}} | collective-permute-start | bytes 196616 | tf_op jit(solution)/shard_map/ppermute | solution.py:429
  11.9 0.7 %collective-permute-start.4 = (bf16[32,1024]{1,0:T(8,128)(2,1)}, bf16[32,1024]{1,0:T(8,128)(2,1)S(1)}, u32[]{:S(2)}, u32[]{:S(2)}) collective-permute-start(bf16[32,1024]{1,0:T(8,128)(2,1)} %get-tuple-element.49), channel_id=1, source_target_pairs={{12,24},{13,25},{14,26},{15,27}} | collective-permute-start | bytes 196616 | tf_op jit(solution)/shard_map/ppermute | solution.py:429
  12.7 9.7 %collective-permute-done.5.came = bf16[256,1024]{1,0:T(8,128)(2,1)S(1)} collective-permute-done((bf16[256,1024]{1,0:T(8,128)(2,1)S(1)}, bf16[256,1024]{1,0:T(8,128)(2,1)S(1)}, u32[]{:S(2)}, u32[]{:S(2)}) %collective-permute-start.5) | collective-permute-done | bytes 524320 | tf_op jit(solution)/shard_map/ppermute | solution.py:442
  22.4 1.3 %collective-permute-start.10 = (bf16[256,1024]{1,0:T(8,128)(2,1)S(1)}, bf16[256,1024]{1,0:T(8,128)(2,1)S(1)}, u32[]{:S(2)}, u32[]{:S(2)}) collective-permute-start(bf16[256,1024]{1,0:T(8,128)(2,1)S(1)} %collective-permute-done.5.came), channel_id=1, source_target_pairs={{15,3},{10,6},{5,9},{0,12},{31,19},{26,22},{21,25},{16,28}} | collective-permute-start | bytes 1572872 | tf_op jit(solution)/shard_map/ppermute | solution.py:446
  23.9 0.5 collective-permute-start.6
  24.5 3.0 %collective-permute-start.9 = (bf16[256,512]{1,0:T(8,128)(2,1)S(1)}, bf16[256,512]{1,0:T(8,128)(2,1)S(1)}, u32[]{:S(2)}, u32[]{:S(2)}) collective-permute-start(bf16[256,512]{1,0:T(8,128)(2,1)S(1)} %get-tuple-element.66.beside), channel_id=1, source_target_pairs={{0,1},{1,0},{2,3},{3,2},{4,6},{5,7},{6,4},{7,5},{8,9},{9,8},{10,11... | collective-permute-start | bytes 786440 | tf_op jit(solution)/shard_map/ppermute | solution.py:468
  27.6 0.6 %merge.1 = (bf16[608,1024]{1,0:T(8,128)(2,1)S(1)}, bf16[1024,608]{1,0:T(8,128)(2,1)S(1)}, bf16[576,1024]{1,0:T(8,128)(2,1)S(1)}) custom-call(bf16[288,1024]{1,0:T(8,128)(2,1)S(1)} %copy-done.2, bf16[288,1024]{1,0:T(8,128)(2,1)S(1)} %collective-permute-done.2.near, bf16[176,1024]{1,0:T(8,128)(2,1)S(1)} %get-tuple-element.56.far, ...), custom_call_target="tpu_custom_call" | custom-call | tf_op jit(solution)/shard_map/merge/pallas_call | solution.py:481
  28.2 0.5 back.1.early
  28.8 0.6 copy-done
  29.4 0.6 %early.1.refs_0_ = f32[608,512]{1,0:T(8,128)S(1)} custom-call(bf16[608,1024]{1,0:T(8,128)(2,1)S(1)} %get-tuple-element.64.x_all, bf16[2,256,768]{2,1,0:T(8,128)(2,1)S(1)} %copy-done, bf16[256,512]{1,0:T(8,128)(2,1)S(1)} %get-tuple-element.66.beside, bf16[256,768]{1,0:T(8,128)(2,1)S(1)} %collective-permute-done.8.swapped_in), custom_call_target="tpu_custom_call" | custom-call | tf_op jit(solution)/shard_map/early/pallas_call | solution.py:507
  30.0 1.7 %collective-permute-start.12 = (bf16[256,256]{1,0:T(8,128)(2,1)S(1)}, bf16[256,256]{1,0:T(8,128)(2,1)S(1)}, u32[]{:S(2)}, u32[]{:S(2)}) collective-permute-start(bf16[256,256]{1,0:T(8,128)(2,1)S(1)} %get-tuple-element.73.beside), channel_id=1, source_target_pairs={{0,1},{1,0},{2,3},{3,2},{4,6},{5,7},{6,4},{7,5},{8,9},{9,8},{10,11... | collective-permute-start | bytes 393224 | tf_op jit(solution)/shard_map/ppermute | solution.py:516
  32.4 1.1 %soft_weights.1.soft = bf16[4,176,576]{2,1,0:T(8,128)(2,1)S(1)} custom-call(bf16[608,1024]{1,0:T(8,128)(2,1)S(1)} %get-tuple-element.64.x_all, f32[2,176,576]{2,1,0:T(8,128)S(1)} %mask.1.bias, f32[608,512]{1,0:T(8,128)S(1)} %early.1.refs_0_, bf16[256,512]{1,0:T(8,128)(2,1)S(1)} %collective-permute-done.9.refs_1_), custom_call_target="tpu_custom_call" | custom-call | tf_op jit(solution)/shard_map/soft_weights/pallas_call | solution.py:518
  33.5 1.2 %values_grad.1 = (bf16[256,1024]{1,0:T(8,128)(2,1)S(1)}, bf16[608,256]{1,0:T(8,128)(2,1)S(1)}, bf16[2,256,256]{2,1,0:T(8,128)(2,1)S(1)}) custom-call(s32[1]{0:T(128)S(6)} %copy.15.lengths, bf16[576,1024]{1,0:T(8,128)(2,1)S(1)} %get-tuple-element.59.u_all, bf16[4,176,576]{2,1,0:T(8,128)(2,1)S(1)} %soft_weights.1.soft, ...), custom_call_target="tpu_custom_call" | custom-call | tf_op jit(solution)/shard_map/values_grad/pallas_call | solution.py:542
  35.0 0.5 values.1
  35.6 0.7 %attend_far.1 = (f32[144,1024]{1,0:T(8,128)S(1)}, bf16[64,1024]{1,0:T(8,128)(2,1)S(1)}, bf16[80,1024]{1,0:T(8,128)(2,1)S(1)}) custom-call(bf16[4,176,576]{2,1,0:T(8,128)(2,1)S(1)} %soft_weights.1.soft, bf16[608,256]{1,0:T(8,128)(2,1)S(1)} %values.1, bf16[256,1024]{1,0:T(8,128)(2,1)S(1)} %get-tuple-element.74.refs_0_), custom_call_target="tpu_custom_call" | custom-call | tf_op jit(solution)/shard_map/attend_far/pallas_call | solution.py:576
  37.2 0.7 %collective-permute-done.13.refs_0_ = bf16[64,1024]{1,0:T(8,128)(2,1)S(1)} collective-permute-done((bf16[64,1024]{1,0:T(8,128)(2,1)S(1)}, bf16[64,1024]{1,0:T(8,128)(2,1)S(1)}, u32[]{:S(2)}, u32[]{:S(2)}) %collective-permute-start.13) | collective-permute-done | bytes 131104 | tf_op jit(solution)/shard_map/ppermute | solution.py:35
  38.0 3.2 %collective-permute-done.11 = bf16[2,256,256]{2,1,0:T(8,128)(2,1)S(1)} collective-permute-done((bf16[2,256,256]{2,1,0:T(8,128)(2,1)S(1)}, bf16[2,256,256]{2,1,0:T(8,128)(2,1)S(1)}, u32[]{:S(2)}, u32[]{:S(2)}) %collective-permute-start.11) | collective-permute-done | bytes 262176 | tf_op jit(solution)/shard_map/ppermute | solution.py:600
  41.2 1.5 %collective-permute-start.15 = (bf16[256,256]{1,0:T(8,128)(2,1)S(1)}, bf16[256,256]{1,0:T(8,128)(2,1)S(1)}, u32[]{:S(2)}, u32[]{:S(2)}) collective-permute-start(bf16[256,256]{1,0:T(8,128)(2,1)S(1)} %fusion.4), channel_id=1, source_target_pairs={{0,1},{1,0},{2,3},{3,2},{4,6},{5,7},{6,4},{7,5},{8,9},{9,8},{10,11... | collective-permute-start | bytes 393224 | tf_op jit(solution)/shard_map/ppermute | solution.py:603
  42.7 0.7 %collective-permute-start.17 = (bf16[144,1024]{1,0:T(8,128)(2,1)S(1)}, bf16[144,1024]{1,0:T(8,128)(2,1)S(1)}, u32[]{:S(2)}, u32[]{:S(2)}) collective-permute-start(bf16[144,1024]{1,0:T(8,128)(2,1)S(1)} %onward.1), channel_id=1, source_target_pairs={{0,8},{4,12},{8,0},{12,4},{16,24},{20,28},{24,16},{28,20},{1,9},{5... | collective-permute-start | bytes 884744 | tf_op jit(solution)/shard_map/ppermute | solution.py:35
  43.4 2.8 %collective-permute-done.15 = bf16[256,256]{1,0:T(8,128)(2,1)S(1)} collective-permute-done((bf16[256,256]{1,0:T(8,128)(2,1)S(1)}, bf16[256,256]{1,0:T(8,128)(2,1)S(1)}, u32[]{:S(2)}, u32[]{:S(2)}) %collective-permute-start.15) | collective-permute-done | bytes 131104 | tf_op jit(solution)/shard_map/ppermute | solution.py:603
  46.3 2.7 %collective-permute-start.16 = (bf16[256,256]{1,0:T(8,128)(2,1)S(1)}, bf16[256,256]{1,0:T(8,128)(2,1)S(1)}, u32[]{:S(2)}, u32[]{:S(2)}) collective-permute-start(bf16[256,256]{1,0:T(8,128)(2,1)S(1)} %fusion.3), channel_id=1, source_target_pairs={{0,16},{4,20},{8,24},{12,28},{16,0},{20,4},{24,8},{28,12},{1,17},{... | collective-permute-start | bytes 393224 | tf_op jit(solution)/shard_map/ppermute | solution.py:35
  48.9 0.7 %attend_near.1 = (f32[144,1024]{1,0:T(8,128)S(1)}, bf16[144,1024]{1,0:T(8,128)(2,1)S(1)}) custom-call(bf16[4,176,576]{2,1,0:T(8,128)(2,1)S(1)} %soft_weights.1.soft, bf16[608,256]{1,0:T(8,128)(2,1)S(1)} %values.1, bf16[256,1024]{1,0:T(8,128)(2,1)S(1)} %get-tuple-element.74.refs_0_), custom_call_target="tpu_custom_call" | custom-call | tf_op jit(solution)/shard_map/attend_near/pallas_call | solution.py:576
  49.7 3.2 %collective-permute-done.16 = bf16[256,256]{1,0:T(8,128)(2,1)S(1)} collective-permute-done((bf16[256,256]{1,0:T(8,128)(2,1)S(1)}, bf16[256,256]{1,0:T(8,128)(2,1)S(1)}, u32[]{:S(2)}, u32[]{:S(2)}) %collective-permute-start.16) | collective-permute-done | bytes 131104 | tf_op jit(solution)/shard_map/ppermute | solution.py:35
  53.0 2.6 %collective-permute-start.18 = (bf16[256,256]{1,0:T(8,128)(2,1)S(1)}, bf16[256,256]{1,0:T(8,128)(2,1)S(1)}, u32[]{:S(2)}, u32[]{:S(2)}) collective-permute-start(bf16[256,256]{1,0:T(8,128)(2,1)S(1)} %add_convert_fusion.refs_0_), channel_id=1, source_target_pairs={{0,8},{4,12},{8,0},{12,4},{16,24},{20,28},{24,16},{28,20},{1,9},{5... | collective-permute-start | bytes 393224 | tf_op jit(solution)/shard_map/ppermute | solution.py:35
  55.5 0.8 %finish.1 = (bf16[128,1024]{1,0:T(8,128)(2,1)}, bf16[8,1024]{1,0:T(8,128)(2,1)}) custom-call(s32[1]{0:T(128)S(6)} %copy.15.lengths, bf16[128,1024]{1,0:T(8,128)(2,1)S(1)} %bitcast.16, f32[144,1024]{1,0:T(8,128)S(1)} %get-tuple-element.81.keep, bf16[144,1024]{1,0:T(8,128)(2,1)S(1)} %collective-permute-done.17.back, ...), custom_call_target="tpu_custom_call" | custom-call | tf_op jit(solution)/shard_map/finish/pallas_call | solution.py:617
  56.4 2.1 %collective-permute-done.18.refs_1_ = bf16[256,256]{1,0:T(8,128)(2,1)S(1)} collective-permute-done((bf16[256,256]{1,0:T(8,128)(2,1)S(1)}, bf16[256,256]{1,0:T(8,128)(2,1)S(1)}, u32[]{:S(2)}, u32[]{:S(2)}) %collective-permute-start.18) | collective-permute-done | bytes 131104 | tf_op jit(solution)/shard_map/ppermute | solution.py:35
  58.5 0.9 %columns.1.refs_1_ = f32[256,1024]{1,0:T(8,128)} custom-call(bf16[256,256]{1,0:T(8,128)(2,1)S(1)} %add_convert_fusion.refs_0_, bf16[256,256]{1,0:T(8,128)(2,1)S(1)} %collective-permute-done.18.refs_1_, bf16[256,256]{1,0:T(8,128)(2,1)S(1)} %collective-permute-done.21.refs_2_), custom_call_target="tpu_custom_call" | custom-call | tf_op jit(solution)/shard_map/columns/pallas_call | solution.py:634
  59.8 0.7 %columns_rest.1 = f32[256,1024]{1,0:T(8,128)} custom-call(bf16[256,256]{1,0:T(8,128)(2,1)S(1)} %collective-permute-done.20.refs_0_, f32[256,1024]{1,0:T(8,128)} %columns.1.refs_1_), custom_call_target="tpu_custom_call", output_to_operand_aliasing={{}: (1, {})} | custom-call | tf_op jit(solution)/shard_map/columns_rest/pallas_call | solution.py:634
  (40 shorter events, 2.4 us)
Async XLA Ops:
  0.6 7.2 %copy-start.3 = (bf16[256,1024]{1,0:T(8,128)(2,1)S(1)}, bf16[256,1024]{1,0:T(8,128)(2,1)}, u32[]{:S(2)}) copy-start(bf16[256,1024]{1,0:T(8,128)(2,1)} %own) | copy-start | bytes 1572868
  3.2 19.2 %collective-permute-start = (bf16[2,256,768]{2,1,0:T(8,128)(2,1)}, bf16[2,256,768]{2,1,0:T(8,128)(2,1)S(1)}, u32[]{:S(2)}, u32[]{:S(2)}) collective-permute-start(bf16[2,256,768]{2,1,0:T(8,128)(2,1)} %get-tuple-element.48.mine), channel_id=1, source_target_pairs={{0,2},{1,3},{2,0},{3,1},{4,5},{5,4},{6,7},{7,6},{8,10},{9,11},{10,... | collective-permute-start | bytes 2359304 | tf_op jit(solution)/shard_map/ppermute | solution.py:441
  6.3 16.1 %collective-permute-start.1 = (bf16[288,1024]{1,0:T(8,128)(2,1)}, bf16[288,1024]{1,0:T(8,128)(2,1)S(1)}, u32[]{:S(2)}, u32[]{:S(2)}) collective-permute-start(bf16[288,1024]{1,0:T(8,128)(2,1)} %get-tuple-element.46.tokens), channel_id=1, source_target_pairs={{0,8},{4,12},{8,0},{12,4},{16,24},{20,28},{24,16},{28,20},{1,9},{5... | collective-permute-start | bytes 1769480 | tf_op jit(solution)/shard_map/ppermute | solution.py:35
  7.8 14.5 %collective-permute-start.2 = (bf16[288,1024]{1,0:T(8,128)(2,1)}, bf16[288,1024]{1,0:T(8,128)(2,1)S(1)}, u32[]{:S(2)}, u32[]{:S(2)}) collective-permute-start(bf16[288,1024]{1,0:T(8,128)(2,1)} %get-tuple-element.46.tokens), channel_id=1, source_target_pairs={{0,4},{4,0},{8,12},{12,8},{16,20},{20,16},{24,28},{28,24},{1,5},{5... | collective-permute-start | bytes 1769480 | tf_op jit(solution)/shard_map/ppermute | solution.py:35
  7.8 14.5 %collective-permute-start.5 = (bf16[256,1024]{1,0:T(8,128)(2,1)S(1)}, bf16[256,1024]{1,0:T(8,128)(2,1)S(1)}, u32[]{:S(2)}, u32[]{:S(2)}) collective-permute-start(bf16[256,1024]{1,0:T(8,128)(2,1)S(1)} %copy-done.3), channel_id=1, source_target_pairs={{0,1},{4,2},{12,15},{5,4},{1,7},{9,10},{10,11},{14,8},{6,5},{15,14... | collective-permute-start | bytes 1572872 | tf_op jit(solution)/shard_map/ppermute | solution.py:442
  11.2 0.7 %collective-permute-start.3 = (bf16[32,1024]{1,0:T(8,128)(2,1)}, bf16[32,1024]{1,0:T(8,128)(2,1)S(1)}, u32[]{:S(2)}, u32[]{:S(2)}) collective-permute-start(bf16[32,1024]{1,0:T(8,128)(2,1)} %get-tuple-element.49), channel_id=1, source_target_pairs={{12,16},{13,17},{14,18},{15,19}} | collective-permute-start | bytes 196616 | tf_op jit(solution)/shard_map/ppermute | solution.py:429
  11.9 0.8 %collective-permute-start.4 = (bf16[32,1024]{1,0:T(8,128)(2,1)}, bf16[32,1024]{1,0:T(8,128)(2,1)S(1)}, u32[]{:S(2)}, u32[]{:S(2)}) collective-permute-start(bf16[32,1024]{1,0:T(8,128)(2,1)} %get-tuple-element.49), channel_id=1, source_target_pairs={{12,24},{13,25},{14,26},{15,27}} | collective-permute-start | bytes 196616 | tf_op jit(solution)/shard_map/ppermute | solution.py:429
  12.7 14.9 %copy-start.2 = (bf16[288,1024]{1,0:T(8,128)(2,1)S(1)}, bf16[288,1024]{1,0:T(8,128)(2,1)}, u32[]{:S(2)}) copy-start(bf16[288,1024]{1,0:T(8,128)(2,1)} %get-tuple-element.46.tokens) | copy-start | bytes 1769476
  22.4 11.2 %collective-permute-start.10 = (bf16[256,1024]{1,0:T(8,128)(2,1)S(1)}, bf16[256,1024]{1,0:T(8,128)(2,1)S(1)}, u32[]{:S(2)}, u32[]{:S(2)}) collective-permute-start(bf16[256,1024]{1,0:T(8,128)(2,1)S(1)} %collective-permute-done.5.came), channel_id=1, source_target_pairs={{15,3},{10,6},{5,9},{0,12},{31,19},{26,22},{21,25},{16,28}} | collective-permute-start | bytes 1572872 | tf_op jit(solution)/shard_map/ppermute | solution.py:446
  23.8 4.9 %collective-permute-start.8 = (bf16[256,768]{1,0:T(8,128)(2,1)S(1)}, bf16[256,768]{1,0:T(8,128)(2,1)S(1)}, u32[]{:S(2)}, u32[]{:S(2)}) collective-permute-start(bf16[256,768]{1,0:T(8,128)(2,1)S(1)} %get-tuple-element.67), channel_id=1, source_target_pairs={{0,4},{4,0},{8,12},{12,8},{16,20},{20,16},{24,28},{28,24},{1,5},{5... | collective-permute-start | bytes 1179656 | tf_op jit(solution)/shard_map/ppermute | solution.py:35
  23.9 3.7 %collective-permute-start.6 = (bf16[176,1024]{1,0:T(8,128)(2,1)S(1)}, bf16[176,1024]{1,0:T(8,128)(2,1)S(1)}, u32[]{:S(2)}, u32[]{:S(2)}) collective-permute-start(bf16[176,1024]{1,0:T(8,128)(2,1)S(1)} %get-tuple-element.56.far), channel_id=1, source_target_pairs={{0,4},{4,0},{8,12},{12,8},{16,20},{20,16},{24,28},{28,24},{1,5},{5... | collective-permute-start | bytes 1081352 | tf_op jit(solution)/shard_map/ppermute | solution.py:35
  24.4 3.2 %collective-permute-start.7 = (bf16[144,1024]{1,0:T(8,128)(2,1)S(1)}, bf16[144,1024]{1,0:T(8,128)(2,1)S(1)}, u32[]{:S(2)}, u32[]{:S(2)}) collective-permute-start(bf16[144,1024]{1,0:T(8,128)(2,1)S(1)} %get-tuple-element.57.far_grads), channel_id=1, source_target_pairs={{0,4},{4,0},{8,12},{12,8},{16,20},{20,16},{24,28},{28,24},{1,5},{5... | collective-permute-start | bytes 884744 | tf_op jit(solution)/shard_map/ppermute | solution.py:35
  24.5 7.9 %collective-permute-start.9 = (bf16[256,512]{1,0:T(8,128)(2,1)S(1)}, bf16[256,512]{1,0:T(8,128)(2,1)S(1)}, u32[]{:S(2)}, u32[]{:S(2)}) collective-permute-start(bf16[256,512]{1,0:T(8,128)(2,1)S(1)} %get-tuple-element.66.beside), channel_id=1, source_target_pairs={{0,1},{1,0},{2,3},{3,2},{4,6},{5,7},{6,4},{7,5},{8,9},{9,8},{10,11... | collective-permute-start | bytes 786440 | tf_op jit(solution)/shard_map/ppermute | solution.py:468
  28.2 1.1 %copy-start = (bf16[2,256,768]{2,1,0:T(8,128)(2,1)S(1)}, bf16[2,256,768]{2,1,0:T(8,128)(2,1)}, u32[]{:S(2)}) copy-start(bf16[2,256,768]{2,1,0:T(8,128)(2,1)} %get-tuple-element.48.mine) | copy-start | bytes 2359300
  30.0 5.0 %collective-permute-start.12 = (bf16[256,256]{1,0:T(8,128)(2,1)S(1)}, bf16[256,256]{1,0:T(8,128)(2,1)S(1)}, u32[]{:S(2)}, u32[]{:S(2)}) collective-permute-start(bf16[256,256]{1,0:T(8,128)(2,1)S(1)} %get-tuple-element.73.beside), channel_id=1, source_target_pairs={{0,1},{1,0},{2,3},{3,2},{4,6},{5,7},{6,4},{7,5},{8,9},{9,8},{10,11... | collective-permute-start | bytes 393224 | tf_op jit(solution)/shard_map/ppermute | solution.py:516
  34.7 6.4 %collective-permute-start.11 = (bf16[2,256,256]{2,1,0:T(8,128)(2,1)S(1)}, bf16[2,256,256]{2,1,0:T(8,128)(2,1)S(1)}, u32[]{:S(2)}, u32[]{:S(2)}) collective-permute-start(bf16[2,256,256]{2,1,0:T(8,128)(2,1)S(1)} %get-tuple-element.72), channel_id=1, source_target_pairs={{0,2},{1,3},{2,0},{3,1},{4,5},{5,4},{6,7},{7,6},{8,10},{9,11},{10,... | collective-permute-start | bytes 786440 | tf_op jit(solution)/shard_map/ppermute | solution.py:600
  36.3 1.7 %collective-permute-start.14 = (bf16[80,1024]{1,0:T(8,128)(2,1)S(1)}, bf16[80,1024]{1,0:T(8,128)(2,1)S(1)}, u32[]{:S(2)}, u32[]{:S(2)}) collective-permute-start(bf16[80,1024]{1,0:T(8,128)(2,1)S(1)} %get-tuple-element.77), channel_id=1, source_target_pairs={{0,4},{4,0},{8,12},{12,8},{16,20},{20,16},{24,28},{28,24},{1,5},{5... | collective-permute-start | bytes 491528 | tf_op jit(solution)/shard_map/ppermute | solution.py:35
  36.5 1.4 %collective-permute-start.13 = (bf16[64,1024]{1,0:T(8,128)(2,1)S(1)}, bf16[64,1024]{1,0:T(8,128)(2,1)S(1)}, u32[]{:S(2)}, u32[]{:S(2)}) collective-permute-start(bf16[64,1024]{1,0:T(8,128)(2,1)S(1)} %get-tuple-element.76), channel_id=1, source_target_pairs={{0,4},{4,0},{8,12},{12,8},{16,20},{20,16},{24,28},{28,24},{1,5},{5... | collective-permute-start | bytes 393224 | tf_op jit(solution)/shard_map/ppermute | solution.py:35
  41.2 14.3 %copy-start.1 = (bf16[1,8,16,1024]{3,2,1,0:T(8,128)(2,1)S(1)}, bf16[1,8,16,1024]{3,2,1,0:T(8,128)(2,1)}, u32[]{:S(2)}) copy-start(bf16[1,8,16,1024]{3,2,1,0:T(8,128)(2,1)} %param.10) | copy-start | bytes 786436
  41.2 5.0 %collective-permute-start.15 = (bf16[256,256]{1,0:T(8,128)(2,1)S(1)}, bf16[256,256]{1,0:T(8,128)(2,1)S(1)}, u32[]{:S(2)}, u32[]{:S(2)}) collective-permute-start(bf16[256,256]{1,0:T(8,128)(2,1)S(1)} %fusion.4), channel_id=1, source_target_pairs={{0,1},{1,0},{2,3},{3,2},{4,6},{5,7},{6,4},{7,5},{8,9},{9,8},{10,11... | collective-permute-start | bytes 393224 | tf_op jit(solution)/shard_map/ppermute | solution.py:603
  42.7 10.2 %collective-permute-start.17 = (bf16[144,1024]{1,0:T(8,128)(2,1)S(1)}, bf16[144,1024]{1,0:T(8,128)(2,1)S(1)}, u32[]{:S(2)}, u32[]{:S(2)}) collective-permute-start(bf16[144,1024]{1,0:T(8,128)(2,1)S(1)} %onward.1), channel_id=1, source_target_pairs={{0,8},{4,12},{8,0},{12,4},{16,24},{20,28},{24,16},{28,20},{1,9},{5... | collective-permute-start | bytes 884744 | tf_op jit(solution)/shard_map/ppermute | solution.py:35
  46.3 6.6 %collective-permute-start.16 = (bf16[256,256]{1,0:T(8,128)(2,1)S(1)}, bf16[256,256]{1,0:T(8,128)(2,1)S(1)}, u32[]{:S(2)}, u32[]{:S(2)}) collective-permute-start(bf16[256,256]{1,0:T(8,128)(2,1)S(1)} %fusion.3), channel_id=1, source_target_pairs={{0,16},{4,20},{8,24},{12,28},{16,0},{20,4},{24,8},{28,12},{1,17},{... | collective-permute-start | bytes 393224 | tf_op jit(solution)/shard_map/ppermute | solution.py:35
  49.7 5.9 %collective-permute-start.19 = (bf16[144,1024]{1,0:T(8,128)(2,1)S(1)}, bf16[144,1024]{1,0:T(8,128)(2,1)S(1)}, u32[]{:S(2)}, u32[]{:S(2)}) collective-permute-start(bf16[144,1024]{1,0:T(8,128)(2,1)S(1)} %get-tuple-element.83), channel_id=1, source_target_pairs={{0,4},{4,0},{8,12},{12,8},{16,20},{20,16},{24,28},{28,24},{1,5},{5... | collective-permute-start | bytes 884744 | tf_op jit(solution)/shard_map/ppermute | solution.py:35
  53.0 5.5 %collective-permute-start.18 = (bf16[256,256]{1,0:T(8,128)(2,1)S(1)}, bf16[256,256]{1,0:T(8,128)(2,1)S(1)}, u32[]{:S(2)}, u32[]{:S(2)}) collective-permute-start(bf16[256,256]{1,0:T(8,128)(2,1)S(1)} %add_convert_fusion.refs_0_), channel_id=1, source_target_pairs={{0,8},{4,12},{8,0},{12,4},{16,24},{20,28},{24,16},{28,20},{1,9},{5... | collective-permute-start | bytes 393224 | tf_op jit(solution)/shard_map/ppermute | solution.py:35
  55.5 3.0 %collective-permute-start.21 = (bf16[256,256]{1,0:T(8,128)(2,1)S(1)}, bf16[256,256]{1,0:T(8,128)(2,1)S(1)}, u32[]{:S(2)}, u32[]{:S(2)}) collective-permute-start(bf16[256,256]{1,0:T(8,128)(2,1)S(1)} %add_convert_fusion.refs_0_), channel_id=1, source_target_pairs={{0,4},{4,0},{8,12},{12,8},{16,20},{20,16},{24,28},{28,24},{1,5},{5... | collective-permute-start | bytes 393224 | tf_op jit(solution)/shard_map/ppermute | solution.py:35
  58.5 1.3 %collective-permute-start.20 = (bf16[256,256]{1,0:T(8,128)(2,1)S(1)}, bf16[256,256]{1,0:T(8,128)(2,1)S(1)}, u32[]{:S(2)}, u32[]{:S(2)}) collective-permute-start(bf16[256,256]{1,0:T(8,128)(2,1)S(1)} %collective-permute-done.18.refs_1_), channel_id=1, source_target_pairs={{0,4},{4,0},{8,12},{12,8},{16,20},{20,16},{24,28},{28,24},{1,5},{5... | collective-permute-start | bytes 393224 | tf_op jit(solution)/shard_map/ppermute | solution.py:35
